TPU v7x, 128 devices: a whole 4x4x4 slice. The times are simulated.
128 devices in a mesh: dp: 64 (over z_lo, y, x, core), mp: 2 (over z_hi).
Axes of the slice: x: 4, y: 4, z: 4 (z_hi: 2, z_lo: 2; z = z_hi * 2 + z_lo), core: 2. Of those that a mesh axis runs over, the one named last changes fastest.
Arguments:
- lowres_in: bfloat16 [384, 1, 24, 1024], P('dp'), may hold values from -6 to 6
- highres_in: bfloat16 [768, 1, 48, 1536], P('dp'), may hold values from -6 to 6
- image_sizes: int32 [16], replicated, may hold values from 24 to 48, as said below
- attn_gain: bfloat16 [1024], replicated, may hold values from 0.5 to 1.5
- query_weight: bfloat16 [1024, 1024], P('dp', 'mp'), may hold values from -0.1875 to 0.1875
- key_weight: bfloat16 [1024, 1024], P('dp', 'mp'), may hold values from -0.1875 to 0.1875
- value_weight: bfloat16 [1024, 1024], P('dp', 'mp'), may hold values from -0.1875 to 0.1875
- output_weight: bfloat16 [1024, 1024], P('mp', 'dp'), may hold values from -0.75 to 0.75
- mlp_gain: bfloat16 [1024], replicated, may hold values from 0.5 to 1.5
- up_weight: bfloat16 [1024, 4096], P('dp', 'mp'), may hold values from -0.1875 to 0.1875
- down_weight: bfloat16 [4096, 1024], P('mp', 'dp'), may hold values from -0.09375 to 0.09375
- depth_kernel: bfloat16 [49, 1536], replicated, may hold values from -0.875 to 0.875
- conv_gain: bfloat16 [1536], replicated, may hold values from 0.5 to 1.5
- expand_weight: bfloat16 [1536, 6144], P('dp', 'mp'), may hold values from -0.15625 to 0.15625
- shrink_weight: bfloat16 [6144, 1536], P('mp', 'dp'), may hold values from -0.078125 to 0.078125
- layer_scale: bfloat16 [1536], replicated, may hold values from 0.5 to 1.5
- adapter_weight: bfloat16 [1536, 1024], P('dp', 'mp'), may hold values from -0.15625 to 0.15625
- adapter_kernel: bfloat16 [9, 1024], P(None, 'mp'), may hold values from -2 to 2
- gate_vector: bfloat16 [1024], replicated, may hold values from -0.1875 to 0.1875
- out_cotangent: bfloat16 [384, 1, 24, 1024], P('dp', None, None, 'mp'), may hold values from -6 to 6
- map_cotangent: bfloat16 [768, 1, 48, 1536], P('dp'), may hold values from -6 to 6
Outputs:
- mixed_out: bfloat16 [384, 1, 24, 1024], P('dp', None, None, 'mp')
- map_out: bfloat16 [768, 1, 48, 1536], P('dp')
- lowres_grad: float32 [384, 1, 24, 1024], P('dp')
- highres_grad: float32 [768, 1, 48, 1536], P('dp')
- attn_gain_grad: float32 [1024], replicated
- query_weight_grad: float32 [1024, 1024], P('dp', 'mp')
- key_weight_grad: float32 [1024, 1024], P('dp', 'mp')
- value_weight_grad: float32 [1024, 1024], P('dp', 'mp')
- output_weight_grad: float32 [1024, 1024], P('mp', 'dp')
- mlp_gain_grad: float32 [1024], replicated
- up_weight_grad: float32 [1024, 4096], P('dp', 'mp')
- down_weight_grad: float32 [4096, 1024], P('mp', 'dp')
- depth_kernel_grad: float32 [49, 1536], replicated
- conv_gain_grad: float32 [1536], replicated
- expand_weight_grad: float32 [1536, 6144], P('dp', 'mp')
- shrink_weight_grad: float32 [6144, 1536], P('mp', 'dp')
- layer_scale_grad: float32 [1536], replicated
- adapter_weight_grad: float32 [1536, 1024], P('dp', 'mp')
- adapter_kernel_grad: float32 [9, 1024], P(None, 'mp')
- gate_vector_grad: float32 [1024], replicated
Inputs may be any that keep to these rules, and one draw needn't show every extreme that they name: `image_sizes`: each image's valid side is 24, 32 or 48, and at least one image has 48.
All inputs are finite; a program needn't handle non-finite values.
Results may differ from a plain program's by a relative error of at most 0.018.
Values may be sent and summed in bfloat16 or wider, within the bound.
No kernel may reach another device: no remote copies, remote signals or barrier semaphores. Data moves between devices by JAX's collectives and lax.ppermute only.
A program may use at most 256 MiB of HBM per device.

v0:
```python
import jax
import jax.numpy as jnp
from jax import lax
from jax.sharding import PartitionSpec as P

HD = 64
TILES = 4


norm_epsilon = 1e-06


def passed_along(value, axis, steps):
    count = lax.axis_size(axis)
    pairs = [(source, (source + steps) % count) for source in range(count)]
    return lax.ppermute(value, axis, pairs)


def with_halo(block, sides, width):
    for axis, dim in sides:
        count = lax.axis_size(axis)
        forward = [(i, i + 1) for i in range(count - 1)]
        forward.append((count - 1, 0))
        backward = [(target, source) for source, target in forward]
        low = lax.ppermute(
            lax.slice_in_dim(block, block.shape[dim] - width, None, axis=dim), axis, forward
        )
        high = lax.ppermute(lax.slice_in_dim(block, 0, width, axis=dim), axis, backward)
        block = jnp.concatenate([low, block, high], axis=dim)
    return block


def normalize(values, scale_gain):
    average = jnp.mean(values, axis=-1, keepdims=True)
    centred = values - average
    spread = jnp.mean(centred * centred, axis=-1, keepdims=True)
    return centred * lax.rsqrt(spread + norm_epsilon) * scale_gain


def gelu_exact(values):
    return jax.nn.gelu(values, approximate=False)


def matmul(former, latter):
    return jnp.dot(former, latter, preferred_element_type=jnp.float32)


def matmul_nt(former, latter):
    return lax.dot_general(
        former, latter, (((1,), (1,)), ((), ())), preferred_element_type=jnp.float32
    )


def matmul_tn(former, latter):
    return lax.dot_general(
        former, latter, (((0,), (0,)), ((), ())), preferred_element_type=jnp.float32
    )


def across_model(values):
    return lax.psum(values.astype(jnp.bfloat16), "mp").astype(jnp.float32)


def group_shift(values, offset):
    return passed_along(values, "dp", offset)


def group_return(values, offset):
    return passed_along(values.astype(jnp.bfloat16), "dp", offset).astype(values.dtype)


def trimmed(padded, radius, position):
    extent = padded.shape[0]
    places = jnp.arange(extent)
    keep_top = (places >= radius) | (position != 0)
    keep_bottom = (places < extent - radius) | (position != TILES - 1)
    retain = (keep_top & keep_bottom).astype(padded.dtype)
    return padded * retain.reshape((extent,) + (1,) * (padded.ndim - 1))


def depth_apply(padded, kernel, radius):
    height = padded.shape[0] - 2 * radius
    breadth = padded.shape[2]
    window = 2 * radius + 1
    widened = jnp.pad(padded, ((0, 0), (0, 0), (radius, radius), (0, 0)))
    summed = jnp.zeros((height,) + padded.shape[1:], jnp.float32)
    for row_shift in range(window):
        for col_shift in range(window):
            summed = (
                summed
                + widened[row_shift : row_shift + height, :, col_shift : col_shift + breadth]
                * kernel[row_shift * window + col_shift]
            )
    return summed


def kernel_slopes(padded, gradient, radius):
    height = gradient.shape[0]
    breadth = gradient.shape[2]
    window = 2 * radius + 1
    widened = jnp.pad(padded, ((0, 0), (0, 0), (radius, radius), (0, 0)))
    columns = []
    for row_shift in range(window):
        for col_shift in range(window):
            columns.append(
                jnp.sum(
                    widened[row_shift : row_shift + height, :, col_shift : col_shift + breadth]
                    * gradient,
                    axis=(0, 1, 2),
                )
            )
    return jnp.stack(columns, 0)


def by_image(values, low_strip, image_count):
    grid_side = values.shape[0] // (low_strip * image_count)
    shaped = values.reshape(low_strip, image_count, grid_side, values.shape[1])
    return shaped.transpose(1, 0, 2, 3).reshape(image_count, low_strip * grid_side, values.shape[1])


def by_token(values, low_strip):
    image_count = values.shape[0]
    grid_side = values.shape[1] // low_strip
    shaped = values.reshape(image_count, low_strip, grid_side, values.shape[2])
    return shaped.transpose(1, 0, 2, 3).reshape(
        low_strip * image_count * grid_side, values.shape[2]
    )


def on_device(
    lowres_in,
    highres_in,
    image_sizes,
    attn_gain,
    query_weight,
    key_weight,
    value_weight,
    output_weight,
    mlp_gain,
    up_weight,
    down_weight,
    depth_kernel,
    conv_gain,
    expand_weight,
    shrink_weight,
    layer_scale,
    adapter_weight,
    adapter_kernel,
    gate_vector,
    out_cotangent,
    map_cotangent,
):
    device = lax.axis_index("dp")
    group_count = lax.axis_size("dp") // TILES
    position = (device + 2) % TILES
    group_id = (device + 2) // TILES % group_count
    model_half = lax.axis_index("mp")
    low_strip, image_count, grid_side, width = lowres_in.shape
    high_strip = highres_in.shape[0]
    high_side = highres_in.shape[2]
    channels = highres_in.shape[3]
    own_width = adapter_kernel.shape[1]
    local_width = query_weight.shape[1]
    local_heads = local_width // HD
    scaling = HD ** (-0.5)
    token_count = low_strip * image_count * grid_side
    pixel_count = high_strip * image_count * high_side
    piece_length = low_strip * grid_side
    gathered = (
        lax.all_gather(query_weight, "dp", axis=0, tiled=True),
        lax.all_gather(key_weight, "dp", axis=0, tiled=True),
        lax.all_gather(value_weight, "dp", axis=0, tiled=True),
        lax.all_gather(output_weight, "dp", axis=1, tiled=True),
        lax.all_gather(up_weight, "dp", axis=0, tiled=True),
        lax.all_gather(down_weight, "dp", axis=1, tiled=True),
        lax.all_gather(expand_weight, "dp", axis=0, tiled=True),
        lax.all_gather(shrink_weight, "dp", axis=1, tiled=True),
        lax.all_gather(adapter_weight, "dp", axis=0, tiled=True),
    )
    (
        query_full,
        key_full,
        value_full,
        output_full,
        up_full,
        down_full,
        expand_full,
        shrink_full,
        adapter_full,
    ) = gathered
    first_image = group_id * image_count
    image_ids = first_image + jnp.arange(image_count)
    table_ids = jnp.arange(image_sizes.shape[0])
    extents = jnp.sum(
        jnp.where(table_ids[None, :] == image_ids[:, None], image_sizes[None, :], 0), axis=1
    )
    row_ids = position * high_strip + jnp.arange(high_strip)
    col_ids = jnp.arange(high_side)
    valid_mask = (
        (row_ids[:, None, None] < extents[None, :, None])
        & (col_ids[None, None, :] < extents[None, :, None])
    ).astype(jnp.float32)[..., None]
    token_rows = lowres_in.astype(jnp.float32).reshape(token_count, width)
    normed, attn_norm_back = jax.vjp(normalize, token_rows, attn_gain.astype(jnp.float32))
    normed_low = normed.astype(jnp.bfloat16)
    queries = matmul(normed_low, query_full).astype(jnp.bfloat16)
    key_rows = matmul(normed_low, key_full).astype(jnp.bfloat16)
    value_rows = matmul(normed_low, value_full).astype(jnp.bfloat16)
    own_pair = jnp.stack(
        [by_image(key_rows, low_strip, image_count), by_image(value_rows, low_strip, image_count)],
        0,
    )
    collected = [own_pair]
    for offset in range(1, TILES):
        nearer = group_shift(own_pair, offset)
        wrapped = group_shift(own_pair, offset - TILES)
        collected.append(jnp.where(position >= offset, nearer, wrapped))
    stacked = jnp.stack(collected, 0)
    order = (position - jnp.arange(TILES)) % TILES
    ordered = jnp.take(stacked, order, axis=0)
    key_pieces = ordered[:, 0]
    value_pieces = ordered[:, 1]
    key_all = key_pieces.transpose(1, 0, 2, 3).reshape(
        image_count, TILES * piece_length, local_heads, HD
    )
    value_all = value_pieces.transpose(1, 0, 2, 3).reshape(
        image_count, TILES * piece_length, local_heads, HD
    )
    query_heads = by_image(queries, low_strip, image_count).reshape(
        image_count, piece_length, local_heads, HD
    )
    scores = (
        jnp.einsum("gqhd,gkhd->ghqk", query_heads, key_all, preferred_element_type=jnp.float32)
        * scaling
    )
    top_score = jnp.max(scores, axis=-1, keepdims=True)
    log_total = top_score + jnp.log(jnp.sum(jnp.exp(scores - top_score), axis=-1, keepdims=True))
    attention_low = jnp.exp(scores - log_total).astype(jnp.bfloat16)
    attended = jnp.einsum(
        "ghqk,gkhd->gqhd", attention_low, value_all, preferred_element_type=jnp.float32
    )
    attended_low = by_token(
        attended.reshape(image_count, piece_length, local_width), low_strip
    ).astype(jnp.bfloat16)
    hidden_rows = token_rows + across_model(matmul(attended_low, output_full))
    normed_two, mlp_norm_back = jax.vjp(normalize, hidden_rows, mlp_gain.astype(jnp.float32))
    normed_two_low = normed_two.astype(jnp.bfloat16)
    expanded = matmul(normed_two_low, up_full)
    activated, up_gelu_back = jax.vjp(gelu_exact, expanded)
    activated_low = activated.astype(jnp.bfloat16)
    result_rows = hidden_rows + across_model(matmul(activated_low, down_full))
    map_low = (highres_in.astype(jnp.float32) * valid_mask).astype(jnp.bfloat16)
    map_padded = trimmed(with_halo(map_low, (("dp", 0),), 3), 3, position).astype(jnp.float32)
    kernel_wide = depth_kernel.astype(jnp.float32)
    convolved = depth_apply(map_padded, kernel_wide, 3).reshape(pixel_count, channels)
    normed_map, conv_norm_back = jax.vjp(normalize, convolved, conv_gain.astype(jnp.float32))
    normed_map_low = normed_map.astype(jnp.bfloat16)
    widened = matmul(normed_map_low, expand_full)
    widened_act, wide_gelu_back = jax.vjp(gelu_exact, widened)
    widened_low = widened_act.astype(jnp.bfloat16)
    narrowed = across_model(matmul(widened_low, shrink_full)).reshape(
        high_strip, image_count, high_side, channels
    )
    scale_wide = layer_scale.astype(jnp.float32)
    mapped = valid_mask * (map_low.astype(jnp.float32) + scale_wide * narrowed)
    pooled = (
        jnp.sum(mapped.reshape(low_strip, 2, image_count, grid_side, 2, channels), axis=(1, 4))
        * 0.25
    )
    pooled_low = pooled.reshape(token_count, channels).astype(jnp.bfloat16)
    lifted = matmul(pooled_low, adapter_full).reshape(low_strip, image_count, grid_side, own_width)
    result_grid = result_rows.reshape(low_strip, image_count, grid_side, width)
    own_result = lax.dynamic_slice_in_dim(result_grid, model_half * own_width, own_width, 3)
    own_low = own_result.astype(jnp.bfloat16)
    own_padded = trimmed(with_halo(own_low, (("dp", 0),), 1), 1, position).astype(jnp.float32)
    adapter_wide = adapter_kernel.astype(jnp.float32)
    local_mix = depth_apply(own_padded, adapter_wide, 1)
    gate_wide = gate_vector.astype(jnp.float32)
    gating = jax.nn.sigmoid(jnp.sum(result_grid * gate_wide, axis=-1, keepdims=True))
    blended = own_result + local_mix + gating * lifted
    gathered = (
        lax.all_gather(query_weight, "dp", axis=0, tiled=True),
        lax.all_gather(key_weight, "dp", axis=0, tiled=True),
        lax.all_gather(value_weight, "dp", axis=0, tiled=True),
        lax.all_gather(output_weight, "dp", axis=1, tiled=True),
        lax.all_gather(up_weight, "dp", axis=0, tiled=True),
        lax.all_gather(down_weight, "dp", axis=1, tiled=True),
        lax.all_gather(expand_weight, "dp", axis=0, tiled=True),
        lax.all_gather(shrink_weight, "dp", axis=1, tiled=True),
        lax.all_gather(adapter_weight, "dp", axis=0, tiled=True),
    )
    (
        query_full,
        key_full,
        value_full,
        output_full,
        up_full,
        down_full,
        expand_full,
        shrink_full,
        adapter_full,
    ) = gathered
    out_grad = out_cotangent.astype(jnp.float32)
    local_grad_low = out_grad.astype(jnp.bfloat16)
    lifted_grad_low = (out_grad * gating).reshape(token_count, own_width).astype(jnp.bfloat16)
    gate_part = jnp.sum(out_grad * lifted, axis=-1, keepdims=True)
    pooled_part = matmul_nt(lifted_grad_low, adapter_full)
    pooled_grad, gate_grad = (
        lax.psum(pooled_part.astype(jnp.bfloat16), "mp").astype(jnp.float32),
        lax.psum(gate_part.astype(jnp.bfloat16), "mp").astype(jnp.float32),
    )
    adapter_weight_slope = matmul_tn(pooled_low, lifted_grad_low)
    local_padded = trimmed(with_halo(local_grad_low, (("dp", 0),), 1), 1, position).astype(
        jnp.float32
    )
    own_grad = out_grad + depth_apply(local_padded, adapter_wide[::-1], 1)
    adapter_kernel_slope = kernel_slopes(own_padded, local_grad_low.astype(jnp.float32), 1)
    result_grad = lax.all_gather(own_grad.astype(jnp.bfloat16), "mp", axis=3, tiled=True).astype(
        own_grad.dtype
    )
    gate_slope = gate_grad * gating * (1.0 - gating)
    gate_vector_slope = jnp.sum((gate_slope * result_grid).reshape(token_count, width), axis=0)
    result_grad = (result_grad + gate_slope * gate_wide).reshape(token_count, width)
    pooled_spread = jnp.broadcast_to(
        (pooled_grad * 0.25).reshape(low_strip, 1, image_count, grid_side, 1, channels),
        (low_strip, 2, image_count, grid_side, 2, channels),
    ).reshape(high_strip, image_count, high_side, channels)
    map_grad = (map_cotangent.astype(jnp.float32) + pooled_spread) * valid_mask
    narrowed_grad_low = (map_grad * scale_wide).reshape(pixel_count, channels).astype(jnp.bfloat16)
    layer_scale_slope = jnp.sum((map_grad * narrowed).reshape(pixel_count, channels), axis=0)
    widened_grad = matmul_nt(narrowed_grad_low, shrink_full)
    shrink_weight_slope = matmul_tn(widened_low, narrowed_grad_low)
    widened_grad_low = wide_gelu_back(widened_grad)[0].astype(jnp.bfloat16)
    expand_weight_slope = matmul_tn(normed_map_low, widened_grad_low)
    normed_map_grad = across_model(matmul_nt(widened_grad_low, expand_full))
    convolved_grad, conv_gain_slope = conv_norm_back(normed_map_grad)
    convolved_grad_low = convolved_grad.reshape(
        high_strip, image_count, high_side, channels
    ).astype(jnp.bfloat16)
    grad_padded = trimmed(with_halo(convolved_grad_low, (("dp", 0),), 3), 3, position).astype(
        jnp.float32
    )
    highres_grad = (map_grad + depth_apply(grad_padded, kernel_wide[::-1], 3)) * valid_mask
    depth_kernel_slope = kernel_slopes(map_padded, convolved_grad_low.astype(jnp.float32), 3)
    result_low = result_grad.astype(jnp.bfloat16)
    activated_grad = matmul_nt(result_low, down_full)
    down_weight_slope = matmul_tn(activated_low, result_low)
    expanded_grad_low = up_gelu_back(activated_grad)[0].astype(jnp.bfloat16)
    up_weight_slope = matmul_tn(normed_two_low, expanded_grad_low)
    normed_two_grad = across_model(matmul_nt(expanded_grad_low, up_full))
    hidden_part, mlp_gain_slope = mlp_norm_back(normed_two_grad)
    hidden_grad = result_grad + hidden_part
    hidden_low = hidden_grad.astype(jnp.bfloat16)
    attended_grad_low = matmul_nt(hidden_low, output_full).astype(jnp.bfloat16)
    output_weight_slope = matmul_tn(attended_low, hidden_low)
    attended_heads_grad = by_image(attended_grad_low, low_strip, image_count).reshape(
        image_count, piece_length, local_heads, HD
    )
    scores_again = (
        jnp.einsum("gqhd,gkhd->ghqk", query_heads, key_all, preferred_element_type=jnp.float32)
        * scaling
    )
    attention_again = jnp.exp(scores_again - log_total)
    attention_again_low = attention_again.astype(jnp.bfloat16)
    attention_grad = jnp.einsum(
        "gqhd,gkhd->ghqk", attended_heads_grad, value_all, preferred_element_type=jnp.float32
    )
    row_dot = jnp.sum(attention_again * attention_grad, axis=-1, keepdims=True)
    score_grad_low = (attention_again * (attention_grad - row_dot)).astype(jnp.bfloat16)
    query_grad_low = (
        jnp.einsum("ghqk,gkhd->gqhd", score_grad_low, key_all, preferred_element_type=jnp.float32)
        * scaling
    ).astype(jnp.bfloat16)
    key_grad_all = (
        jnp.einsum(
            "ghqk,gqhd->gkhd", score_grad_low, query_heads, preferred_element_type=jnp.float32
        )
        * scaling
    )
    value_grad_all = jnp.einsum(
        "ghqk,gqhd->gkhd",
        attention_again_low,
        attended_heads_grad,
        preferred_element_type=jnp.float32,
    )
    key_back = key_grad_all.reshape(image_count, TILES, piece_length, local_width).transpose(
        1, 0, 2, 3
    )
    value_back = value_grad_all.reshape(image_count, TILES, piece_length, local_width).transpose(
        1, 0, 2, 3
    )
    pair_back = jnp.stack([key_back, value_back], 1)
    pair_total = lax.dynamic_index_in_dim(pair_back, position, 0, keepdims=False)
    for offset in range(1, TILES):
        outgoing = lax.dynamic_index_in_dim(
            pair_back, (position - offset) % TILES, 0, keepdims=False
        )
        nearer = group_return(outgoing, -offset)
        wrapped = group_return(outgoing, TILES - offset)
        pair_total = pair_total + jnp.where(position + offset < TILES, nearer, wrapped)
    key_grad_low = by_token(pair_total[0], low_strip).astype(jnp.bfloat16)
    value_grad_low = by_token(pair_total[1], low_strip).astype(jnp.bfloat16)
    query_grad_rows = by_token(
        query_grad_low.reshape(image_count, piece_length, local_width), low_strip
    )
    normed_part = (
        matmul_nt(query_grad_rows, query_full)
        + matmul_nt(key_grad_low, key_full)
        + matmul_nt(value_grad_low, value_full)
    )
    query_weight_slope = matmul_tn(normed_low, query_grad_rows)
    key_weight_slope = matmul_tn(normed_low, key_grad_low)
    value_weight_slope = matmul_tn(normed_low, value_grad_low)
    normed_grad = across_model(normed_part)
    input_part, attn_gain_slope = attn_norm_back(normed_grad)
    lowres_grad = (hidden_grad + input_part).reshape(low_strip, image_count, grid_side, width)
    slopes = (
        lax.psum_scatter(query_weight_slope, "dp", scatter_dimension=0, tiled=True),
        lax.psum_scatter(key_weight_slope, "dp", scatter_dimension=0, tiled=True),
        lax.psum_scatter(value_weight_slope, "dp", scatter_dimension=0, tiled=True),
        lax.psum_scatter(output_weight_slope, "dp", scatter_dimension=1, tiled=True),
        lax.psum_scatter(up_weight_slope, "dp", scatter_dimension=0, tiled=True),
        lax.psum_scatter(down_weight_slope, "dp", scatter_dimension=1, tiled=True),
        lax.psum_scatter(expand_weight_slope, "dp", scatter_dimension=0, tiled=True),
        lax.psum_scatter(shrink_weight_slope, "dp", scatter_dimension=1, tiled=True),
        lax.psum_scatter(adapter_weight_slope, "dp", scatter_dimension=0, tiled=True),
    )
    minor_slopes = lax.psum(
        (
            attn_gain_slope,
            mlp_gain_slope,
            depth_kernel_slope,
            conv_gain_slope,
            layer_scale_slope,
            adapter_kernel_slope,
            gate_vector_slope,
        ),
        "dp",
    )
    return (
        blended.astype(jnp.bfloat16),
        mapped.astype(jnp.bfloat16),
        lowres_grad,
        highres_grad,
        minor_slopes[0],
        slopes[0],
        slopes[1],
        slopes[2],
        slopes[3],
        minor_slopes[1],
        slopes[4],
        slopes[5],
        minor_slopes[2],
        minor_slopes[3],
        slopes[6],
        slopes[7],
        minor_slopes[4],
        slopes[8],
        minor_slopes[5],
        minor_slopes[6],
    )


def solution(mesh):
    in_specs = (
        P("dp", None, None, None),
        P("dp", None, None, None),
        P(),
        P(),
        P("dp", "mp"),
        P("dp", "mp"),
        P("dp", "mp"),
        P("mp", "dp"),
        P(),
        P("dp", "mp"),
        P("mp", "dp"),
        P(),
        P(),
        P("dp", "mp"),
        P("mp", "dp"),
        P(),
        P("dp", "mp"),
        P(None, "mp"),
        P(),
        P("dp", None, None, "mp"),
        P("dp", None, None, None),
    )
    out_specs = (
        P("dp", None, None, "mp"),
        P("dp", None, None, None),
        P("dp", None, None, None),
        P("dp", None, None, None),
        P(),
        P("dp", "mp"),
        P("dp", "mp"),
        P("dp", "mp"),
        P("mp", "dp"),
        P(),
        P("dp", "mp"),
        P("mp", "dp"),
        P(),
        P(),
        P("dp", "mp"),
        P("mp", "dp"),
        P(),
        P("dp", "mp"),
        P(None, "mp"),
        P(),
    )
    return jax.shard_map(
        on_device, mesh=mesh, in_specs=in_specs, out_specs=out_specs, check_vma=False
    )
```

profile of v0, /device:TPU:1, one launch (start us, length us, event | category | flops | bytes accessed | tf_op | source)
XLA Modules:
  0.0 4554.2 jit_solution(3140081610820928543)
XLA Ops:
  15.6 99.1 %all-gather.12.cloned.1.call-done = bf16[1024,512]{1,0:T(8,128)(2,1)} async-done(((bf16[16,512]{1,0:T(8,128)(2,1)}), bf16[1024,512]{1,0:T(8,128)(2,1)}) %all-gather.12.cloned.1.call-update) | async-done | bytes 1048592 | tf_op jit(solution)/shard_map/all_gather | solution.py:172
  116.3 100.7 %all-gather.10.cloned.1.call-done = bf16[1024,512]{1,0:T(8,128)(2,1)} async-done(((bf16[16,512]{1,0:T(8,128)(2,1)}), bf16[1024,512]{1,0:T(8,128)(2,1)}) %all-gather.10.cloned.1.call-update) | async-done | bytes 1048592 | tf_op jit(solution)/shard_map/all_gather | solution.py:171
  220.7 5.7 collective-permute-start.3
  227.0 102.5 %all-gather.14.cloned.1.call-done = bf16[1024,512]{1,0:T(8,128)(2,1)} async-done(((bf16[16,512]{1,0:T(8,128)(2,1)}), bf16[1024,512]{1,0:T(8,128)(2,1)}) %all-gather.14.cloned.1.call-update) | async-done | bytes 1048592 | tf_op jit(solution)/shard_map/all_gather | solution.py:170
  331.2 2.9 collective-permute-start.1
  334.2 6.7 collective-permute-done.1
  349.0 82.6 %all-gather.16.cloned.1.call-done = bf16[512,1024]{0,1:T(8,128)(2,1)} async-done(((bf16[512,16]{0,1:T(8,128)(2,1)}), bf16[512,1024]{0,1:T(8,128)(2,1)}) %all-gather.16.cloned.1.call-update) | async-done | bytes 1048592 | tf_op jit(solution)/shard_map/all_gather | solution.py:173
  431.6 2.5 convolution_convert_fusion.3
  447.6 3.6 fusion.154
  451.6 82.1 %fusion.250 = (f32[12,48]{1,0:T(8,128)S(1)}, f32[12,1,48,1536]{3,2,1,0:T(8,128)S(1)}) fusion(f32[1536]{0:T(1024)S(1)} %get-tuple-element.183, f32[1536]{0:T(1024)S(1)} %get-tuple-element.184, f32[1536]{0:T(1024)S(1)} %get-tuple-element.185, f32[1536]{0:T(1024)S(1)} %get-tuple-element.186, f32[18,1,48,1536]{3,2,1,0:T(8,128)} %fusion.154, ...), kind=kLoop, calls=%fused_computation.590 | loop fusion | flops 86703552 | bytes 33943808 | tf_op jit(solution)/shard_map/jvp()/reduce_sum | solution.py:34
  539.6 2.5 multiply_convert_fusion.2
  544.8 31.5 all-gather.18.cloned.1.call-done
  576.2 6.8 multiply_convert_fusion.5
  583.0 100.0 %all-gather.20.cloned.1.call-done = bf16[2048,1024]{0,1:T(8,128)(2,1)} async-done(((bf16[2048,16]{0,1:T(8,128)(2,1)}), bf16[2048,1024]{0,1:T(8,128)(2,1)}) %all-gather.20.cloned.1.call-update) | async-done | bytes 4194320 | tf_op jit(solution)/shard_map/all_gather | solution.py:175
  683.0 4.4 convolution_convert_fusion.5
  687.4 109.4 %all-gather.22.cloned.1.call-done = bf16[1536,3072]{1,0:T(8,128)(2,1)} async-done(((bf16[24,3072]{1,0:T(8,128)(2,1)}), bf16[1536,3072]{1,0:T(8,128)(2,1)}) %all-gather.22.cloned.1.call-update) | async-done | bytes 9437200 | tf_op jit(solution)/shard_map/all_gather | solution.py:176
  796.8 23.6 multiply_convert_fusion
  820.4 91.0 %all-gather.24.cloned.1.call-done = bf16[3072,1536]{0,1:T(8,128)(2,1)} async-done(((bf16[3072,24]{0,1:T(8,128)(2,1)}), bf16[3072,1536]{0,1:T(8,128)(2,1)}) %all-gather.24.cloned.1.call-update) | async-done | bytes 9437200 | tf_op jit(solution)/shard_map/all_gather | solution.py:177
  911.4 10.6 convolution_convert_fusion.1
  924.8 66.4 %all-reduce.22.cloned.1.call-done = (bf16[12,1,48,1536]{3,2,1,0:T(8,128)(2,1)}, bf16[144,1024]{1,0:T(8,128)(2,1)}) async-done(((bf16[12,1,48,1536]{3,2,1,0:T(8,128)(2,1)}, bf16[144,1024]{1,0:T(8,128)(2,1)}), (bf16[12,1,48,1536]{3,2,1,0:T(8,128)(2,1)}, bf16[144,1024]{1,0:T(8,128)(2,1)})) %all-reduce.22.cloned.1.call-update) | async-done | bytes 2064400 | tf_op jit(solution)/shard_map/psum | solution.py:61
  991.2 4.7 fusion.245
  995.9 5.4 reshape.1239
  1004.3 4.6 reduce_sum.774
  1008.9 86.3 %all-gather.26.cloned.1.call-done = bf16[1536,512]{1,0:T(8,128)(2,1)} async-done(((bf16[24,512]{1,0:T(8,128)(2,1)}), bf16[1536,512]{1,0:T(8,128)(2,1)}) %all-gather.26.cloned.1.call-update) | async-done | bytes 1572880 | tf_op jit(solution)/shard_map/all_gather | solution.py:178
  1097.7 7.3 all_gather.48
  1106.1 5.5 psum.108
  1113.3 4.3 add_convert_fusion.2
  1121.5 42.3 all-reduce.20.cloned.1.call-done
  1177.8 2.9 stack_transpose_reshape.6
  1181.5 4.2 stack_transpose_reshape.7
  1190.5 3.5 collective-permute-start.16
  1194.0 5.7 collective-permute-start.14
  1200.2 3.0 broadcast_in_dim.40
  1203.1 4.2 broadcast_in_dim.41
  1207.4 5.0 fusion.11
  1212.4 14.6 add_convert_fusion
  1227.1 6.9 convolution_convert_fusion
  1244.3 71.9 %all-reduce.18.cloned.1.call-done = (bf16[144,1024]{1,0:T(8,128)(2,1)}, bf16[576,1536]{1,0:T(8,128)(2,1)}) async-done(((bf16[144,1024]{1,0:T(8,128)(2,1)}, bf16[576,1536]{1,0:T(8,128)(2,1)}), (bf16[144,1024]{1,0:T(8,128)(2,1)}, bf16[576,1536]{1,0:T(8,128)(2,1)})) %all-reduce.18.cloned.1.call-update) | async-done | bytes 2064400 | tf_op jit(solution)/shard_map/psum | solution.py:61
  1316.3 3.6 fusion.12
  1319.9 2.7 add_add_fusion
  1322.6 2.3 reduce_sum.782
  1324.8 2.4 add_convert_fusion.1
  1327.2 23.0 fusion.150
  1350.3 8.4 fusion.152
  1358.8 8.6 fusion.151
  1372.1 6.2 stack.257
  1386.7 3.3 convolution_bitcast_fusion
  1390.2 5.7 fusion.243
  1397.0 4.7 fusion.260
  1401.7 13.5 fusion.261
  1415.5 13.7 fusion.262
  1440.5 277.7 %all-reduce.4 = (f32[1024]{0:T(1024)}, f32[1024]{0:T(1024)}, f32[1536]{0:T(1024)}, f32[1536]{0:T(1024)}, f32[9,512]{1,0:T(8,128)}, /*index=5*/f32[1024]{0:T(1024)}) all-reduce(f32[1024]{0:T(1024)S(1)} %get-tuple-element.231, f32[1024]{0:T(1024)S(1)} %copy-done.141, ...), channel_id=1, replica_groups=mesh['dp'=64,'mp'=2] {'dp'}, use_global_device_ids=true, to_apply=%region_28.29 | all-reduce | flops 10752 | bytes 86016 | tf_op jit(solution)/shard_map/psum | solution.py:428
  1719.1 4.1 fusion.155
  1723.2 80.1 %fusion.101 = f32[12,1,48,1536]{3,2,1,0:T(8,128)} fusion(f32[18,1,48,1536]{3,2,1,0:T(8,128)} %fusion.155, f32[1536]{0:T(1024)} %copy-done.77, f32[1536]{0:T(1024)} %copy-done.78, f32[1536]{0:T(1024)} %copy-done.79, f32[1536]{0:T(1024)} %copy-done.80, f32[1536]{0:T(1024)} %copy-done.81, f32[1536]{0:T(1024)} %copy-done.82, f32[1536]{0:T(1024)} %copy-done.83, ...), kind=kLoop, calls=%fused_computation.259 | loop fusion | flops 90243072 | bytes 39332096 | tf_op jit(solution)/shard_map/mul | solution.py:343
  1803.3 87.7 %all-reduce.16.cloned.1.call-done = f32[49,1536]{1,0:T(8,128)} async-done(((f32[49,1536]{1,0:T(8,128)}), f32[49,1536]{1,0:T(8,128)}) %all-reduce.16.cloned.1.call-update) | async-done | bytes 301072 | tf_op jit(solution)/shard_map/psum | solution.py:428
  1891.0 285.3 %reduce-scatter.10.cloned.1.call-done = f32[16,512]{1,0:T(8,128)} async-done(((f32[1024,512]{1,0:T(8,128)}), f32[16,512]{1,0:T(8,128)}) %reduce-scatter.10.cloned.1.call-update) | async-done | bytes 32784 | tf_op jit(solution)/shard_map/reduce_scatter | solution.py:418
  2176.4 286.3 %reduce-scatter.16.cloned.1.call-done = f32[512,16]{0,1:T(8,128)} async-done(((f32[512,1024]{0,1:T(8,128)}), f32[512,16]{0,1:T(8,128)}) %reduce-scatter.16.cloned.1.call-update) | async-done | bytes 32784 | tf_op jit(solution)/shard_map/reduce_scatter | solution.py:421
  2462.7 285.7 %reduce-scatter.12.cloned.1.call-done = f32[16,512]{1,0:T(8,128)} async-done(((f32[1024,512]{1,0:T(8,128)}), f32[16,512]{1,0:T(8,128)}) %reduce-scatter.12.cloned.1.call-update) | async-done | bytes 32784 | tf_op jit(solution)/shard_map/reduce_scatter | solution.py:419
  2748.3 285.6 %reduce-scatter.14.cloned.1.call-done = f32[16,512]{1,0:T(8,128)} async-done(((f32[1024,512]{1,0:T(8,128)}), f32[16,512]{1,0:T(8,128)}) %reduce-scatter.14.cloned.1.call-update) | async-done | bytes 32784 | tf_op jit(solution)/shard_map/reduce_scatter | solution.py:420
  3033.9 287.9 %reduce-scatter.26.cloned.1.call-done = f32[24,512]{1,0:T(8,128)} async-done(((f32[1536,512]{1,0:T(8,128)}), f32[24,512]{1,0:T(8,128)}) %reduce-scatter.26.cloned.1.call-update) | async-done | bytes 49168 | tf_op jit(solution)/shard_map/reduce_scatter | solution.py:426
  3321.9 296.8 %reduce-scatter.18.cloned.1.call-done = f32[16,2048]{1,0:T(8,128)} async-done(((f32[1024,2048]{1,0:T(8,128)}), f32[16,2048]{1,0:T(8,128)}) %reduce-scatter.18.cloned.1.call-update) | async-done | bytes 131088 | tf_op jit(solution)/shard_map/reduce_scatter | solution.py:422
  3618.7 297.1 %reduce-scatter.20.cloned.1.call-done = f32[2048,16]{0,1:T(8,128)} async-done(((f32[2048,1024]{0,1:T(8,128)}), f32[2048,16]{0,1:T(8,128)}) %reduce-scatter.20.cloned.1.call-update) | async-done | bytes 131088 | tf_op jit(solution)/shard_map/reduce_scatter | solution.py:423
  3915.8 314.8 %reduce-scatter.22.cloned.1.call-done = f32[24,3072]{1,0:T(8,128)} async-done(((f32[1536,3072]{1,0:T(8,128)}), f32[24,3072]{1,0:T(8,128)}) %reduce-scatter.22.cloned.1.call-update) | async-done | bytes 294928 | tf_op jit(solution)/shard_map/reduce_scatter | solution.py:424
  4230.6 314.9 %reduce-scatter.24.cloned.1.call-done = f32[3072,24]{0,1:T(8,128)} async-done(((f32[3072,1536]{0,1:T(8,128)}), f32[3072,24]{0,1:T(8,128)}) %reduce-scatter.24.cloned.1.call-update) | async-done | bytes 294928 | tf_op jit(solution)/shard_map/reduce_scatter | solution.py:425
  (588 shorter events, 118.1 us)
Async XLA Ops:
  7.2 107.5 %all-gather.12.cloned.1.call-start = ((), (), s32[]{:S(2)}) async-start(), calls=%async_computation.10 | async-start | bytes 1064960 | tf_op jit(solution)/shard_map/all_gather | solution.py:172
  7.9 209.0 %all-gather.10.cloned.1.call-start = ((), (), s32[]{:S(2)}) async-start(), calls=%async_computation.9 | async-start | bytes 1064960 | tf_op jit(solution)/shard_map/all_gather | solution.py:171
  8.7 320.8 %all-gather.14.cloned.1.call-start = ((), (), s32[]{:S(2)}) async-start(), calls=%async_computation.11 | async-start | bytes 1064960 | tf_op jit(solution)/shard_map/all_gather | solution.py:170
  9.4 422.2 %all-gather.16.cloned.1.call-start = ((), (), s32[]{:S(2)}) async-start(), calls=%async_computation.12 | async-start | bytes 1064960 | tf_op jit(solution)/shard_map/all_gather | solution.py:173
  10.0 532.0 %all-reduce.14.cloned.1.call-start = ((), (), s32[]{:S(2)}) async-start(), calls=%async_computation.13 | async-start | bytes 589824 | tf_op jit(solution)/shard_map/psum | solution.py:61
  218.6 112.6 %collective-permute-start.4 = (bf16[2,1,144,512]{3,2,1,0:T(8,128)(2,1)S(1)}, bf16[2,1,144,512]{3,2,1,0:T(8,128)(2,1)S(1)}, u32[]{:S(2)}, u32[]{:S(2)}) collective-permute-start(bf16[2,1,144,512]{3,2,1,0:T(8,128)(2,1)S(1)} %get-tuple-element.272), channel_id=1, source_target_pairs={{0,6},{2,8},{4,10},{6,12},{8,14},{10,16},{12,18},{14,20},{16,22},{... | collective-permute-start | bytes 884744 | tf_op jit(solution)/shard_map/ppermute | solution.py:16
  220.6 113.6 %collective-permute-start.5 = (bf16[2,1,144,512]{3,2,1,0:T(8,128)(2,1)S(1)}, bf16[2,1,144,512]{3,2,1,0:T(8,128)(2,1)S(1)}, u32[]{:S(2)}, u32[]{:S(2)}) collective-permute-start(bf16[2,1,144,512]{3,2,1,0:T(8,128)(2,1)S(1)} %get-tuple-element.272), channel_id=1, source_target_pairs={{0,126},{2,0},{4,2},{6,4},{8,6},{10,8},{12,10},{14,12},{16,14},{18... | collective-permute-start | bytes 884744 | tf_op jit(solution)/shard_map/ppermute | solution.py:16
  220.6 113.6 %collective-permute-start.2 = (bf16[2,1,144,512]{3,2,0,1:T(8,128)(2,1)S(1)}, bf16[2,1,144,512]{3,2,0,1:T(8,128)(2,1)S(1)}, u32[]{:S(2)}, u32[]{:S(2)}) collective-permute-start(bf16[2,1,144,512]{3,2,0,1:T(8,128)(2,1)S(1)} %get-tuple-element.271), channel_id=1, source_target_pairs={{0,4},{2,6},{4,8},{6,10},{8,12},{10,14},{12,16},{14,18},{16,20},{1... | collective-permute-start | bytes 884744 | tf_op jit(solution)/shard_map/ppermute | solution.py:16
  220.7 113.5 %collective-permute-start.3 = (bf16[2,1,144,512]{3,2,0,1:T(8,128)(2,1)S(1)}, bf16[2,1,144,512]{3,2,0,1:T(8,128)(2,1)S(1)}, u32[]{:S(2)}, u32[]{:S(2)}) collective-permute-start(bf16[2,1,144,512]{3,2,0,1:T(8,128)(2,1)S(1)} %get-tuple-element.271), channel_id=1, source_target_pairs={{0,124},{2,126},{4,0},{6,2},{8,4},{10,6},{12,8},{14,10},{16,12},{1... | collective-permute-start | bytes 884744 | tf_op jit(solution)/shard_map/ppermute | solution.py:16
  226.4 107.9 %collective-permute-start = (bf16[2,1,144,512]{3,2,0,1:T(8,128)(2,1)S(1)}, bf16[2,1,144,512]{3,2,0,1:T(8,128)(2,1)S(1)}, u32[]{:S(2)}, u32[]{:S(2)}) collective-permute-start(bf16[2,1,144,512]{3,2,0,1:T(8,128)(2,1)S(1)} %get-tuple-element.271), channel_id=1, source_target_pairs={{0,2},{2,4},{4,6},{6,8},{8,10},{10,12},{12,14},{14,16},{16,18},{18... | collective-permute-start | bytes 884744 | tf_op jit(solution)/shard_map/ppermute | solution.py:16
  331.2 9.7 collective-permute-start.1
  347.4 89.6 %copy-start.163 = (s32[16]{0:T(128)S(1)}, s32[16]{0:T(128)}, u32[]{:S(2)}) copy-start(s32[16]{0:T(128)} %param.23) | copy-start | bytes 196
  347.4 91.6 %copy-start.18 = (bf16[12,1,48,1536]{3,2,1,0:T(8,128)(2,1)S(1)}, bf16[12,1,48,1536]{3,2,1,0:T(8,128)(2,1)}, u32[]{:S(2)}) copy-start(bf16[12,1,48,1536]{3,2,1,0:T(8,128)(2,1)} %param.22) | copy-start | bytes 5308420
  349.0 90.0 %copy-start.40 = (bf16[8,64,144]{2,1,0:T(8,128)(2,1)}, bf16[8,64,144]{2,1,0:T(8,128)(2,1)S(1)}, u32[]{:S(2)}) copy-start(bf16[8,64,144]{2,1,0:T(8,128)(2,1)S(1)} %convolution_convert_fusion.6) | copy-start | bytes 442372
  434.1 142.1 %all-gather.18.cloned.1.call-start = ((), (), s32[]{:S(2)}) async-start(), calls=%async_computation.14 | async-start | bytes 4259840 | tf_op jit(solution)/shard_map/all_gather | solution.py:174
  434.7 248.3 %all-gather.20.cloned.1.call-start = ((), (), s32[]{:S(2)}) async-start(), calls=%async_computation.15 | async-start | bytes 4259840 | tf_op jit(solution)/shard_map/all_gather | solution.py:175
  435.4 361.4 %all-gather.22.cloned.1.call-start = ((), (), s32[]{:S(2)}) async-start(), calls=%async_computation.16 | async-start | bytes 9584640 | tf_op jit(solution)/shard_map/all_gather | solution.py:176
  436.2 475.2 %all-gather.24.cloned.1.call-start = ((), (), s32[]{:S(2)}) async-start(), calls=%async_computation.17 | async-start | bytes 9584640 | tf_op jit(solution)/shard_map/all_gather | solution.py:177
  436.9 554.3 %all-reduce.22.cloned.1.call-start = ((), (), s32[]{:S(2)}) async-start(), calls=%async_computation.31 | async-start | bytes 4128768 | tf_op jit(solution)/shard_map/psum | solution.py:61
  439.4 8.2 collective-permute-start.9
  439.8 7.9 collective-permute-start.8
  544.0 623.8 %copy-start.4 = (f32[144,1024]{1,0:T(8,128)}, f32[144,1024]{1,0:T(8,128)S(1)}, u32[]{:S(2)}) copy-start(f32[144,1024]{1,0:T(8,128)S(1)} %get-tuple-element.253) | copy-start | bytes 1769476
  544.0 623.8 %copy-start.110 = (f32[144]{0:T(256)}, f32[144]{0:T(256)S(1)}, u32[]{:S(2)}) copy-start(f32[144]{0:T(256)S(1)} %broadcast_multiply_fusion.2) | copy-start | bytes 1732
  583.0 237.4 %copy-start.33 = (bf16[144,2048]{1,0:T(8,128)(2,1)}, bf16[144,2048]{1,0:T(8,128)(2,1)S(1)}, u32[]{:S(2)}) copy-start(bf16[144,2048]{1,0:T(8,128)(2,1)S(1)} %get-tuple-element.250) | copy-start | bytes 1769476
  583.0 213.8 %copy-start.47 = (bf16[576,1536]{1,0:T(8,128)(2,1)S(1)}, bf16[576,1536]{1,0:T(8,128)(2,1)}, u32[]{:S(2)}) copy-start(bf16[576,1536]{1,0:T(8,128)(2,1)} %multiply_convert_fusion.2) | copy-start | bytes 5308420
  911.4 79.8 %copy-start.19 = (bf16[12,1,48,1536]{3,2,1,0:T(8,128)(2,1)S(1)}, bf16[12,1,48,1536]{3,2,1,0:T(8,128)(2,1)}, u32[]{:S(2)}) copy-start(bf16[12,1,48,1536]{3,2,1,0:T(8,128)(2,1)} %param.22) | copy-start | bytes 5308420
  911.4 79.8 %copy-start.58 = (f32[12,48]{1,0:T(8,128)S(1)}, f32[12,48]{1,0:T(8,128)}, u32[]{:S(2)}) copy-start(f32[12,48]{1,0:T(8,128)} %copy-done.57) | copy-start | bytes 6916
  922.0 173.2 %all-gather.26.cloned.1.call-start = ((), (), s32[]{:S(2)}) async-start(), calls=%async_computation.18 | async-start | bytes 1597440 | tf_op jit(solution)/shard_map/all_gather | solution.py:178
  922.8 241.1 %all-reduce.20.cloned.1.call-start = ((), (), s32[]{:S(2)}) async-start(), calls=%async_computation.30 | async-start | bytes 1474560 | tf_op jit(solution)/shard_map/psum | solution.py:61
  922.8 174.4 %collective-permute-start.11 = (bf16[1,1,24,512]{3,2,1,0:T(8,128)(2,1)S(1)}, bf16[1,1,24,512]{3,2,1,0:T(8,128)(2,1)S(1)}, u32[]{:S(2)}, u32[]{:S(2)}) collective-permute-start(bf16[1,1,24,512]{3,2,1,0:T(8,128)(2,1)S(1)} %get-tuple-element.275), channel_id=1, source_target_pairs={{2,0},{4,2},{6,4},{8,6},{10,8},{12,10},{14,12},{16,14},{18,16},{20... | collective-permute-start | bytes 73736 | tf_op jit(solution)/shard_map/ppermute | solution.py:28
  923.2 174.0 %collective-permute-start.10 = (bf16[1,1,24,512]{3,2,1,0:T(8,128)(2,1)S(1)}, bf16[1,1,24,512]{3,2,1,0:T(8,128)(2,1)S(1)}, u32[]{:S(2)}, u32[]{:S(2)}) collective-permute-start(bf16[1,1,24,512]{3,2,1,0:T(8,128)(2,1)S(1)} %get-tuple-element.274), channel_id=1, source_target_pairs={{0,2},{2,4},{4,6},{6,8},{8,10},{10,12},{12,14},{14,16},{16,18},{18... | collective-permute-start | bytes 73736 | tf_op jit(solution)/shard_map/ppermute | solution.py:25
  924.7 172.6 %copy-start.122 = (f32[1,512]{1,0:T(1,128)}, f32[1,512]{1,0:T(1,128)S(1)}, u32[]{:S(2)}) copy-start(f32[1,512]{1,0:T(1,128)S(1)} %get-tuple-element.278) | copy-start | bytes 6148
  924.7 172.6 %copy-start.124 = (f32[1,512]{1,0:T(1,128)}, f32[1,512]{1,0:T(1,128)S(1)}, u32[]{:S(2)}) copy-start(f32[1,512]{1,0:T(1,128)S(1)} %get-tuple-element.279) | copy-start | bytes 6148
  924.8 172.6 %copy-start.126 = (f32[1,512]{1,0:T(1,128)}, f32[1,512]{1,0:T(1,128)S(1)}, u32[]{:S(2)}) copy-start(f32[1,512]{1,0:T(1,128)S(1)} %get-tuple-element.280) | copy-start | bytes 6148
  924.8 172.6 %copy-start.128 = (f32[1,512]{1,0:T(1,128)}, f32[1,512]{1,0:T(1,128)S(1)}, u32[]{:S(2)}) copy-start(f32[1,512]{1,0:T(1,128)S(1)} %get-tuple-element.281) | copy-start | bytes 6148
  924.8 172.6 %copy-start.130 = (f32[1,512]{1,0:T(1,128)}, f32[1,512]{1,0:T(1,128)S(1)}, u32[]{:S(2)}) copy-start(f32[1,512]{1,0:T(1,128)S(1)} %get-tuple-element.282) | copy-start | bytes 6148
  924.8 172.6 %copy-start.132 = (f32[1,512]{1,0:T(1,128)}, f32[1,512]{1,0:T(1,128)S(1)}, u32[]{:S(2)}) copy-start(f32[1,512]{1,0:T(1,128)S(1)} %get-tuple-element.283) | copy-start | bytes 6148
  924.8 172.6 %copy-start.134 = (f32[1,512]{1,0:T(1,128)}, f32[1,512]{1,0:T(1,128)S(1)}, u32[]{:S(2)}) copy-start(f32[1,512]{1,0:T(1,128)S(1)} %get-tuple-element.284) | copy-start | bytes 6148
  924.8 172.6 %copy-start.136 = (f32[1,512]{1,0:T(1,128)}, f32[1,512]{1,0:T(1,128)S(1)}, u32[]{:S(2)}) copy-start(f32[1,512]{1,0:T(1,128)S(1)} %get-tuple-element.285) | copy-start | bytes 6148
  924.8 172.6 %copy-start.138 = (f32[1,512]{1,0:T(1,128)}, f32[1,512]{1,0:T(1,128)S(1)}, u32[]{:S(2)}) copy-start(f32[1,512]{1,0:T(1,128)S(1)} %get-tuple-element.286) | copy-start | bytes 6148
  1002.4 94.9 %collective-permute-start.7 = (bf16[1,1,24,512]{3,2,1,0:T(8,128)(2,1)S(1)}, bf16[1,1,24,512]{3,2,1,0:T(8,128)(2,1)S(1)}, u32[]{:S(2)}, u32[]{:S(2)}) collective-permute-start(bf16[1,1,24,512]{3,2,1,0:T(8,128)(2,1)S(1)} %get-tuple-element.277), channel_id=1, source_target_pairs={{2,0},{4,2},{6,4},{8,6},{10,8},{12,10},{14,12},{16,14},{18,16},{20... | collective-permute-start | bytes 73736 | tf_op jit(solution)/shard_map/ppermute | solution.py:28
  1003.1 94.1 %collective-permute-start.6 = (bf16[1,1,24,512]{3,2,1,0:T(8,128)(2,1)S(1)}, bf16[1,1,24,512]{3,2,1,0:T(8,128)(2,1)S(1)}, u32[]{:S(2)}, u32[]{:S(2)}) collective-permute-start(bf16[1,1,24,512]{3,2,1,0:T(8,128)(2,1)S(1)} %get-tuple-element.276), channel_id=1, source_target_pairs={{0,2},{2,4},{4,6},{6,8},{8,10},{10,12},{12,14},{14,16},{16,18},{18... | collective-permute-start | bytes 73736 | tf_op jit(solution)/shard_map/ppermute | solution.py:25
  1008.9 97.2 %copy-start.48 = (bf16[6,24,1536]{2,1,0:T(8,128)(2,1)}, bf16[6,24,1536]{2,1,0:T(8,128)(2,1)S(1)}, u32[]{:S(2)}) copy-start(bf16[6,24,1536]{2,1,0:T(8,128)(2,1)S(1)} %multiply_convert_fusion.6) | copy-start | bytes 1327108
  1121.4 194.8 %all-reduce.18.cloned.1.call-start = ((), (), s32[]{:S(2)}) async-start(), calls=%async_computation.29 | async-start | bytes 4128768 | tf_op jit(solution)/shard_map/psum | solution.py:61
  1188.7 45.3 collective-permute-start.17
  1190.5 47.7 %collective-permute-start.16 = (bf16[2,1,144,512]{3,2,0,1:T(8,128)(2,1)}, bf16[2,1,144,512]{3,2,0,1:T(8,128)(2,1)}, u32[]{:S(2)}, u32[]{:S(2)}) collective-permute-start(bf16[2,1,144,512]{3,2,0,1:T(8,128)(2,1)} %get-tuple-element.263), channel_id=1, source_target_pairs={{0,122},{2,124},{4,126},{6,0},{8,2},{10,4},{12,6},{14,8},{16,10},{... | collective-permute-start | bytes 884744 | tf_op jit(solution)/shard_map/ppermute | solution.py:16
  1194.0 44.2 collective-permute-start.15
  1194.0 44.2 collective-permute-start.14
  1199.7 38.6 collective-permute-start.13
  1234.1 6.4 collective-permute-start.12
  1242.1 74.1 %copy-start.1 = (f32[12,1,48,1536]{3,2,1,0:T(8,128)S(1)}, f32[12,1,48,1536]{3,2,1,0:T(8,128)}, u32[]{:S(2)}) copy-start(f32[12,1,48,1536]{3,2,1,0:T(8,128)} %copy-done) | copy-start | bytes 10616836
  1242.2 74.1 %copy-start.107 = (f32[576]{0:T(1024)S(1)}, f32[576]{0:T(1024)}, u32[]{:S(2)}) copy-start(f32[576]{0:T(1024)} %copy-done.106) | copy-start | bytes 6916
  1244.1 646.9 %all-reduce.16.cloned.1.call-start = ((), (), s32[]{:S(2)}) async-start(), calls=%async_computation.25 | async-start | bytes 688128 | tf_op jit(solution)/shard_map/psum | solution.py:428
  1378.4 798.0 %reduce-scatter.10.cloned.1.call-start = ((), (), s32[]{:S(2)}) async-start(), calls=%async_computation.19 | async-start | bytes 2129920 | tf_op jit(solution)/shard_map/reduce_scatter | solution.py:418
  1380.6 1082.0 %reduce-scatter.16.cloned.1.call-start = ((), (), s32[]{:S(2)}) async-start(), calls=%async_computation.22 | async-start | bytes 2129920 | tf_op jit(solution)/shard_map/reduce_scatter | solution.py:421
  1382.6 1365.8 %reduce-scatter.12.cloned.1.call-start = ((), (), s32[]{:S(2)}) async-start(), calls=%async_computation.20 | async-start | bytes 2129920 | tf_op jit(solution)/shard_map/reduce_scatter | solution.py:419
  1384.5 1649.5 %reduce-scatter.14.cloned.1.call-start = ((), (), s32[]{:S(2)}) async-start(), calls=%async_computation.21 | async-start | bytes 2129920 | tf_op jit(solution)/shard_map/reduce_scatter | solution.py:420
  1386.7 1935.2 %reduce-scatter.26.cloned.1.call-start = ((), (), s32[]{:S(2)}) async-start(), calls=%async_computation.28 | async-start | bytes 3194880 | tf_op jit(solution)/shard_map/reduce_scatter | solution.py:426
  1390.1 2228.6 %reduce-scatter.18.cloned.1.call-start = ((), (), s32[]{:S(2)}) async-start(), calls=%async_computation.23 | async-start | bytes 8519680 | tf_op jit(solution)/shard_map/reduce_scatter | solution.py:422
  1395.9 2519.9 %reduce-scatter.20.cloned.1.call-start = ((), (), s32[]{:S(2)}) async-start(), calls=%async_computation.24 | async-start | bytes 8519680 | tf_op jit(solution)/shard_map/reduce_scatter | solution.py:423
  1401.7 2828.9 %reduce-scatter.22.cloned.1.call-start = ((), (), s32[]{:S(2)}) async-start(), calls=%async_computation.26 | async-start | bytes 19169280 | tf_op jit(solution)/shard_map/reduce_scatter | solution.py:424
  1415.2 3130.3 %reduce-scatter.24.cloned.1.call-start = ((), (), s32[]{:S(2)}) async-start(), calls=%async_computation.27 | async-start | bytes 19169280 | tf_op jit(solution)/shard_map/reduce_scatter | solution.py:425
  1438.7 280.4 %collective-permute-start.19 = (bf16[3,1,48,1536]{3,2,1,0:T(8,128)(2,1)}, bf16[3,1,48,1536]{3,2,1,0:T(8,128)(2,1)}, u32[]{:S(2)}, u32[]{:S(2)}) collective-permute-start(bf16[3,1,48,1536]{3,2,1,0:T(8,128)(2,1)} %bitcast.61), channel_id=1, source_target_pairs={{2,0},{4,2},{6,4},{8,6},{10,8},{12,10},{14,12},{16,14},{18,16},{20... | collective-permute-start | bytes 1327112 | tf_op jit(solution)/shard_map/ppermute | solution.py:28
  1439.4 279.7 %collective-permute-start.18 = (bf16[3,1,48,1536]{3,2,1,0:T(8,128)(2,1)}, bf16[3,1,48,1536]{3,2,1,0:T(8,128)(2,1)}, u32[]{:S(2)}, u32[]{:S(2)}) collective-permute-start(bf16[3,1,48,1536]{3,2,1,0:T(8,128)(2,1)} %bitcast.57), channel_id=1, source_target_pairs={{0,2},{2,4},{4,6},{6,8},{8,10},{10,12},{12,14},{14,16},{16,18},{18... | collective-permute-start | bytes 1327112 | tf_op jit(solution)/shard_map/ppermute | solution.py:25
  (149 other events, 1120.5 us)
Sparse Core Ops, SparseCore 0:
  9.7 104.9 all-gather.11
  116.4 100.4 all-gather.9
  218.7 110.7 all-gather.13
  331.1 100.4 all-gather.15
  434.5 34.2 all-reduce.13
  470.3 105.8 all-gather.17
  577.9 104.9 all-gather.19
  684.7 112.0 all-gather.21
  798.5 112.8 all-gather.23
  922.2 68.9 all-reduce.21
  992.9 102.2 all-gather.25
  1121.5 42.2 all-reduce.19
  1244.2 71.9 all-reduce.17
  1378.5 512.4 all-reduce.15
  1893.9 282.4 reduce-scatter.9
  2179.1 283.4 reduce-scatter.15
  2465.6 282.7 reduce-scatter.11
  2751.1 282.7 reduce-scatter.13
  3037.0 284.8 reduce-scatter.25
  3324.7 293.9 reduce-scatter.17
  3621.7 294.0 reduce-scatter.19
  3918.8 311.8 reduce-scatter.21
  4233.6 311.8 reduce-scatter.23
where the time goes:
time: 4570 us; the launch traced here: 4550 us
  waiting for transfers between devices  3740 us (82%)
  blocking collectives  290 us (6%)
  other arithmetic  271 us (6%)
  matrix products  142 us (3%)
  local copies, waits for them, and re-layouts  56.1 us (1%)
    reduce_scatter x1, waiting for transfers between devices, on_device(): lax.psum_scatter(shrink_weight_slope, 'dp', scatter_dimension=1, tiled=True)  315 us
    reduce_scatter x1, waiting for transfers between devices, on_device(): lax.psum_scatter(expand_weight_slope, 'dp', scatter_dimension=0, tiled=True)  315 us
    reduce_scatter x1, waiting for transfers between devices, on_device(): lax.psum_scatter(down_weight_slope, 'dp', scatter_dimension=1, tiled=True)  297 us
    reduce_scatter x1, waiting for transfers between devices, on_device(): lax.psum_scatter(up_weight_slope, 'dp', scatter_dimension=0, tiled=True)  297 us
    reduce_scatter x1, waiting for transfers between devices, on_device(): lax.psum_scatter(adapter_weight_slope, 'dp', scatter_dimension=0, tiled=T...  288 us
    reduce_scatter x1, waiting for transfers between devices, on_device(): lax.psum_scatter(output_weight_slope, 'dp', scatter_dimension=1, tiled=True)  286 us
    reduce_scatter x1, waiting for transfers between devices, on_device(): lax.psum_scatter(key_weight_slope, 'dp', scatter_dimension=0, tiled=True)  286 us
    reduce_scatter x1, waiting for transfers between devices, on_device(): lax.psum_scatter(value_weight_slope, 'dp', scatter_dimension=0, tiled=True)  286 us
  transfers between devices with their start and end apart: 43, of which 25 were waited for; matrix products, arithmetic and copies ran while one was open for 8% of the time, Pallas kernels for 0%

commit v1 on v0

v1 whole, which is shorter than its diff:
```python
import functools

import jax
import jax.numpy as jnp
from jax import lax
from jax.experimental import pallas as pl
from jax.experimental.pallas import tpu as pltpu
from jax.sharding import PartitionSpec as P

HD = 64
TILES = 4
CHIPS = 32
CORE = 1
RINGS = (2, 6, 8, 24, 32)

norm_epsilon = 1e-06

LANES = 128
RADIUS = 3
WINDOW = 7
PAD = 8


def masked_rows(place, main_ref, low_ref, high_ref, wide, strip, side, bounded):
    first, extent = place[0], place[1]
    cols = lax.broadcasted_iota(jnp.int32, (side, LANES), 0)

    def put(slot, value):
        row = first + slot - RADIUS
        limit = extent if bounded else side
        keep = (cols < limit) & (row >= 0) & (row < limit)
        wide[slot] = jnp.where(keep, value.astype(jnp.float32), 0.0)

    for slot in range(RADIUS):
        put(slot, low_ref[slot])
        put(RADIUS + strip + slot, high_ref[slot])
    for slot in range(strip):
        put(RADIUS + slot, main_ref[slot])


def window_sum(wide, taps_ref, shifted, row, side, flipped):
    sums = [None] * WINDOW
    for a in range(WINDOW):
        line = wide[row + a]
        for b in range(WINDOW):
            tap = WINDOW * a + b
            if flipped:
                tap = WINDOW * WINDOW - 1 - tap
            term = line * taps_ref[tap : tap + 1]
            sums[b] = term if sums[b] is None else sums[b] + term
    total = sums[RADIUS]
    for b in range(WINDOW):
        if b != RADIUS:
            shifted[b, PAD : PAD + side] = sums[b]
    for b in range(WINDOW):
        if b != RADIUS:
            total = total + shifted[b, PAD + b - RADIUS : PAD + b - RADIUS + side]
    return total


def clear_edges(shifted, side):
    for b in range(WINDOW):
        shifted[b, 0:PAD] = jnp.zeros((PAD, LANES), jnp.float32)
        shifted[b, PAD + side : 2 * PAD + side] = jnp.zeros((PAD, LANES), jnp.float32)


def forward_kernel(place, main_ref, low_ref, high_ref, taps_in, out_ref, wide, taps, shifted):
    strip, side = main_ref.shape[0], main_ref.shape[1]
    masked_rows(place, main_ref, low_ref, high_ref, wide, strip, side, True)
    clear_edges(shifted, side)
    taps[...] = taps_in[...].astype(jnp.float32)

    def step(row, carry):
        out_ref[row] = window_sum(wide, taps, shifted, row, side, False)
        return carry

    lax.fori_loop(0, strip, step, 0)


def backward_kernel(place, main_ref, low_ref, high_ref, taps_in, add_ref, out_ref, wide, taps, shifted):
    strip, side = main_ref.shape[0], main_ref.shape[1]
    masked_rows(place, main_ref, low_ref, high_ref, wide, strip, side, False)
    clear_edges(shifted, side)
    taps[...] = taps_in[...].astype(jnp.float32)
    cols = lax.broadcasted_iota(jnp.int32, (side, LANES), 0)

    def step(row, carry):
        total = window_sum(wide, taps, shifted, row, side, True) + add_ref[row]
        keep = (cols < place[1]) & (place[0] + row < place[1])
        out_ref[row] = jnp.where(keep, total, 0.0)
        return carry

    lax.fori_loop(0, strip, step, 0)


def slope_kernel(place, main_ref, low_ref, high_ref, grad_ref, out_ref, wide, padded):
    strip, side = main_ref.shape[0], main_ref.shape[1]
    masked_rows(place, main_ref, low_ref, high_ref, wide, strip, side, True)
    edge = jnp.zeros((PAD, LANES), jnp.float32)
    for row in range(strip):
        padded[row, 0:PAD] = edge
        padded[row, PAD : PAD + side] = grad_ref[row].astype(jnp.float32)
        padded[row, PAD + side : 2 * PAD + side] = edge
    for group in ((0, 1, 2, 3), (4, 5, 6)):

        def step(row, sums):
            lines = [wide[row + a] for a in group]
            fresh = list(sums)
            for b in range(WINDOW):
                start = PAD + RADIUS - b
                part = padded[row, start : start + side]
                for i in range(len(group)):
                    term = (lines[i] * part).reshape(side // 8, 8, LANES)
                    fresh[i * WINDOW + b] = fresh[i * WINDOW + b] + jnp.sum(term, axis=0)
            return tuple(fresh)

        start = tuple(jnp.zeros((8, LANES), jnp.float32) for _ in range(len(group) * WINDOW))
        sums = lax.fori_loop(0, strip, step, start)
        for i, a in enumerate(group):
            for b in range(WINDOW):
                tap = a * WINDOW + b
                out_ref[tap : tap + 1] = jnp.sum(sums[i * WINDOW + b], axis=0, keepdims=True)


def block3(rows, side):
    return pl.BlockSpec((rows, side, LANES), lambda i: (0, 0, i))


SCALARS = pl.BlockSpec(memory_space=pltpu.SMEM)


def map_conv(place, main, low, high, taps, added=None):
    strip, side, channels = main.shape
    count = taps.shape[0]
    tap_spec = pl.BlockSpec((count, LANES), lambda i: (0, i))
    specs = [SCALARS, block3(strip, side), block3(RADIUS, side), block3(RADIUS, side), tap_spec]
    args = [place, main, low, high, taps]
    if added is not None:
        specs.append(block3(strip, side))
        args.append(added)
    work = strip * side * channels
    return pl.pallas_call(
        forward_kernel if added is None else backward_kernel,
        grid=(channels // LANES,),
        in_specs=specs,
        out_specs=block3(strip, side),
        out_shape=jax.ShapeDtypeStruct((strip, side, channels), jnp.float32),
        scratch_shapes=[
            pltpu.VMEM((strip + 2 * RADIUS, side, LANES), jnp.float32),
            pltpu.VMEM((count, LANES), jnp.float32),
            pltpu.VMEM((WINDOW, side + 2 * PAD, LANES), jnp.float32),
        ],
        compiler_params=pltpu.CompilerParams(vmem_limit_bytes=24 * 1024 * 1024),
        cost_estimate=pl.CostEstimate(flops=2 * count * work, bytes_accessed=8 * work, transcendentals=0),
    )(*args)


def map_slopes(place, main, low, high, grad):
    strip, side, channels = main.shape
    count = WINDOW * WINDOW
    work = strip * side * channels
    return pl.pallas_call(
        slope_kernel,
        grid=(channels // LANES,),
        in_specs=[SCALARS, block3(strip, side), block3(RADIUS, side), block3(RADIUS, side), block3(strip, side)],
        out_specs=pl.BlockSpec((count, LANES), lambda i: (0, i)),
        out_shape=jax.ShapeDtypeStruct((count, channels), jnp.float32),
        scratch_shapes=[
            pltpu.VMEM((strip + 2 * RADIUS, side, LANES), jnp.float32),
            pltpu.VMEM((strip, side + 2 * PAD, LANES), jnp.float32),
        ],
        compiler_params=pltpu.CompilerParams(vmem_limit_bytes=24 * 1024 * 1024),
        cost_estimate=pl.CostEstimate(flops=2 * count * work, bytes_accessed=4 * work, transcendentals=0),
    )(place, main, low, high, grad)


def rotated(start):
    return tuple(RINGS[(start + i) % len(RINGS)] for i in range(len(RINGS)))


def xor_swap(values, mask):
    count = lax.axis_size("dp")
    return lax.ppermute(values, "dp", [(i, i ^ mask) for i in range(count)])


def chip_steps(offset):
    x, y, z = offset & 3, (offset >> 2) & 3, offset >> 4
    return {2: (x ^ (x >> 1)) & 1, 6: x >> 1, 8: (y ^ (y >> 1)) & 1, 24: y >> 1, 32: z}


def gather_place(offset, order):
    steps = chip_steps(offset)
    place = steps[order[0]]
    for k in range(1, len(order)):
        place = place + (steps[order[k]] << k)
    return place


def scatter_place(offset, order):
    return gather_place(offset, order[::-1])


def gathered_part(block, order):
    held = block[None]
    for mask in order:
        held = jnp.concatenate([held, xor_swap(held, mask)], axis=0)
    return held


def scattered_part(held, order):
    for mask in order:
        half = held.shape[0] // 2
        kept, given = held[:half], held[half:]
        summed = kept.astype(jnp.float32) + xor_swap(given, mask).astype(jnp.float32)
        held = summed if half == 1 else summed.astype(jnp.bfloat16)
    return held[0]


def route_kernel(moves, n_in, n_out, place, *refs):
    ins, outs = refs[:n_in], refs[n_in : n_in + n_out]
    held = refs[n_in + n_out : n_in + 2 * n_out]
    sems = refs[n_in + 2 * n_out]
    device = place[0]
    chip, core = device >> 1, device & 1

    for target in range(n_out):

        def step(offset, carry):
            for source, take, goal, put, source_box, target_box in moves:
                if goal == target:
                    pltpu.make_async_copy(
                        ins[source].at[(take(chip, core, offset),) + source_box],
                        held[goal].at[(put(chip, core, offset),) + target_box],
                        sems.at[goal],
                    ).start()
            return carry

        lax.fori_loop(0, CHIPS, step, 0)
    for target in range(n_out):
        pltpu.make_async_copy(held[target], held[target], sems.at[target]).wait()
        pltpu.make_async_copy(held[target], outs[target], sems.at[target]).start()
    for target in range(n_out):
        pltpu.make_async_copy(held[target], outs[target], sems.at[target]).wait()


def route(moves, place, arrays, shapes):
    anywhere = pl.BlockSpec(memory_space=pl.ANY)
    volume = sum(2 * a.size for a in arrays)
    return pl.pallas_call(
        functools.partial(route_kernel, moves, len(arrays), len(shapes)),
        in_specs=[SCALARS] + [anywhere] * len(arrays),
        out_specs=[anywhere] * len(shapes),
        out_shape=[jax.ShapeDtypeStruct(s, jnp.bfloat16) for s in shapes],
        scratch_shapes=[pltpu.VMEM(s, jnp.bfloat16) for s in shapes]
        + [pltpu.SemaphoreType.DMA((len(shapes),))],
        compiler_params=pltpu.CompilerParams(vmem_limit_bytes=volume + volume // 4 + (4 << 20)),
        cost_estimate=pl.CostEstimate(flops=0, bytes_accessed=2 * volume, transcendentals=0),
    )(place, *arrays)


def box(rows, cols):
    return (pl.ds(rows[0], rows[1] - rows[0]), pl.ds(cols[0], cols[1] - cols[0]))


def overlap(first, second):
    low, high = max(first[0], second[0]), min(first[1], second[1])
    return (low, high) if low < high else None


def shifted_span(span, base):
    return (span[0] - base, span[1] - base)


def core_swap(values):
    return xor_swap(values, CORE)


def exchange(values):
    low = values.astype(jnp.bfloat16)
    other = lax.ppermute(low, "mp", [(0, 1), (1, 0)])
    return low.astype(jnp.float32) + other.astype(jnp.float32)


def halo_rows(block, width):
    count = lax.axis_size("dp")
    forward = [(i, (i + 1) % count) for i in range(count)]
    backward = [((i + 1) % count, i) for i in range(count)]
    low = lax.ppermute(block[block.shape[0] - width :], "dp", forward)
    high = lax.ppermute(block[:width], "dp", backward)
    return low, high


def normalize(values, scale_gain):
    average = jnp.mean(values, axis=-1, keepdims=True)
    centred = values - average
    spread = jnp.mean(centred * centred, axis=-1, keepdims=True)
    return centred * lax.rsqrt(spread + norm_epsilon) * scale_gain


def gelu_exact(values):
    return jax.nn.gelu(values, approximate=False)


def matmul(former, latter):
    return jnp.dot(former, latter, preferred_element_type=jnp.float32)


def matmul_nt(former, latter):
    return lax.dot_general(
        former, latter, (((1,), (1,)), ((), ())), preferred_element_type=jnp.float32
    )


def matmul_tn(former, latter):
    return lax.dot_general(
        former, latter, (((0,), (0,)), ((), ())), preferred_element_type=jnp.float32
    )


def pair_swap(values):
    chips = lax.axis_size("dp") // 2
    pairs = []
    for chip in range(chips):
        other = (chip + 1) % chips if chip % 2 else (chip - 1) % chips
        pairs += [(2 * chip + core, 2 * other + core) for core in range(2)]
    return lax.ppermute(values, "dp", pairs)


def with_edges(block, position):
    low, high = halo_rows(block, 1)
    low = jnp.where(position != 0, low, jnp.zeros_like(low))
    high = jnp.where(position != TILES - 1, high, jnp.zeros_like(high))
    return jnp.concatenate([low, block, high], axis=0).astype(jnp.float32)


def depth_apply(padded, kernel, radius):
    height = padded.shape[0] - 2 * radius
    breadth = padded.shape[1]
    window = 2 * radius + 1
    widened = jnp.pad(padded, ((0, 0), (radius, radius), (0, 0)))
    summed = jnp.zeros((height,) + padded.shape[1:], jnp.float32)
    for row_shift in range(window):
        for col_shift in range(window):
            summed = (
                summed
                + widened[row_shift : row_shift + height, col_shift : col_shift + breadth]
                * kernel[row_shift * window + col_shift]
            )
    return summed


def kernel_slopes(padded, gradient, radius):
    height, breadth = gradient.shape[0], gradient.shape[1]
    window = 2 * radius + 1
    widened = jnp.pad(padded, ((0, 0), (radius, radius), (0, 0)))
    columns = []
    for row_shift in range(window):
        for col_shift in range(window):
            columns.append(
                jnp.sum(
                    widened[row_shift : row_shift + height, col_shift : col_shift + breadth]
                    * gradient,
                    axis=(0, 1),
                )
            )
    return jnp.stack(columns, 0)


def own_half(first, core, axis, other=False):
    size = first.shape[axis] // 2
    low = lax.slice_in_dim(first, 0, size, axis=axis)
    high = lax.slice_in_dim(first, size, 2 * size, axis=axis)
    return jnp.where((core == 0) != other, low, high)


def in_core_order(own, other, core, axis):
    return jnp.where(
        core == 0,
        jnp.concatenate([own, other], axis=axis),
        jnp.concatenate([other, own], axis=axis),
    )


def all_weights(place, core, small_rows, adapter_weight, expand_weight, shrink_rows):
    depth = small_rows[0].shape[0]
    fine = expand_weight.shape[0]
    whole = jnp.concatenate(small_rows[:4], axis=1)
    wide = whole.shape[1]
    split = 3 * small_rows[0].shape[1]
    adapter_half = adapter_weight.shape[1] // 2
    private = jnp.concatenate(
        [
            jnp.concatenate([whole, small_rows[4], small_rows[5]], axis=0),
            jnp.concatenate([adapter_weight[:, :adapter_half], adapter_weight[:, adapter_half:]], axis=0),
        ],
        axis=1,
    )
    kept = jnp.concatenate([own_half(expand_weight, core, 1), own_half(shrink_rows, core, 1)], axis=1)
    given = jnp.concatenate(
        [own_half(expand_weight, core, 1, True), own_half(shrink_rows, core, 1, True)], axis=1
    )
    common = in_core_order(kept, core_swap(given), core, 0)
    hidden = common.shape[1] // 2
    rows = common.shape[0]
    middle = private.shape[1] // 2
    third = common.shape[1] // 3
    spans = [(0, middle), (middle, 2 * middle)] + [(i * third, (i + 1) * third) for i in range(3)]
    orders = [rotated(i) for i in range(5)]
    parts = [
        gathered_part((private if i < 2 else common)[:, low:high], orders[i])
        for i, (low, high) in enumerate(spans)
    ]
    arrays = [parts[0], core_swap(parts[0]), parts[1], core_swap(parts[1])] + parts[2:]
    shapes = [
        (2 * CHIPS, depth, split),
        (2 * CHIPS, depth, wide - split),
        (2 * CHIPS, depth, wide),
        (2 * CHIPS, depth, wide),
        (2 * CHIPS, rows, adapter_half),
        (CHIPS, rows, hidden),
        (CHIPS, rows, hidden),
    ]
    moves = []

    def add(source, order, target, rows_span, cols_span, part_span, out_span, plane):
        common_cols = overlap(cols_span, part_span)
        if common_cols is None:
            return
        take = lambda chip, core, offset: gather_place(offset, order)
        if plane is None:
            put = lambda chip, core, offset: chip ^ offset
        else:
            put = lambda chip, core, offset: 2 * (chip ^ offset) + (core ^ plane)
        moves.append(
            (
                source,
                take,
                target,
                put,
                box(rows_span, shifted_span(common_cols, part_span[0])),
                box(out_span, shifted_span(common_cols, cols_span[0])),
            )
        )

    for i in range(2):
        for plane in range(2):
            source = 2 * i + plane
            everything = ((0, (0, depth), (0, split)), (1, (0, depth), (split, wide)))
            for target, rows_span, cols_span in everything:
                add(source, orders[i], target, rows_span, cols_span, spans[i], (0, depth), plane)
            for target in (2, 3):
                rows_span = ((target - 1) * depth, target * depth)
                add(source, orders[i], target, rows_span, (0, wide), spans[i], (0, depth), plane)
            add(source, orders[i], 4, (0, rows), (wide, 2 * middle), spans[i], (0, rows), plane)
    for i in range(2, 5):
        for target in (5, 6):
            cols_span = ((target - 5) * hidden, (target - 4) * hidden)
            add(i + 2, orders[i], target, (0, rows), cols_span, spans[i], (0, rows), None)
    qkv, out, up, down, adapter, expand, shrink = route(moves, place, arrays, shapes)
    adapter = adapter.reshape(2 * CHIPS, 2, fine, adapter_half).transpose(0, 2, 1, 3)
    return (
        qkv.reshape(2 * CHIPS * depth, split),
        out.reshape(2 * CHIPS * depth, wide - split),
        up.reshape(2 * CHIPS * depth, wide),
        down.reshape(2 * CHIPS * depth, wide),
        adapter.reshape(2 * CHIPS * fine, 2 * adapter_half),
        expand.reshape(CHIPS * rows, hidden),
        shrink.reshape(CHIPS * rows, hidden),
    )


def reduced_map_slopes(place, core, expand_slope, shrink_slope):
    hidden = expand_slope.shape[1]
    rows = expand_slope.shape[0] // CHIPS
    arrays = [expand_slope.reshape(CHIPS, rows, hidden), shrink_slope.reshape(CHIPS, rows, hidden)]
    tiles = 2 * hidden // LANES
    edges = [LANES * ((tiles * i + 4) // 5) for i in range(6)]
    spans = [(edges[i], edges[i + 1]) for i in range(5)]
    orders = [rotated(i) for i in range(5)]
    moves = []
    for i, span in enumerate(spans):
        for source in range(2):
            cols_span = (source * hidden, (source + 1) * hidden)
            shared = overlap(cols_span, span)
            if shared is None:
                continue
            moves.append(
                (
                    source,
                    lambda chip, core, offset: chip ^ offset,
                    i,
                    lambda chip, core, offset, order=orders[i]: scatter_place(offset, order),
                    box((0, rows), shifted_span(shared, cols_span[0])),
                    box((0, rows), shifted_span(shared, span[0])),
                )
            )
    packed = route(moves, place, arrays, [(CHIPS, rows, high - low) for low, high in spans])
    block = jnp.concatenate(
        [scattered_part(packed[i], orders[i]) for i in range(5)], axis=1
    )
    kept = own_half(block, core, 0)
    given = own_half(block, core, 0, True)
    got = core_swap(given.astype(jnp.bfloat16)).astype(jnp.float32)
    return tuple(
        in_core_order(
            kept[:, i * hidden : (i + 1) * hidden], got[:, i * hidden : (i + 1) * hidden], core, 1
        )
        for i in range(2)
    )


def reduced_other_slopes(place, core, qkv, out, up, down, adapter, minor):
    fine = adapter.shape[0] // (2 * CHIPS)
    depth = qkv.shape[0] // (2 * CHIPS)
    split, wide = qkv.shape[1], up.shape[1]
    adapter_half = adapter.shape[1] // 2
    rows = 3 * depth
    adapter = (
        adapter.reshape(2 * CHIPS, fine, 2, adapter_half)
        .transpose(0, 2, 1, 3)
        .reshape(2 * CHIPS, rows, adapter_half)
    )
    arrays = [
        qkv.reshape(2 * CHIPS, depth, split),
        out.reshape(2 * CHIPS, depth, wide - split),
        up.reshape(2 * CHIPS, depth, wide),
        down.reshape(2 * CHIPS, depth, wide),
        adapter,
        minor,
    ]
    quarter = wide // 4
    orders = [rotated(i) for i in range(5)]
    moves = []

    def add(source, source_cols, target, rows_span, target_cols):
        order = orders[target]
        size = rows_span[1] - rows_span[0]

        def put(chip, core, offset, plane):
            return CHIPS * plane + scatter_place(offset, order)

        for plane in range(2):
            moves.append(
                (
                    source,
                    lambda chip, core, offset, plane=plane: 2 * (chip ^ offset) + (core ^ plane),
                    target,
                    functools.partial(put, plane=plane),
                    box((0, size), source_cols),
                    box(rows_span, target_cols),
                )
            )

    for i in range(4):
        cols = (i * quarter, (i + 1) * quarter)
        first = 0 if cols[1] <= split else 1
        add(first, shifted_span(cols, first * split), i, (0, depth), (0, quarter))
        add(2, cols, i, (depth, 2 * depth), (0, quarter))
        add(3, cols, i, (2 * depth, rows), (0, quarter))
    minor_width = minor.shape[2]
    add(4, (0, adapter_half), 4, (0, rows), (0, adapter_half))
    add(5, (0, minor_width), 4, (0, rows), (adapter_half, adapter_half + minor_width))
    shapes = [(2 * CHIPS, rows, quarter)] * 4 + [(2 * CHIPS, rows, adapter_half + minor_width)]
    packed = route(moves, place, arrays, shapes)
    blocks = [scattered_part(packed[i], (CORE,) + orders[i]) for i in range(5)]
    whole = jnp.concatenate(blocks[:4], axis=1)
    last = blocks[4]
    adapter_own = jnp.concatenate(
        [last[:fine, :adapter_half], last[fine:, :adapter_half]], axis=1
    )
    return (
        [blocks[i][:depth] for i in range(4)],
        whole[depth : 2 * depth],
        whole[2 * depth :],
        adapter_own,
        last[:, adapter_half:],
    )


def gathered_rows(row, device):
    held = row[None]
    count = lax.axis_size("dp")
    step = 1
    while step < count:
        other = xor_swap(held, step)
        held = jnp.where(
            (device & step) != 0,
            jnp.concatenate([other, held], axis=0),
            jnp.concatenate([held, other], axis=0),
        )
        step *= 2
    return held


def on_device(
    lowres_in,
    highres_in,
    image_sizes,
    attn_gain,
    query_weight,
    key_weight,
    value_weight,
    output_weight,
    mlp_gain,
    up_weight,
    down_weight,
    depth_kernel,
    conv_gain,
    expand_weight,
    shrink_weight,
    layer_scale,
    adapter_weight,
    adapter_kernel,
    gate_vector,
    out_cotangent,
    map_cotangent,
):
    device = lax.axis_index("dp")
    core = device & 1
    place = device.reshape(1).astype(jnp.int32)
    group_count = lax.axis_size("dp") // TILES
    position = (device + 2) % TILES
    group_id = (device + 2) // TILES % group_count
    model_half = lax.axis_index("mp")
    low_strip, _, grid_side, width = lowres_in.shape
    high_strip, _, high_side, channels = highres_in.shape
    own_width = adapter_kernel.shape[1]
    local_width = query_weight.shape[1]
    local_heads = local_width // HD
    scaling = HD ** (-0.5)
    token_count = low_strip * grid_side
    pixel_count = high_strip * high_side

    high_map = highres_in.reshape(high_strip, high_side, channels)
    map_low, map_high = halo_rows(high_map, RADIUS)

    qkv_full, output_full, up_full, down_full, adapter_full, expand_full, shrink_full = all_weights(
        place,
        core,
        (query_weight, key_weight, value_weight, output_weight.T, up_weight, down_weight.T),
        adapter_weight,
        expand_weight,
        shrink_weight.T,
    )

    table_ids = jnp.arange(image_sizes.shape[0])
    extent = jnp.sum(jnp.where(table_ids == group_id, image_sizes, 0))
    first_row = position * high_strip
    map_place = jnp.stack([first_row, extent]).astype(jnp.int32)
    row_ids = first_row + jnp.arange(high_strip)
    col_ids = jnp.arange(high_side)
    valid_mask = (
        ((row_ids < extent)[:, None] & (col_ids < extent)[None, :])
        .astype(jnp.float32)[..., None]
    )

    convolved = map_conv(map_place, high_map, map_low, map_high, depth_kernel).reshape(
        pixel_count, channels
    )
    normed_map, conv_norm_back = jax.vjp(normalize, convolved, conv_gain.astype(jnp.float32))
    normed_map_low = normed_map.astype(jnp.bfloat16)
    normed_map_pair = jnp.concatenate([normed_map_low, core_swap(normed_map_low)], axis=0)

    token_rows = lowres_in.astype(jnp.float32).reshape(token_count, width)
    normed, attn_norm_back = jax.vjp(normalize, token_rows, attn_gain.astype(jnp.float32))
    normed_low = normed.astype(jnp.bfloat16)
    qkv_rows = matmul(normed_low, qkv_full).astype(jnp.bfloat16)
    queries = qkv_rows[:, :local_width]
    pair = qkv_rows[:, local_width:]
    pair = jnp.concatenate([pair, core_swap(pair)], axis=0)
    pair = jnp.concatenate([pair, pair_swap(pair)], axis=0)
    key_all = pair[:, :local_width].reshape(-1, local_heads, HD)
    value_all = pair[:, local_width:].reshape(-1, local_heads, HD)
    query_heads = queries.reshape(token_count, local_heads, HD)
    scores = (
        jnp.einsum("qhd,khd->hqk", query_heads, key_all, preferred_element_type=jnp.float32)
        * scaling
    )
    top_score = jnp.max(scores, axis=-1, keepdims=True)
    log_total = top_score + jnp.log(jnp.sum(jnp.exp(scores - top_score), axis=-1, keepdims=True))
    attention_low = jnp.exp(scores - log_total).astype(jnp.bfloat16)
    attended = jnp.einsum(
        "hqk,khd->qhd", attention_low, value_all, preferred_element_type=jnp.float32
    )
    attended_low = attended.reshape(token_count, local_width).astype(jnp.bfloat16)
    hidden_rows = token_rows + exchange(matmul_nt(attended_low, output_full))
    normed_two, mlp_norm_back = jax.vjp(normalize, hidden_rows, mlp_gain.astype(jnp.float32))
    normed_two_low = normed_two.astype(jnp.bfloat16)
    expanded = matmul(normed_two_low, up_full)
    activated, up_gelu_back = jax.vjp(gelu_exact, expanded)
    activated_low = activated.astype(jnp.bfloat16)
    result_rows = hidden_rows + exchange(matmul_nt(activated_low, down_full))

    widened = matmul(normed_map_pair, expand_full)
    widened_act, wide_gelu_back = jax.vjp(gelu_exact, widened)
    widened_low = widened_act.astype(jnp.bfloat16)
    narrowed_part = matmul_nt(widened_low, shrink_full)
    narrowed_part = narrowed_part[:pixel_count] + core_swap(
        narrowed_part[pixel_count:].astype(jnp.bfloat16)
    ).astype(jnp.float32)
    narrowed = exchange(narrowed_part).reshape(high_strip, high_side, channels)
    scale_wide = layer_scale.astype(jnp.float32)
    masked_map = high_map.astype(jnp.float32) * valid_mask
    mapped = valid_mask * (masked_map + scale_wide * narrowed)
    pooled = (
        jnp.sum(mapped.reshape(low_strip, 2, grid_side, 2, channels), axis=(1, 3)) * 0.25
    )
    pooled_low = pooled.reshape(token_count, channels).astype(jnp.bfloat16)
    lifted = matmul(pooled_low, adapter_full).reshape(low_strip, grid_side, own_width)

    result_grid = result_rows.reshape(low_strip, grid_side, width)
    own_result = lax.dynamic_slice_in_dim(result_grid, model_half * own_width, own_width, 2)
    own_padded = with_edges(own_result.astype(jnp.bfloat16), position)
    adapter_wide = adapter_kernel.astype(jnp.float32)
    local_mix = depth_apply(own_padded, adapter_wide, 1)
    gate_wide = gate_vector.astype(jnp.float32)
    gating = jax.nn.sigmoid(jnp.sum(result_grid * gate_wide, axis=-1, keepdims=True))
    blended = own_result + local_mix + gating * lifted

    local_grad_low = out_cotangent.reshape(low_strip, grid_side, own_width)
    out_grad = local_grad_low.astype(jnp.float32)
    lifted_grad_low = (out_grad * gating).reshape(token_count, own_width).astype(jnp.bfloat16)
    gate_part = jnp.sum(out_grad * lifted, axis=-1, keepdims=True)
    pooled_part = matmul_nt(lifted_grad_low, adapter_full)
    pooled_grad = exchange(pooled_part)
    gate_grad = exchange(gate_part)
    adapter_weight_slope = matmul_tn(pooled_low, lifted_grad_low).astype(jnp.bfloat16)
    local_padded = with_edges(local_grad_low, position)
    own_grad = out_grad + depth_apply(local_padded, adapter_wide[::-1], 1)
    adapter_kernel_slope = kernel_slopes(own_padded, out_grad, 1)
    own_grad_low = own_grad.astype(jnp.bfloat16)
    other_grad = lax.ppermute(own_grad_low, "mp", [(0, 1), (1, 0)])
    result_grad = in_core_order(own_grad_low, other_grad, model_half, 2).astype(jnp.float32)
    gate_slope = gate_grad * gating * (1.0 - gating)
    gate_vector_slope = jnp.sum((gate_slope * result_grid).reshape(token_count, width), axis=0)
    result_grad = (result_grad + gate_slope * gate_wide).reshape(token_count, width)

    pooled_spread = jnp.broadcast_to(
        (pooled_grad * 0.25).reshape(low_strip, 1, grid_side, 1, channels),
        (low_strip, 2, grid_side, 2, channels),
    ).reshape(high_strip, high_side, channels)
    map_grad = (
        map_cotangent.reshape(high_strip, high_side, channels).astype(jnp.float32) + pooled_spread
    ) * valid_mask
    narrowed_grad_low = (map_grad * scale_wide).reshape(pixel_count, channels).astype(jnp.bfloat16)
    layer_scale_slope = jnp.sum((map_grad * narrowed).reshape(pixel_count, channels), axis=0)
    narrowed_grad_pair = jnp.concatenate([narrowed_grad_low, core_swap(narrowed_grad_low)], axis=0)
    widened_grad = matmul(narrowed_grad_pair, shrink_full)
    widened_grad_low = wide_gelu_back(widened_grad)[0].astype(jnp.bfloat16)
    normed_map_part = matmul_nt(widened_grad_low, expand_full)
    normed_map_part = normed_map_part[:pixel_count] + core_swap(
        normed_map_part[pixel_count:].astype(jnp.bfloat16)
    ).astype(jnp.float32)
    normed_map_grad = exchange(normed_map_part)
    shrink_weight_slope = matmul_tn(narrowed_grad_pair, widened_low).astype(jnp.bfloat16)
    expand_weight_slope = matmul_tn(normed_map_pair, widened_grad_low).astype(jnp.bfloat16)
    expand_own, shrink_own = reduced_map_slopes(
        place, core, expand_weight_slope, shrink_weight_slope
    )

    result_low = result_grad.astype(jnp.bfloat16)
    activated_grad = matmul(result_low, down_full)
    down_weight_slope = matmul_tn(result_low, activated_low).astype(jnp.bfloat16)
    expanded_grad_low = up_gelu_back(activated_grad)[0].astype(jnp.bfloat16)
    up_weight_slope = matmul_tn(normed_two_low, expanded_grad_low).astype(jnp.bfloat16)
    normed_two_grad = exchange(matmul_nt(expanded_grad_low, up_full))
    hidden_part, mlp_gain_slope = mlp_norm_back(normed_two_grad)
    hidden_grad = result_grad + hidden_part
    hidden_low = hidden_grad.astype(jnp.bfloat16)
    attended_grad_low = matmul(hidden_low, output_full).astype(jnp.bfloat16)
    output_weight_slope = matmul_tn(hidden_low, attended_low).astype(jnp.bfloat16)
    attended_heads_grad = attended_grad_low.reshape(token_count, local_heads, HD)
    scores_again = (
        jnp.einsum("qhd,khd->hqk", query_heads, key_all, preferred_element_type=jnp.float32)
        * scaling
    )
    attention_again = jnp.exp(scores_again - log_total)
    attention_again_low = attention_again.astype(jnp.bfloat16)
    attention_grad = jnp.einsum(
        "qhd,khd->hqk", attended_heads_grad, value_all, preferred_element_type=jnp.float32
    )
    row_dot = jnp.sum(attention_again * attention_grad, axis=-1, keepdims=True)
    score_grad_low = (attention_again * (attention_grad - row_dot)).astype(jnp.bfloat16)
    query_grad_rows = (
        jnp.einsum("hqk,khd->qhd", score_grad_low, key_all, preferred_element_type=jnp.float32)
        * scaling
    ).astype(jnp.bfloat16).reshape(token_count, local_width)
    key_grad_all = (
        jnp.einsum("hqk,qhd->khd", score_grad_low, query_heads, preferred_element_type=jnp.float32)
        * scaling
    )
    value_grad_all = jnp.einsum(
        "hqk,qhd->khd", attention_again_low, attended_heads_grad, preferred_element_type=jnp.float32
    )
    pair_back = jnp.concatenate(
        [key_grad_all.reshape(-1, local_width), value_grad_all.reshape(-1, local_width)], axis=1
    )
    pair_back = pair_back[: 2 * token_count] + pair_swap(
        pair_back[2 * token_count :].astype(jnp.bfloat16)
    ).astype(jnp.float32)
    pair_back = pair_back[:token_count] + core_swap(
        pair_back[token_count:].astype(jnp.bfloat16)
    ).astype(jnp.float32)
    qkv_grad = jnp.concatenate([query_grad_rows, pair_back.astype(jnp.bfloat16)], axis=1)
    normed_grad = exchange(matmul_nt(qkv_grad, qkv_full))
    qkv_slope = matmul_tn(normed_low, qkv_grad).astype(jnp.bfloat16)
    input_part, attn_gain_slope = attn_norm_back(normed_grad)
    lowres_grad = (hidden_grad + input_part).reshape(low_strip, 1, grid_side, width)

    convolved_grad, conv_gain_slope = conv_norm_back(normed_map_grad)
    convolved_grad_low = convolved_grad.reshape(high_strip, high_side, channels).astype(
        jnp.bfloat16
    )
    grad_low, grad_high = halo_rows(convolved_grad_low, RADIUS)
    depth_kernel_slope = map_slopes(map_place, high_map, map_low, map_high, convolved_grad_low)
    highres_grad = map_conv(
        map_place, convolved_grad_low, grad_low, grad_high, depth_kernel, map_grad
    )

    def as_rows(values):
        return jnp.pad(values, ((0, 0), (0, channels - values.shape[1])))

    minor_rows = jnp.concatenate(
        [
            depth_kernel_slope,
            conv_gain_slope[None],
            layer_scale_slope[None],
            as_rows(jnp.stack([attn_gain_slope, mlp_gain_slope, gate_vector_slope], 0)),
            as_rows(adapter_kernel_slope),
        ],
        axis=0,
    )
    minor_used = minor_rows.shape[0]
    lines = channels // LANES
    minor = jnp.pad(
        minor_rows.astype(jnp.bfloat16).reshape(minor_used, lines, LANES),
        ((0, 2 * CHIPS - minor_used), (0, 3 * query_weight.shape[0] - lines), (0, 0)),
    )
    firsts, up_own, down_own, adapter_own, minor_own = reduced_other_slopes(
        place,
        core,
        qkv_slope,
        output_weight_slope,
        up_weight_slope,
        down_weight_slope,
        adapter_weight_slope,
        minor,
    )
    minor_all = gathered_rows(minor_own[:lines], device).reshape(2 * CHIPS, channels)
    taps = depth_kernel.shape[0]
    side_taps = adapter_kernel.shape[0]
    return (
        blended.astype(jnp.bfloat16)[:, None],
        mapped.astype(jnp.bfloat16)[:, None],
        lowres_grad,
        highres_grad[:, None],
        minor_all[taps + 2, :width],
        firsts[0],
        firsts[1],
        firsts[2],
        firsts[3].T,
        minor_all[taps + 3, :width],
        up_own,
        down_own.T,
        minor_all[:taps],
        minor_all[taps],
        expand_own,
        shrink_own.T,
        minor_all[taps + 1],
        adapter_own,
        minor_all[taps + 5 : taps + 5 + side_taps, :own_width],
        minor_all[taps + 4, :width],
    )


def solution(mesh):
    in_specs = (
        P("dp", None, None, None),
        P("dp", None, None, None),
        P(),
        P(),
        P("dp", "mp"),
        P("dp", "mp"),
        P("dp", "mp"),
        P("mp", "dp"),
        P(),
        P("dp", "mp"),
        P("mp", "dp"),
        P(),
        P(),
        P("dp", "mp"),
        P("mp", "dp"),
        P(),
        P("dp", "mp"),
        P(None, "mp"),
        P(),
        P("dp", None, None, "mp"),
        P("dp", None, None, None),
    )
    out_specs = (
        P("dp", None, None, "mp"),
        P("dp", None, None, None),
        P("dp", None, None, None),
        P("dp", None, None, None),
        P(),
        P("dp", "mp"),
        P("dp", "mp"),
        P("dp", "mp"),
        P("mp", "dp"),
        P(),
        P("dp", "mp"),
        P("mp", "dp"),
        P(),
        P(),
        P("dp", "mp"),
        P("mp", "dp"),
        P(),
        P("dp", "mp"),
        P(None, "mp"),
        P(),
    )
    return jax.shard_map(
        on_device, mesh=mesh, in_specs=in_specs, out_specs=out_specs, check_vma=False
    )
```

time: 4570 us -> 882 us (0.19)
  the two profiles are of different devices: /device:TPU:1 before, /device:TPU:2 now
where the time goes in v1:
time: 882 us; the launch traced here: 871 us
  waiting for transfers between devices  269 us (30%)
  starting transfers between devices  163 us (18%)
  local copies, waits for them, and re-layouts  134 us (15%)
  matrix products  120 us (14%)
  other arithmetic  97.3 us (11%)
  Pallas kernels  83.8 us (10%)
    ppermute x96, waiting for transfers between devices, xor_swap(): return lax.ppermute(values, 'dp', [(i, i ^ mask) for i in range(count)])  235 us
    ppermute x96, starting transfers between devices, xor_swap(): return lax.ppermute(values, 'dp', [(i, i ^ mask) for i in range(count)])  134 us
    dot_general x7, matrix products, matmul(): return jnp.dot(former, latter, preferred_element_type=jnp.float32)  52.5 us
    unnamed x335, local copies, waits for them, and re-layouts  38.9 us
    pallas_call x3, Pallas kernels, route(): pl.pallas_call(functools.partial(route_kernel, moves, len(arrays), len(sh...  33.5 us
    dot_general x7, matrix products, matmul_tn(): lax.dot_general(former, latter, (((0,), (0,)), ((), ())), preferred_eleme...  33.3 us
    pallas_call x2, Pallas kernels, map_conv(): pl.pallas_call(forward_kernel if added is None else backward_kernel, grid...  32.3 us
    ppermute x8, waiting for transfers between devices, exchange(): other = lax.ppermute(low, 'mp', [(0, 1), (1, 0)])  24.3 us
  transfers between devices with their start and end apart: 115, of which 40 were waited for; matrix products, arithmetic and copies ran while one was open for 33% of the time, Pallas kernels for 9%

profile of v1, /device:TPU:2, one launch (start us, length us, event | category | flops | bytes accessed | tf_op | source)
XLA Modules:
  0.0 871.1 jit_solution(11188740673937759206)
XLA Ops:
  16.2 3.6 reshape.613
  29.4 3.8 bitcast_convert_fusion
  49.0 8.4 collective-permute-done.8
  65.4 12.2 %collective-permute-done.9 = bf16[8,48,1152]{2,1,0:T(8,128)(2,1)S(1)} collective-permute-done((bf16[8,48,1152]{2,1,0:T(8,128)(2,1)S(1)}, bf16[8,48,1152]{2,1,0:T(8,128)(2,1)S(1)}, u32[]{:S(2)}, u32[]{:S(2)}) %collective-permute-start.9) | collective-permute-done | bytes 884768 | tf_op jit(solution)/shard_map/ppermute | solution.py:183
  78.9 3.8 collective-permute-start.10
  96.0 29.4 %collective-permute-done.24 = bf16[2,48,1024]{2,1,0:T(8,128)(2,1)S(1)} collective-permute-done((bf16[2,48,1024]{2,1,0:T(8,128)(2,1)S(1)}, bf16[2,48,1024]{2,1,0:T(8,128)(2,1)S(1)}, u32[]{:S(2)}, u32[]{:S(2)}) %collective-permute-start.24) | collective-permute-done | bytes 196640 | tf_op jit(solution)/shard_map/ppermute | solution.py:183
  138.5 4.5 collective-permute-start.20
  145.8 15.6 %shard_map.357 = f32[12,48,1536]{2,1,0:T(8,128)S(1)} custom-call(s32[2]{0:T(128)S(1)} %pad_add_fusion.place, bf16[12,48,1536]{2,1,0:T(8,128)(2,1)S(1)} %bitcast.265, bf16[3,48,1536]{2,1,0:T(8,128)(2,1)S(1)} %copy-done.11, bf16[3,48,1536]{2,1,0:T(8,128)(2,1)S(1)} %collective-permute-done.35.high_ref, bf16[49,1536]{1,0:T(8,128)(2,1)S(1)} %copy-done.16), custom_call_target="tpu_custom_call" | custom-call | flops 86704128 | bytes 7077888 | tf_op jit(solution)/shard_map/pallas_call | solution.py:142
  178.2 5.0 collective-permute-done.26
  184.5 3.7 collective-permute-start.27
  206.7 14.2 %collective-permute-done.27 = bf16[16,48,1024]{2,1,0:T(8,128)(2,1)} collective-permute-done((bf16[16,48,1024]{2,1,0:T(8,128)(2,1)}, bf16[16,48,1024]{2,1,0:T(8,128)(2,1)}, u32[]{:S(2)}, u32[]{:S(2)}) %collective-permute-start.27) | collective-permute-done | bytes 1572896 | tf_op jit(solution)/shard_map/ppermute | solution.py:183
  224.5 7.6 collective-permute-done.22
  238.0 14.9 %shard_map.356 = (bf16[64,16,1536]{2,1,0:T(8,128)(2,1)S(1)}, bf16[64,16,512]{2,1,0:T(8,128)(2,1)S(1)}, bf16[64,16,2048]{2,1,0:T(8,128)(2,1)}, bf16[64,16,2048]{2...) custom-call(s32[1]{0:T(128)} %bitcast.2.place, ...), custom_call_target="tpu_custom_call" | custom-call | bytes 47185920 | tf_op jit(solution)/shard_map/pallas_call | solution.py:249
  258.0 23.0 %multiply_convert_fusion = (bf16[1152,1536]{1,0:T(8,128)(2,1)}, f32[1152,1536]{1,0:T(8,128)}, f32[1152,1536]{1,0:T(8,128)}) fusion(bf16[1536,1536]{1,0:T(8,128)(2,1)S(1)} %bitcast.351, bf16[576,1536]{1,0:T(8,128)(2,1)S(1)} %collective-permute-done.36, bf16[576,1536]{1,0:T(8,128)(2,1)S(1)} %get-tuple-element.139), kind=kOutput, calls=%fused_computation.5 | convolution fusion | flops 5557911552 | bytes 25952256 | tf_op jit(solution)/shard_map/dot_general | solution.py:305
  294.7 3.7 collective-permute-start.30
  298.3 7.7 fusion.109
  311.6 4.9 multiply_convert_fusion.5
  325.8 3.9 reshape.616
  336.1 6.0 collective-permute-start.33
  345.2 3.6 collective-permute-start.38
  352.8 5.5 reshape.601
  358.3 5.5 reshape.602
  363.8 4.9 fusion.8.add_ref
  368.7 17.0 %collective-permute-done.38 = bf16[576,1536]{1,0:T(8,128)(2,1)} collective-permute-done((bf16[576,1536]{1,0:T(8,128)(2,1)S(1)}, bf16[576,1536]{1,0:T(8,128)(2,1)}, u32[]{:S(2)}, u32[]{:S(2)}) %collective-permute-start.38) | collective-permute-done | bytes 1769504 | tf_op jit(solution)/shard_map/ppermute | solution.py:280
  385.7 6.4 multiply_reduce_fusion
  392.1 5.4 reshape.591
  397.5 6.6 multiply_reduce_fusion.3
  407.6 4.1 multiply_convert_fusion.2
  412.4 6.4 add_convert_fusion.17
  425.4 3.5 reshape.607
  439.8 4.7 multiply_reduce_fusion.5
  449.1 3.5 multiply_convert_fusion.4
  459.9 4.5 convolution_convert_fusion.3
  467.8 7.0 collective-permute-done.44
  488.9 6.6 collective-permute-done.46
  499.9 9.2 %convolution_convert_fusion = bf16[1536,1536]{1,0:T(8,128)(2,1)S(1)} fusion(bf16[1152,1536]{1,0:T(8,128)(2,1)} %get-tuple-element.137, bf16[576,1536]{1,0:T(8,128)(2,1)} %collective-permute-done.48, bf16[576,1536]{1,0:T(8,128)(2,1)} %get-tuple-element.146), kind=kOutput, calls=%fused_computation.1 | convolution fusion | flops 5445255168 | bytes 11796480 | tf_op jit(solution)/shard_map/dot_general | solution.py:315
  509.2 13.6 %add_convert_fusion = bf16[1152,1536]{1,0:T(8,128)(2,1)} fusion(f32[1152,1536]{1,0:T(8,128)} %get-tuple-element.138, f32[1152,1536]{1,0:T(8,128)} %get-tuple-element.253, bf16[1536,1536]{1,0:T(8,128)(2,1)} %bitcast.356, bf16[576,1536]{1,0:T(8,128)(2,1)} %collective-permute-done.48, bf16[576,1536]{1,0:T(8,128)(2,1)S(1)} %copy-done.52), kind=kOutput, calls=%fused_computation.4 | convolution fusion | flops 5467668480 | bytes 25952256 | tf_op jit(solution)/shard_map/dot_general | solution.py:305
  522.8 8.6 convolution_convert_fusion.1
  531.4 5.1 shard_map.361
  536.8 3.8 collective-permute-start.104
  541.3 5.7 fusion.110
  548.5 7.3 collective-permute-done.109
  555.8 11.6 %collective-permute-start.89 = (bf16[16,48,640]{2,1,0:T(8,128)(2,1)S(1)}, bf16[16,48,640]{2,1,0:T(8,128)(2,1)S(1)}, u32[]{:S(2)}, u32[]{:S(2)}) collective-permute-start(bf16[16,48,640]{2,1,0:T(8,128)(2,1)S(1)} %slice.791), channel_id=1, source_target_pairs={{0,4},{2,6},{4,0},{6,2},{8,12},{10,14},{12,8},{14,10},{16,20},{18,... | collective-permute-start | bytes 2949128 | tf_op jit(solution)/shard_map/ppermute | solution.py:183
  567.7 5.9 collective-permute-start.110
  575.4 21.1 %collective-permute-done.110 = bf16[8,48,512]{2,1,0:T(8,128)(2,1)S(1)} collective-permute-done((bf16[8,48,512]{2,1,0:T(8,128)(2,1)S(1)}, bf16[8,48,512]{2,1,0:T(8,128)(2,1)S(1)}, u32[]{:S(2)}, u32[]{:S(2)}) %collective-permute-start.110) | collective-permute-done | bytes 393248 | tf_op jit(solution)/shard_map/ppermute | solution.py:183
  597.1 5.3 collective-permute-done.111
  605.0 9.7 %collective-permute-done.112 = bf16[2,48,512]{2,1,0:T(8,128)(2,1)S(1)} collective-permute-done((bf16[2,48,512]{2,1,0:T(8,128)(2,1)S(1)}, bf16[2,48,512]{2,1,0:T(8,128)(2,1)S(1)}, u32[]{:S(2)}, u32[]{:S(2)}) %collective-permute-start.112) | collective-permute-done | bytes 98336 | tf_op jit(solution)/shard_map/ppermute | solution.py:183
  624.0 4.4 collective-permute-start.96
  636.9 4.2 collective-permute-start.92
  645.5 31.0 %collective-permute-done.93 = bf16[1,48,640]{2,1,0:T(8,128)(2,1)S(1)} collective-permute-done((bf16[1,48,640]{2,1,0:T(8,128)(2,1)S(1)}, bf16[1,48,640]{2,1,0:T(8,128)(2,1)S(1)}, u32[]{:S(2)}, u32[]{:S(2)}) %collective-permute-start.93) | collective-permute-done | bytes 61472 | tf_op jit(solution)/shard_map/ppermute | solution.py:183
  676.9 3.9 collective-permute-done.98
  686.4 18.0 %shard_map.359 = f32[49,1536]{1,0:T(8,128)S(1)} custom-call(s32[2]{0:T(128)S(1)} %copy-done.19, bf16[12,48,1536]{2,1,0:T(8,128)(2,1)S(1)} %bitcast.266, bf16[3,48,1536]{2,1,0:T(8,128)(2,1)S(1)} %copy-done.12, bf16[3,48,1536]{2,1,0:T(8,128)(2,1)S(1)} %copy-done.14, bf16[12,48,1536]{2,1,0:T(8,128)(2,1)S(1)} %bitcast.268), custom_call_target="tpu_custom_call" | custom-call | flops 86704128 | bytes 3538944 | tf_op jit(solution)/shard_map/pallas_call | solution.py:162
  716.0 13.5 %shard_map.360 = (bf16[64,48,512]{2,1,0:T(8,128)(2,1)S(1)}, bf16[64,48,512]{2,1,0:T(8,128)(2,1)S(1)}, bf16[64,48,512]{2,1,0:T(8,128)(2,1)S(1)}, bf16[64,48,512]{2,1,0:T(8,128)(2,1)S(1)}, bf16[64,48,384]{2,1,0:T(8,128)(2,1)S(1)}) custom-call(s32[1]{0:T(128)} %bitcast.2.place, bf16[64,16,1536]{2,1,0:T(8,128)(2,1)S(1)} %bitcast.270, ...), custom_call_target="tpu_custom_call" | custom-call | bytes 29884416 | tf_op jit(solution)/shard_map/pallas_call | solution.py:249
  741.7 16.7 %shard_map.358 = f32[12,48,1536]{2,1,0:T(8,128)} custom-call(s32[2]{0:T(128)S(1)} %copy-done.19, bf16[12,48,1536]{2,1,0:T(8,128)(2,1)S(1)} %bitcast.269, bf16[3,48,1536]{2,1,0:T(8,128)(2,1)S(1)} %collective-permute-done.51.low_ref, bf16[3,48,1536]{2,1,0:T(8,128)(2,1)S(1)} %collective-permute-done.52.high_ref, bf16[49,1536]{1,0:T(8,128)(2,1)S(1)} %copy-done.17, ...), custom_call_target="tpu_custom_call" | custom-call | flops 86704128 | bytes 7077888 | tf_op jit(solution)/shard_map/pallas_call | solution.py:142
  758.6 4.9 collective-permute-start.55
  764.2 6.5 collective-permute-done.55
  771.6 4.5 collective-permute-done.56
  777.3 14.8 %collective-permute-done.57 = bf16[2,48,384]{2,1,0:T(8,128)(2,1)S(1)} collective-permute-done((bf16[2,48,384]{2,1,0:T(8,128)(2,1)S(1)}, bf16[2,48,384]{2,1,0:T(8,128)(2,1)S(1)}, u32[]{:S(2)}, u32[]{:S(2)}) %collective-permute-start.57) | collective-permute-done | bytes 73760 | tf_op jit(solution)/shard_map/ppermute | solution.py:183
  792.2 5.3 collective-permute-start.58
  803.3 12.6 %collective-permute-done.60 = f32[2,12,128]{2,1,0:T(8,128)S(1)} collective-permute-done((f32[2,12,128]{2,1,0:T(8,128)S(1)}, f32[2,12,128]{2,1,0:T(8,128)S(1)}, u32[]{:S(2)}, u32[]{:S(2)}) %collective-permute-start.60) | collective-permute-done | bytes 12320 | tf_op jit(solution)/shard_map/ppermute | solution.py:183
  823.4 6.9 collective-permute-done.62
  831.4 5.5 collective-permute-done.63
  837.1 6.3 collective-permute-done.64
  847.9 5.6 collective-permute-start.74
  (838 shorter events, 324.7 us)
Async XLA Ops:
  2.5 38.0 %collective-permute-start.12 = (bf16[24,3072]{1,0:T(8,128)(2,1)}, bf16[24,3072]{1,0:T(8,128)(2,1)}, u32[]{:S(2)}, u32[]{:S(2)}) collective-permute-start(bf16[24,3072]{1,0:T(8,128)(2,1)} %pad_maximum_fusion.29), channel_id=1, source_target_pairs={{0,2},{2,0},{4,6},{6,4},{8,10},{10,8},{12,14},{14,12},{16,18},{18,... | collective-permute-start | bytes 442376 | tf_op jit(solution)/shard_map/ppermute | solution.py:183
  4.8 32.5 %collective-permute-start.6 = (bf16[1,48,1152]{2,1,0:T(8,128)(2,1)S(1)}, bf16[1,48,1152]{2,1,0:T(8,128)(2,1)S(1)}, u32[]{:S(2)}, u32[]{:S(2)}) collective-permute-start(bf16[1,48,1152]{2,1,0:T(8,128)(2,1)S(1)} %get-tuple-element.142), channel_id=1, source_target_pairs={{0,12},{2,14},{4,8},{6,10},{8,4},{10,6},{12,0},{14,2},{16,28},{18,... | collective-permute-start | bytes 331784 | tf_op jit(solution)/shard_map/ppermute | solution.py:183
  6.3 32.7 %collective-permute-start = (bf16[1,48,1152]{2,1,0:T(8,128)(2,1)S(1)}, bf16[1,48,1152]{2,1,0:T(8,128)(2,1)S(1)}, u32[]{:S(2)}, u32[]{:S(2)}) collective-permute-start(bf16[1,48,1152]{2,1,0:T(8,128)(2,1)S(1)} %get-tuple-element.203), channel_id=1, source_target_pairs={{0,4},{2,6},{4,0},{6,2},{8,12},{10,14},{12,8},{14,10},{16,20},{18,... | collective-permute-start | bytes 331784 | tf_op jit(solution)/shard_map/ppermute | solution.py:183
  10.1 127.7 %collective-permute-start.34 = (bf16[3,48,1536]{2,1,0:T(8,128)(2,1)}, bf16[3,48,1536]{2,1,0:T(8,128)(2,1)S(1)}, u32[]{:S(2)}, u32[]{:S(2)}) collective-permute-start(bf16[3,48,1536]{2,1,0:T(8,128)(2,1)} %get-tuple-element.151), channel_id=1, source_target_pairs={{0,2},{2,4},{4,6},{6,8},{8,10},{10,12},{12,14},{14,16},{16,18},{18... | collective-permute-start | bytes 1327112 | tf_op jit(solution)/shard_map/ppermute | solution.py:288
  41.6 48.1 %collective-permute-start.23 = (bf16[1,48,1024]{2,1,0:T(8,128)(2,1)S(1)}, bf16[1,48,1024]{2,1,0:T(8,128)(2,1)S(1)}, u32[]{:S(2)}, u32[]{:S(2)}) collective-permute-start(bf16[1,48,1024]{2,1,0:T(8,128)(2,1)S(1)} %get-tuple-element.189), channel_id=1, source_target_pairs={{0,64},{2,66},{4,68},{6,70},{8,72},{10,74},{12,76},{14,78},{16,80}... | collective-permute-start | bytes 294920 | tf_op jit(solution)/shard_map/ppermute | solution.py:183
  57.5 20.1 %collective-permute-start.9 = (bf16[8,48,1152]{2,1,0:T(8,128)(2,1)S(1)}, bf16[8,48,1152]{2,1,0:T(8,128)(2,1)S(1)}, u32[]{:S(2)}, u32[]{:S(2)}) collective-permute-start(bf16[8,48,1152]{2,1,0:T(8,128)(2,1)S(1)} %pad_maximum_fusion.11), channel_id=1, source_target_pairs={{0,64},{2,66},{4,68},{6,70},{8,72},{10,74},{12,76},{14,78},{16,80}... | collective-permute-start | bytes 2654216 | tf_op jit(solution)/shard_map/ppermute | solution.py:183
  59.6 23.1 %collective-permute-start.3 = (bf16[8,48,1152]{2,1,0:T(8,128)(2,1)S(1)}, bf16[8,48,1152]{2,1,0:T(8,128)(2,1)S(1)}, u32[]{:S(2)}, u32[]{:S(2)}) collective-permute-start(bf16[8,48,1152]{2,1,0:T(8,128)(2,1)S(1)} %pad_maximum_fusion.10), channel_id=1, source_target_pairs={{0,48},{2,50},{4,52},{6,54},{8,56},{10,58},{12,60},{14,62},{16,32}... | collective-permute-start | bytes 2654216 | tf_op jit(solution)/shard_map/ppermute | solution.py:183
  78.9 86.2 %collective-permute-start.10 = (bf16[16,48,1152]{2,1,0:T(8,128)(2,1)}, bf16[16,48,1152]{2,1,0:T(8,128)(2,1)}, u32[]{:S(2)}, u32[]{:S(2)}) collective-permute-start(bf16[16,48,1152]{2,1,0:T(8,128)(2,1)} %get-tuple-element.154), channel_id=1, source_target_pairs={{0,4},{2,6},{4,0},{6,2},{8,12},{10,14},{12,8},{14,10},{16,20},{18,... | collective-permute-start | bytes 5308424 | tf_op jit(solution)/shard_map/ppermute | solution.py:183
  84.0 83.9 %collective-permute-start.4 = (bf16[16,48,1152]{2,1,0:T(8,128)(2,1)}, bf16[16,48,1152]{2,1,0:T(8,128)(2,1)}, u32[]{:S(2)}, u32[]{:S(2)}) collective-permute-start(bf16[16,48,1152]{2,1,0:T(8,128)(2,1)} %get-tuple-element.156), channel_id=1, source_target_pairs={{0,64},{2,66},{4,68},{6,70},{8,72},{10,74},{12,76},{14,78},{16,80}... | collective-permute-start | bytes 5308424 | tf_op jit(solution)/shard_map/ppermute | solution.py:183
  92.5 33.0 %collective-permute-start.24 = (bf16[2,48,1024]{2,1,0:T(8,128)(2,1)S(1)}, bf16[2,48,1024]{2,1,0:T(8,128)(2,1)S(1)}, u32[]{:S(2)}, u32[]{:S(2)}) collective-permute-start(bf16[2,48,1024]{2,1,0:T(8,128)(2,1)S(1)} %pad_maximum_fusion.28), channel_id=1, source_target_pairs={{0,4},{2,6},{4,0},{6,2},{8,12},{10,14},{12,8},{14,10},{16,20},{18,... | collective-permute-start | bytes 589832 | tf_op jit(solution)/shard_map/ppermute | solution.py:183
  94.3 33.9 %collective-permute-start.19 = (bf16[2,48,1024]{2,1,0:T(8,128)(2,1)S(1)}, bf16[2,48,1024]{2,1,0:T(8,128)(2,1)S(1)}, u32[]{:S(2)}, u32[]{:S(2)}) collective-permute-start(bf16[2,48,1024]{2,1,0:T(8,128)(2,1)S(1)} %pad_maximum_fusion.27), channel_id=1, source_target_pairs={{0,64},{2,66},{4,68},{6,70},{8,72},{10,74},{12,76},{14,78},{16,80}... | collective-permute-start | bytes 589832 | tf_op jit(solution)/shard_map/ppermute | solution.py:183
  125.5 17.6 %collective-permute-start.35 = (bf16[3,48,1536]{2,1,0:T(8,128)(2,1)S(1)}, bf16[3,48,1536]{2,1,0:T(8,128)(2,1)S(1)}, u32[]{:S(2)}, u32[]{:S(2)}) collective-permute-start(bf16[3,48,1536]{2,1,0:T(8,128)(2,1)S(1)} %get-tuple-element.150), channel_id=1, source_target_pairs={{2,0},{4,2},{6,4},{8,6},{10,8},{12,10},{14,12},{16,14},{18,16},{20... | collective-permute-start | bytes 1327112 | tf_op jit(solution)/shard_map/ppermute | solution.py:289
  135.2 28.6 %collective-permute-start.25 = (bf16[4,48,1024]{2,1,0:T(8,128)(2,1)}, bf16[4,48,1024]{2,1,0:T(8,128)(2,1)}, u32[]{:S(2)}, u32[]{:S(2)}) collective-permute-start(bf16[4,48,1024]{2,1,0:T(8,128)(2,1)} %pad_maximum_fusion.21), channel_id=1, source_target_pairs={{0,12},{2,14},{4,8},{6,10},{8,4},{10,6},{12,0},{14,2},{16,28},{18,... | collective-permute-start | bytes 1179656 | tf_op jit(solution)/shard_map/ppermute | solution.py:183
  138.5 35.3 %collective-permute-start.20 = (bf16[4,48,1024]{2,1,0:T(8,128)(2,1)}, bf16[4,48,1024]{2,1,0:T(8,128)(2,1)}, u32[]{:S(2)}, u32[]{:S(2)}) collective-permute-start(bf16[4,48,1024]{2,1,0:T(8,128)(2,1)} %pad_maximum_fusion.20), channel_id=1, source_target_pairs={{0,4},{2,6},{4,0},{6,2},{8,12},{10,14},{12,8},{14,10},{16,20},{18,... | collective-permute-start | bytes 1179656 | tf_op jit(solution)/shard_map/ppermute | solution.py:183
  143.1 31.9 %collective-permute-start.15 = (bf16[4,48,1024]{2,1,0:T(8,128)(2,1)}, bf16[4,48,1024]{2,1,0:T(8,128)(2,1)}, u32[]{:S(2)}, u32[]{:S(2)}) collective-permute-start(bf16[4,48,1024]{2,1,0:T(8,128)(2,1)} %pad_maximum_fusion.19), channel_id=1, source_target_pairs={{0,64},{2,66},{4,68},{6,70},{8,72},{10,74},{12,76},{14,78},{16,80}... | collective-permute-start | bytes 1179656 | tf_op jit(solution)/shard_map/ppermute | solution.py:183
  165.0 18.2 %collective-permute-start.26 = (bf16[8,48,1024]{2,1,0:T(8,128)(2,1)S(1)}, bf16[8,48,1024]{2,1,0:T(8,128)(2,1)S(1)}, u32[]{:S(2)}, u32[]{:S(2)}) collective-permute-start(bf16[8,48,1024]{2,1,0:T(8,128)(2,1)S(1)} %pad_maximum_fusion.14), channel_id=1, source_target_pairs={{0,16},{2,18},{4,20},{6,22},{8,24},{10,26},{12,28},{14,30},{16,0},... | collective-permute-start | bytes 2359304 | tf_op jit(solution)/shard_map/ppermute | solution.py:183
  167.9 70.1 %collective-permute-start.11 = (bf16[32,48,1152]{2,1,0:T(8,128)(2,1)}, bf16[32,48,1152]{2,1,0:T(8,128)(2,1)}, u32[]{:S(2)}, u32[]{:S(2)}) collective-permute-start(bf16[32,48,1152]{2,1,0:T(8,128)(2,1)} %constant_dynamic-update-slice_fusion.16.refs_2_), channel_id=1, source_target_pairs={{0,2},{2,0},{4,6},{6,4},{8,10},{10,8},{12,14},{14,12},{16,18},{18,... | collective-permute-start | bytes 10616840 | tf_op jit(solution)/shard_map/ppermute | solution.py:183
  170.8 67.2 %collective-permute-start.5 = (bf16[32,48,1152]{2,1,0:T(8,128)(2,1)}, bf16[32,48,1152]{2,1,0:T(8,128)(2,1)}, u32[]{:S(2)}, u32[]{:S(2)}) collective-permute-start(bf16[32,48,1152]{2,1,0:T(8,128)(2,1)} %constant_dynamic-update-slice_fusion.5.refs_0_), channel_id=1, source_target_pairs={{0,2},{2,0},{4,6},{6,4},{8,10},{10,8},{12,14},{14,12},{16,18},{18,... | collective-permute-start | bytes 10616840 | tf_op jit(solution)/shard_map/ppermute | solution.py:183
  174.9 19.6 %collective-permute-start.21 = (bf16[8,48,1024]{2,1,0:T(8,128)(2,1)S(1)}, bf16[8,48,1024]{2,1,0:T(8,128)(2,1)S(1)}, u32[]{:S(2)}, u32[]{:S(2)}) collective-permute-start(bf16[8,48,1024]{2,1,0:T(8,128)(2,1)S(1)} %pad_maximum_fusion.13), channel_id=1, source_target_pairs={{0,12},{2,14},{4,8},{6,10},{8,4},{10,6},{12,0},{14,2},{16,28},{18,... | collective-permute-start | bytes 2359304 | tf_op jit(solution)/shard_map/ppermute | solution.py:183
  176.1 21.7 %collective-permute-start.16 = (bf16[8,48,1024]{2,1,0:T(8,128)(2,1)S(1)}, bf16[8,48,1024]{2,1,0:T(8,128)(2,1)S(1)}, u32[]{:S(2)}, u32[]{:S(2)}) collective-permute-start(bf16[8,48,1024]{2,1,0:T(8,128)(2,1)S(1)} %pad_maximum_fusion.12), channel_id=1, source_target_pairs={{0,4},{2,6},{4,0},{6,2},{8,12},{10,14},{12,8},{14,10},{16,20},{18,... | collective-permute-start | bytes 2359304 | tf_op jit(solution)/shard_map/ppermute | solution.py:183
  184.5 36.3 %collective-permute-start.27 = (bf16[16,48,1024]{2,1,0:T(8,128)(2,1)}, bf16[16,48,1024]{2,1,0:T(8,128)(2,1)}, u32[]{:S(2)}, u32[]{:S(2)}) collective-permute-start(bf16[16,48,1024]{2,1,0:T(8,128)(2,1)} %get-tuple-element.158), channel_id=1, source_target_pairs={{0,48},{2,50},{4,52},{6,54},{8,56},{10,58},{12,60},{14,62},{16,32}... | collective-permute-start | bytes 4718600 | tf_op jit(solution)/shard_map/ppermute | solution.py:183
  195.9 36.2 %collective-permute-start.22 = (bf16[16,48,1024]{2,1,0:T(8,128)(2,1)}, bf16[16,48,1024]{2,1,0:T(8,128)(2,1)}, u32[]{:S(2)}, u32[]{:S(2)}) collective-permute-start(bf16[16,48,1024]{2,1,0:T(8,128)(2,1)} %get-tuple-element.160), channel_id=1, source_target_pairs={{0,16},{2,18},{4,20},{6,22},{8,24},{10,26},{12,28},{14,30},{16,0},... | collective-permute-start | bytes 4718600 | tf_op jit(solution)/shard_map/ppermute | solution.py:183
  199.2 35.7 %collective-permute-start.17 = (bf16[16,48,1024]{2,1,0:T(8,128)(2,1)}, bf16[16,48,1024]{2,1,0:T(8,128)(2,1)}, u32[]{:S(2)}, u32[]{:S(2)}) collective-permute-start(bf16[16,48,1024]{2,1,0:T(8,128)(2,1)} %get-tuple-element.162), channel_id=1, source_target_pairs={{0,12},{2,14},{4,8},{6,10},{8,4},{10,6},{12,0},{14,2},{16,28},{18,... | collective-permute-start | bytes 4718600 | tf_op jit(solution)/shard_map/ppermute | solution.py:183
  220.8 37.1 %collective-permute-start.36 = (bf16[576,1536]{1,0:T(8,128)(2,1)S(1)}, bf16[576,1536]{1,0:T(8,128)(2,1)S(1)}, u32[]{:S(2)}, u32[]{:S(2)}) collective-permute-start(bf16[576,1536]{1,0:T(8,128)(2,1)S(1)} %get-tuple-element.139), channel_id=1, source_target_pairs={{0,2},{2,0},{4,6},{6,4},{8,10},{10,8},{12,14},{14,12},{16,18},{18,... | collective-permute-start | bytes 5308424 | tf_op jit(solution)/shard_map/ppermute | solution.py:183
  232.1 22.0 %collective-permute-start.40 = (bf16[1,24,512]{2,1,0:T(8,128)(2,1)S(1)}, bf16[1,24,512]{2,1,0:T(8,128)(2,1)S(1)}, u32[]{:S(2)}, u32[]{:S(2)}) collective-permute-start(bf16[1,24,512]{2,1,0:T(8,128)(2,1)S(1)} %copy-done.109), channel_id=1, source_target_pairs={{2,0},{4,2},{6,4},{8,6},{10,8},{12,10},{14,12},{16,14},{18,16},{20... | collective-permute-start | bytes 73736 | tf_op jit(solution)/shard_map/ppermute | solution.py:289
  234.9 19.2 %collective-permute-start.39 = (bf16[1,24,512]{2,1,0:T(8,128)(2,1)S(1)}, bf16[1,24,512]{2,1,0:T(8,128)(2,1)S(1)}, u32[]{:S(2)}, u32[]{:S(2)}) collective-permute-start(bf16[1,24,512]{2,1,0:T(8,128)(2,1)S(1)} %copy-done.108), channel_id=1, source_target_pairs={{0,2},{2,4},{4,6},{6,8},{8,10},{10,12},{12,14},{14,16},{16,18},{18... | collective-permute-start | bytes 73736 | tf_op jit(solution)/shard_map/ppermute | solution.py:288
  256.1 25.7 %collective-permute-start.29 = (bf16[288,1024]{1,0:T(8,128)(2,1)}, bf16[288,1024]{1,0:T(8,128)(2,1)}, u32[]{:S(2)}, u32[]{:S(2)}) collective-permute-start(bf16[288,1024]{1,0:T(8,128)(2,1)} %pad_maximum_fusion.15), channel_id=1, source_target_pairs={{0,124},{2,126},{4,8},{6,10},{8,4},{10,6},{12,16},{14,18},{16,12},... | collective-permute-start | bytes 1769480 | tf_op jit(solution)/shard_map/ppermute | solution.py:326
  307.5 34.6 %collective-permute-start.37 = (bf16[576,1536]{1,0:T(8,128)(2,1)}, bf16[576,1536]{1,0:T(8,128)(2,1)}, u32[]{:S(2)}, u32[]{:S(2)}) collective-permute-start(bf16[576,1536]{1,0:T(8,128)(2,1)} %slice.1248), channel_id=1, source_target_pairs={{0,2},{2,0},{4,6},{6,4},{8,10},{10,8},{12,14},{14,12},{16,18},{18,... | collective-permute-start | bytes 5308424 | tf_op jit(solution)/shard_map/ppermute | solution.py:183
  320.0 92.4 %collective-permute-start.41 = (bf16[6,24,512]{2,1,0:T(8,128)(2,1)}, bf16[6,24,512]{2,1,0:T(8,128)(2,1)}, u32[]{:S(2)}, u32[]{:S(2)}) collective-permute-start(bf16[6,24,512]{2,1,0:T(8,128)(2,1)} %fusion.57), channel_id=1, source_target_pairs={{0,1},{1,0},{2,3},{3,2},{4,5},{5,4},{6,7},{7,6},{8,9},{9,8},{10,11... | collective-permute-start | bytes 442376 | tf_op jit(solution)/shard_map/ppermute | solution.py:732
  334.8 14.8 %collective-permute-start.47 = (bf16[144,1536]{1,0:T(8,128)(2,1)S(1)}, bf16[144,1536]{1,0:T(8,128)(2,1)S(1)}, u32[]{:S(2)}, u32[]{:S(2)}) collective-permute-start(bf16[144,1536]{1,0:T(8,128)(2,1)S(1)} %convolution_convert_fusion.6), channel_id=1, source_target_pairs={{0,1},{1,0},{2,3},{3,2},{4,5},{5,4},{6,7},{7,6},{8,9},{9,8},{10,11... | collective-permute-start | bytes 1327112 | tf_op jit(solution)/shard_map/ppermute | solution.py:280
  345.2 40.5 %collective-permute-start.38 = (bf16[576,1536]{1,0:T(8,128)(2,1)S(1)}, bf16[576,1536]{1,0:T(8,128)(2,1)}, u32[]{:S(2)}, u32[]{:S(2)}) collective-permute-start(bf16[576,1536]{1,0:T(8,128)(2,1)S(1)} %fusion.7), channel_id=1, source_target_pairs={{0,1},{1,0},{2,3},{3,2},{4,5},{5,4},{6,7},{7,6},{8,9},{9,8},{10,11... | collective-permute-start | bytes 5308424 | tf_op jit(solution)/shard_map/ppermute | solution.py:280
  407.4 92.5 %collective-permute-start.48 = (bf16[576,1536]{1,0:T(8,128)(2,1)}, bf16[576,1536]{1,0:T(8,128)(2,1)}, u32[]{:S(2)}, u32[]{:S(2)}) collective-permute-start(bf16[576,1536]{1,0:T(8,128)(2,1)} %get-tuple-element.146), channel_id=1, source_target_pairs={{0,2},{2,0},{4,6},{6,4},{8,10},{10,8},{12,14},{14,12},{16,18},{18,... | collective-permute-start | bytes 5308424 | tf_op jit(solution)/shard_map/ppermute | solution.py:183
  459.3 15.5 %collective-permute-start.44 = (bf16[288,1024]{1,0:T(8,128)(2,1)S(1)}, bf16[288,1024]{1,0:T(8,128)(2,1)S(1)}, u32[]{:S(2)}, u32[]{:S(2)}) collective-permute-start(bf16[288,1024]{1,0:T(8,128)(2,1)S(1)} %fusion.18), channel_id=1, source_target_pairs={{0,124},{2,126},{4,8},{6,10},{8,4},{10,6},{12,16},{14,18},{16,12},... | collective-permute-start | bytes 1769480 | tf_op jit(solution)/shard_map/ppermute | solution.py:326
  536.6 19.2 %collective-permute-start.109 = (bf16[16,48,512]{2,1,0:T(8,128)(2,1)S(1)}, bf16[16,48,512]{2,1,0:T(8,128)(2,1)S(1)}, u32[]{:S(2)}, u32[]{:S(2)}) collective-permute-start(bf16[16,48,512]{2,1,0:T(8,128)(2,1)S(1)} %slice.831), channel_id=1, source_target_pairs={{0,64},{2,66},{4,68},{6,70},{8,72},{10,74},{12,76},{14,78},{16,80}... | collective-permute-start | bytes 2359304 | tf_op jit(solution)/shard_map/ppermute | solution.py:183
  536.8 30.9 %collective-permute-start.104 = (bf16[16,48,640]{2,1,0:T(8,128)(2,1)S(1)}, bf16[16,48,640]{2,1,0:T(8,128)(2,1)S(1)}, u32[]{:S(2)}, u32[]{:S(2)}) collective-permute-start(bf16[16,48,640]{2,1,0:T(8,128)(2,1)S(1)} %slice.821), channel_id=1, source_target_pairs={{0,48},{2,50},{4,52},{6,54},{8,56},{10,58},{12,60},{14,62},{16,32}... | collective-permute-start | bytes 2949128 | tf_op jit(solution)/shard_map/ppermute | solution.py:183
  540.6 33.3 %collective-permute-start.99 = (bf16[16,48,640]{2,1,0:T(8,128)(2,1)S(1)}, bf16[16,48,640]{2,1,0:T(8,128)(2,1)S(1)}, u32[]{:S(2)}, u32[]{:S(2)}) collective-permute-start(bf16[16,48,640]{2,1,0:T(8,128)(2,1)S(1)} %slice.811), channel_id=1, source_target_pairs={{0,16},{2,18},{4,20},{6,22},{8,24},{10,26},{12,28},{14,30},{16,0},... | collective-permute-start | bytes 2949128 | tf_op jit(solution)/shard_map/ppermute | solution.py:183
  547.2 89.6 %collective-permute-start.49 = (bf16[576,1536]{1,0:T(8,128)(2,1)S(1)}, bf16[576,1536]{1,0:T(8,128)(2,1)S(1)}, u32[]{:S(2)}, u32[]{:S(2)}) collective-permute-start(bf16[576,1536]{1,0:T(8,128)(2,1)S(1)} %slice.1247), channel_id=1, source_target_pairs={{0,2},{2,0},{4,6},{6,4},{8,10},{10,8},{12,14},{14,12},{16,18},{18,... | collective-permute-start | bytes 5308424 | tf_op jit(solution)/shard_map/ppermute | solution.py:183
  547.4 49.3 %collective-permute-start.94 = (bf16[16,48,640]{2,1,0:T(8,128)(2,1)S(1)}, bf16[16,48,640]{2,1,0:T(8,128)(2,1)S(1)}, u32[]{:S(2)}, u32[]{:S(2)}) collective-permute-start(bf16[16,48,640]{2,1,0:T(8,128)(2,1)S(1)} %slice.801), channel_id=1, source_target_pairs={{0,12},{2,14},{4,8},{6,10},{8,4},{10,6},{12,0},{14,2},{16,28},{18,... | collective-permute-start | bytes 2949128 | tf_op jit(solution)/shard_map/ppermute | solution.py:183
  555.8 46.7 %collective-permute-start.89 = (bf16[16,48,640]{2,1,0:T(8,128)(2,1)S(1)}, bf16[16,48,640]{2,1,0:T(8,128)(2,1)S(1)}, u32[]{:S(2)}, u32[]{:S(2)}) collective-permute-start(bf16[16,48,640]{2,1,0:T(8,128)(2,1)S(1)} %slice.791), channel_id=1, source_target_pairs={{0,4},{2,6},{4,0},{6,2},{8,12},{10,14},{12,8},{14,10},{16,20},{18,... | collective-permute-start | bytes 2949128 | tf_op jit(solution)/shard_map/ppermute | solution.py:183
  567.7 28.9 %collective-permute-start.110 = (bf16[8,48,512]{2,1,0:T(8,128)(2,1)S(1)}, bf16[8,48,512]{2,1,0:T(8,128)(2,1)S(1)}, u32[]{:S(2)}, u32[]{:S(2)}) collective-permute-start(bf16[8,48,512]{2,1,0:T(8,128)(2,1)S(1)} %slice.981), channel_id=1, source_target_pairs={{0,4},{2,6},{4,0},{6,2},{8,12},{10,14},{12,8},{14,10},{16,20},{18,... | collective-permute-start | bytes 1179656 | tf_op jit(solution)/shard_map/ppermute | solution.py:183
  573.9 41.4 %collective-permute-start.105 = (bf16[8,48,640]{2,1,0:T(8,128)(2,1)S(1)}, bf16[8,48,640]{2,1,0:T(8,128)(2,1)S(1)}, u32[]{:S(2)}, u32[]{:S(2)}) collective-permute-start(bf16[8,48,640]{2,1,0:T(8,128)(2,1)S(1)} %slice.973), channel_id=1, source_target_pairs={{0,64},{2,66},{4,68},{6,70},{8,72},{10,74},{12,76},{14,78},{16,80}... | collective-permute-start | bytes 1474568 | tf_op jit(solution)/shard_map/ppermute | solution.py:183
  596.6 22.0 %collective-permute-start.100 = (bf16[8,48,640]{2,1,0:T(8,128)(2,1)S(1)}, bf16[8,48,640]{2,1,0:T(8,128)(2,1)S(1)}, u32[]{:S(2)}, u32[]{:S(2)}) collective-permute-start(bf16[8,48,640]{2,1,0:T(8,128)(2,1)S(1)} %slice.965), channel_id=1, source_target_pairs={{0,48},{2,50},{4,52},{6,54},{8,56},{10,58},{12,60},{14,62},{16,32}... | collective-permute-start | bytes 1474568 | tf_op jit(solution)/shard_map/ppermute | solution.py:183
  602.5 19.0 %collective-permute-start.95 = (bf16[8,48,640]{2,1,0:T(8,128)(2,1)S(1)}, bf16[8,48,640]{2,1,0:T(8,128)(2,1)S(1)}, u32[]{:S(2)}, u32[]{:S(2)}) collective-permute-start(bf16[8,48,640]{2,1,0:T(8,128)(2,1)S(1)} %slice.957), channel_id=1, source_target_pairs={{0,16},{2,18},{4,20},{6,22},{8,24},{10,26},{12,28},{14,30},{16,0},... | collective-permute-start | bytes 1474568 | tf_op jit(solution)/shard_map/ppermute | solution.py:183
  615.4 65.5 %collective-permute-start.113 = (bf16[1,48,512]{2,1,0:T(8,128)(2,1)S(1)}, bf16[1,48,512]{2,1,0:T(8,128)(2,1)S(1)}, u32[]{:S(2)}, u32[]{:S(2)}) collective-permute-start(bf16[1,48,512]{2,1,0:T(8,128)(2,1)S(1)} %slice.987), channel_id=1, source_target_pairs={{0,48},{2,50},{4,52},{6,54},{8,56},{10,58},{12,60},{14,62},{16,32}... | collective-permute-start | bytes 147464 | tf_op jit(solution)/shard_map/ppermute | solution.py:183
  641.7 40.6 %collective-permute-start.50 = (bf16[576,1536]{1,0:T(8,128)(2,1)S(1)}, bf16[576,1536]{1,0:T(8,128)(2,1)S(1)}, u32[]{:S(2)}, u32[]{:S(2)}) collective-permute-start(bf16[576,1536]{1,0:T(8,128)(2,1)S(1)} %fusion.6), channel_id=1, source_target_pairs={{0,1},{1,0},{2,3},{3,2},{4,5},{5,4},{6,7},{7,6},{8,9},{9,8},{10,11... | collective-permute-start | bytes 5308424 | tf_op jit(solution)/shard_map/ppermute | solution.py:280
  644.2 36.6 %collective-permute-start.108 = (bf16[1,48,640]{2,1,0:T(8,128)(2,1)S(1)}, bf16[1,48,640]{2,1,0:T(8,128)(2,1)S(1)}, u32[]{:S(2)}, u32[]{:S(2)}) collective-permute-start(bf16[1,48,640]{2,1,0:T(8,128)(2,1)S(1)} %slice.979), channel_id=1, source_target_pairs={{0,16},{2,18},{4,20},{6,22},{8,24},{10,26},{12,28},{14,30},{16,0},... | collective-permute-start | bytes 184328 | tf_op jit(solution)/shard_map/ppermute | solution.py:183
  644.4 36.4 %collective-permute-start.103 = (bf16[1,48,640]{2,1,0:T(8,128)(2,1)S(1)}, bf16[1,48,640]{2,1,0:T(8,128)(2,1)S(1)}, u32[]{:S(2)}, u32[]{:S(2)}) collective-permute-start(bf16[1,48,640]{2,1,0:T(8,128)(2,1)S(1)} %slice.971), channel_id=1, source_target_pairs={{0,12},{2,14},{4,8},{6,10},{8,4},{10,6},{12,0},{14,2},{16,28},{18,... | collective-permute-start | bytes 184328 | tf_op jit(solution)/shard_map/ppermute | solution.py:183
  644.5 32.0 %collective-permute-start.93 = (bf16[1,48,640]{2,1,0:T(8,128)(2,1)S(1)}, bf16[1,48,640]{2,1,0:T(8,128)(2,1)S(1)}, u32[]{:S(2)}, u32[]{:S(2)}) collective-permute-start(bf16[1,48,640]{2,1,0:T(8,128)(2,1)S(1)} %slice.955), channel_id=1, source_target_pairs={{0,64},{2,66},{4,68},{6,70},{8,72},{10,74},{12,76},{14,78},{16,80}... | collective-permute-start | bytes 184328 | tf_op jit(solution)/shard_map/ppermute | solution.py:183
  681.6 49.0 %collective-permute-start.114 = (bf16[24,3072]{1,0:T(8,128)(2,1)}, bf16[24,3072]{1,0:T(8,128)(2,1)}, u32[]{:S(2)}, u32[]{:S(2)}) collective-permute-start(bf16[24,3072]{1,0:T(8,128)(2,1)} %select_convert_fusion), channel_id=1, source_target_pairs={{0,2},{2,0},{4,6},{6,4},{8,10},{10,8},{12,14},{14,12},{16,18},{18,... | collective-permute-start | bytes 442376 | tf_op jit(solution)/shard_map/ppermute | solution.py:183
  731.6 31.8 %collective-permute-start.83 = (bf16[32,48,512]{2,1,0:T(8,128)(2,1)S(1)}, bf16[32,48,512]{2,1,0:T(8,128)(2,1)S(1)}, u32[]{:S(2)}, u32[]{:S(2)}) collective-permute-start(bf16[32,48,512]{2,1,0:T(8,128)(2,1)S(1)} %slice.771), channel_id=1, source_target_pairs={{0,2},{2,0},{4,6},{6,4},{8,10},{10,8},{12,14},{14,12},{16,18},{18,... | collective-permute-start | bytes 4718600 | tf_op jit(solution)/shard_map/ppermute | solution.py:183
  732.3 38.6 %collective-permute-start.77 = (bf16[32,48,512]{2,1,0:T(8,128)(2,1)S(1)}, bf16[32,48,512]{2,1,0:T(8,128)(2,1)S(1)}, u32[]{:S(2)}, u32[]{:S(2)}) collective-permute-start(bf16[32,48,512]{2,1,0:T(8,128)(2,1)S(1)} %slice.757), channel_id=1, source_target_pairs={{0,2},{2,0},{4,6},{6,4},{8,10},{10,8},{12,14},{14,12},{16,18},{18,... | collective-permute-start | bytes 4718600 | tf_op jit(solution)/shard_map/ppermute | solution.py:183
  734.7 23.7 %collective-permute-start.54 = (bf16[16,48,384]{2,1,0:T(8,128)(2,1)S(1)}, bf16[16,48,384]{2,1,0:T(8,128)(2,1)S(1)}, u32[]{:S(2)}, u32[]{:S(2)}) collective-permute-start(bf16[16,48,384]{2,1,0:T(8,128)(2,1)S(1)} %slice.890), channel_id=1, source_target_pairs={{0,64},{2,66},{4,68},{6,70},{8,72},{10,74},{12,76},{14,78},{16,80}... | collective-permute-start | bytes 1769480 | tf_op jit(solution)/shard_map/ppermute | solution.py:183
  740.3 36.0 %collective-permute-start.71 = (bf16[32,48,512]{2,1,0:T(8,128)(2,1)S(1)}, bf16[32,48,512]{2,1,0:T(8,128)(2,1)S(1)}, u32[]{:S(2)}, u32[]{:S(2)}) collective-permute-start(bf16[32,48,512]{2,1,0:T(8,128)(2,1)S(1)} %slice.743), channel_id=1, source_target_pairs={{0,2},{2,0},{4,6},{6,4},{8,10},{10,8},{12,14},{14,12},{16,18},{18,... | collective-permute-start | bytes 4718600 | tf_op jit(solution)/shard_map/ppermute | solution.py:183
  741.1 56.3 %collective-permute-start.65 = (bf16[32,48,512]{2,1,0:T(8,128)(2,1)S(1)}, bf16[32,48,512]{2,1,0:T(8,128)(2,1)S(1)}, u32[]{:S(2)}, u32[]{:S(2)}) collective-permute-start(bf16[32,48,512]{2,1,0:T(8,128)(2,1)S(1)} %slice.729), channel_id=1, source_target_pairs={{0,2},{2,0},{4,6},{6,4},{8,10},{10,8},{12,14},{14,12},{16,18},{18,... | collective-permute-start | bytes 4718600 | tf_op jit(solution)/shard_map/ppermute | solution.py:183
  764.1 53.0 %collective-permute-start.84 = (bf16[16,48,512]{2,1,0:T(8,128)(2,1)S(1)}, bf16[16,48,512]{2,1,0:T(8,128)(2,1)S(1)}, u32[]{:S(2)}, u32[]{:S(2)}) collective-permute-start(bf16[16,48,512]{2,1,0:T(8,128)(2,1)S(1)} %slice.935), channel_id=1, source_target_pairs={{0,48},{2,50},{4,52},{6,54},{8,56},{10,58},{12,60},{14,62},{16,32}... | collective-permute-start | bytes 2359304 | tf_op jit(solution)/shard_map/ppermute | solution.py:183
  771.5 46.0 %collective-permute-start.78 = (bf16[16,48,512]{2,1,0:T(8,128)(2,1)S(1)}, bf16[16,48,512]{2,1,0:T(8,128)(2,1)S(1)}, u32[]{:S(2)}, u32[]{:S(2)}) collective-permute-start(bf16[16,48,512]{2,1,0:T(8,128)(2,1)S(1)} %slice.924), channel_id=1, source_target_pairs={{0,16},{2,18},{4,20},{6,22},{8,24},{10,26},{12,28},{14,30},{16,0},... | collective-permute-start | bytes 2359304 | tf_op jit(solution)/shard_map/ppermute | solution.py:183
  776.2 15.9 %collective-permute-start.57 = (bf16[2,48,384]{2,1,0:T(8,128)(2,1)S(1)}, bf16[2,48,384]{2,1,0:T(8,128)(2,1)S(1)}, u32[]{:S(2)}, u32[]{:S(2)}) collective-permute-start(bf16[2,48,384]{2,1,0:T(8,128)(2,1)S(1)} %slice.896), channel_id=1, source_target_pairs={{0,16},{2,18},{4,20},{6,22},{8,24},{10,26},{12,28},{14,30},{16,0},... | collective-permute-start | bytes 221192 | tf_op jit(solution)/shard_map/ppermute | solution.py:183
  776.9 43.2 %collective-permute-start.72 = (bf16[16,48,512]{2,1,0:T(8,128)(2,1)S(1)}, bf16[16,48,512]{2,1,0:T(8,128)(2,1)S(1)}, u32[]{:S(2)}, u32[]{:S(2)}) collective-permute-start(bf16[16,48,512]{2,1,0:T(8,128)(2,1)S(1)} %slice.913), channel_id=1, source_target_pairs={{0,12},{2,14},{4,8},{6,10},{8,4},{10,6},{12,0},{14,2},{16,28},{18,... | collective-permute-start | bytes 2359304 | tf_op jit(solution)/shard_map/ppermute | solution.py:183
  798.0 22.4 %collective-permute-start.66 = (bf16[16,48,512]{2,1,0:T(8,128)(2,1)S(1)}, bf16[16,48,512]{2,1,0:T(8,128)(2,1)S(1)}, u32[]{:S(2)}, u32[]{:S(2)}) collective-permute-start(bf16[16,48,512]{2,1,0:T(8,128)(2,1)S(1)} %slice.902), channel_id=1, source_target_pairs={{0,4},{2,6},{4,0},{6,2},{8,12},{10,14},{12,8},{14,10},{16,20},{18,... | collective-permute-start | bytes 2359304 | tf_op jit(solution)/shard_map/ppermute | solution.py:183
  801.4 14.5 %collective-permute-start.60 = (f32[2,12,128]{2,1,0:T(8,128)S(1)}, f32[2,12,128]{2,1,0:T(8,128)S(1)}, u32[]{:S(2)}, u32[]{:S(2)}) collective-permute-start(f32[2,12,128]{2,1,0:T(8,128)S(1)} %maximum_select_fusion.13), channel_id=1, source_target_pairs={{0,4},{2,6},{4,0},{6,2},{8,12},{10,14},{12,8},{14,10},{16,20},{18,... | collective-permute-start | bytes 36872 | tf_op jit(solution)/shard_map/ppermute | solution.py:183
  817.4 29.0 %collective-permute-start.85 = (bf16[8,48,512]{2,1,0:T(8,128)(2,1)S(1)}, bf16[8,48,512]{2,1,0:T(8,128)(2,1)S(1)}, u32[]{:S(2)}, u32[]{:S(2)}) collective-permute-start(bf16[8,48,512]{2,1,0:T(8,128)(2,1)S(1)} %slice.937), channel_id=1, source_target_pairs={{0,64},{2,66},{4,68},{6,70},{8,72},{10,74},{12,76},{14,78},{16,80}... | collective-permute-start | bytes 1179656 | tf_op jit(solution)/shard_map/ppermute | solution.py:183
  817.7 28.8 %collective-permute-start.79 = (bf16[8,48,512]{2,1,0:T(8,128)(2,1)S(1)}, bf16[8,48,512]{2,1,0:T(8,128)(2,1)S(1)}, u32[]{:S(2)}, u32[]{:S(2)}) collective-permute-start(bf16[8,48,512]{2,1,0:T(8,128)(2,1)S(1)} %slice.926), channel_id=1, source_target_pairs={{0,48},{2,50},{4,52},{6,54},{8,56},{10,58},{12,60},{14,62},{16,32}... | collective-permute-start | bytes 1179656 | tf_op jit(solution)/shard_map/ppermute | solution.py:183
  820.4 27.4 %collective-permute-start.73 = (bf16[8,48,512]{2,1,0:T(8,128)(2,1)S(1)}, bf16[8,48,512]{2,1,0:T(8,128)(2,1)S(1)}, u32[]{:S(2)}, u32[]{:S(2)}) collective-permute-start(bf16[8,48,512]{2,1,0:T(8,128)(2,1)S(1)} %slice.915), channel_id=1, source_target_pairs={{0,16},{2,18},{4,20},{6,22},{8,24},{10,26},{12,28},{14,30},{16,0},... | collective-permute-start | bytes 1179656 | tf_op jit(solution)/shard_map/ppermute | solution.py:183
  820.8 32.8 %collective-permute-start.67 = (bf16[8,48,512]{2,1,0:T(8,128)(2,1)S(1)}, bf16[8,48,512]{2,1,0:T(8,128)(2,1)S(1)}, u32[]{:S(2)}, u32[]{:S(2)}) collective-permute-start(bf16[8,48,512]{2,1,0:T(8,128)(2,1)S(1)} %slice.904), channel_id=1, source_target_pairs={{0,12},{2,14},{4,8},{6,10},{8,4},{10,6},{12,0},{14,2},{16,28},{18,... | collective-permute-start | bytes 1179656 | tf_op jit(solution)/shard_map/ppermute | solution.py:183
  (204 other events, 2751.5 us)

commit v2 on v1

v2 whole, which is shorter than its diff:
```python
import functools

import jax
import jax.numpy as jnp
from jax import lax
from jax.experimental import pallas as pl
from jax.experimental.pallas import tpu as pltpu
from jax.sharding import PartitionSpec as P

HD = 64
TILES = 4
CHIPS = 32
CORE = 1
RINGS = (2, 6, 8, 24, 32)

norm_epsilon = 1e-06

LANES = 128
RADIUS = 3
WINDOW = 7
PAD = 8


def masked_rows(place, main_ref, low_ref, high_ref, wide, strip, side, bounded):
    first, extent = place[0], place[1]
    cols = lax.broadcasted_iota(jnp.int32, (side, LANES), 0)

    def put(slot, value):
        row = first + slot - RADIUS
        limit = extent if bounded else side
        keep = (cols < limit) & (row >= 0) & (row < limit)
        wide[slot] = jnp.where(keep, value.astype(jnp.float32), 0.0)

    for slot in range(RADIUS):
        put(slot, low_ref[slot])
        put(RADIUS + strip + slot, high_ref[slot])
    for slot in range(strip):
        put(RADIUS + slot, main_ref[slot])


def window_sum(wide, taps_ref, shifted, row, side, flipped):
    sums = [None] * WINDOW
    for a in range(WINDOW):
        line = wide[row + a]
        for b in range(WINDOW):
            tap = WINDOW * a + b
            if flipped:
                tap = WINDOW * WINDOW - 1 - tap
            term = line * taps_ref[tap : tap + 1]
            sums[b] = term if sums[b] is None else sums[b] + term
    total = sums[RADIUS]
    for b in range(WINDOW):
        if b != RADIUS:
            shifted[b, PAD : PAD + side] = sums[b]
    for b in range(WINDOW):
        if b != RADIUS:
            total = total + shifted[b, PAD + b - RADIUS : PAD + b - RADIUS + side]
    return total


def clear_edges(shifted, side):
    for b in range(WINDOW):
        shifted[b, 0:PAD] = jnp.zeros((PAD, LANES), jnp.float32)
        shifted[b, PAD + side : 2 * PAD + side] = jnp.zeros((PAD, LANES), jnp.float32)


def forward_kernel(place, main_ref, low_ref, high_ref, taps_in, out_ref, wide, taps, shifted):
    strip, side = main_ref.shape[0], main_ref.shape[1]
    masked_rows(place, main_ref, low_ref, high_ref, wide, strip, side, True)
    clear_edges(shifted, side)
    taps[...] = taps_in[...].astype(jnp.float32)

    def step(row, carry):
        out_ref[row] = window_sum(wide, taps, shifted, row, side, False)
        return carry

    lax.fori_loop(0, strip, step, 0)


def backward_kernel(place, main_ref, low_ref, high_ref, taps_in, add_ref, out_ref, wide, taps, shifted):
    strip, side = main_ref.shape[0], main_ref.shape[1]
    masked_rows(place, main_ref, low_ref, high_ref, wide, strip, side, False)
    clear_edges(shifted, side)
    taps[...] = taps_in[...].astype(jnp.float32)
    cols = lax.broadcasted_iota(jnp.int32, (side, LANES), 0)

    def step(row, carry):
        total = window_sum(wide, taps, shifted, row, side, True) + add_ref[row]
        keep = (cols < place[1]) & (place[0] + row < place[1])
        out_ref[row] = jnp.where(keep, total, 0.0)
        return carry

    lax.fori_loop(0, strip, step, 0)


def slope_kernel(place, main_ref, low_ref, high_ref, grad_ref, out_ref, wide, padded):
    strip, side = main_ref.shape[0], main_ref.shape[1]
    masked_rows(place, main_ref, low_ref, high_ref, wide, strip, side, True)
    edge = jnp.zeros((PAD, LANES), jnp.float32)
    for row in range(strip):
        padded[row, 0:PAD] = edge
        padded[row, PAD : PAD + side] = grad_ref[row].astype(jnp.float32)
        padded[row, PAD + side : 2 * PAD + side] = edge
    for group in ((0, 1, 2, 3), (4, 5, 6)):

        def step(row, sums):
            lines = [wide[row + a] for a in group]
            fresh = list(sums)
            for b in range(WINDOW):
                start = PAD + RADIUS - b
                part = padded[row, start : start + side]
                for i in range(len(group)):
                    term = (lines[i] * part).reshape(side // 8, 8, LANES)
                    fresh[i * WINDOW + b] = fresh[i * WINDOW + b] + jnp.sum(term, axis=0)
            return tuple(fresh)

        start = tuple(jnp.zeros((8, LANES), jnp.float32) for _ in range(len(group) * WINDOW))
        sums = lax.fori_loop(0, strip, step, start)
        for i, a in enumerate(group):
            for b in range(WINDOW):
                tap = a * WINDOW + b
                out_ref[tap : tap + 1] = jnp.sum(sums[i * WINDOW + b], axis=0, keepdims=True)


def block3(rows, side):
    return pl.BlockSpec((rows, side, LANES), lambda i: (0, 0, i))


SCALARS = pl.BlockSpec(memory_space=pltpu.SMEM)


def map_conv(place, main, low, high, taps, added=None):
    strip, side, channels = main.shape
    count = taps.shape[0]
    tap_spec = pl.BlockSpec((count, LANES), lambda i: (0, i))
    specs = [SCALARS, block3(strip, side), block3(RADIUS, side), block3(RADIUS, side), tap_spec]
    args = [place, main, low, high, taps]
    if added is not None:
        specs.append(block3(strip, side))
        args.append(added)
    work = strip * side * channels
    return pl.pallas_call(
        forward_kernel if added is None else backward_kernel,
        grid=(channels // LANES,),
        in_specs=specs,
        out_specs=block3(strip, side),
        out_shape=jax.ShapeDtypeStruct((strip, side, channels), jnp.float32),
        scratch_shapes=[
            pltpu.VMEM((strip + 2 * RADIUS, side, LANES), jnp.float32),
            pltpu.VMEM((count, LANES), jnp.float32),
            pltpu.VMEM((WINDOW, side + 2 * PAD, LANES), jnp.float32),
        ],
        compiler_params=pltpu.CompilerParams(vmem_limit_bytes=24 * 1024 * 1024),
        cost_estimate=pl.CostEstimate(flops=0, bytes_accessed=work // 8, transcendentals=0),
    )(*args)


def map_slopes(place, main, low, high, grad):
    strip, side, channels = main.shape
    count = WINDOW * WINDOW
    work = strip * side * channels
    return pl.pallas_call(
        slope_kernel,
        grid=(channels // LANES,),
        in_specs=[SCALARS, block3(strip, side), block3(RADIUS, side), block3(RADIUS, side), block3(strip, side)],
        out_specs=pl.BlockSpec((count, LANES), lambda i: (0, i)),
        out_shape=jax.ShapeDtypeStruct((count, channels), jnp.float32),
        scratch_shapes=[
            pltpu.VMEM((strip + 2 * RADIUS, side, LANES), jnp.float32),
            pltpu.VMEM((strip, side + 2 * PAD, LANES), jnp.float32),
        ],
        compiler_params=pltpu.CompilerParams(vmem_limit_bytes=24 * 1024 * 1024),
        cost_estimate=pl.CostEstimate(flops=0, bytes_accessed=work // 8, transcendentals=0),
    )(place, main, low, high, grad)


WIDE = 384


def inside(place, row, side):
    cols = lax.broadcasted_iota(jnp.int32, (side, LANES), 0)
    return (cols < place[1]) & (place[0] + row < place[1])


def blend_kernel(
    place, own_ref, other_ref, map_ref, scale_ref, grad_ref, out_ref, pool_ref, slope_ref, line
):
    strip, side = map_ref.shape[0], map_ref.shape[1]
    half = side // 2
    for part in range(map_ref.shape[2] // LANES):
        lanes = slice(part * LANES, (part + 1) * LANES)
        scale = scale_ref[:, lanes].astype(jnp.float32)

        def step(pair, slope):
            total = None
            for i in range(2):
                row = 2 * pair + i
                narrow = own_ref[row, :, lanes].astype(jnp.float32) + other_ref[
                    row, :, lanes
                ].astype(jnp.float32)
                value = map_ref[row, :, lanes].astype(jnp.float32) + scale * narrow
                value = jnp.where(inside(place, row, side), value, 0.0)
                out_ref[row, :, lanes] = value.astype(out_ref.dtype)
                total = value if total is None else total + value
                product = grad_ref[row, :, lanes] * narrow
                slope = slope + jnp.sum(product.reshape(side // 8, 8, LANES), axis=0)
            line[...] = total
            pooled = line[pl.ds(0, half, 2), :] + line[pl.ds(1, half, 2), :]
            pool_ref[pair, :, lanes] = (pooled * 0.25).astype(pool_ref.dtype)
            return slope

        slope = lax.fori_loop(0, strip // 2, step, jnp.zeros((8, LANES), jnp.float32))
        slope_ref[:, lanes] = jnp.sum(slope, axis=0, keepdims=True)


def spread_kernel(place, pool_ref, pool_other_ref, cot_ref, scale_ref, grad_ref, low_ref, line):
    strip, side = cot_ref.shape[0], cot_ref.shape[1]
    half = side // 2
    for part in range(cot_ref.shape[2] // LANES):
        lanes = slice(part * LANES, (part + 1) * LANES)
        scale = scale_ref[:, lanes].astype(jnp.float32)

        def step(pair, carry):
            pooled = pool_ref[pair, :, lanes].astype(jnp.float32) + pool_other_ref[
                pair, :, lanes
            ].astype(jnp.float32)
            pooled = pooled * 0.25
            line[pl.ds(0, half, 2), :] = pooled
            line[pl.ds(1, half, 2), :] = pooled
            spread = line[...]
            for i in range(2):
                row = 2 * pair + i
                value = cot_ref[row, :, lanes].astype(jnp.float32) + spread
                value = jnp.where(inside(place, row, side), value, 0.0)
                grad_ref[row, :, lanes] = value
                low_ref[row, :, lanes] = (value * scale).astype(low_ref.dtype)
            return carry

        lax.fori_loop(0, strip // 2, step, 0)


def wide_block(*lead):
    return pl.BlockSpec(lead + (WIDE,), lambda i: (0,) * len(lead) + (i,))


def blend_map(place, own, other, main, scale, grad):
    strip, side, channels = main.shape
    full = wide_block(strip, side)
    pool = (strip // 2, side // 2)
    return pl.pallas_call(
        blend_kernel,
        grid=(channels // WIDE,),
        in_specs=[SCALARS, full, full, full, wide_block(1), full],
        out_specs=[full, wide_block(*pool), wide_block(1)],
        out_shape=[
            jax.ShapeDtypeStruct(main.shape, jnp.bfloat16),
            jax.ShapeDtypeStruct(pool + (channels,), jnp.bfloat16),
            jax.ShapeDtypeStruct((1, channels), jnp.float32),
        ],
        scratch_shapes=[pltpu.VMEM((side, LANES), jnp.float32)],
        compiler_params=pltpu.CompilerParams(vmem_limit_bytes=24 * 1024 * 1024),
        cost_estimate=pl.CostEstimate(flops=0, bytes_accessed=1 << 20, transcendentals=0),
    )(place, own, other, main, scale, grad)


def spread_map(place, pool, pool_other, cot, scale):
    strip, side, channels = cot.shape
    full = wide_block(strip, side)
    pooled = wide_block(strip // 2, side // 2)
    return pl.pallas_call(
        spread_kernel,
        grid=(channels // WIDE,),
        in_specs=[SCALARS, pooled, pooled, full, wide_block(1)],
        out_specs=[full, full],
        out_shape=[
            jax.ShapeDtypeStruct(cot.shape, jnp.float32),
            jax.ShapeDtypeStruct(cot.shape, jnp.bfloat16),
        ],
        scratch_shapes=[pltpu.VMEM((side, LANES), jnp.float32)],
        compiler_params=pltpu.CompilerParams(vmem_limit_bytes=24 * 1024 * 1024),
        cost_estimate=pl.CostEstimate(flops=0, bytes_accessed=1 << 20, transcendentals=0),
    )(place, pool, pool_other, cot, scale)


def head_lanes(rows, head):
    lanes = lax.broadcasted_iota(jnp.int32, (rows, LANES), 1)
    return (lanes >= head * HD) & (lanes < (head + 1) * HD)


def nt(former, latter):
    return lax.dot_general(
        former, latter, (((1,), (1,)), ((), ())), preferred_element_type=jnp.float32
    )


def tn(former, latter):
    return lax.dot_general(
        former, latter, (((0,), (0,)), ((), ())), preferred_element_type=jnp.float32
    )


def softmax_rows(scores):
    top = jnp.max(scores, axis=-1, keepdims=True)
    raised = jnp.exp(scores - top)
    return raised * (1.0 / jnp.sum(raised, axis=-1, keepdims=True))


def attend_kernel(query_ref, key_ref, value_ref, out_ref):
    rows = query_ref.shape[0]
    query, key, value = query_ref[...], key_ref[...], value_ref[...]
    total = jnp.zeros((rows, LANES), jnp.float32)
    for head in range(LANES // HD):
        mine = head_lanes(rows, head)
        scores = nt(jnp.where(mine, query, jnp.zeros_like(query)), key) * HD ** (-0.5)
        weights = softmax_rows(scores).astype(jnp.bfloat16)
        part = jnp.dot(weights, value, preferred_element_type=jnp.float32)
        total = jnp.where(mine, part, total)
    out_ref[...] = total.astype(out_ref.dtype)


def attend_back_kernel(
    query_ref, key_ref, value_ref, grad_ref, query_out, key_out, value_out
):
    rows = query_ref.shape[0]
    query, key, value, grad = query_ref[...], key_ref[...], value_ref[...], grad_ref[...]
    none = jnp.zeros_like(query)
    query_grad = jnp.zeros((rows, LANES), jnp.float32)
    key_grad, value_grad = None, None
    for head in range(LANES // HD):
        mine = head_lanes(rows, head)
        query_own = jnp.where(mine, query, none)
        grad_own = jnp.where(mine, grad, none)
        weights = softmax_rows(nt(query_own, key) * HD ** (-0.5))
        weight_grad = nt(grad_own, value)
        row_dot = jnp.sum(weights * weight_grad, axis=-1, keepdims=True)
        score_grad = (weights * (weight_grad - row_dot)).astype(jnp.bfloat16)
        part = jnp.dot(score_grad, key, preferred_element_type=jnp.float32)
        query_grad = jnp.where(mine, part, query_grad)
        key_part = tn(score_grad, query_own)
        value_part = tn(weights.astype(jnp.bfloat16), grad_own)
        key_grad = key_part if key_grad is None else key_grad + key_part
        value_grad = value_part if value_grad is None else value_grad + value_part
    query_out[...] = (query_grad * HD ** (-0.5)).astype(query_out.dtype)
    key_out[...] = key_grad * HD ** (-0.5)
    value_out[...] = value_grad


def lane_block(rows, shift=0):
    return pl.BlockSpec((rows, LANES), lambda i: (0, i + shift))


def attend(rows, pair):
    count, keys = rows.shape[0], pair.shape[0]
    width = pair.shape[1] // 2
    steps = width // LANES
    work = 4 * count * keys * width
    return pl.pallas_call(
        attend_kernel,
        grid=(steps,),
        in_specs=[lane_block(count), lane_block(keys), lane_block(keys, steps)],
        out_specs=lane_block(count),
        out_shape=jax.ShapeDtypeStruct((count, width), jnp.bfloat16),
        compiler_params=pltpu.CompilerParams(vmem_limit_bytes=24 * 1024 * 1024),
        cost_estimate=pl.CostEstimate(flops=0, bytes_accessed=1 << 20, transcendentals=0),
    )(rows, pair, pair)


def attend_back(rows, pair, grad):
    count, keys = rows.shape[0], pair.shape[0]
    width = pair.shape[1] // 2
    steps = width // LANES
    work = 10 * count * keys * width
    return pl.pallas_call(
        attend_back_kernel,
        grid=(steps,),
        in_specs=[
            lane_block(count),
            lane_block(keys),
            lane_block(keys, steps),
            lane_block(count),
        ],
        out_specs=[lane_block(count), lane_block(keys), lane_block(keys)],
        out_shape=[
            jax.ShapeDtypeStruct((count, width), jnp.bfloat16),
            jax.ShapeDtypeStruct((keys, width), jnp.float32),
            jax.ShapeDtypeStruct((keys, width), jnp.float32),
        ],
        compiler_params=pltpu.CompilerParams(vmem_limit_bytes=24 * 1024 * 1024),
        cost_estimate=pl.CostEstimate(flops=0, bytes_accessed=1 << 20, transcendentals=0),
    )(rows, pair, pair, grad)


def slopes_kernel(ends, *refs):
    count = len(ends)
    lefts, rights = refs[:count], refs[count : 2 * count]
    near_ref, far_ref = refs[2 * count :]
    half = near_ref.shape[0]
    step = pl.program_id(0)
    first = 0
    for left, right, end in zip(lefts, rights, ends):

        @pl.when((step >= first) & (step < end))
        def _(left=left, right=right):
            near_ref[...] = tn(left[:, :half], right[...]).astype(near_ref.dtype)
            far_ref[...] = tn(left[:, half:], right[...]).astype(far_ref.dtype)

        first = end


def paired_slopes(lefts, rights):
    tile = 512
    rows, depth = lefts[0].shape
    half = depth // 2
    starts, ends = [], []
    total = 0
    for right in rights:
        starts.append(total)
        total += right.shape[1] // tile
        ends.append(total)

    def column(start, end):
        return lambda i: (0, jnp.clip(i - start, 0, end - start - 1))

    whole = pl.BlockSpec((rows, depth), lambda i: (0, 0))
    out = pl.BlockSpec((half, tile), lambda i: (0, i))
    shape = jax.ShapeDtypeStruct((half, total * tile), jnp.bfloat16)
    near, far = pl.pallas_call(
        functools.partial(slopes_kernel, tuple(ends)),
        grid=(total,),
        in_specs=[whole] * len(lefts)
        + [pl.BlockSpec((rows, tile), column(a, b)) for a, b in zip(starts, ends)],
        out_specs=[out, out],
        out_shape=[shape, shape],
        compiler_params=pltpu.CompilerParams(vmem_limit_bytes=24 * 1024 * 1024),
        cost_estimate=pl.CostEstimate(
            flops=0,
            bytes_accessed=1 << 20,
            transcendentals=0,
        ),
    )(*lefts, *rights)
    return near, far


def split_rows(pair):
    return [part.reshape(CHIPS, part.shape[0] // CHIPS, part.shape[1]) for part in pair]


def dense_kernel(flipped, scaled, halves, left_ref, right_ref, *refs):
    scale_ref, outs = (refs[0], refs[1:]) if scaled else (None, refs)
    rows = left_ref.shape[0]
    chunk = rows // 6
    for part in range(6):
        lines = slice(part * chunk, (part + 1) * chunk)
        product = nt if flipped else functools.partial(jnp.dot, preferred_element_type=jnp.float32)
        value = product(left_ref[lines, :], right_ref[...])
        if scaled:
            value = value * scale_ref[lines, :].astype(jnp.float32)
        if halves:
            out, first = (outs[0], 0) if part < 3 else (outs[1], rows // 2)
            out[part * chunk - first : (part + 1) * chunk - first, :] = value.astype(out.dtype)
        else:
            outs[0][lines, :] = value.astype(outs[0].dtype)


def dense(left, right, flipped, scale=None, halves=False):
    rows, depth = left.shape
    count = right.shape[0] if flipped else right.shape[1]
    tile = 512
    specs = [
        pl.BlockSpec((rows, depth), lambda i: (0, 0), pipeline_mode=pl.Buffered(1)),
        pl.BlockSpec((tile, depth), lambda i: (i, 0))
        if flipped
        else pl.BlockSpec((depth, tile), lambda i: (0, i)),
    ]
    args = [left, right]
    if scale is not None:
        specs.append(pl.BlockSpec((rows, tile), lambda i: (0, i)))
        args.append(scale)
    if halves:
        kinds = [(rows // 2, jnp.float32), (rows // 2, jnp.bfloat16)]
    else:
        kinds = [(rows, jnp.bfloat16)]
    return pl.pallas_call(
        functools.partial(dense_kernel, flipped, scale is not None, halves),
        grid=(count // tile,),
        in_specs=specs,
        out_specs=[pl.BlockSpec((size, tile), lambda i: (0, i)) for size, _ in kinds],
        out_shape=[jax.ShapeDtypeStruct((size, count), kind) for size, kind in kinds],
        compiler_params=pltpu.CompilerParams(vmem_limit_bytes=24 * 1024 * 1024),
        cost_estimate=pl.CostEstimate(flops=0, bytes_accessed=1 << 20, transcendentals=0),
    )(*args)


def mix_kernel(place, main_ref, low_ref, high_ref, taps_ref, mix_ref, back_ref, slope_ref, wide):
    strip, side, width = mix_ref.shape
    top, bottom = place[0] > 0, place[0] + strip < place[1]
    blank = jnp.zeros((PAD, LANES), jnp.float32)
    for first in range(0, width, LANES):
        for kind in range(2):
            lanes = slice(kind * width + first, kind * width + first + LANES)
            for slot in range(strip + 2):
                if slot == 0:
                    value = jnp.where(top, low_ref[0, :, lanes].astype(jnp.float32), 0.0)
                elif slot == strip + 1:
                    value = jnp.where(bottom, high_ref[0, :, lanes].astype(jnp.float32), 0.0)
                else:
                    value = main_ref[slot - 1, :, lanes].astype(jnp.float32)
                wide[kind, slot, 0:PAD] = blank
                wide[kind, slot, PAD : PAD + side] = value
                wide[kind, slot, PAD + side : 2 * PAD + side] = blank
        own = slice(first, first + LANES)
        taps = taps_ref[:, own].astype(jnp.float32)
        sums = [jnp.zeros((side, LANES), jnp.float32) for _ in range(9)]
        for row in range(strip):
            grad = wide[1, row + 1, PAD : PAD + side]
            mixed = jnp.zeros((side, LANES), jnp.float32)
            back = jnp.zeros((side, LANES), jnp.float32)
            for a in range(3):
                for b in range(3):
                    tap = 3 * a + b
                    span = slice(PAD + b - 1, PAD + b - 1 + side)
                    value = wide[0, row + a, span]
                    mixed = mixed + value * taps[tap : tap + 1]
                    back = back + wide[1, row + a, span] * taps[8 - tap : 9 - tap]
                    sums[tap] = sums[tap] + value * grad
            mix_ref[row, :, own] = mixed
            back_ref[row, :, own] = back
        for tap in range(9):
            slope_ref[tap : tap + 1, own] = jnp.sum(sums[tap], axis=0, keepdims=True)


def mix(place, both, low, high, taps):
    strip, side, double = both.shape
    width = double // 2
    grid = jax.ShapeDtypeStruct((strip, side, width), jnp.float32)
    return pl.pallas_call(
        mix_kernel,
        in_specs=[SCALARS] + [pl.BlockSpec(memory_space=pltpu.VMEM)] * 4,
        out_specs=[pl.BlockSpec(memory_space=pltpu.VMEM)] * 3,
        out_shape=[grid, grid, jax.ShapeDtypeStruct(taps.shape, jnp.float32)],
        scratch_shapes=[pltpu.VMEM((2, strip + 2, side + 2 * PAD, LANES), jnp.float32)],
        compiler_params=pltpu.CompilerParams(vmem_limit_bytes=16 * 1024 * 1024),
        cost_estimate=pl.CostEstimate(flops=0, bytes_accessed=1 << 20, transcendentals=0),
    )(place, both, low, high, taps)


def rotated(start):
    return tuple(RINGS[(start + i) % len(RINGS)] for i in range(len(RINGS)))


def xor_swap(values, mask):
    count = lax.axis_size("dp")
    return lax.ppermute(values, "dp", [(i, i ^ mask) for i in range(count)])


def chip_offset(place, order, low_first):
    offset = 0
    for k, mask in enumerate(order):
        bit = k if low_first else len(order) - 1 - k
        offset = offset ^ (((place >> bit) & 1) * (mask >> 1))
    return offset


def together(values):
    return list(lax.optimization_barrier(tuple(values)))


def after(value, *others):
    return lax.optimization_barrier((value,) + others)[0]


def gathered_parts(blocks, orders, early, work):
    held = [block[None] for block in blocks]
    count, last = len(blocks), len(RINGS) - 1
    for step in range(last):
        other = [xor_swap(part, order[step]) for part, order in zip(held, orders)]
        held = [jnp.concatenate([a, b], axis=0) for a, b in zip(held, other)]
        done = together(held + (early if step == last - 1 else []))
        held = done[:count]
    other = [xor_swap(part, order[last]) for part, order in zip(held, orders)]
    done = together(other + work(*done[count:]))
    return held, done[:count], done[count:]


def split_sum(kept, other):
    half = kept.shape[0] // 2
    if half == 0:
        return kept.astype(jnp.float32) + other.astype(jnp.float32), None
    return kept[:half] + other[:half], kept[half:] + other[half:]


class Scatter:
    def __init__(self, kept, given, orders):
        self.kept, self.given, self.orders = list(kept), list(given), orders
        self.step = 0

    def advance(self, *tied):
        other = [
            xor_swap(part, order[self.step]) for part, order in zip(self.given, self.orders)
        ]
        done = together(other + list(tied))
        sums = [split_sum(own, got) for own, got in zip(self.kept, done)]
        self.kept, self.given = [low for low, _ in sums], [high for _, high in sums]
        self.step += 1
        return done[len(other) :]

    def result(self):
        return [part[0] for part in self.kept]


def route_kernel(moves, steps, n_in, n_out, place, *refs):
    ins, outs = refs[:n_in], refs[n_in : n_in + n_out]
    held = refs[n_in + n_out : n_in + 2 * n_out]
    sems = refs[n_in + 2 * n_out]
    device = place[0]
    chip, core = device >> 1, device & 1

    for target in range(n_out):

        def step(index, carry):
            for source, take, goal, put, source_box, target_box in moves:
                if goal == target:
                    pltpu.make_async_copy(
                        ins[source].at[(take(chip, core, index),) + source_box],
                        held[goal].at[(put(chip, core, index),) + target_box],
                        sems.at[goal],
                    ).start()
            return carry

        lax.fori_loop(0, steps, step, 0)
    for target in range(n_out):
        pltpu.make_async_copy(held[target], held[target], sems.at[target]).wait()
        pltpu.make_async_copy(held[target], outs[target], sems.at[target]).start()
    for target in range(n_out):
        pltpu.make_async_copy(held[target], outs[target], sems.at[target]).wait()


def route(moves, steps, place, arrays, shapes):
    anywhere = pl.BlockSpec(memory_space=pl.ANY)
    volume = sum(2 * a.size for a in arrays)
    return pl.pallas_call(
        functools.partial(route_kernel, moves, steps, len(arrays), len(shapes)),
        in_specs=[SCALARS] + [anywhere] * len(arrays),
        out_specs=[anywhere] * len(shapes),
        out_shape=[jax.ShapeDtypeStruct(s, jnp.bfloat16) for s in shapes],
        scratch_shapes=[pltpu.VMEM(s, jnp.bfloat16) for s in shapes]
        + [pltpu.SemaphoreType.DMA((len(shapes),))],
        compiler_params=pltpu.CompilerParams(vmem_limit_bytes=volume + volume // 4 + (4 << 20)),
        cost_estimate=pl.CostEstimate(flops=0, bytes_accessed=2 * volume, transcendentals=0),
    )(place, *arrays)


def box(rows, cols):
    return (pl.ds(rows[0], rows[1] - rows[0]), pl.ds(cols[0], cols[1] - cols[0]))


def overlap(first, second):
    low, high = max(first[0], second[0]), min(first[1], second[1])
    return (low, high) if low < high else None


def shifted_span(span, base):
    return (span[0] - base, span[1] - base)


def core_swap(values):
    return xor_swap(values, CORE)


def model_swap(values):
    return lax.ppermute(values, "mp", [(0, 1), (1, 0)])


def exchange(values):
    low = values.astype(jnp.bfloat16)
    other = model_swap(low)
    return low.astype(jnp.float32) + other.astype(jnp.float32)


def halo_rows(block, width):
    count = lax.axis_size("dp")
    forward = [(i, (i + 1) % count) for i in range(count)]
    backward = [((i + 1) % count, i) for i in range(count)]
    low = lax.ppermute(block[block.shape[0] - width :], "dp", forward)
    high = lax.ppermute(block[:width], "dp", backward)
    return low, high


def normalize(values, scale_gain):
    average = jnp.mean(values, axis=-1, keepdims=True)
    centred = values - average
    spread = jnp.mean(centred * centred, axis=-1, keepdims=True)
    return centred * lax.rsqrt(spread + norm_epsilon) * scale_gain


def gelu_pair(values):
    below = 0.5 * (1.0 + lax.erf(values * 0.5**0.5))
    slope = below + values * (jnp.exp(-0.5 * values * values) * (2.0 * jnp.pi) ** -0.5)
    return (values * below).astype(jnp.bfloat16), slope.astype(jnp.bfloat16)


def matmul(former, latter):
    return jnp.dot(former, latter, preferred_element_type=jnp.float32)


def matmul_nt(former, latter):
    return lax.dot_general(
        former, latter, (((1,), (1,)), ((), ())), preferred_element_type=jnp.float32
    )


def matmul_tn(former, latter):
    return lax.dot_general(
        former, latter, (((0,), (0,)), ((), ())), preferred_element_type=jnp.float32
    )


def pair_swap(values):
    chips = lax.axis_size("dp") // 2
    pairs = []
    for chip in range(chips):
        other = (chip + 1) % chips if chip % 2 else (chip - 1) % chips
        pairs += [(2 * chip + core, 2 * other + core) for core in range(2)]
    return lax.ppermute(values, "dp", pairs)


def own_half(first, core, axis, other=False):
    size = first.shape[axis] // 2
    low = lax.slice_in_dim(first, 0, size, axis=axis)
    high = lax.slice_in_dim(first, size, 2 * size, axis=axis)
    return jnp.where((core == 0) != other, low, high)


def in_core_order(own, other, core, axis):
    return jnp.where(
        core == 0,
        jnp.concatenate([own, other], axis=axis),
        jnp.concatenate([other, own], axis=axis),
    )


def row_places(device, order, depth):
    chip, core = device >> 1, device & 1
    place = jnp.arange(2 * CHIPS * depth)
    block, line = place // depth, place % depth
    owner = 2 * (chip ^ chip_offset(block % CHIPS, order, True)) + (core ^ (block // CHIPS))
    return owner * depth + line


def row_picker(device, order, depth):
    places = row_places(device, order, depth)
    rows = lax.broadcasted_iota(jnp.int32, (places.shape[0], places.shape[0]), 0)
    return (rows == places[None, :]).astype(jnp.bfloat16)


def all_weights(place, core, small_rows, common_rows, *ties):
    middle = small_rows[4].shape[1] // 2
    first = jnp.concatenate(small_rows[:4] + (small_rows[4][:, :middle],), axis=1)
    second = jnp.concatenate([small_rows[4][:, middle:], small_rows[5]], axis=1)
    kept = jnp.concatenate([own_half(rows, core, 1) for rows in common_rows], axis=1)
    given = jnp.concatenate([own_half(rows, core, 1, True) for rows in common_rows], axis=1)
    common = in_core_order(kept, core_swap(given), core, 0)
    rows = common.shape[0]
    widths = [block.shape[1] // 2 for block in common_rows]
    spans = even_edges(common.shape[1], 3)
    orders = [rotated(i) for i in range(5)]
    held, other, extra = gathered_parts(
        [first, second] + [common[:, low:high] for low, high in spans], orders, *ties
    )
    near = [jnp.concatenate([a, b], axis=0) for a, b in zip(held[:2], other[:2])]
    far = [core_swap(part) for part in near]
    small = [
        tuple(part.reshape(-1, part.shape[2]) for part in pair) for pair in zip(near, far)
    ]
    starts = [0]
    for width in widths:
        starts.append(starts[-1] + width)
    moves = []
    half = CHIPS // 2
    for i, span in enumerate(spans):
        order = orders[i + 2]
        for target in range(len(widths)):
            cols_span = (starts[target], starts[target + 1])
            shared = overlap(cols_span, span)
            if shared is None:
                continue
            for side in range(2):

                def put(chip, core, index, side=side, order=order):
                    return chip ^ chip_offset(index + side * half, order, True)

                moves.append(
                    (
                        2 * i + side,
                        lambda chip, core, index: index,
                        target,
                        put,
                        box((0, rows), shifted_span(shared, span[0])),
                        box((0, rows), shifted_span(shared, cols_span[0])),
                    )
                )
    arrays = [part for pair in zip(held[2:], other[2:]) for part in pair]
    large = route(moves, half, place, arrays, [(CHIPS, rows, width) for width in widths])
    expand, shrink, adapter = [part.reshape(CHIPS * rows, part.shape[2]) for part in large]
    adapter = in_core_order(adapter, core_swap(adapter), core, 1)
    return small, expand, shrink, adapter, extra


def even_edges(width, count):
    tiles = width // LANES
    edges = [LANES * ((tiles * i + count - 1) // count) for i in range(count + 1)]
    return [(edges[i], edges[i + 1]) for i in range(count)]


def turn(left_ref, turned):
    for first in range(0, left_ref.shape[1], LANES):
        lanes = slice(first, first + LANES)
        turned[lanes, :] = left_ref[:, lanes].T


def slope_pack_kernel(
    orders, spans, place, left_a, right_a, left_b, right_b, extra_ref, *refs
):
    outs, (turned, tile, sems) = refs[:-3], refs[-3:]
    width = right_a.shape[1]
    step = pl.program_id(0)
    per_side = left_a.shape[1] // width
    total = 2 * per_side + 1
    blocks, rows = tile.shape[1], tile.shape[2]
    group = blocks // 4
    chip = place[0] >> 1
    slot = step % 2

    def sent(which, wide):
        box_ref = tile.at[which, :, :, pl.ds(0, wide)]
        return pltpu.make_async_copy(box_ref, box_ref, sems.at[which])

    @pl.when(step >= 2)
    def _():
        sent(slot, width).wait()

    @pl.when(step == 0)
    def _():
        turn(left_a, turned)

    @pl.when(step == per_side)
    def _():
        turn(left_b, turned)

    def fill(right):
        for part in range(4):
            lines = slice(part * group * rows, (part + 1) * group * rows)
            value = jnp.dot(turned[lines, :], right[...], preferred_element_type=jnp.float32)
            tile[slot, part * group : (part + 1) * group] = value.astype(tile.dtype).reshape(
                group, rows, width
            )

    @pl.when(step < per_side)
    def _():
        fill(right_a)

    @pl.when((step >= per_side) & (step < 2 * per_side))
    def _():
        fill(right_b)

    last = extra_ref.shape[2]

    @pl.when(step == 2 * per_side)
    def _():
        tile[slot, :, :, 0:last] = extra_ref[...]

    for index in range(total):
        begin = index * width
        wide = width if index < 2 * per_side else last
        goal = [i for i, span in enumerate(spans) if span[0] <= begin < span[1]][0]
        cols = pl.ds(begin - spans[goal][0], wide)

        @pl.when(step == index)
        def _(goal=goal, cols=cols, wide=wide):
            def send(place_in, carry):
                for side in range(2):
                    owner = chip ^ chip_offset(
                        place_in + side * (blocks // 2), orders[goal], True
                    )
                    pltpu.make_async_copy(
                        tile.at[slot, owner, :, pl.ds(0, wide)],
                        outs[2 * goal + side].at[place_in, :, cols],
                        sems.at[slot],
                    ).start()
                return carry

            lax.fori_loop(0, blocks // 2, send, 0)

    @pl.when(step == total - 1)
    def _():
        sent(1 - slot, width).wait()
        sent(slot, last).wait()


def packed_map_slopes(place, orders, spans, left_a, right_a, left_b, right_b, extra):
    depth, channels = left_a.shape
    hidden = right_a.shape[1]
    width = 384
    steps = hidden // width
    rows = channels // CHIPS
    extra = extra.reshape(CHIPS, rows, extra.shape[1])
    whole = pl.BlockSpec((depth, channels), lambda i: (0, 0), pipeline_mode=pl.Buffered(1))
    return pl.pallas_call(
        functools.partial(slope_pack_kernel, orders, spans),
        grid=(2 * steps + 1,),
        in_specs=[
            SCALARS,
            whole,
            pl.BlockSpec((depth, width), lambda i: (0, jnp.minimum(i, steps - 1))),
            whole,
            pl.BlockSpec((depth, width), lambda i: (0, jnp.clip(i - steps, 0, steps - 1))),
            pl.BlockSpec(extra.shape, lambda i: (0, 0, 0), pipeline_mode=pl.Buffered(1)),
        ],
        out_specs=[pl.BlockSpec(memory_space=pl.ANY)] * (2 * len(spans)),
        out_shape=[
            jax.ShapeDtypeStruct((CHIPS // 2, rows, high - low), jnp.bfloat16)
            for low, high in spans
            for _ in range(2)
        ],
        scratch_shapes=[
            pltpu.VMEM((channels, depth), jnp.bfloat16),
            pltpu.VMEM((2, CHIPS, rows, width), jnp.bfloat16),
            pltpu.SemaphoreType.DMA((2,)),
        ],
        compiler_params=pltpu.CompilerParams(vmem_limit_bytes=40 * 1024 * 1024),
        cost_estimate=pl.CostEstimate(flops=0, bytes_accessed=1 << 20, transcendentals=0),
    )(place, left_a, right_a, left_b, right_b, extra)


def unpacked_map_slopes(core, blocks, widths):
    block = jnp.concatenate(blocks, axis=1)
    own = own_half(block, core, 0)
    got = core_swap(own_half(block, core, 0, True).astype(jnp.bfloat16)).astype(jnp.float32)
    outs = []
    start = 0
    for width in widths:
        outs.append(
            in_core_order(own[:, start : start + width], got[:, start : start + width], core, 1)
        )
        start += width
    return outs


def row_sums(values):
    count = values.shape[0]
    pieces = lax.all_to_all(values, "dp", 0, 0, tiled=True)
    return jnp.sum(pieces.astype(jnp.float32), axis=0)


def row_copies(row):
    count = lax.axis_size("dp")
    return lax.all_to_all(jnp.broadcast_to(row[None], (count,) + row.shape), "dp", 0, 0, tiled=True)


def on_device(
    lowres_in,
    highres_in,
    image_sizes,
    attn_gain,
    query_weight,
    key_weight,
    value_weight,
    output_weight,
    mlp_gain,
    up_weight,
    down_weight,
    depth_kernel,
    conv_gain,
    expand_weight,
    shrink_weight,
    layer_scale,
    adapter_weight,
    adapter_kernel,
    gate_vector,
    out_cotangent,
    map_cotangent,
):
    device = lax.axis_index("dp")
    core = device & 1
    place = device.reshape(1).astype(jnp.int32)
    group_count = lax.axis_size("dp") // TILES
    position = (device + 2) % TILES
    group_id = (device + 2) // TILES % group_count
    model_half = lax.axis_index("mp")
    low_strip, _, grid_side, width = lowres_in.shape
    high_strip, _, high_side, channels = highres_in.shape
    own_width = adapter_kernel.shape[1]
    local_width = query_weight.shape[1]
    local_heads = local_width // HD
    scaling = HD ** (-0.5)
    token_count = low_strip * grid_side
    pixel_count = high_strip * high_side

    high_map = highres_in.reshape(high_strip, high_side, channels)
    table_ids = jnp.arange(image_sizes.shape[0])
    extent = jnp.sum(jnp.where(table_ids == group_id, image_sizes, 0))
    first_row = position * high_strip
    map_place = jnp.stack([first_row, extent]).astype(jnp.int32)
    token_rows = lowres_in.astype(jnp.float32).reshape(token_count, width)
    local_grad_low = out_cotangent.reshape(low_strip, grid_side, own_width)
    backs = []
    depth = query_weight.shape[0]
    pickers = [row_picker(device, rotated(i), depth) for i in range(2)]

    def convolve(map_low, map_high):
        backs.extend([map_low, map_high])
        return [map_conv(map_place, high_map, map_low, map_high, depth_kernel)]

    small, expand_full, shrink_full, adapter_full, extra = all_weights(
        place,
        core,
        (query_weight, key_weight, value_weight, output_weight.T, up_weight, down_weight.T),
        (expand_weight, shrink_weight.T, adapter_weight),
        list(halo_rows(high_map, RADIUS)),
        convolve,
    )
    map_low, map_high = backs
    convolved = extra[0].reshape(pixel_count, channels)
    normed_map, conv_norm_back = jax.vjp(normalize, convolved, conv_gain.astype(jnp.float32))
    normed_map_low = normed_map.astype(jnp.bfloat16)
    normed, attn_norm_back = jax.vjp(normalize, token_rows, attn_gain.astype(jnp.float32))
    normed_low = normed.astype(jnp.bfloat16)
    normed_first = matmul(normed_low, pickers[0]).astype(jnp.bfloat16)
    normed_map_pair = jnp.concatenate([normed_map_low, core_swap(normed_map_low)], axis=0)
    triple = 3 * local_width
    quad = 4 * local_width
    hidden_width = up_weight.shape[1]
    hidden_half = hidden_width // 2

    def pieces(index, low, high):
        return [part[:, low:high] for part in small[index]]

    qkv_parts = pieces(0, 0, triple)
    output_parts = pieces(0, triple, quad)
    up_parts = [pieces(0, quad, quad + hidden_half), pieces(1, 0, hidden_half)]
    down_parts = pieces(1, hidden_half, hidden_half + hidden_width)

    def picked(values, index):
        return matmul(values, pickers[index]).astype(jnp.bfloat16)

    def restored(values, index):
        return matmul_nt(values.astype(jnp.bfloat16), pickers[index])

    def into(values, parts):
        half = values.shape[1] // 2
        return matmul(values[:, :half], parts[0]) + matmul(values[:, half:], parts[1])

    def outof(values, parts):
        return jnp.concatenate([matmul_nt(values, part) for part in parts], axis=1)

    qkv_rows = into(normed_first, qkv_parts).astype(jnp.bfloat16)
    pair = qkv_rows[:, local_width:]
    pair = jnp.concatenate([pair, core_swap(pair)], axis=0)
    pair = jnp.concatenate([pair, pair_swap(pair)], axis=0)
    attended_low = attend(qkv_rows, pair)
    hidden_rows = token_rows + exchange(restored(outof(attended_low, output_parts), 0))
    normed_two, mlp_norm_back = jax.vjp(normalize, hidden_rows, mlp_gain.astype(jnp.float32))
    normed_two_low = normed_two.astype(jnp.bfloat16)
    normed_two_picked = [picked(normed_two_low, i) for i in range(2)]
    expanded = jnp.concatenate(
        [into(normed_two_picked[i], up_parts[i]) for i in range(2)], axis=1
    )
    activated_low, activated_slope = gelu_pair(expanded)
    result_own = restored(outof(activated_low, down_parts), 1).astype(jnp.bfloat16)
    result_rows = (
        hidden_rows + result_own.astype(jnp.float32) + model_swap(result_own).astype(jnp.float32)
    )

    result_grid = result_rows.reshape(low_strip, grid_side, width)
    gate_wide = gate_vector.astype(jnp.float32)
    gating = jax.nn.sigmoid(jnp.sum(result_grid * gate_wide, axis=-1, keepdims=True))
    out_grad = local_grad_low.astype(jnp.float32)
    lifted_grad_low = (out_grad * gating).reshape(token_count, own_width).astype(jnp.bfloat16)
    grid_shape = (low_strip, grid_side, channels)
    pooled_own = matmul_nt(lifted_grad_low, adapter_full).astype(jnp.bfloat16).reshape(grid_shape)
    pooled_other = model_swap(pooled_own)

    widened = matmul(normed_map_pair, expand_full)
    widened_low, widened_slope = gelu_pair(widened)
    widened_low = after(widened_low, pooled_own)
    narrowed_part, narrowed_given = dense(widened_low, shrink_full, True, halves=True)
    narrowed_part = narrowed_part + core_swap(narrowed_given).astype(jnp.float32)
    map_shape = (high_strip, high_side, channels)
    narrowed_own = narrowed_part.astype(jnp.bfloat16).reshape(map_shape)
    narrowed_own, pooled_other = together([narrowed_own, pooled_other])
    narrowed_other = model_swap(narrowed_own)

    map_grad, narrowed_grad_low = spread_map(
        map_place, pooled_own, pooled_other, map_cotangent.reshape(map_shape), layer_scale[None]
    )
    narrowed_grad_low = narrowed_grad_low.reshape(pixel_count, channels)
    narrowed_grad_pair = jnp.concatenate([narrowed_grad_low, core_swap(narrowed_grad_low)], axis=0)
    (widened_grad_low,) = dense(narrowed_grad_pair, shrink_full, False, widened_slope)
    normed_map_part, normed_map_given = dense(widened_grad_low, expand_full, True, halves=True)
    normed_map_given, narrowed_other = together([normed_map_given, narrowed_other])
    normed_map_part = normed_map_part + core_swap(normed_map_given).astype(jnp.float32)
    normed_map_own = normed_map_part.astype(jnp.bfloat16)

    mapped, pooled_low, layer_scale_slope = blend_map(
        map_place, narrowed_own, narrowed_other, high_map, layer_scale[None], map_grad
    )
    pooled_low = pooled_low.reshape(token_count, channels)
    lifted = matmul(pooled_low, adapter_full).reshape(low_strip, grid_side, own_width)

    own_result = lax.dynamic_slice_in_dim(result_grid, model_half * own_width, own_width, 2)
    own_result_low = own_result.astype(jnp.bfloat16)
    both_low = jnp.concatenate([own_result_low, local_grad_low], axis=2)
    both_edges = halo_rows(after(both_low, widened_grad_low), 1)
    mix_place = jnp.stack([position * low_strip, TILES * low_strip]).astype(jnp.int32)
    local_mix, local_back, adapter_kernel_slope = mix(
        mix_place, both_low, *both_edges, adapter_kernel
    )
    blended = own_result + local_mix + gating * lifted

    gate_part = jnp.sum(out_grad * lifted, axis=-1, keepdims=True)
    gate_grad = exchange(gate_part)
    adapter_slope = matmul_tn(pooled_low, lifted_grad_low)
    adapter_slope = own_half(adapter_slope, core, 1) + core_swap(
        own_half(adapter_slope, core, 1, True).astype(jnp.bfloat16)
    ).astype(jnp.float32)
    own_grad = out_grad + local_back
    own_grad_low = own_grad.astype(jnp.bfloat16)
    other_grad = model_swap(own_grad_low)
    result_grad = in_core_order(own_grad_low, other_grad, model_half, 2).astype(jnp.float32)
    gate_slope = gate_grad * gating * (1.0 - gating)
    gate_vector_slope = jnp.sum((gate_slope * result_grid).reshape(token_count, width), axis=0)
    result_grad = (result_grad + gate_slope * gate_wide).reshape(token_count, width)

    result_low = after(result_grad.astype(jnp.bfloat16), widened_grad_low)
    result_picked = picked(result_low, 1)
    activated_grad = into(result_picked, down_parts)
    expanded_grad_low = (activated_grad * activated_slope.astype(jnp.float32)).astype(jnp.bfloat16)
    expanded_grad_parts = [expanded_grad_low[:, :hidden_half], expanded_grad_low[:, hidden_half:]]
    second_slopes = split_rows(
        paired_slopes(
            (normed_two_picked[1], result_picked), (expanded_grad_parts[1], activated_low)
        )
    )
    second_far = core_swap(second_slopes[1])
    normed_two_own = sum(
        restored(outof(expanded_grad_parts[i], up_parts[i]), i) for i in range(2)
    ).astype(jnp.bfloat16)
    normed_two_other = model_swap(normed_two_own)
    normed_two_other, normed_map_own = together([normed_two_other, normed_map_own])
    normed_map_other = model_swap(normed_map_own)
    normed_two_grad = normed_two_own.astype(jnp.float32) + normed_two_other.astype(jnp.float32)
    hidden_part, mlp_gain_slope = mlp_norm_back(normed_two_grad)
    hidden_grad = result_grad + hidden_part
    hidden_low = hidden_grad.astype(jnp.bfloat16)
    hidden_picked = picked(hidden_low, 0)
    attended_grad_low = into(hidden_picked, output_parts).astype(jnp.bfloat16)
    query_grad_rows, key_grad_all, value_grad_all = attend_back(qkv_rows, pair, attended_grad_low)
    pair_back = jnp.concatenate(
        [key_grad_all, value_grad_all], axis=1
    )
    pair_other = pair_swap(pair_back[2 * token_count :].astype(jnp.bfloat16))
    map_widths = (widened_low.shape[1], widened_low.shape[1], adapter_slope.shape[1])
    map_slopes_packed = packed_map_slopes(
        after(place, attended_grad_low),
        [rotated(i) for i in range(2, 5)],
        even_edges(sum(map_widths), 3),
        normed_map_pair,
        widened_grad_low,
        narrowed_grad_pair,
        widened_low,
        adapter_slope.astype(jnp.bfloat16),
    )
    pair_other, normed_map_other, *map_slopes_packed = together(
        [pair_other, normed_map_other, *map_slopes_packed]
    )
    pair_back = pair_back[: 2 * token_count] + pair_other.astype(jnp.float32)
    pair_back = pair_back[:token_count] + core_swap(
        pair_back[token_count:].astype(jnp.bfloat16)
    ).astype(jnp.float32)
    qkv_grad = jnp.concatenate([query_grad_rows, pair_back.astype(jnp.bfloat16)], axis=1)
    normed_own = restored(outof(qkv_grad, qkv_parts), 0).astype(jnp.bfloat16)
    normed_other = model_swap(normed_own)
    first_slopes = split_rows(
        paired_slopes(
            (normed_first, hidden_picked, normed_two_picked[0]),
            (qkv_grad, attended_low, expanded_grad_parts[0]),
        )
    )
    first_far = core_swap(first_slopes[1])
    normed_map_grad = normed_map_own.astype(jnp.float32) + normed_map_other.astype(jnp.float32)
    convolved_grad, conv_gain_slope = conv_norm_back(normed_map_grad)
    convolved_grad_low = convolved_grad.reshape(map_shape).astype(jnp.bfloat16)
    grad_low, grad_high = halo_rows(convolved_grad_low, RADIUS)
    grad_low, grad_high, *map_slopes_packed = together(
        [grad_low, grad_high, *map_slopes_packed]
    )
    near = [
        split_sum(pair[0], part)
        for pair, part in ((first_slopes, first_far), (second_slopes, second_far))
    ]
    scatter = Scatter(
        [low for low, _ in near] + list(map_slopes_packed[0::2]),
        [high for _, high in near] + list(map_slopes_packed[1::2]),
        [rotated(i)[::-1] for i in range(5)],
    )

    depth_kernel_slope = map_slopes(map_place, high_map, map_low, map_high, convolved_grad_low)
    highres_grad = map_conv(
        map_place, convolved_grad_low, grad_low, grad_high, depth_kernel, map_grad
    )
    normed_grad = normed_own.astype(jnp.float32) + normed_other.astype(jnp.float32)
    input_part, attn_gain_slope = attn_norm_back(normed_grad)
    lowres_grad = (hidden_grad + input_part).reshape(low_strip, 1, grid_side, width)

    def as_rows(values):
        return jnp.pad(values, ((0, 0), (0, channels - values.shape[1])))

    minor_rows = jnp.concatenate(
        [
            depth_kernel_slope,
            conv_gain_slope[None],
            layer_scale_slope,
            as_rows(jnp.stack([attn_gain_slope, mlp_gain_slope, gate_vector_slope], 0)),
            as_rows(adapter_kernel_slope),
        ],
        axis=0,
    )
    lines = channels // LANES
    block_rows = -(-lines // 16) * 16
    minor = jnp.pad(
        minor_rows.astype(jnp.bfloat16).reshape(minor_rows.shape[0], lines, LANES),
        ((0, 2 * CHIPS - minor_rows.shape[0]), (0, block_rows - lines), (0, 0)),
    )
    depth_kernel_slope, highres_grad = scatter.advance(depth_kernel_slope, highres_grad)
    minor_own = row_sums(minor).astype(jnp.bfloat16)
    (minor_own,) = scatter.advance(minor_own)
    minor_copies = row_copies(minor_own)
    (minor_copies,) = scatter.advance(minor_copies)
    minor_all = (
        minor_copies[:, :lines].reshape(2 * CHIPS, channels).astype(jnp.float32)
    )
    while scatter.step < len(RINGS):
        scatter.advance()
    first_own, second_own, *map_blocks = scatter.result()
    up_own = jnp.concatenate([first_own[:, quad:], second_own[:, :hidden_half]], axis=1)
    down_own = second_own[:, hidden_half:]
    expand_own, shrink_own, adapter_own = unpacked_map_slopes(
        core,
        map_blocks,
        map_widths,
    )
    firsts = [first_own[:, i * local_width : (i + 1) * local_width] for i in range(4)]
    taps = depth_kernel.shape[0]
    side_taps = adapter_kernel.shape[0]
    return (
        blended.astype(jnp.bfloat16)[:, None],
        mapped[:, None],
        lowres_grad,
        highres_grad[:, None],
        minor_all[taps + 2, :width],
        firsts[0],
        firsts[1],
        firsts[2],
        firsts[3].T,
        minor_all[taps + 3, :width],
        up_own,
        down_own.T,
        minor_all[:taps],
        minor_all[taps],
        expand_own,
        shrink_own.T,
        minor_all[taps + 1],
        adapter_own,
        minor_all[taps + 5 : taps + 5 + side_taps, :own_width],
        minor_all[taps + 4, :width],
    )


def solution(mesh):
    in_specs = (
        P("dp", None, None, None),
        P("dp", None, None, None),
        P(),
        P(),
        P("dp", "mp"),
        P("dp", "mp"),
        P("dp", "mp"),
        P("mp", "dp"),
        P(),
        P("dp", "mp"),
        P("mp", "dp"),
        P(),
        P(),
        P("dp", "mp"),
        P("mp", "dp"),
        P(),
        P("dp", "mp"),
        P(None, "mp"),
        P(),
        P("dp", None, None, "mp"),
        P("dp", None, None, None),
    )
    out_specs = (
        P("dp", None, None, "mp"),
        P("dp", None, None, None),
        P("dp", None, None, None),
        P("dp", None, None, None),
        P(),
        P("dp", "mp"),
        P("dp", "mp"),
        P("dp", "mp"),
        P("mp", "dp"),
        P(),
        P("dp", "mp"),
        P("mp", "dp"),
        P(),
        P(),
        P("dp", "mp"),
        P("mp", "dp"),
        P(),
        P("dp", "mp"),
        P(None, "mp"),
        P(),
    )
    return jax.shard_map(
        on_device, mesh=mesh, in_specs=in_specs, out_specs=out_specs, check_vma=False
    )
```

time: 882 us -> 596 us (0.68)
  the two profiles are of different devices: /device:TPU:2 before, /device:TPU:1 now
where the time goes in v2:
time: 596 us; the launch traced here: 586 us
  Pallas kernels  136 us (23%)
  starting transfers between devices  107 us (18%)
  waiting for transfers between devices  101 us (17%)
  other arithmetic  83 us (14%)
  local copies, waits for them, and re-layouts  64.3 us (11%)
  matrix products  52.7 us (9%)
  blocking collectives  38.4 us (6%)
    ppermute x64, starting transfers between devices, xor_swap(): return lax.ppermute(values, 'dp', [(i, i ^ mask) for i in range(count)])  63.6 us
    ppermute x64, waiting for transfers between devices, xor_swap(): return lax.ppermute(values, 'dp', [(i, i ^ mask) for i in range(count)])  49.9 us
    unnamed x292, local copies, waits for them, and re-layouts  39.9 us
    pallas_call x2, Pallas kernels, map_conv(): pl.pallas_call(forward_kernel if added is None else backward_kernel, grid...  32.3 us
    dot_general x17, matrix products, matmul(): return jnp.dot(former, latter, preferred_element_type=jnp.float32)  32.2 us
    add x22, other arithmetic, split_sum(): return (kept[:half] + other[:half], kept[half:] + other[half:])  28.8 us
    pallas_call x3, Pallas kernels, dense(): pl.pallas_call(functools.partial(dense_kernel, flipped, scale is not None...  26.6 us
    pallas_call x1, Pallas kernels, packed_map_slopes(): pl.pallas_call(functools.partial(slope_pack_kernel, orders, spans), grid=...  26.6 us
  transfers between devices with their start and end apart: 81, of which 26 were waited for; matrix products, arithmetic and copies ran while one was open for 26% of the time, Pallas kernels for 21%

profile of v2, /device:TPU:1, one launch (start us, length us, event | category | flops | bytes accessed | tf_op | source)
XLA Modules:
  0.0 585.6 jit_solution(14661552477964785175)
XLA Ops:
  5.2 3.3 collective-permute-start.1
  12.2 4.3 collective-permute-done
  18.3 2.8 collective-permute-start.4
  27.0 2.6 collective-permute-done.7
  29.7 2.7 collective-permute-done.6
  36.5 4.4 collective-permute-done.12
  46.5 11.3 %collective-permute-start.21 = (bf16[3,48,1536]{2,1,0:T(8,128)(2,1)S(1)}, bf16[3,48,1536]{2,1,0:T(8,128)(2,1)S(1)}, u32[]{:S(2)}, u32[]{:S(2)}) collective-permute-start(bf16[3,48,1536]{2,1,0:T(8,128)(2,1)S(1)} %get-tuple-element.321), channel_id=1, source_target_pairs={{0,2},{2,4},{4,6},{6,8},{8,10},{10,12},{12,14},{14,16},{16,18},{18... | collective-permute-start | bytes 1327112 | tf_op jit(solution)/shard_map/ppermute | solution.py:684
  61.2 9.1 %collective-permute-start.22 = (bf16[3,48,1536]{2,1,0:T(8,128)(2,1)S(1)}, bf16[3,48,1536]{2,1,0:T(8,128)(2,1)S(1)}, u32[]{:S(2)}, u32[]{:S(2)}) collective-permute-start(bf16[3,48,1536]{2,1,0:T(8,128)(2,1)S(1)} %get-tuple-element.320), channel_id=1, source_target_pairs={{2,0},{4,2},{6,4},{8,6},{10,8},{12,10},{14,12},{16,14},{18,16},{20... | collective-permute-start | bytes 1327112 | tf_op jit(solution)/shard_map/ppermute | solution.py:685
  73.0 9.9 %collective-permute-done.19 = bf16[8,48,1152]{2,1,0:T(8,128)(2,1)S(1)} collective-permute-done((bf16[8,48,1152]{2,1,0:T(8,128)(2,1)S(1)}, bf16[8,48,1152]{2,1,0:T(8,128)(2,1)S(1)}, u32[]{:S(2)}, u32[]{:S(2)}) %collective-permute-start.19) | collective-permute-done | bytes 884768 | tf_op jit(solution)/shard_map/ppermute | solution.py:553
  97.6 15.6 %shard_map.356 = f32[12,48,1536]{2,1,0:T(8,128)S(1)} custom-call(s32[2]{0:T(128)S(1)} %pad_add_fusion.place, bf16[12,48,1536]{2,1,0:T(8,128)(2,1)S(1)} %bitcast.135, bf16[3,48,1536]{2,1,0:T(8,128)(2,1)S(1)} %copy-done.25, bf16[3,48,1536]{2,1,0:T(8,128)(2,1)S(1)} %copy-done.28, bf16[49,1536]{1,0:T(8,128)(2,1)S(1)} %copy-done.43), custom_call_target="tpu_custom_call" | custom-call | bytes 110592 | tf_op jit(solution)/shard_map/pallas_call | solution.py:142
  113.2 2.7 constant_dynamic-update-slice_fusion.6
  116.0 7.1 %collective-permute-done.23 = bf16[16,16,3072]{2,1,0:T(8,128)(2,1)} collective-permute-done((bf16[16,16,3072]{2,1,0:T(8,128)(2,1)}, bf16[16,16,3072]{2,1,0:T(8,128)(2,1)}, u32[]{:S(2)}, u32[]{:S(2)}) %collective-permute-start.23) | collective-permute-done | bytes 1572896 | tf_op jit(solution)/shard_map/ppermute | solution.py:553
  123.1 2.5 collective-permute-done.24
  125.6 3.2 collective-permute-done.27.refs_5_
  128.8 2.7 constant_dynamic-update-slice_fusion.5
  140.0 2.7 fusion.46.refs_0_
  142.7 2.7 constant_dynamic-update-slice_fusion.8
  156.7 2.3 collective-permute-start.30
  161.6 2.8 constant_dynamic-update-slice_fusion.7
  165.1 10.5 %collective-permute-done.30 = bf16[288,1024]{1,0:T(8,128)(2,1)} collective-permute-done((bf16[288,1024]{1,0:T(8,128)(2,1)}, bf16[288,1024]{1,0:T(8,128)(2,1)}, u32[]{:S(2)}, u32[]{:S(2)}) %collective-permute-start.30) | collective-permute-done | bytes 589856 | tf_op jit(solution)/shard_map/ppermute | solution.py:724
  177.0 4.5 shard_map.357.refs_4_
  185.3 3.4 collective-permute-start.31
  188.7 2.3 multiply_convert_fusion.1
  192.7 4.4 shard_map.358
  200.6 2.6 fusion.81
  210.3 10.1 %fusion.4 = (bf16[1152,1536]{1,0:T(8,128)(2,1)}, bf16[1152,1536]{1,0:T(8,128)(2,1)S(1)}) fusion(bf16[1536,1536]{1,0:T(8,128)(2,1)S(1)} %bitcast.142, bf16[576,1536]{1,0:T(8,128)(2,1)S(1)} %collective-permute-done.35, bf16[576,1536]{1,0:T(8,128)(2,1)S(1)} %get-tuple-element.292), kind=kOutput, calls=%fused_computation.5 | convolution fusion | flops 5462360064 | bytes 15335424 | tf_op jit(solution)/shard_map/dot_general | solution.py:703
  222.7 9.9 %shard_map.359 = (f32[576,1536]{1,0:T(8,128)S(1)}, bf16[576,1536]{1,0:T(8,128)(2,1)S(1)}) custom-call(bf16[1152,1536]{1,0:T(8,128)(2,1)S(1)} %get-tuple-element.160.left_ref.right_b, bf16[1536,1536]{1,0:T(8,128)(2,1)S(1)} %bitcast.140), custom_call_target="tpu_custom_call" | custom-call | bytes 1048576 | tf_op jit(solution)/shard_map/pallas_call | solution.py:483
  233.6 3.0 collective-permute-start.37
  238.6 8.3 %collective-permute-done.37.pool_other_ref = bf16[6,24,1536]{2,1,0:T(8,128)(2,1)S(1)} collective-permute-done((bf16[6,24,1536]{2,1,0:T(8,128)(2,1)S(1)}, bf16[6,24,1536]{2,1,0:T(8,128)(2,1)S(1)}, u32[]{:S(2)}, u32[]{:S(2)}) %collective-permute-start.37) | collective-permute-done | bytes 442400 | tf_op jit(solution)/shard_map/ppermute | solution.py:671
  246.9 2.9 shard_map.360
  252.6 3.1 collective-permute-start.41
  255.7 4.1 pad_maximum_fusion.left_a
  268.4 2.9 copy-done.9
  271.3 6.8 %shard_map.361.left_ref.right_a = bf16[1152,1536]{1,0:T(8,128)(2,1)S(1)} custom-call(bf16[1152,1536]{1,0:T(8,128)(2,1)S(1)} %pad_maximum_fusion.1.left_ref.left_b, bf16[1536,1536]{1,0:T(8,128)(2,1)S(1)} %bitcast.141, bf16[1152,1536]{1,0:T(8,128)(2,1)S(1)} %copy-done.21), custom_call_target="tpu_custom_call" | custom-call | bytes 1048576 | tf_op jit(solution)/shard_map/pallas_call | solution.py:483
  278.2 9.9 %shard_map.363 = (f32[576,1536]{1,0:T(8,128)S(1)}, bf16[576,1536]{1,0:T(8,128)(2,1)S(1)}) custom-call(bf16[1152,1536]{1,0:T(8,128)(2,1)S(1)} %shard_map.361.left_ref.right_a, bf16[1536,1536]{1,0:T(8,128)(2,1)S(1)} %bitcast.145), custom_call_target="tpu_custom_call" | custom-call | bytes 1048576 | tf_op jit(solution)/shard_map/pallas_call | solution.py:483
  289.9 4.8 collective-permute-done.41.other_ref
  295.7 4.9 shard_map.364
  306.1 2.9 collective-permute-start.43
  308.9 6.2 %collective-permute-start.48 = (bf16[1536,256]{1,0:T(8,128)(2,1)}, bf16[1536,256]{1,0:T(8,128)(2,1)}, u32[]{:S(2)}, u32[]{:S(2)}) collective-permute-start(bf16[1536,256]{1,0:T(8,128)(2,1)} %select_convert_fusion), channel_id=1, source_target_pairs={{0,2},{2,0},{4,6},{6,4},{8,10},{10,8},{12,14},{14,12},{16,18},{18,... | collective-permute-start | bytes 2359304 | tf_op jit(solution)/shard_map/ppermute | solution.py:553
  315.5 6.2 %collective-permute-done.42 = bf16[6,24,512]{2,1,0:T(8,128)(2,1)S(1)} collective-permute-done((bf16[6,24,512]{2,1,0:T(8,128)(2,1)S(1)}, bf16[6,24,512]{2,1,0:T(8,128)(2,1)S(1)}, u32[]{:S(2)}, u32[]{:S(2)}) %collective-permute-start.42) | collective-permute-done | bytes 147488 | tf_op jit(solution)/shard_map/ppermute | solution.py:671
  322.8 2.4 fusion.32
  334.0 3.8 shard_map.368
  345.6 3.0 collective-permute-start.47
  353.5 7.0 %shard_map.365 = (bf16[144,512]{1,0:T(8,128)(2,1)S(1)}, f32[576,512]{1,0:T(8,128)S(1)}, f32[576,512]{1,0:T(8,128)S(1)}) custom-call(bf16[144,1536]{1,0:T(8,128)(2,1)S(1)} %copy-done.17, bf16[576,1024]{1,0:T(8,128)(2,1)S(1)} %copy-done.3, bf16[576,1024]{1,0:T(8,128)(2,1)S(1)} %copy-done.3, bf16[144,512]{1,0:T(8,128)(2,1)S(1)} %fusion.60.grad_ref), custom_call_target="tpu_custom_call" | custom-call | bytes 1048576 | tf_op jit(solution)/shard_map/pallas_call | solution.py:373
  363.4 26.6 %shard_map.366 = (bf16[16,48,1152]{2,1,0:T(8,128)(2,1)S(1)}, bf16[16,48,1152]{2,1,0:T(8,128)(2,1)}, bf16[16,48,1152]{2,1,0:T(8,128)(2,1)S(1)}, bf16[16,48,1152]{...) custom-call(s32[1]{0:T(128)} %bitcast.24.place, bf16[1152,1536]{1,0:T(8,128)(2,1)S(1)} %copy-done.10, ...), custom_call_target="tpu_custom_call" | custom-call | bytes 1048576 | tf_op jit(solution)/shard_map/pallas_call | solution.py:908
  390.1 6.3 %slice_add_fusion = (bf16[16,16,3072]{2,1,0:T(8,128)(2,1)}, bf16[16,16,3072]{2,1,0:T(8,128)(2,1)}) fusion(bf16[16,16,3072]{2,1,0:T(8,128)(2,1)S(1)} %bitcast.165, bf16[32,16,3072]{2,1,0:T(8,128)(2,1)} %collective-permute-done.53, bf16[16,16,3072]{2,1,0:T(8,128)(2,1)} %bitcast.166), kind=kLoop, calls=%fused_computation.59 | loop fusion | flops 1572864 | bytes 9437184 | tf_op jit(solution)/shard_map/add | solution.py:589
  396.6 3.4 collective-permute-done.47
  403.6 3.8 shard_map.367
  416.5 3.0 collective-permute-start.50
  419.7 16.0 %collective-permute-done.55.low_ref = bf16[3,48,1536]{2,1,0:T(8,128)(2,1)S(1)} collective-permute-done((bf16[3,48,1536]{2,1,0:T(8,128)(2,1)S(1)}, bf16[3,48,1536]{2,1,0:T(8,128)(2,1)S(1)}, u32[]{:S(2)}, u32[]{:S(2)}) %collective-permute-start.55) | collective-permute-done | bytes 442400 | tf_op jit(solution)/shard_map/ppermute | solution.py:684
  447.2 18.0 %shard_map.369 = f32[49,1536]{1,0:T(8,128)S(1)} custom-call(s32[2]{0:T(128)S(1)} %pad_add_fusion.place, bf16[12,48,1536]{2,1,0:T(8,128)(2,1)S(1)} %bitcast.137, bf16[3,48,1536]{2,1,0:T(8,128)(2,1)S(1)} %copy-done.26, bf16[3,48,1536]{2,1,0:T(8,128)(2,1)S(1)} %copy-done.29, bf16[12,48,1536]{2,1,0:T(8,128)(2,1)S(1)} %bitcast.138), custom_call_target="tpu_custom_call" | custom-call | bytes 110592 | tf_op jit(solution)/shard_map/pallas_call | solution.py:162
  470.4 16.7 %shard_map.370 = f32[12,48,1536]{2,1,0:T(8,128)} custom-call(s32[2]{0:T(128)S(1)} %pad_add_fusion.place, bf16[12,48,1536]{2,1,0:T(8,128)(2,1)S(1)} %bitcast.139, bf16[3,48,1536]{2,1,0:T(8,128)(2,1)S(1)} %copy-done.48, bf16[3,48,1536]{2,1,0:T(8,128)(2,1)S(1)} %copy-done.50, bf16[49,1536]{1,0:T(8,128)(2,1)S(1)} %copy-done.44, f32[12,48,1536]{2,1,0:T(8,128)S(1)} %copy-done.14), custom_call_target="tpu_custom_call" | custom-call | bytes 110592 | tf_op jit(solution)/shard_map/pallas_call | solution.py:142
  488.5 2.7 slice_add_fusion.13
  492.6 2.6 slice_add_fusion.5
  495.2 2.7 collective-permute-start.63
  497.9 2.6 slice_add_fusion.6
  500.5 2.9 slice_add_fusion.9
  504.2 2.8 slice_add_fusion.11
  510.4 20.7 %all_to_all.10 = bf16[64,16,128]{2,1,0:T(8,128)(2,1)S(1)} all-to-all(bf16[64,16,128]{2,1,0:T(8,128)(2,1)S(1)} %pad.16), channel_id=1, replica_groups=mesh['dp'=64,'mp'=2] {'dp'}, dimensions={0} | all-to-all | bytes 524288 | tf_op jit(solution)/shard_map/all_to_all | solution.py:951
  542.6 17.7 %all_to_all.11 = bf16[64,16,128]{2,1,0:T(8,128)(2,1)S(1)} all-to-all(bf16[64,16,128]{2,1,0:T(8,128)(2,1)S(1)} %broadcast_in_dim.88), channel_id=1, replica_groups=mesh['dp'=64,'mp'=2] {'dp'}, dimensions={0} | all-to-all | bytes 524288 | tf_op jit(solution)/shard_map/all_to_all | solution.py:957
  564.0 2.5 collective-permute-done.74
  569.8 2.2 collective-permute-start.78
  575.3 2.4 collective-permute-done.76
  578.0 4.3 collective-permute-start.80
  (611 shorter events, 197.8 us)
Async XLA Ops:
  5.2 7.0 %collective-permute-start.1 = (bf16[1,16,3072]{2,1,0:T(8,128)(2,1)S(1)}, bf16[1,16,3072]{2,1,0:T(8,128)(2,1)S(1)}, u32[]{:S(2)}, u32[]{:S(2)}) collective-permute-start(bf16[1,16,3072]{2,1,0:T(8,128)(2,1)S(1)} %maximum_bitcast_fusion), channel_id=1, source_target_pairs={{0,12},{2,14},{4,8},{6,10},{8,4},{10,6},{12,0},{14,2},{16,28},{18,... | collective-permute-start | bytes 294920 | tf_op jit(solution)/shard_map/ppermute | solution.py:553
  25.2 7.3 %collective-permute-start.10 = (bf16[2,48,1024]{2,1,0:T(8,128)(2,1)S(1)}, bf16[2,48,1024]{2,1,0:T(8,128)(2,1)S(1)}, u32[]{:S(2)}, u32[]{:S(2)}) collective-permute-start(bf16[2,48,1024]{2,1,0:T(8,128)(2,1)S(1)} %pad_maximum_fusion.27), channel_id=1, source_target_pairs={{0,4},{2,6},{4,0},{6,2},{8,12},{10,14},{12,8},{14,10},{16,20},{18,... | collective-permute-start | bytes 589832 | tf_op jit(solution)/shard_map/ppermute | solution.py:553
  25.3 7.2 %collective-permute-start.9 = (bf16[2,48,1152]{2,1,0:T(8,128)(2,1)S(1)}, bf16[2,48,1152]{2,1,0:T(8,128)(2,1)S(1)}, u32[]{:S(2)}, u32[]{:S(2)}) collective-permute-start(bf16[2,48,1152]{2,1,0:T(8,128)(2,1)S(1)} %pad_maximum_fusion.24), channel_id=1, source_target_pairs={{0,64},{2,66},{4,68},{6,70},{8,72},{10,74},{12,76},{14,78},{16,80}... | collective-permute-start | bytes 663560 | tf_op jit(solution)/shard_map/ppermute | solution.py:553
  25.4 7.2 %collective-permute-start.8 = (bf16[2,48,1152]{2,1,0:T(8,128)(2,1)S(1)}, bf16[2,48,1152]{2,1,0:T(8,128)(2,1)S(1)}, u32[]{:S(2)}, u32[]{:S(2)}) collective-permute-start(bf16[2,48,1152]{2,1,0:T(8,128)(2,1)S(1)} %pad_maximum_fusion.23), channel_id=1, source_target_pairs={{0,48},{2,50},{4,52},{6,54},{8,56},{10,58},{12,60},{14,62},{16,32}... | collective-permute-start | bytes 663560 | tf_op jit(solution)/shard_map/ppermute | solution.py:553
  32.6 8.3 %collective-permute-start.12 = (bf16[4,16,3072]{2,1,0:T(8,128)(2,1)S(1)}, bf16[4,16,3072]{2,1,0:T(8,128)(2,1)S(1)}, u32[]{:S(2)}, u32[]{:S(2)}) collective-permute-start(bf16[4,16,3072]{2,1,0:T(8,128)(2,1)S(1)} %pad_maximum_fusion.20), channel_id=1, source_target_pairs={{0,48},{2,50},{4,52},{6,54},{8,56},{10,58},{12,60},{14,62},{16,32}... | collective-permute-start | bytes 1179656 | tf_op jit(solution)/shard_map/ppermute | solution.py:553
  34.4 6.9 %collective-permute-start.11 = (bf16[4,16,3072]{2,1,0:T(8,128)(2,1)S(1)}, bf16[4,16,3072]{2,1,0:T(8,128)(2,1)S(1)}, u32[]{:S(2)}, u32[]{:S(2)}) collective-permute-start(bf16[4,16,3072]{2,1,0:T(8,128)(2,1)S(1)} %pad_maximum_fusion.19), channel_id=1, source_target_pairs={{0,16},{2,18},{4,20},{6,22},{8,24},{10,26},{12,28},{14,30},{16,0},... | collective-permute-start | bytes 1179656 | tf_op jit(solution)/shard_map/ppermute | solution.py:553
  34.4 8.1 %collective-permute-start.15 = (bf16[4,48,1024]{2,1,0:T(8,128)(2,1)S(1)}, bf16[4,48,1024]{2,1,0:T(8,128)(2,1)S(1)}, u32[]{:S(2)}, u32[]{:S(2)}) collective-permute-start(bf16[4,48,1024]{2,1,0:T(8,128)(2,1)S(1)} %pad_maximum_fusion.21), channel_id=1, source_target_pairs={{0,12},{2,14},{4,8},{6,10},{8,4},{10,6},{12,0},{14,2},{16,28},{18,... | collective-permute-start | bytes 1179656 | tf_op jit(solution)/shard_map/ppermute | solution.py:553
  35.1 7.6 %collective-permute-start.14 = (bf16[4,48,1152]{2,1,0:T(8,128)(2,1)S(1)}, bf16[4,48,1152]{2,1,0:T(8,128)(2,1)S(1)}, u32[]{:S(2)}, u32[]{:S(2)}) collective-permute-start(bf16[4,48,1152]{2,1,0:T(8,128)(2,1)S(1)} %pad_maximum_fusion.17), channel_id=1, source_target_pairs={{0,4},{2,6},{4,0},{6,2},{8,12},{10,14},{12,8},{14,10},{16,20},{18,... | collective-permute-start | bytes 1327112 | tf_op jit(solution)/shard_map/ppermute | solution.py:553
  35.1 7.7 %collective-permute-start.13 = (bf16[4,48,1152]{2,1,0:T(8,128)(2,1)S(1)}, bf16[4,48,1152]{2,1,0:T(8,128)(2,1)S(1)}, u32[]{:S(2)}, u32[]{:S(2)}) collective-permute-start(bf16[4,48,1152]{2,1,0:T(8,128)(2,1)S(1)} %pad_maximum_fusion.16), channel_id=1, source_target_pairs={{0,64},{2,66},{4,68},{6,70},{8,72},{10,74},{12,76},{14,78},{16,80}... | collective-permute-start | bytes 1327112 | tf_op jit(solution)/shard_map/ppermute | solution.py:553
  42.9 15.7 %collective-permute-start.17 = (bf16[8,16,3072]{2,1,0:T(8,128)(2,1)S(1)}, bf16[8,16,3072]{2,1,0:T(8,128)(2,1)S(1)}, u32[]{:S(2)}, u32[]{:S(2)}) collective-permute-start(bf16[8,16,3072]{2,1,0:T(8,128)(2,1)S(1)} %pad_maximum_fusion.12), channel_id=1, source_target_pairs={{0,64},{2,66},{4,68},{6,70},{8,72},{10,74},{12,76},{14,78},{16,80}... | collective-permute-start | bytes 2359304 | tf_op jit(solution)/shard_map/ppermute | solution.py:553
  44.3 16.9 %collective-permute-start.20 = (bf16[8,48,1024]{2,1,0:T(8,128)(2,1)S(1)}, bf16[8,48,1024]{2,1,0:T(8,128)(2,1)S(1)}, u32[]{:S(2)}, u32[]{:S(2)}) collective-permute-start(bf16[8,48,1024]{2,1,0:T(8,128)(2,1)S(1)} %pad_maximum_fusion.13), channel_id=1, source_target_pairs={{0,16},{2,18},{4,20},{6,22},{8,24},{10,26},{12,28},{14,30},{16,0},... | collective-permute-start | bytes 2359304 | tf_op jit(solution)/shard_map/ppermute | solution.py:553
  45.7 25.8 %collective-permute-start.16 = (bf16[8,16,3072]{2,1,0:T(8,128)(2,1)S(1)}, bf16[8,16,3072]{2,1,0:T(8,128)(2,1)S(1)}, u32[]{:S(2)}, u32[]{:S(2)}) collective-permute-start(bf16[8,16,3072]{2,1,0:T(8,128)(2,1)S(1)} %pad_maximum_fusion.11), channel_id=1, source_target_pairs={{0,48},{2,50},{4,52},{6,54},{8,56},{10,58},{12,60},{14,62},{16,32}... | collective-permute-start | bytes 2359304 | tf_op jit(solution)/shard_map/ppermute | solution.py:553
  46.5 39.2 %collective-permute-start.21 = (bf16[3,48,1536]{2,1,0:T(8,128)(2,1)S(1)}, bf16[3,48,1536]{2,1,0:T(8,128)(2,1)S(1)}, u32[]{:S(2)}, u32[]{:S(2)}) collective-permute-start(bf16[3,48,1536]{2,1,0:T(8,128)(2,1)S(1)} %get-tuple-element.321), channel_id=1, source_target_pairs={{0,2},{2,4},{4,6},{6,8},{8,10},{10,12},{12,14},{14,16},{16,18},{18... | collective-permute-start | bytes 1327112 | tf_op jit(solution)/shard_map/ppermute | solution.py:684
  57.8 25.0 %collective-permute-start.19 = (bf16[8,48,1152]{2,1,0:T(8,128)(2,1)S(1)}, bf16[8,48,1152]{2,1,0:T(8,128)(2,1)S(1)}, u32[]{:S(2)}, u32[]{:S(2)}) collective-permute-start(bf16[8,48,1152]{2,1,0:T(8,128)(2,1)S(1)} %pad_maximum_fusion.10), channel_id=1, source_target_pairs={{0,12},{2,14},{4,8},{6,10},{8,4},{10,6},{12,0},{14,2},{16,28},{18,... | collective-permute-start | bytes 2654216 | tf_op jit(solution)/shard_map/ppermute | solution.py:553
  58.6 25.6 %collective-permute-start.18 = (bf16[8,48,1152]{2,1,0:T(8,128)(2,1)S(1)}, bf16[8,48,1152]{2,1,0:T(8,128)(2,1)S(1)}, u32[]{:S(2)}, u32[]{:S(2)}) collective-permute-start(bf16[8,48,1152]{2,1,0:T(8,128)(2,1)S(1)} %pad_maximum_fusion.9), channel_id=1, source_target_pairs={{0,4},{2,6},{4,0},{6,2},{8,12},{10,14},{12,8},{14,10},{16,20},{18,... | collective-permute-start | bytes 2654216 | tf_op jit(solution)/shard_map/ppermute | solution.py:553
  61.2 25.2 %collective-permute-start.22 = (bf16[3,48,1536]{2,1,0:T(8,128)(2,1)S(1)}, bf16[3,48,1536]{2,1,0:T(8,128)(2,1)S(1)}, u32[]{:S(2)}, u32[]{:S(2)}) collective-permute-start(bf16[3,48,1536]{2,1,0:T(8,128)(2,1)S(1)} %get-tuple-element.320), channel_id=1, source_target_pairs={{2,0},{4,2},{6,4},{8,6},{10,8},{12,10},{14,12},{16,14},{18,16},{20... | collective-permute-start | bytes 1327112 | tf_op jit(solution)/shard_map/ppermute | solution.py:685
  87.2 41.6 %collective-permute-start.25 = (bf16[16,48,1152]{2,1,0:T(8,128)(2,1)}, bf16[16,48,1152]{2,1,0:T(8,128)(2,1)}, u32[]{:S(2)}, u32[]{:S(2)}) collective-permute-start(bf16[16,48,1152]{2,1,0:T(8,128)(2,1)} %pad_maximum_fusion.2.refs_0_), channel_id=1, source_target_pairs={{0,12},{2,14},{4,8},{6,10},{8,4},{10,6},{12,0},{14,2},{16,28},{18,... | collective-permute-start | bytes 5308424 | tf_op jit(solution)/shard_map/ppermute | solution.py:553
  87.2 41.6 %collective-permute-start.26 = (bf16[16,48,1152]{2,1,0:T(8,128)(2,1)}, bf16[16,48,1152]{2,1,0:T(8,128)(2,1)}, u32[]{:S(2)}, u32[]{:S(2)}) collective-permute-start(bf16[16,48,1152]{2,1,0:T(8,128)(2,1)} %pad_maximum_fusion.3.refs_2_), channel_id=1, source_target_pairs={{0,16},{2,18},{4,20},{6,22},{8,24},{10,26},{12,28},{14,30},{16,0},... | collective-permute-start | bytes 5308424 | tf_op jit(solution)/shard_map/ppermute | solution.py:553
  88.1 35.0 %collective-permute-start.23 = (bf16[16,16,3072]{2,1,0:T(8,128)(2,1)}, bf16[16,16,3072]{2,1,0:T(8,128)(2,1)}, u32[]{:S(2)}, u32[]{:S(2)}) collective-permute-start(bf16[16,16,3072]{2,1,0:T(8,128)(2,1)} %pad_maximum_fusion.4), channel_id=1, source_target_pairs={{0,64},{2,66},{4,68},{6,70},{8,72},{10,74},{12,76},{14,78},{16,80}... | collective-permute-start | bytes 4718600 | tf_op jit(solution)/shard_map/ppermute | solution.py:553
  89.2 36.4 %collective-permute-start.24 = (bf16[16,16,3072]{2,1,0:T(8,128)(2,1)}, bf16[16,16,3072]{2,1,0:T(8,128)(2,1)}, u32[]{:S(2)}, u32[]{:S(2)}) collective-permute-start(bf16[16,16,3072]{2,1,0:T(8,128)(2,1)} %pad_maximum_fusion.5), channel_id=1, source_target_pairs={{0,4},{2,6},{4,0},{6,2},{8,12},{10,14},{12,8},{14,10},{16,20},{18,... | collective-permute-start | bytes 4718600 | tf_op jit(solution)/shard_map/ppermute | solution.py:553
  91.2 37.6 %collective-permute-start.27 = (bf16[16,48,1024]{2,1,0:T(8,128)(2,1)}, bf16[16,48,1024]{2,1,0:T(8,128)(2,1)}, u32[]{:S(2)}, u32[]{:S(2)}) collective-permute-start(bf16[16,48,1024]{2,1,0:T(8,128)(2,1)} %pad_maximum_fusion.6.refs_4_), channel_id=1, source_target_pairs={{0,48},{2,50},{4,52},{6,54},{8,56},{10,58},{12,60},{14,62},{16,32}... | collective-permute-start | bytes 4718600 | tf_op jit(solution)/shard_map/ppermute | solution.py:553
  131.5 16.7 %collective-permute-start.28 = (bf16[32,16,3072]{2,1,0:T(8,128)(2,1)}, bf16[32,16,3072]{2,1,0:T(8,128)(2,1)}, u32[]{:S(2)}, u32[]{:S(2)}) collective-permute-start(bf16[32,16,3072]{2,1,0:T(8,128)(2,1)} %constant_dynamic-update-slice_fusion.5), channel_id=1, source_target_pairs={{0,2},{2,0},{4,6},{6,4},{8,10},{10,8},{12,14},{14,12},{16,18},{18,... | collective-permute-start | bytes 9437192 | tf_op jit(solution)/shard_map/ppermute | solution.py:553
  156.7 19.0 %collective-permute-start.30 = (bf16[288,1024]{1,0:T(8,128)(2,1)}, bf16[288,1024]{1,0:T(8,128)(2,1)}, u32[]{:S(2)}, u32[]{:S(2)}) collective-permute-start(bf16[288,1024]{1,0:T(8,128)(2,1)} %pad_maximum_fusion.15), channel_id=1, source_target_pairs={{0,124},{2,126},{4,8},{6,10},{8,4},{10,6},{12,16},{14,18},{16,12},... | collective-permute-start | bytes 1769480 | tf_op jit(solution)/shard_map/ppermute | solution.py:724
  164.4 40.8 %collective-permute-start.32 = (bf16[32,16,3072]{2,1,0:T(8,128)(2,1)}, bf16[32,16,3072]{2,1,0:T(8,128)(2,1)S(1)}, u32[]{:S(2)}, u32[]{:S(2)}) collective-permute-start(bf16[32,16,3072]{2,1,0:T(8,128)(2,1)} %constant_dynamic-update-slice_fusion.7), channel_id=1, source_target_pairs={{0,2},{2,0},{4,6},{6,4},{8,10},{10,8},{12,14},{14,12},{16,18},{18,... | collective-permute-start | bytes 9437192 | tf_op jit(solution)/shard_map/ppermute | solution.py:553
  185.3 12.8 %collective-permute-start.31 = (bf16[144,1024]{1,0:T(8,128)(2,1)S(1)}, bf16[144,1024]{1,0:T(8,128)(2,1)S(1)}, u32[]{:S(2)}, u32[]{:S(2)}) collective-permute-start(bf16[144,1024]{1,0:T(8,128)(2,1)S(1)} %fusion.47), channel_id=1, source_target_pairs={{0,1},{1,0},{2,3},{3,2},{4,5},{5,4},{6,7},{7,6},{8,9},{9,8},{10,11... | collective-permute-start | bytes 884744 | tf_op jit(solution)/shard_map/ppermute | solution.py:671
  191.0 19.2 %collective-permute-start.35 = (bf16[576,1536]{1,0:T(8,128)(2,1)S(1)}, bf16[576,1536]{1,0:T(8,128)(2,1)S(1)}, u32[]{:S(2)}, u32[]{:S(2)}) collective-permute-start(bf16[576,1536]{1,0:T(8,128)(2,1)S(1)} %get-tuple-element.292), channel_id=1, source_target_pairs={{0,2},{2,0},{4,6},{6,4},{8,10},{10,8},{12,14},{14,12},{16,18},{18,... | collective-permute-start | bytes 5308424 | tf_op jit(solution)/shard_map/ppermute | solution.py:553
  197.1 24.5 %collective-permute-start.34 = (bf16[1536,256]{1,0:T(8,128)(2,1)S(1)}, bf16[1536,256]{1,0:T(8,128)(2,1)S(1)}, u32[]{:S(2)}, u32[]{:S(2)}) collective-permute-start(bf16[1536,256]{1,0:T(8,128)(2,1)S(1)} %bitcast.155), channel_id=1, source_target_pairs={{0,2},{2,0},{4,6},{6,4},{8,10},{10,8},{12,14},{14,12},{16,18},{18,... | collective-permute-start | bytes 2359304 | tf_op jit(solution)/shard_map/ppermute | solution.py:553
  210.1 10.2 %collective-permute-start.33 = (bf16[144,1024]{1,0:T(8,128)(2,1)S(1)}, bf16[144,1024]{1,0:T(8,128)(2,1)S(1)}, u32[]{:S(2)}, u32[]{:S(2)}) collective-permute-start(bf16[144,1024]{1,0:T(8,128)(2,1)S(1)} %fusion.52), channel_id=1, source_target_pairs={{0,1},{1,0},{2,3},{3,2},{4,5},{5,4},{6,7},{7,6},{8,9},{9,8},{10,11... | collective-permute-start | bytes 884744 | tf_op jit(solution)/shard_map/ppermute | solution.py:671
  233.6 13.4 %collective-permute-start.37 = (bf16[6,24,1536]{2,1,0:T(8,128)(2,1)S(1)}, bf16[6,24,1536]{2,1,0:T(8,128)(2,1)S(1)}, u32[]{:S(2)}, u32[]{:S(2)}) collective-permute-start(bf16[6,24,1536]{2,1,0:T(8,128)(2,1)S(1)} %bitcast.151), channel_id=1, source_target_pairs={{0,1},{1,0},{2,3},{3,2},{4,5},{5,4},{6,7},{7,6},{8,9},{9,8},{10,11... | collective-permute-start | bytes 1327112 | tf_op jit(solution)/shard_map/ppermute | solution.py:671
  251.7 14.1 %collective-permute-start.38 = (bf16[576,1536]{1,0:T(8,128)(2,1)S(1)}, bf16[576,1536]{1,0:T(8,128)(2,1)}, u32[]{:S(2)}, u32[]{:S(2)}) collective-permute-start(bf16[576,1536]{1,0:T(8,128)(2,1)S(1)} %bitcast.147), channel_id=1, source_target_pairs={{0,2},{2,0},{4,6},{6,4},{8,10},{10,8},{12,14},{14,12},{16,18},{18,... | collective-permute-start | bytes 5308424 | tf_op jit(solution)/shard_map/ppermute | solution.py:553
  252.6 42.1 %collective-permute-start.41 = (bf16[12,48,1536]{2,1,0:T(8,128)(2,1)}, bf16[12,48,1536]{2,1,0:T(8,128)(2,1)S(1)}, u32[]{:S(2)}, u32[]{:S(2)}) collective-permute-start(bf16[12,48,1536]{2,1,0:T(8,128)(2,1)} %bitcast.30.own_ref), channel_id=1, source_target_pairs={{0,1},{1,0},{2,3},{3,2},{4,5},{5,4},{6,7},{7,6},{8,9},{9,8},{10,11... | collective-permute-start | bytes 5308424 | tf_op jit(solution)/shard_map/ppermute | solution.py:671
  294.7 8.2 %collective-permute-start.39 = (bf16[1,24,1024]{2,1,0:T(8,128)(2,1)S(1)}, bf16[1,24,1024]{2,1,0:T(8,128)(2,1)S(1)}, u32[]{:S(2)}, u32[]{:S(2)}) collective-permute-start(bf16[1,24,1024]{2,1,0:T(8,128)(2,1)S(1)} %get-tuple-element.352), channel_id=1, source_target_pairs={{0,2},{2,4},{4,6},{6,8},{8,10},{10,12},{12,14},{14,16},{16,18},{18... | collective-permute-start | bytes 147464 | tf_op jit(solution)/shard_map/ppermute | solution.py:684
  294.8 8.1 %collective-permute-start.40 = (bf16[1,24,1024]{2,1,0:T(8,128)(2,1)S(1)}, bf16[1,24,1024]{2,1,0:T(8,128)(2,1)S(1)}, u32[]{:S(2)}, u32[]{:S(2)}) collective-permute-start(bf16[1,24,1024]{2,1,0:T(8,128)(2,1)S(1)} %get-tuple-element.351), channel_id=1, source_target_pairs={{2,0},{4,2},{6,4},{8,6},{10,8},{12,10},{14,12},{16,14},{18,16},{20... | collective-permute-start | bytes 147464 | tf_op jit(solution)/shard_map/ppermute | solution.py:685
  306.1 9.3 %collective-permute-start.43 = (bf16[6,24,1]{1,0,2:T(8,128)(2,1)S(1)}, bf16[6,24,1]{1,0,2:T(8,128)(2,1)S(1)}, u32[]{:S(2)}, u32[]{:S(2)}) collective-permute-start(bf16[6,24,1]{1,0,2:T(8,128)(2,1)S(1)} %bitcast.199), channel_id=1, source_target_pairs={{0,1},{1,0},{2,3},{3,2},{4,5},{5,4},{6,7},{7,6},{8,9},{9,8},{10,11... | collective-permute-start | bytes 872 | tf_op jit(solution)/shard_map/ppermute | solution.py:671
  308.9 31.9 %collective-permute-start.48 = (bf16[1536,256]{1,0:T(8,128)(2,1)}, bf16[1536,256]{1,0:T(8,128)(2,1)}, u32[]{:S(2)}, u32[]{:S(2)}) collective-permute-start(bf16[1536,256]{1,0:T(8,128)(2,1)} %select_convert_fusion), channel_id=1, source_target_pairs={{0,2},{2,0},{4,6},{6,4},{8,10},{10,8},{12,14},{14,12},{16,18},{18,... | collective-permute-start | bytes 2359304 | tf_op jit(solution)/shard_map/ppermute | solution.py:553
  315.1 28.3 %collective-permute-start.45 = (bf16[576,1536]{1,0:T(8,128)(2,1)S(1)}, bf16[576,1536]{1,0:T(8,128)(2,1)}, u32[]{:S(2)}, u32[]{:S(2)}) collective-permute-start(bf16[576,1536]{1,0:T(8,128)(2,1)S(1)} %get-tuple-element.177), channel_id=1, source_target_pairs={{0,2},{2,0},{4,6},{6,4},{8,10},{10,8},{12,14},{14,12},{16,18},{18,... | collective-permute-start | bytes 5308424 | tf_op jit(solution)/shard_map/ppermute | solution.py:553
  315.1 6.6 %collective-permute-start.42 = (bf16[6,24,512]{2,1,0:T(8,128)(2,1)S(1)}, bf16[6,24,512]{2,1,0:T(8,128)(2,1)S(1)}, u32[]{:S(2)}, u32[]{:S(2)}) collective-permute-start(bf16[6,24,512]{2,1,0:T(8,128)(2,1)S(1)} %get-tuple-element.359), channel_id=1, source_target_pairs={{0,1},{1,0},{2,3},{3,2},{4,5},{5,4},{6,7},{7,6},{8,9},{9,8},{10,11... | collective-permute-start | bytes 442376 | tf_op jit(solution)/shard_map/ppermute | solution.py:671
  333.8 11.8 %collective-permute-start.44 = (bf16[144,1024]{1,0:T(8,128)(2,1)S(1)}, bf16[144,1024]{1,0:T(8,128)(2,1)S(1)}, u32[]{:S(2)}, u32[]{:S(2)}) collective-permute-start(bf16[144,1024]{1,0:T(8,128)(2,1)S(1)} %fusion.54), channel_id=1, source_target_pairs={{0,1},{1,0},{2,3},{3,2},{4,5},{5,4},{6,7},{7,6},{8,9},{9,8},{10,11... | collective-permute-start | bytes 884744 | tf_op jit(solution)/shard_map/ppermute | solution.py:671
  337.8 52.3 %collective-permute-start.53 = (bf16[32,16,3072]{2,1,0:T(8,128)(2,1)S(1)}, bf16[32,16,3072]{2,1,0:T(8,128)(2,1)}, u32[]{:S(2)}, u32[]{:S(2)}) collective-permute-start(bf16[32,16,3072]{2,1,0:T(8,128)(2,1)S(1)} %bitcast.153), channel_id=1, source_target_pairs={{0,2},{2,0},{4,6},{6,4},{8,10},{10,8},{12,14},{14,12},{16,18},{18,... | collective-permute-start | bytes 9437192 | tf_op jit(solution)/shard_map/ppermute | solution.py:553
  345.6 54.5 %collective-permute-start.47 = (bf16[576,1536]{1,0:T(8,128)(2,1)S(1)}, bf16[576,1536]{1,0:T(8,128)(2,1)S(1)}, u32[]{:S(2)}, u32[]{:S(2)}) collective-permute-start(bf16[576,1536]{1,0:T(8,128)(2,1)S(1)} %add_convert_fusion.1), channel_id=1, source_target_pairs={{0,1},{1,0},{2,3},{3,2},{4,5},{5,4},{6,7},{7,6},{8,9},{9,8},{10,11... | collective-permute-start | bytes 5308424 | tf_op jit(solution)/shard_map/ppermute | solution.py:671
  360.8 35.8 %collective-permute-start.46 = (bf16[288,1024]{1,0:T(8,128)(2,1)S(1)}, bf16[288,1024]{1,0:T(8,128)(2,1)}, u32[]{:S(2)}, u32[]{:S(2)}) collective-permute-start(bf16[288,1024]{1,0:T(8,128)(2,1)S(1)} %slice.983), channel_id=1, source_target_pairs={{0,124},{2,126},{4,8},{6,10},{8,4},{10,6},{12,16},{14,18},{16,12},... | collective-permute-start | bytes 1769480 | tf_op jit(solution)/shard_map/ppermute | solution.py:724
  396.5 91.5 %collective-permute-start.54 = (bf16[16,16,3072]{2,1,0:T(8,128)(2,1)}, bf16[16,16,3072]{2,1,0:T(8,128)(2,1)}, u32[]{:S(2)}, u32[]{:S(2)}) collective-permute-start(bf16[16,16,3072]{2,1,0:T(8,128)(2,1)} %get-tuple-element.305), channel_id=1, source_target_pairs={{0,4},{2,6},{4,0},{6,2},{8,12},{10,14},{12,8},{14,10},{16,20},{18,... | collective-permute-start | bytes 4718600 | tf_op jit(solution)/shard_map/ppermute | solution.py:553
  407.4 31.5 %collective-permute-start.51 = (bf16[32,16,3072]{2,1,0:T(8,128)(2,1)S(1)}, bf16[32,16,3072]{2,1,0:T(8,128)(2,1)S(1)}, u32[]{:S(2)}, u32[]{:S(2)}) collective-permute-start(bf16[32,16,3072]{2,1,0:T(8,128)(2,1)S(1)} %bitcast.154), channel_id=1, source_target_pairs={{0,2},{2,0},{4,6},{6,4},{8,10},{10,8},{12,14},{14,12},{16,18},{18,... | collective-permute-start | bytes 9437192 | tf_op jit(solution)/shard_map/ppermute | solution.py:553
  410.6 25.1 %collective-permute-start.55 = (bf16[3,48,1536]{2,1,0:T(8,128)(2,1)S(1)}, bf16[3,48,1536]{2,1,0:T(8,128)(2,1)S(1)}, u32[]{:S(2)}, u32[]{:S(2)}) collective-permute-start(bf16[3,48,1536]{2,1,0:T(8,128)(2,1)S(1)} %bitcast.186), channel_id=1, source_target_pairs={{0,2},{2,4},{4,6},{6,8},{8,10},{10,12},{12,14},{14,16},{16,18},{18... | collective-permute-start | bytes 1327112 | tf_op jit(solution)/shard_map/ppermute | solution.py:684
  410.7 27.3 %collective-permute-start.56 = (bf16[3,48,1536]{2,1,0:T(8,128)(2,1)S(1)}, bf16[3,48,1536]{2,1,0:T(8,128)(2,1)S(1)}, u32[]{:S(2)}, u32[]{:S(2)}) collective-permute-start(bf16[3,48,1536]{2,1,0:T(8,128)(2,1)S(1)} %bitcast.185), channel_id=1, source_target_pairs={{2,0},{4,2},{6,4},{8,6},{10,8},{12,10},{14,12},{16,14},{18,16},{20... | collective-permute-start | bytes 1327112 | tf_op jit(solution)/shard_map/ppermute | solution.py:685
  416.5 24.6 %collective-permute-start.50 = (bf16[144,1024]{1,0:T(8,128)(2,1)S(1)}, bf16[144,1024]{1,0:T(8,128)(2,1)S(1)}, u32[]{:S(2)}, u32[]{:S(2)}) collective-permute-start(bf16[144,1024]{1,0:T(8,128)(2,1)S(1)} %fusion.50), channel_id=1, source_target_pairs={{0,1},{1,0},{2,3},{3,2},{4,5},{5,4},{6,7},{7,6},{8,9},{9,8},{10,11... | collective-permute-start | bytes 884744 | tf_op jit(solution)/shard_map/ppermute | solution.py:671
  438.8 49.2 %collective-permute-start.57 = (bf16[16,48,1152]{2,1,0:T(8,128)(2,1)}, bf16[16,48,1152]{2,1,0:T(8,128)(2,1)}, u32[]{:S(2)}, u32[]{:S(2)}) collective-permute-start(bf16[16,48,1152]{2,1,0:T(8,128)(2,1)} %get-tuple-element.202), channel_id=1, source_target_pairs={{0,12},{2,14},{4,8},{6,10},{8,4},{10,6},{12,0},{14,2},{16,28},{18,... | collective-permute-start | bytes 5308424 | tf_op jit(solution)/shard_map/ppermute | solution.py:553
  438.8 49.2 %collective-permute-start.58 = (bf16[16,48,1152]{2,1,0:T(8,128)(2,1)}, bf16[16,48,1152]{2,1,0:T(8,128)(2,1)}, u32[]{:S(2)}, u32[]{:S(2)}) collective-permute-start(bf16[16,48,1152]{2,1,0:T(8,128)(2,1)} %get-tuple-element.203), channel_id=1, source_target_pairs={{0,16},{2,18},{4,20},{6,22},{8,24},{10,26},{12,28},{14,30},{16,0},... | collective-permute-start | bytes 5308424 | tf_op jit(solution)/shard_map/ppermute | solution.py:553
  438.8 49.2 %collective-permute-start.59 = (bf16[16,48,1024]{2,1,0:T(8,128)(2,1)}, bf16[16,48,1024]{2,1,0:T(8,128)(2,1)}, u32[]{:S(2)}, u32[]{:S(2)}) collective-permute-start(bf16[16,48,1024]{2,1,0:T(8,128)(2,1)} %get-tuple-element.204), channel_id=1, source_target_pairs={{0,48},{2,50},{4,52},{6,54},{8,56},{10,58},{12,60},{14,62},{16,32}... | collective-permute-start | bytes 4718600 | tf_op jit(solution)/shard_map/ppermute | solution.py:553
  441.1 46.9 %collective-permute-start.52 = (bf16[16,16,3072]{2,1,0:T(8,128)(2,1)}, bf16[16,16,3072]{2,1,0:T(8,128)(2,1)}, u32[]{:S(2)}, u32[]{:S(2)}) collective-permute-start(bf16[16,16,3072]{2,1,0:T(8,128)(2,1)} %get-tuple-element.311), channel_id=1, source_target_pairs={{0,64},{2,66},{4,68},{6,70},{8,72},{10,74},{12,76},{14,78},{16,80}... | collective-permute-start | bytes 4718600 | tf_op jit(solution)/shard_map/ppermute | solution.py:553
  491.2 39.9 %collective-permute-start.64 = (bf16[8,48,1024]{2,1,0:T(8,128)(2,1)}, bf16[8,48,1024]{2,1,0:T(8,128)(2,1)}, u32[]{:S(2)}, u32[]{:S(2)}) collective-permute-start(bf16[8,48,1024]{2,1,0:T(8,128)(2,1)} %get-tuple-element.301), channel_id=1, source_target_pairs={{0,16},{2,18},{4,20},{6,22},{8,24},{10,26},{12,28},{14,30},{16,0},... | collective-permute-start | bytes 2359304 | tf_op jit(solution)/shard_map/ppermute | solution.py:553
  495.2 36.0 %collective-permute-start.63 = (bf16[8,48,1152]{2,1,0:T(8,128)(2,1)}, bf16[8,48,1152]{2,1,0:T(8,128)(2,1)}, u32[]{:S(2)}, u32[]{:S(2)}) collective-permute-start(bf16[8,48,1152]{2,1,0:T(8,128)(2,1)} %get-tuple-element.297), channel_id=1, source_target_pairs={{0,12},{2,14},{4,8},{6,10},{8,4},{10,6},{12,0},{14,2},{16,28},{18,... | collective-permute-start | bytes 2654216 | tf_op jit(solution)/shard_map/ppermute | solution.py:553
  500.5 30.7 %collective-permute-start.62 = (bf16[8,48,1152]{2,1,0:T(8,128)(2,1)}, bf16[8,48,1152]{2,1,0:T(8,128)(2,1)}, u32[]{:S(2)}, u32[]{:S(2)}) collective-permute-start(bf16[8,48,1152]{2,1,0:T(8,128)(2,1)} %get-tuple-element.299), channel_id=1, source_target_pairs={{0,4},{2,6},{4,0},{6,2},{8,12},{10,14},{12,8},{14,10},{16,20},{18,... | collective-permute-start | bytes 2654216 | tf_op jit(solution)/shard_map/ppermute | solution.py:553
  503.4 27.8 %collective-permute-start.61 = (bf16[8,16,3072]{2,1,0:T(8,128)(2,1)}, bf16[8,16,3072]{2,1,0:T(8,128)(2,1)}, u32[]{:S(2)}, u32[]{:S(2)}) collective-permute-start(bf16[8,16,3072]{2,1,0:T(8,128)(2,1)} %get-tuple-element.303), channel_id=1, source_target_pairs={{0,64},{2,66},{4,68},{6,70},{8,72},{10,74},{12,76},{14,78},{16,80}... | collective-permute-start | bytes 2359304 | tf_op jit(solution)/shard_map/ppermute | solution.py:553
  507.0 24.1 %collective-permute-start.60 = (bf16[8,16,3072]{2,1,0:T(8,128)(2,1)}, bf16[8,16,3072]{2,1,0:T(8,128)(2,1)}, u32[]{:S(2)}, u32[]{:S(2)}) collective-permute-start(bf16[8,16,3072]{2,1,0:T(8,128)(2,1)} %get-tuple-element.308), channel_id=1, source_target_pairs={{0,48},{2,50},{4,52},{6,54},{8,56},{10,58},{12,60},{14,62},{16,32}... | collective-permute-start | bytes 2359304 | tf_op jit(solution)/shard_map/ppermute | solution.py:553
  532.6 27.6 %collective-permute-start.69 = (bf16[4,48,1024]{2,1,0:T(8,128)(2,1)S(1)}, bf16[4,48,1024]{2,1,0:T(8,128)(2,1)S(1)}, u32[]{:S(2)}, u32[]{:S(2)}) collective-permute-start(bf16[4,48,1024]{2,1,0:T(8,128)(2,1)S(1)} %get-tuple-element.323), channel_id=1, source_target_pairs={{0,12},{2,14},{4,8},{6,10},{8,4},{10,6},{12,0},{14,2},{16,28},{18,... | collective-permute-start | bytes 1179656 | tf_op jit(solution)/shard_map/ppermute | solution.py:553
  535.7 24.6 %collective-permute-start.68 = (bf16[4,48,1152]{2,1,0:T(8,128)(2,1)S(1)}, bf16[4,48,1152]{2,1,0:T(8,128)(2,1)S(1)}, u32[]{:S(2)}, u32[]{:S(2)}) collective-permute-start(bf16[4,48,1152]{2,1,0:T(8,128)(2,1)S(1)} %get-tuple-element.315), channel_id=1, source_target_pairs={{0,4},{2,6},{4,0},{6,2},{8,12},{10,14},{12,8},{14,10},{16,20},{18,... | collective-permute-start | bytes 1327112 | tf_op jit(solution)/shard_map/ppermute | solution.py:553
  537.1 23.2 %collective-permute-start.67 = (bf16[4,48,1152]{2,1,0:T(8,128)(2,1)S(1)}, bf16[4,48,1152]{2,1,0:T(8,128)(2,1)S(1)}, u32[]{:S(2)}, u32[]{:S(2)}) collective-permute-start(bf16[4,48,1152]{2,1,0:T(8,128)(2,1)S(1)} %get-tuple-element.317), channel_id=1, source_target_pairs={{0,64},{2,66},{4,68},{6,70},{8,72},{10,74},{12,76},{14,78},{16,80}... | collective-permute-start | bytes 1327112 | tf_op jit(solution)/shard_map/ppermute | solution.py:553
  539.0 21.2 %collective-permute-start.66 = (bf16[4,16,3072]{2,1,0:T(8,128)(2,1)S(1)}, bf16[4,16,3072]{2,1,0:T(8,128)(2,1)S(1)}, u32[]{:S(2)}, u32[]{:S(2)}) collective-permute-start(bf16[4,16,3072]{2,1,0:T(8,128)(2,1)S(1)} %get-tuple-element.325), channel_id=1, source_target_pairs={{0,48},{2,50},{4,52},{6,54},{8,56},{10,58},{12,60},{14,62},{16,32}... | collective-permute-start | bytes 1179656 | tf_op jit(solution)/shard_map/ppermute | solution.py:553
  542.4 17.8 %collective-permute-start.65 = (bf16[4,16,3072]{2,1,0:T(8,128)(2,1)S(1)}, bf16[4,16,3072]{2,1,0:T(8,128)(2,1)S(1)}, u32[]{:S(2)}, u32[]{:S(2)}) collective-permute-start(bf16[4,16,3072]{2,1,0:T(8,128)(2,1)S(1)} %get-tuple-element.327), channel_id=1, source_target_pairs={{0,16},{2,18},{4,20},{6,22},{8,24},{10,26},{12,28},{14,30},{16,0},... | collective-permute-start | bytes 1179656 | tf_op jit(solution)/shard_map/ppermute | solution.py:553
  560.8 7.5 %collective-permute-start.73 = (bf16[2,48,1152]{2,1,0:T(8,128)(2,1)S(1)}, bf16[2,48,1152]{2,1,0:T(8,128)(2,1)S(1)}, u32[]{:S(2)}, u32[]{:S(2)}) collective-permute-start(bf16[2,48,1152]{2,1,0:T(8,128)(2,1)S(1)} %get-tuple-element.329), channel_id=1, source_target_pairs={{0,64},{2,66},{4,68},{6,70},{8,72},{10,74},{12,76},{14,78},{16,80}... | collective-permute-start | bytes 663560 | tf_op jit(solution)/shard_map/ppermute | solution.py:553
  561.0 7.3 %collective-permute-start.72 = (bf16[2,48,1152]{2,1,0:T(8,128)(2,1)S(1)}, bf16[2,48,1152]{2,1,0:T(8,128)(2,1)S(1)}, u32[]{:S(2)}, u32[]{:S(2)}) collective-permute-start(bf16[2,48,1152]{2,1,0:T(8,128)(2,1)S(1)} %get-tuple-element.331), channel_id=1, source_target_pairs={{0,48},{2,50},{4,52},{6,54},{8,56},{10,58},{12,60},{14,62},{16,32}... | collective-permute-start | bytes 663560 | tf_op jit(solution)/shard_map/ppermute | solution.py:553
  568.2 7.1 %collective-permute-start.79 = (bf16[1,48,1024]{2,1,0:T(8,128)(2,1)S(1)}, bf16[1,48,1024]{2,1,0:T(8,128)(2,1)S(1)}, u32[]{:S(2)}, u32[]{:S(2)}) collective-permute-start(bf16[1,48,1024]{2,1,0:T(8,128)(2,1)S(1)} %slice_add_fusion.42), channel_id=1, source_target_pairs={{0,64},{2,66},{4,68},{6,70},{8,72},{10,74},{12,76},{14,78},{16,80}... | collective-permute-start | bytes 294920 | tf_op jit(solution)/shard_map/ppermute | solution.py:553
  569.8 8.0 %collective-permute-start.78 = (bf16[1,48,1152]{2,1,0:T(8,128)(2,1)S(1)}, bf16[1,48,1152]{2,1,0:T(8,128)(2,1)S(1)}, u32[]{:S(2)}, u32[]{:S(2)}) collective-permute-start(bf16[1,48,1152]{2,1,0:T(8,128)(2,1)S(1)} %slice_add_fusion.38), channel_id=1, source_target_pairs={{0,48},{2,50},{4,52},{6,54},{8,56},{10,58},{12,60},{14,62},{16,32}... | collective-permute-start | bytes 331784 | tf_op jit(solution)/shard_map/ppermute | solution.py:553
  (156 other events, 1113.5 us)

commit v3 on v2

--- a/solution.py
+++ b/solution.py
@@ -445,14 +445,17 @@
     return [part.reshape(CHIPS, part.shape[0] // CHIPS, part.shape[1]) for part in pair]
 
 
-def dense_kernel(flipped, scaled, halves, left_ref, right_ref, *refs):
+def dense_kernel(flipped, scaled, halves, lefts, *refs):
+    left_refs, right_ref, refs = refs[:lefts], refs[lefts], refs[lefts + 1 :]
     scale_ref, outs = (refs[0], refs[1:]) if scaled else (None, refs)
-    rows = left_ref.shape[0]
+    rows = sum(ref.shape[0] for ref in left_refs)
     chunk = rows // 6
     for part in range(6):
         lines = slice(part * chunk, (part + 1) * chunk)
         product = nt if flipped else functools.partial(jnp.dot, preferred_element_type=jnp.float32)
-        value = product(left_ref[lines, :], right_ref[...])
+        left = left_refs[part * lefts // 6]
+        start = part * chunk % left.shape[0]
+        value = product(left[start : start + chunk, :], right_ref[...])
         if scaled:
             value = value * scale_ref[lines, :].astype(jnp.float32)
         if halves:
@@ -462,17 +465,20 @@
             outs[0][lines, :] = value.astype(outs[0].dtype)
 
 
-def dense(left, right, flipped, scale=None, halves=False):
-    rows, depth = left.shape
+def dense(lefts, right, flipped, scale=None, halves=False):
+    rows, depth = sum(left.shape[0] for left in lefts), lefts[0].shape[1]
     count = right.shape[0] if flipped else right.shape[1]
     tile = 512
     specs = [
-        pl.BlockSpec((rows, depth), lambda i: (0, 0), pipeline_mode=pl.Buffered(1)),
+        *(
+            pl.BlockSpec(left.shape, lambda i: (0, 0), pipeline_mode=pl.Buffered(1))
+            for left in lefts
+        ),
         pl.BlockSpec((tile, depth), lambda i: (i, 0))
         if flipped
         else pl.BlockSpec((depth, tile), lambda i: (0, i)),
     ]
-    args = [left, right]
+    args = [*lefts, right]
     if scale is not None:
         specs.append(pl.BlockSpec((rows, tile), lambda i: (0, i)))
         args.append(scale)
@@ -481,14 +487,14 @@
     else:
         kinds = [(rows, jnp.bfloat16)]
     return pl.pallas_call(
-        functools.partial(dense_kernel, flipped, scale is not None, halves),
+        functools.partial(dense_kernel, flipped, scale is not None, halves, len(lefts)),
         grid=(count // tile,),
         in_specs=specs,
         out_specs=[pl.BlockSpec((size, tile), lambda i: (0, i)) for size, _ in kinds],
         out_shape=[jax.ShapeDtypeStruct((size, count), kind) for size, kind in kinds],
         compiler_params=pltpu.CompilerParams(vmem_limit_bytes=24 * 1024 * 1024),
         cost_estimate=pl.CostEstimate(flops=0, bytes_accessed=1 << 20, transcendentals=0),
-    )(*args)
+    )(*[pltpu.with_memory_space_constraint(a, pltpu.MemorySpace.HBM) for a in args])
 
 
 def mix_kernel(place, main_ref, low_ref, high_ref, taps_ref, mix_ref, back_ref, slope_ref, wide):
@@ -544,6 +550,117 @@
     )(place, both, low, high, taps)
 
 
+def row_moments(value):
+    average = jnp.mean(value, axis=-1, keepdims=True)
+    centred = value - average
+    spread = jnp.mean(centred * centred, axis=-1, keepdims=True)
+    rate = lax.rsqrt(spread + norm_epsilon)
+    return centred * rate, rate
+
+
+def wide_sum(refs):
+    total = refs[0][...].astype(jnp.float32)
+    for ref in refs[1:]:
+        total = total + ref[...].astype(jnp.float32)
+    return total
+
+
+def norm_kernel(count, *refs):
+    gain = refs[count][...].astype(jnp.float32)
+    total = wide_sum(refs[:count])
+    outs = refs[count + 1 :]
+    shape, _ = row_moments(total)
+    outs[-1][...] = (shape * gain).astype(outs[-1].dtype)
+    if count > 1:
+        outs[0][...] = total
+
+
+def norm_back_kernel(kinds, value_ref, own_ref, other_ref, gain_ref, *refs):
+    extra, (slope_ref, *outs) = (refs[0], refs[1:]) if kinds[0] else (None, refs)
+    gain = gain_ref[...].astype(jnp.float32)
+    shape, rate = row_moments(value_ref[...].astype(jnp.float32))
+    grad = own_ref[...].astype(jnp.float32) + other_ref[...].astype(jnp.float32)
+    scaled = grad * gain
+    first = jnp.mean(scaled, axis=-1, keepdims=True)
+    second = jnp.mean(scaled * shape, axis=-1, keepdims=True)
+    result = rate * (scaled - first - shape * second)
+    if extra is not None:
+        result = result + extra[...]
+    for out in outs:
+        out[...] = result.astype(out.dtype)
+    slope = jnp.sum(grad * shape, axis=0, keepdims=True)
+
+    @pl.when(pl.program_id(0) == 0)
+    def _():
+        slope_ref[...] = slope
+
+    @pl.when(pl.program_id(0) > 0)
+    def _():
+        slope_ref[...] += slope
+
+
+ROWS = 144
+CHEAP = pl.CostEstimate(flops=0, bytes_accessed=1 << 20, transcendentals=0)
+
+
+def row_block(width):
+    return pl.BlockSpec((ROWS, width), lambda i: (i, 0))
+
+
+def norm(values, gain):
+    rows, width = values[0].shape
+    whole = pl.BlockSpec((1, width), lambda i: (0, 0))
+    kinds = [jnp.float32, jnp.bfloat16] if len(values) > 1 else [jnp.bfloat16]
+    return pl.pallas_call(
+        functools.partial(norm_kernel, len(values)),
+        grid=(rows // ROWS,),
+        in_specs=[row_block(width)] * len(values) + [whole],
+        out_specs=[row_block(width)] * len(kinds),
+        out_shape=[jax.ShapeDtypeStruct((rows, width), kind) for kind in kinds],
+        compiler_params=pltpu.CompilerParams(vmem_limit_bytes=24 * 1024 * 1024),
+        cost_estimate=CHEAP,
+    )(*values, gain[None])
+
+
+def norm_back(value, own, other, gain, kinds, extra=None):
+    rows, width = value.shape
+    whole = pl.BlockSpec((1, width), lambda i: (0, 0))
+    more = [] if extra is None else [extra]
+    return pl.pallas_call(
+        functools.partial(norm_back_kernel, (extra is not None,)),
+        grid=(rows // ROWS,),
+        in_specs=[row_block(width)] * 3 + [whole] + [row_block(width)] * len(more),
+        out_specs=[whole] + [row_block(width)] * len(kinds),
+        out_shape=[jax.ShapeDtypeStruct((1, width), jnp.float32)]
+        + [jax.ShapeDtypeStruct((rows, width), kind) for kind in kinds],
+        compiler_params=pltpu.CompilerParams(vmem_limit_bytes=24 * 1024 * 1024),
+        cost_estimate=CHEAP,
+    )(value, own, other, gain[None], *more)
+
+
+def gate_kernel(hidden_ref, own_ref, other_ref, gate_ref, cot_ref, result_ref, gating_ref, low_ref):
+    result = wide_sum((hidden_ref, own_ref, other_ref))
+    result_ref[...] = result
+    total = jnp.sum(result * gate_ref[...].astype(jnp.float32), axis=-1, keepdims=True)
+    gating = jax.nn.sigmoid(total)
+    gating_ref[...] = jnp.broadcast_to(gating, gating_ref.shape)
+    low_ref[...] = (cot_ref[...].astype(jnp.float32) * gating).astype(low_ref.dtype)
+
+
+def gate(hidden, own, other, vector, cot):
+    rows, width = hidden.shape
+    return pl.pallas_call(
+        gate_kernel,
+        out_shape=[
+            jax.ShapeDtypeStruct((rows, width), jnp.float32),
+            jax.ShapeDtypeStruct((rows, LANES), jnp.float32),
+            jax.ShapeDtypeStruct(cot.shape, jnp.bfloat16),
+        ],
+        compiler_params=pltpu.CompilerParams(vmem_limit_bytes=24 * 1024 * 1024),
+        cost_estimate=CHEAP,
+    )(hidden, own, other, vector[None], cot)
+
+
 def rotated(start):
     return tuple(RINGS[(start + i) % len(RINGS)] for i in range(len(RINGS)))
 
@@ -646,7 +763,7 @@
         scratch_shapes=[pltpu.VMEM(s, jnp.bfloat16) for s in shapes]
         + [pltpu.SemaphoreType.DMA((len(shapes),))],
         compiler_params=pltpu.CompilerParams(vmem_limit_bytes=volume + volume // 4 + (4 << 20)),
-        cost_estimate=pl.CostEstimate(flops=0, bytes_accessed=2 * volume, transcendentals=0),
+        cost_estimate=CHEAP,
     )(place, *arrays)
 
 
@@ -684,13 +801,6 @@
     low = lax.ppermute(block[block.shape[0] - width :], "dp", forward)
     high = lax.ppermute(block[:width], "dp", backward)
     return low, high
-
-
-def normalize(values, scale_gain):
-    average = jnp.mean(values, axis=-1, keepdims=True)
-    centred = values - average
-    spread = jnp.mean(centred * centred, axis=-1, keepdims=True)
-    return centred * lax.rsqrt(spread + norm_epsilon) * scale_gain
 
 
 def gelu_pair(values):
@@ -812,20 +922,24 @@
     return [(edges[i], edges[i + 1]) for i in range(count)]
 
 
-def turn(left_ref, turned):
-    for first in range(0, left_ref.shape[1], LANES):
-        lanes = slice(first, first + LANES)
-        turned[lanes, :] = left_ref[:, lanes].T
-
-
-def slope_pack_kernel(
-    orders, spans, place, left_a, right_a, left_b, right_b, extra_ref, *refs
-):
-    outs, (turned, tile, sems) = refs[:-3], refs[-3:]
-    width = right_a.shape[1]
+def turn(left_refs, turned):
+    first = 0
+    for left_ref in left_refs:
+        rows = left_ref.shape[0]
+        for start in range(0, left_ref.shape[1], LANES):
+            lanes = slice(start, start + LANES)
+            turned[lanes, first : first + rows] = left_ref[:, lanes].T
+        first += rows
+
+
+def slope_pack_kernel(order, lefts, place, *refs):
+    left_refs, right_ref = refs[:lefts], refs[lefts]
+    extra_ref = refs[lefts + 1] if len(refs) > lefts + 6 else None
+    near_ref, far_ref, turned, tile, sems = refs[-5:]
+    width = right_ref.shape[1]
     step = pl.program_id(0)
-    per_side = left_a.shape[1] // width
-    total = 2 * per_side + 1
+    full = turned.shape[0] // width
+    total = full + (extra_ref is not None)
     blocks, rows = tile.shape[1], tile.shape[2]
     group = blocks // 4
     chip = place[0] >> 1
@@ -841,50 +955,37 @@
 
     @pl.when(step == 0)
     def _():
-        turn(left_a, turned)
-
-    @pl.when(step == per_side)
+        turn(left_refs, turned)
+
+    @pl.when(step < full)
     def _():
-        turn(left_b, turned)
-
-    def fill(right):
         for part in range(4):
             lines = slice(part * group * rows, (part + 1) * group * rows)
-            value = jnp.dot(turned[lines, :], right[...], preferred_element_type=jnp.float32)
+            value = jnp.dot(turned[lines, :], right_ref[...], preferred_element_type=jnp.float32)
             tile[slot, part * group : (part + 1) * group] = value.astype(tile.dtype).reshape(
                 group, rows, width
             )
 
-    @pl.when(step < per_side)
-    def _():
-        fill(right_a)
-
-    @pl.when((step >= per_side) & (step < 2 * per_side))
-    def _():
-        fill(right_b)
-
-    last = extra_ref.shape[2]
-
-    @pl.when(step == 2 * per_side)
-    def _():
-        tile[slot, :, :, 0:last] = extra_ref[...]
+    last = width
+    if extra_ref is not None:
+        last = extra_ref.shape[2]
+
+        @pl.when(step == full)
+        def _():
+            tile[slot, :, :, 0:last] = extra_ref[...]
 
     for index in range(total):
-        begin = index * width
-        wide = width if index < 2 * per_side else last
-        goal = [i for i, span in enumerate(spans) if span[0] <= begin < span[1]][0]
-        cols = pl.ds(begin - spans[goal][0], wide)
+        wide = width if index < full else last
+        cols = pl.ds(index * width, wide)
 
         @pl.when(step == index)
-        def _(goal=goal, cols=cols, wide=wide):
-            def send(place_in, carry):
-                for side in range(2):
-                    owner = chip ^ chip_offset(
-                        place_in + side * (blocks // 2), orders[goal], True
-                    )
+        def _(cols=cols, wide=wide):
+            def send(spot, carry):
+                for side, out in enumerate((near_ref, far_ref)):
+                    owner = chip ^ chip_offset(spot + side * (blocks // 2), order, True)
                     pltpu.make_async_copy(
                         tile.at[slot, owner, :, pl.ds(0, wide)],
-                        outs[2 * goal + side].at[place_in, :, cols],
+                        out.at[spot, :, cols],
                         sems.at[slot],
                     ).start()
                 return carry
@@ -897,39 +998,40 @@
         sent(slot, last).wait()
 
 
-def packed_map_slopes(place, orders, spans, left_a, right_a, left_b, right_b, extra):
-    depth, channels = left_a.shape
-    hidden = right_a.shape[1]
+def packed_slopes(place, order, lefts, right, extra=None):
+    channels = lefts[0].shape[1]
+    depth, hidden = right.shape
     width = 384
     steps = hidden // width
     rows = channels // CHIPS
-    extra = extra.reshape(CHIPS, rows, extra.shape[1])
-    whole = pl.BlockSpec((depth, channels), lambda i: (0, 0), pipeline_mode=pl.Buffered(1))
+    total, more, specs = hidden, [], []
+    if extra is not None:
+        total += extra.shape[1]
+        more = [extra.reshape(CHIPS, rows, extra.shape[1])]
+        specs = [
+            pl.BlockSpec(more[0].shape, lambda i: (0, 0, 0), pipeline_mode=pl.Buffered(1))
+        ]
+    shape = jax.ShapeDtypeStruct((CHIPS // 2, rows, total), jnp.bfloat16)
     return pl.pallas_call(
-        functools.partial(slope_pack_kernel, orders, spans),
-        grid=(2 * steps + 1,),
-        in_specs=[
-            SCALARS,
-            whole,
-            pl.BlockSpec((depth, width), lambda i: (0, jnp.minimum(i, steps - 1))),
-            whole,
-            pl.BlockSpec((depth, width), lambda i: (0, jnp.clip(i - steps, 0, steps - 1))),
-            pl.BlockSpec(extra.shape, lambda i: (0, 0, 0), pipeline_mode=pl.Buffered(1)),
-        ],
-        out_specs=[pl.BlockSpec(memory_space=pl.ANY)] * (2 * len(spans)),
-        out_shape=[
-            jax.ShapeDtypeStruct((CHIPS // 2, rows, high - low), jnp.bfloat16)
-            for low, high in spans
-            for _ in range(2)
-        ],
+        functools.partial(slope_pack_kernel, order, len(lefts)),
+        grid=(steps + len(more),),
+        in_specs=[SCALARS]
+        + [
+            pl.BlockSpec(left.shape, lambda i: (0, 0), pipeline_mode=pl.Buffered(1))
+            for left in lefts
+        ]
+        + [pl.BlockSpec((depth, width), lambda i: (0, jnp.minimum(i, steps - 1)))]
+        + specs,
+        out_specs=[pl.BlockSpec(memory_space=pl.ANY)] * 2,
+        out_shape=[shape, shape],
         scratch_shapes=[
             pltpu.VMEM((channels, depth), jnp.bfloat16),
             pltpu.VMEM((2, CHIPS, rows, width), jnp.bfloat16),
             pltpu.SemaphoreType.DMA((2,)),
         ],
-        compiler_params=pltpu.CompilerParams(vmem_limit_bytes=40 * 1024 * 1024),
+        compiler_params=pltpu.CompilerParams(vmem_limit_bytes=32 * 1024 * 1024),
         cost_estimate=pl.CostEstimate(flops=0, bytes_accessed=1 << 20, transcendentals=0),
-    )(place, left_a, right_a, left_b, right_b, extra)
+    )(place, *lefts, right, *more)
 
 
 def unpacked_map_slopes(core, blocks, widths):
@@ -1001,15 +1103,19 @@
     extent = jnp.sum(jnp.where(table_ids == group_id, image_sizes, 0))
     first_row = position * high_strip
     map_place = jnp.stack([first_row, extent]).astype(jnp.int32)
-    token_rows = lowres_in.astype(jnp.float32).reshape(token_count, width)
+    token_low = lowres_in.reshape(token_count, width)
     local_grad_low = out_cotangent.reshape(low_strip, grid_side, own_width)
     backs = []
     depth = query_weight.shape[0]
     pickers = [row_picker(device, rotated(i), depth) for i in range(2)]
 
     def convolve(map_low, map_high):
-        backs.extend([map_low, map_high])
-        return [map_conv(map_place, high_map, map_low, map_high, depth_kernel)]
+        convolved = map_conv(map_place, high_map, map_low, map_high, depth_kernel)
+        convolved = convolved.reshape(pixel_count, channels)
+        (normed_low,) = norm([token_low], attn_gain)
+        normed_first = matmul(normed_low, pickers[0]).astype(jnp.bfloat16)
+        backs.extend([map_low, map_high, convolved])
+        return [*norm([convolved], conv_gain), normed_low, normed_first]
 
     small, expand_full, shrink_full, adapter_full, extra = all_weights(
         place,
@@ -1019,14 +1125,10 @@
         list(halo_rows(high_map, RADIUS)),
         convolve,
     )
-    map_low, map_high = backs
-    convolved = extra[0].reshape(pixel_count, channels)
-    normed_map, conv_norm_back = jax.vjp(normalize, convolved, conv_gain.astype(jnp.float32))
-    normed_map_low = normed_map.astype(jnp.bfloat16)
-    normed, attn_norm_back = jax.vjp(normalize, token_rows, attn_gain.astype(jnp.float32))
-    normed_low = normed.astype(jnp.bfloat16)
-    normed_first = matmul(normed_low, pickers[0]).astype(jnp.bfloat16)
-    normed_map_pair = jnp.concatenate([normed_map_low, core_swap(normed_map_low)], axis=0)
+    map_low, map_high, convolved = backs
+    normed_map_low, normed_low, normed_first = extra
+    normed_map_given_low = core_swap(normed_map_low)
+    normed_map_pair = jnp.concatenate([normed_map_low, normed_map_given_low], axis=0)
     triple = 3 * local_width
     quad = 4 * local_width
     hidden_width = up_weight.shape[1]
@@ -1055,27 +1157,30 @@
 
     qkv_rows = into(normed_first, qkv_parts).astype(jnp.bfloat16)
     pair = qkv_rows[:, local_width:]
+    pair_other, expand_full, shrink_full = together([pair_swap(pair), expand_full, shrink_full])
+    pair = jnp.concatenate([pair, pair_other], axis=0)
     pair = jnp.concatenate([pair, core_swap(pair)], axis=0)
-    pair = jnp.concatenate([pair, pair_swap(pair)], axis=0)
     attended_low = attend(qkv_rows, pair)
-    hidden_rows = token_rows + exchange(restored(outof(attended_low, output_parts), 0))
-    normed_two, mlp_norm_back = jax.vjp(normalize, hidden_rows, mlp_gain.astype(jnp.float32))
-    normed_two_low = normed_two.astype(jnp.bfloat16)
+    hidden_own = restored(outof(attended_low, output_parts), 0).astype(jnp.bfloat16)
+    hidden_rows, normed_two_low = norm([token_low, hidden_own, model_swap(hidden_own)], mlp_gain)
     normed_two_picked = [picked(normed_two_low, i) for i in range(2)]
     expanded = jnp.concatenate(
         [into(normed_two_picked[i], up_parts[i]) for i in range(2)], axis=1
     )
     activated_low, activated_slope = gelu_pair(expanded)
     result_own = restored(outof(activated_low, down_parts), 1).astype(jnp.bfloat16)
-    result_rows = (
-        hidden_rows + result_own.astype(jnp.float32) + model_swap(result_own).astype(jnp.float32)
+    result_rows, gating, lifted_grad_low = gate(
+        hidden_rows,
+        result_own,
+        model_swap(result_own),
+        gate_vector,
+        local_grad_low.reshape(token_count, own_width),
     )
 
     result_grid = result_rows.reshape(low_strip, grid_side, width)
     gate_wide = gate_vector.astype(jnp.float32)
-    gating = jax.nn.sigmoid(jnp.sum(result_grid * gate_wide, axis=-1, keepdims=True))
+    gating = gating[:, :1].reshape(low_strip, grid_side, 1)
     out_grad = local_grad_low.astype(jnp.float32)
-    lifted_grad_low = (out_grad * gating).reshape(token_count, own_width).astype(jnp.bfloat16)
     grid_shape = (low_strip, grid_side, channels)
     pooled_own = matmul_nt(lifted_grad_low, adapter_full).astype(jnp.bfloat16).reshape(grid_shape)
     pooled_other = model_swap(pooled_own)
@@ -1083,7 +1188,7 @@
     widened = matmul(normed_map_pair, expand_full)
     widened_low, widened_slope = gelu_pair(widened)
     widened_low = after(widened_low, pooled_own)
-    narrowed_part, narrowed_given = dense(widened_low, shrink_full, True, halves=True)
+    narrowed_part, narrowed_given = dense([widened_low], shrink_full, True, halves=True)
     narrowed_part = narrowed_part + core_swap(narrowed_given).astype(jnp.float32)
     map_shape = (high_strip, high_side, channels)
     narrowed_own = narrowed_part.astype(jnp.bfloat16).reshape(map_shape)
@@ -1094,9 +1199,9 @@
         map_place, pooled_own, pooled_other, map_cotangent.reshape(map_shape), layer_scale[None]
     )
     narrowed_grad_low = narrowed_grad_low.reshape(pixel_count, channels)
-    narrowed_grad_pair = jnp.concatenate([narrowed_grad_low, core_swap(narrowed_grad_low)], axis=0)
+    narrowed_grad_pair = [narrowed_grad_low, core_swap(narrowed_grad_low)]
     (widened_grad_low,) = dense(narrowed_grad_pair, shrink_full, False, widened_slope)
-    normed_map_part, normed_map_given = dense(widened_grad_low, expand_full, True, halves=True)
+    normed_map_part, normed_map_given = dense([widened_grad_low], expand_full, True, halves=True)
     normed_map_given, narrowed_other = together([normed_map_given, narrowed_other])
     normed_map_part = normed_map_part + core_swap(normed_map_given).astype(jnp.float32)
     normed_map_own = normed_map_part.astype(jnp.bfloat16)
@@ -1141,42 +1246,49 @@
             (normed_two_picked[1], result_picked), (expanded_grad_parts[1], activated_low)
         )
     )
-    second_far = core_swap(second_slopes[1])
     normed_two_own = sum(
         restored(outof(expanded_grad_parts[i], up_parts[i]), i) for i in range(2)
     ).astype(jnp.bfloat16)
     normed_two_other = model_swap(normed_two_own)
-    normed_two_other, normed_map_own = together([normed_two_other, normed_map_own])
+    normed_two_other, normed_map_own, *second_slopes = together(
+        [normed_two_other, normed_map_own, *second_slopes]
+    )
+    second_far = core_swap(second_slopes[1])
     normed_map_other = model_swap(normed_map_own)
-    normed_two_grad = normed_two_own.astype(jnp.float32) + normed_two_other.astype(jnp.float32)
-    hidden_part, mlp_gain_slope = mlp_norm_back(normed_two_grad)
-    hidden_grad = result_grad + hidden_part
-    hidden_low = hidden_grad.astype(jnp.bfloat16)
+    mlp_gain_slope, hidden_grad, hidden_low = norm_back(
+        hidden_rows,
+        normed_two_own,
+        normed_two_other,
+        mlp_gain,
+        (jnp.float32, jnp.bfloat16),
+        result_grad,
+    )
     hidden_picked = picked(hidden_low, 0)
     attended_grad_low = into(hidden_picked, output_parts).astype(jnp.bfloat16)
     query_grad_rows, key_grad_all, value_grad_all = attend_back(qkv_rows, pair, attended_grad_low)
     pair_back = jnp.concatenate(
         [key_grad_all, value_grad_all], axis=1
     )
-    pair_other = pair_swap(pair_back[2 * token_count :].astype(jnp.bfloat16))
-    map_widths = (widened_low.shape[1], widened_low.shape[1], adapter_slope.shape[1])
-    map_slopes_packed = packed_map_slopes(
-        after(place, attended_grad_low),
-        [rotated(i) for i in range(2, 5)],
-        even_edges(sum(map_widths), 3),
-        normed_map_pair,
+    pair_back = pair_back[: 2 * token_count] + core_swap(
+        pair_back[2 * token_count :].astype(jnp.bfloat16)
+    ).astype(jnp.float32)
+    pair_given, late_place = together([pair_back[token_count:].astype(jnp.bfloat16), place])
+    pair_other = pair_swap(pair_given)
+    shrink_packed = packed_slopes(late_place, rotated(3), narrowed_grad_pair, widened_low)
+    expand_packed = packed_slopes(
+        late_place,
+        rotated(2),
+        [normed_map_low, normed_map_given_low],
         widened_grad_low,
-        narrowed_grad_pair,
-        widened_low,
         adapter_slope.astype(jnp.bfloat16),
     )
-    pair_other, normed_map_other, *map_slopes_packed = together(
-        [pair_other, normed_map_other, *map_slopes_packed]
-    )
-    pair_back = pair_back[: 2 * token_count] + pair_other.astype(jnp.float32)
-    pair_back = pair_back[:token_count] + core_swap(
-        pair_back[token_count:].astype(jnp.bfloat16)
-    ).astype(jnp.float32)
+    map_slopes_packed = [*expand_packed, *shrink_packed]
+    second_near = split_sum(second_slopes[0], second_far)
+    pair_other, normed_map_other, *rest = together(
+        [pair_other, normed_map_other, *second_near, *map_slopes_packed]
+    )
+    second_near, map_slopes_packed = rest[:2], rest[2:]
+    pair_back = pair_back[:token_count] + pair_other.astype(jnp.float32)
     qkv_grad = jnp.concatenate([query_grad_rows, pair_back.astype(jnp.bfloat16)], axis=1)
     normed_own = restored(outof(qkv_grad, qkv_parts), 0).astype(jnp.bfloat16)
     normed_other = model_swap(normed_own)
@@ -1187,30 +1299,29 @@
         )
     )
     first_far = core_swap(first_slopes[1])
-    normed_map_grad = normed_map_own.astype(jnp.float32) + normed_map_other.astype(jnp.float32)
-    convolved_grad, conv_gain_slope = conv_norm_back(normed_map_grad)
-    convolved_grad_low = convolved_grad.reshape(map_shape).astype(jnp.bfloat16)
+    conv_gain_slope, convolved_grad_low = norm_back(
+        convolved, normed_map_own, normed_map_other, conv_gain, (jnp.bfloat16,)
+    )
+    convolved_grad_low = convolved_grad_low.reshape(map_shape)
     grad_low, grad_high = halo_rows(convolved_grad_low, RADIUS)
     grad_low, grad_high, *map_slopes_packed = together(
         [grad_low, grad_high, *map_slopes_packed]
     )
-    near = [
-        split_sum(pair[0], part)
-        for pair, part in ((first_slopes, first_far), (second_slopes, second_far))
-    ]
+    near = [split_sum(first_slopes[0], first_far), second_near]
     scatter = Scatter(
         [low for low, _ in near] + list(map_slopes_packed[0::2]),
         [high for _, high in near] + list(map_slopes_packed[1::2]),
-        [rotated(i)[::-1] for i in range(5)],
+        [rotated(i)[::-1] for i in range(4)],
     )
 
     depth_kernel_slope = map_slopes(map_place, high_map, map_low, map_high, convolved_grad_low)
     highres_grad = map_conv(
         map_place, convolved_grad_low, grad_low, grad_high, depth_kernel, map_grad
     )
-    normed_grad = normed_own.astype(jnp.float32) + normed_other.astype(jnp.float32)
-    input_part, attn_gain_slope = attn_norm_back(normed_grad)
-    lowres_grad = (hidden_grad + input_part).reshape(low_strip, 1, grid_side, width)
+    attn_gain_slope, lowres_grad = norm_back(
+        token_low, normed_own, normed_other, attn_gain, (jnp.float32,), hidden_grad
+    )
+    lowres_grad = lowres_grad.reshape(low_strip, 1, grid_side, width)
 
     def as_rows(values):
         return jnp.pad(values, ((0, 0), (0, channels - values.shape[1])))
@@ -1218,9 +1329,11 @@
     minor_rows = jnp.concatenate(
         [
             depth_kernel_slope,
-            conv_gain_slope[None],
+            conv_gain_slope,
             layer_scale_slope,
-            as_rows(jnp.stack([attn_gain_slope, mlp_gain_slope, gate_vector_slope], 0)),
+            as_rows(
+                jnp.concatenate([attn_gain_slope, mlp_gain_slope, gate_vector_slope[None]], axis=0)
+            ),
             as_rows(adapter_kernel_slope),
         ],
         axis=0,
@@ -1244,10 +1357,10 @@
     first_own, second_own, *map_blocks = scatter.result()
     up_own = jnp.concatenate([first_own[:, quad:], second_own[:, :hidden_half]], axis=1)
     down_own = second_own[:, hidden_half:]
-    expand_own, shrink_own, adapter_own = unpacked_map_slopes(
+    expand_own, adapter_own, shrink_own = unpacked_map_slopes(
         core,
         map_blocks,
-        map_widths,
+        (widened_low.shape[1], adapter_slope.shape[1], widened_low.shape[1]),
     )
     firsts = [first_own[:, i * local_width : (i + 1) * local_width] for i in range(4)]
     taps = depth_kernel.shape[0]

time: 596 us -> 557 us (0.935)
  other arithmetic: 83 us -> 52.6 us
  Pallas kernels: 136 us -> 156 us
  matrix products: 52.7 us -> 39.1 us
  local copies, waits for them, and re-layouts: 64.3 us -> 52.2 us
  starting transfers between devices: 107 us -> 101 us
    ppermute x64 -> x59, waiting for transfers between devices: 49.9 us -> 62 us  [xor_swap(): return lax.ppermute(values, 'dp', [(i, i ^ mask) for i in range(count)])]
    ppermute x9, waiting for transfers between devices: 22.8 us -> 34.9 us  [model_swap(): return lax.ppermute(values, 'mp', [(0, 1), (1, 0)])]
    ppermute x3, waiting for transfers between devices: 16 us -> 4.75 us  [halo_rows(): low = lax.ppermute(block[block.shape[0] - width:], 'dp', forward)]
    reduce_sum x14 -> x0, other arithmetic: 10.9 us -> none  [the longest x4 3.64 us: normalize(): return centred * lax.rsqrt(spread + norm_epsilon) * scale_gain]
    pallas_call x1 -> x9, Pallas kernels: 26.6 us -> 36.3 us  [the longest x2 28.6 us: packed_slopes(): pl.pallas_call(functools.partial(slope_pack_kernel, order, len(lefts)), g...]
    dot_general x17, matrix products: 32.2 us -> 22.6 us  [matmul(): return jnp.dot(former, latter, preferred_element_type=jnp.float32)]
    ppermute x2, waiting for transfers between devices: 10.5 us -> 1.22 us  [pair_swap(): return lax.ppermute(values, 'dp', pairs)]
    pallas_call x3, Pallas kernels: 26.6 us -> 34.3 us  [dense(): pl.pallas_call(functools.partial(dense_kernel, flipped, scale is not None...]
  transfers between devices with their start and end apart: 81 -> 76, of which waited for: 26 -> 34; matrix products, arithmetic and copies ran while one was open for 26% -> 19% of each run, Pallas kernels for 21% -> 25%
where the time goes in v3:
time: 557 us; the launch traced here: 548 us
  Pallas kernels  156 us (28%)
  waiting for transfers between devices  105 us (19%)
  starting transfers between devices  101 us (18%)
  other arithmetic  52.6 us (9%)
  local copies, waits for them, and re-layouts  52.2 us (9%)
  matrix products  39.1 us (7%)
  blocking collectives  38.1 us (7%)
    ppermute x59, waiting for transfers between devices, xor_swap(): return lax.ppermute(values, 'dp', [(i, i ^ mask) for i in range(count)])  62 us
    ppermute x59, starting transfers between devices, xor_swap(): return lax.ppermute(values, 'dp', [(i, i ^ mask) for i in range(count)])  58 us
    ppermute x9, waiting for transfers between devices, model_swap(): return lax.ppermute(values, 'mp', [(0, 1), (1, 0)])  34.9 us
    unnamed x270, local copies, waits for them, and re-layouts  34.6 us
    pallas_call x3, Pallas kernels, dense(): pl.pallas_call(functools.partial(dense_kernel, flipped, scale is not None...  34.3 us
    pallas_call x2, Pallas kernels, map_conv(): pl.pallas_call(forward_kernel if added is None else backward_kernel, grid...  32.3 us
    pallas_call x2, Pallas kernels, packed_slopes(): pl.pallas_call(functools.partial(slope_pack_kernel, order, len(lefts)), g...  28.6 us
    add x18, other arithmetic, split_sum(): return (kept[:half] + other[:half], kept[half:] + other[half:])  24.1 us
  transfers between devices with their start and end apart: 76, of which 34 were waited for; matrix products, arithmetic and copies ran while one was open for 19% of the time, Pallas kernels for 25%

profile of v3, /device:TPU:1, one launch (start us, length us, event | category | flops | bytes accessed | tf_op | source)
XLA Modules:
  0.0 547.6 jit_solution(2469009880079085330)
XLA Ops:
  5.2 3.3 collective-permute-start.1
  12.2 4.3 collective-permute-done
  18.3 2.8 collective-permute-start.4
  21.2 2.1 collective-permute-done.4
  27.0 2.6 collective-permute-done.7
  29.7 2.7 collective-permute-done.6
  36.5 4.4 collective-permute-done.12
  46.5 11.3 %collective-permute-start.21 = (bf16[3,48,1536]{2,1,0:T(8,128)(2,1)S(1)}, bf16[3,48,1536]{2,1,0:T(8,128)(2,1)S(1)}, u32[]{:S(2)}, u32[]{:S(2)}) collective-permute-start(bf16[3,48,1536]{2,1,0:T(8,128)(2,1)S(1)} %get-tuple-element.323), channel_id=1, source_target_pairs={{0,2},{2,4},{4,6},{6,8},{8,10},{10,12},{12,14},{14,16},{16,18},{18... | collective-permute-start | bytes 1327112 | tf_op jit(solution)/shard_map/ppermute | solution.py:801
  61.2 9.1 %collective-permute-start.22 = (bf16[3,48,1536]{2,1,0:T(8,128)(2,1)S(1)}, bf16[3,48,1536]{2,1,0:T(8,128)(2,1)S(1)}, u32[]{:S(2)}, u32[]{:S(2)}) collective-permute-start(bf16[3,48,1536]{2,1,0:T(8,128)(2,1)S(1)} %get-tuple-element.322), channel_id=1, source_target_pairs={{2,0},{4,2},{6,4},{8,6},{10,8},{12,10},{14,12},{16,14},{18,16},{20... | collective-permute-start | bytes 1327112 | tf_op jit(solution)/shard_map/ppermute | solution.py:802
  73.0 9.8 %collective-permute-done.19 = bf16[8,48,1152]{2,1,0:T(8,128)(2,1)S(1)} collective-permute-done((bf16[8,48,1152]{2,1,0:T(8,128)(2,1)S(1)}, bf16[8,48,1152]{2,1,0:T(8,128)(2,1)S(1)}, u32[]{:S(2)}, u32[]{:S(2)}) %collective-permute-start.19) | collective-permute-done | bytes 884768 | tf_op jit(solution)/shard_map/ppermute | solution.py:670
  97.2 15.6 %shard_map.356 = f32[12,48,1536]{2,1,0:T(8,128)S(1)} custom-call(s32[2]{0:T(128)S(1)} %pad_add_fusion.place, bf16[12,48,1536]{2,1,0:T(8,128)(2,1)S(1)} %bitcast.127, bf16[3,48,1536]{2,1,0:T(8,128)(2,1)S(1)} %copy-done.35, bf16[3,48,1536]{2,1,0:T(8,128)(2,1)S(1)} %copy-done.38, bf16[49,1536]{1,0:T(8,128)(2,1)S(1)} %copy-done.53), custom_call_target="tpu_custom_call" | custom-call | bytes 110592 | tf_op jit(solution)/shard_map/pallas_call | solution.py:142
  114.1 2.2 constant_dynamic-update-slice_fusion.6
  116.3 6.7 %collective-permute-done.23 = bf16[16,16,3072]{2,1,0:T(8,128)(2,1)} collective-permute-done((bf16[16,16,3072]{2,1,0:T(8,128)(2,1)}, bf16[16,16,3072]{2,1,0:T(8,128)(2,1)}, u32[]{:S(2)}, u32[]{:S(2)}) %collective-permute-start.23) | collective-permute-done | bytes 1572896 | tf_op jit(solution)/shard_map/ppermute | solution.py:670
  123.0 2.5 collective-permute-done.24
  125.6 3.4 collective-permute-done.27.refs_5_
  133.1 3.5 collective-permute-done.28
  137.4 2.2 collective-permute-start.29
  141.9 4.6 shard_map.359
  146.6 2.2 copy-done.8
  153.0 4.5 shard_map.360.refs_4_
  159.2 3.4 collective-permute-start.31
  163.9 5.7 %collective-permute-done.31.refs_2_ = bf16[144,1024]{1,0:T(8,128)(2,1)S(1)} collective-permute-done((bf16[144,1024]{1,0:T(8,128)(2,1)S(1)}, bf16[144,1024]{1,0:T(8,128)(2,1)S(1)}, u32[]{:S(2)}, u32[]{:S(2)}) %collective-permute-start.31) | collective-permute-done | bytes 294944 | tf_op jit(solution)/shard_map/ppermute | solution.py:788
  176.9 2.7 collective-permute-start.33
  179.6 10.5 %fusion.4 = (bf16[1152,1536]{1,0:T(8,128)(2,1)}, bf16[1152,1536]{1,0:T(8,128)(2,1)}) fusion(bf16[1536,1536]{1,0:T(8,128)(2,1)S(1)} %bitcast.134, bf16[576,1536]{1,0:T(8,128)(2,1)S(1)} %collective-permute-done.35.refs_1_, bf16[576,1536]{1,0:T(8,128)(2,1)S(1)} %shard_map.357.refs_0_), kind=kOutput, calls=%fused_computation.5 | convolution fusion | flops 5462360064 | bytes 15335424 | tf_op jit(solution)/shard_map/dot_general | solution.py:813
  191.6 12.4 %shard_map.363 = (f32[576,1536]{1,0:T(8,128)S(1)}, bf16[576,1536]{1,0:T(8,128)(2,1)S(1)}) custom-call(bf16[1152,1536]{1,0:T(8,128)(2,1)} %get-tuple-element.178.refs_0_.refs_2_, bf16[1536,1536]{1,0:T(8,128)(2,1)} %bitcast.130), custom_call_target="tpu_custom_call" | custom-call | bytes 1048576 | tf_op jit(solution)/shard_map/pallas_call | solution.py:489
  205.7 3.2 collective-permute-done.36
  210.8 8.2 %collective-permute-done.37.pool_other_ref = bf16[6,24,1536]{2,1,0:T(8,128)(2,1)S(1)} collective-permute-done((bf16[6,24,1536]{2,1,0:T(8,128)(2,1)S(1)}, bf16[6,24,1536]{2,1,0:T(8,128)(2,1)S(1)}, u32[]{:S(2)}, u32[]{:S(2)}) %collective-permute-start.37) | collective-permute-done | bytes 442400 | tf_op jit(solution)/shard_map/ppermute | solution.py:788
  219.0 3.8 shard_map.364
  229.3 9.3 %shard_map.365.refs_0_.refs_2_ = bf16[1152,1536]{1,0:T(8,128)(2,1)S(1)} custom-call(bf16[576,1536]{1,0:T(8,128)(2,1)} %bitcast.32.refs_0_, bf16[576,1536]{1,0:T(8,128)(2,1)} %collective-permute-done.38.refs_1_, bf16[1536,1536]{1,0:T(8,128)(2,1)} %bitcast.131, bf16[1152,1536]{1,0:T(8,128)(2,1)} %get-tuple-element.300.refs_3_), custom_call_target="tpu_custom_call" | custom-call | bytes 1048576 | tf_op jit(solution)/shard_map/pallas_call | solution.py:489
  243.6 12.6 %shard_map.367 = (f32[576,1536]{1,0:T(8,128)S(1)}, bf16[576,1536]{1,0:T(8,128)(2,1)S(1)}) custom-call(bf16[1152,1536]{1,0:T(8,128)(2,1)} %copy-done, bf16[1536,1536]{1,0:T(8,128)(2,1)} %bitcast.135), custom_call_target="tpu_custom_call" | custom-call | bytes 1048576 | tf_op jit(solution)/shard_map/pallas_call | solution.py:489
  259.2 8.8 %collective-permute-done.41.other_ref = bf16[12,48,1536]{2,1,0:T(8,128)(2,1)} collective-permute-done((bf16[12,48,1536]{2,1,0:T(8,128)(2,1)}, bf16[12,48,1536]{2,1,0:T(8,128)(2,1)}, u32[]{:S(2)}, u32[]{:S(2)}) %collective-permute-start.41) | collective-permute-done | bytes 1769504 | tf_op jit(solution)/shard_map/ppermute | solution.py:788
  268.2 5.4 shard_map.368
  278.9 3.0 collective-permute-start.42
  283.9 2.2 collective-permute-done.42
  286.2 2.3 multiply_add_fusion
  290.6 2.5 fusion.20
  293.2 4.8 shard_map.369
  303.4 3.1 collective-permute-start.44
  306.4 2.1 add_convert_fusion.own_ref
  308.5 4.2 collective-permute-done.44.other_ref
  318.2 7.0 %shard_map.371 = (bf16[144,512]{1,0:T(8,128)(2,1)S(1)}, f32[576,512]{1,0:T(8,128)S(1)}, f32[576,512]{1,0:T(8,128)S(1)}) custom-call(bf16[144,1536]{1,0:T(8,128)(2,1)S(1)} %copy-done.19, bf16[576,1024]{1,0:T(8,128)(2,1)S(1)} %copy-done.3, bf16[576,1024]{1,0:T(8,128)(2,1)S(1)} %copy-done.3, bf16[144,512]{1,0:T(8,128)(2,1)S(1)} %fusion.63.grad_ref), custom_call_target="tpu_custom_call" | custom-call | bytes 1048576 | tf_op jit(solution)/shard_map/pallas_call | solution.py:373
  325.2 3.0 collective-permute-start.48
  332.8 15.0 %shard_map.373 = (bf16[16,48,1536]{2,1,0:T(8,128)(2,1)S(1)}, bf16[16,48,1536]{2,1,0:T(8,128)(2,1)}) custom-call(s32[1]{0:T(128)} %bitcast.19.place, bf16[576,1536]{1,0:T(8,128)(2,1)} %bitcast.32.refs_0_, bf16[576,1536]{1,0:T(8,128)(2,1)} %collective-permute-done.38.refs_1_, bf16[1152,1536]{1,0:T(8,128)(2,1)S(1)} %copy-done.9), custom_call_target="tpu_custom_call" | custom-call | bytes 1048576 | tf_op jit(solution)/shard_map/pallas_call | solution.py:1015
  349.3 13.5 %shard_map.372 = (bf16[16,48,1792]{2,1,0:T(8,128)(2,1)S(1)}, bf16[16,48,1792]{2,1,0:T(8,128)(2,1)}) custom-call(s32[1]{0:T(128)} %bitcast.19.place, bf16[576,1536]{1,0:T(8,128)(2,1)S(1)} %copy-done.17, bf16[576,1536]{1,0:T(8,128)(2,1)S(1)} %copy-done.42, bf16[1152,1536]{1,0:T(8,128)(2,1)S(1)} %copy-done.1, bf16[32,48,256]{2,1,0:T(8,128)(2,1)S(1)} %bitcast.137), custom_call_target="tpu_custom_call" | custom-call | bytes 1048576 | tf_op jit(solution)/shard_map/pallas_call | solution.py:1015
  362.8 4.8 slice_add_fusion.2
  367.7 5.7 %collective-permute-done.48.other_ref = bf16[576,1536]{1,0:T(8,128)(2,1)S(1)} collective-permute-done((bf16[576,1536]{1,0:T(8,128)(2,1)S(1)}, bf16[576,1536]{1,0:T(8,128)(2,1)S(1)}, u32[]{:S(2)}, u32[]{:S(2)}) %collective-permute-start.48) | collective-permute-done | bytes 1769504 | tf_op jit(solution)/shard_map/ppermute | solution.py:788
  374.2 3.8 shard_map.375
  378.8 2.8 shard_map.376
  383.4 4.7 collective-permute-done.55.low_ref
  398.6 2.2 fusion.73
  402.5 2.7 collective-permute-start.51
  405.3 18.0 %shard_map.377 = f32[49,1536]{1,0:T(8,128)S(1)} custom-call(s32[2]{0:T(128)S(1)} %copy-done.82, bf16[12,48,1536]{2,1,0:T(8,128)(2,1)S(1)} %bitcast.129, bf16[3,48,1536]{2,1,0:T(8,128)(2,1)S(1)} %copy-done.36, bf16[3,48,1536]{2,1,0:T(8,128)(2,1)S(1)} %copy-done.39, bf16[12,48,1536]{2,1,0:T(8,128)(2,1)S(1)} %bitcast.132), custom_call_target="tpu_custom_call" | custom-call | bytes 110592 | tf_op jit(solution)/shard_map/pallas_call | solution.py:162
  431.2 16.7 %shard_map.378 = f32[12,48,1536]{2,1,0:T(8,128)} custom-call(s32[2]{0:T(128)S(1)} %copy-done.82, bf16[12,48,1536]{2,1,0:T(8,128)(2,1)S(1)} %bitcast.133, bf16[3,48,1536]{2,1,0:T(8,128)(2,1)S(1)} %copy-done.64, bf16[3,48,1536]{2,1,0:T(8,128)(2,1)S(1)} %copy-done.66, bf16[49,1536]{1,0:T(8,128)(2,1)S(1)} %copy-done.54, f32[12,48,1536]{2,1,0:T(8,128)S(1)} %copy-done.12), custom_call_target="tpu_custom_call" | custom-call | bytes 110592 | tf_op jit(solution)/shard_map/pallas_call | solution.py:142
  449.5 3.1 slice_add_fusion.7
  452.6 3.4 collective-permute-start.62
  456.0 3.3 slice_add_fusion.4
  459.2 2.6 slice_add_fusion.11
  462.5 2.8 slice_add_fusion.9
  465.3 7.4 %collective-permute-start.59 = (bf16[8,16,3072]{2,1,0:T(8,128)(2,1)}, bf16[8,16,3072]{2,1,0:T(8,128)(2,1)}, u32[]{:S(2)}, u32[]{:S(2)}) collective-permute-start(bf16[8,16,3072]{2,1,0:T(8,128)(2,1)} %get-tuple-element.310), channel_id=1, source_target_pairs={{0,48},{2,50},{4,52},{6,54},{8,56},{10,58},{12,60},{14,62},{16,32}... | collective-permute-start | bytes 2359304 | tf_op jit(solution)/shard_map/ppermute | solution.py:670
  472.8 2.4 shard_map.374
  477.6 19.8 %all_to_all.10 = bf16[64,16,128]{2,1,0:T(8,128)(2,1)} all-to-all(bf16[64,16,128]{2,1,0:T(8,128)(2,1)S(1)} %pad.16), channel_id=1, replica_groups=mesh['dp'=64,'mp'=2] {'dp'}, dimensions={0} | all-to-all | bytes 524288 | tf_op jit(solution)/shard_map/all_to_all | solution.py:1053
  505.2 18.2 %all_to_all.11 = bf16[64,16,128]{2,1,0:T(8,128)(2,1)S(1)} all-to-all(bf16[64,16,128]{2,1,0:T(8,128)(2,1)S(1)} %broadcast_in_dim.76), channel_id=1, replica_groups=mesh['dp'=64,'mp'=2] {'dp'}, dimensions={0} | all-to-all | bytes 524288 | tf_op jit(solution)/shard_map/all_to_all | solution.py:1059
  526.8 3.0 collective-permute-done.68
  541.3 3.6 collective-permute-start.75
  (541 shorter events, 164.7 us)
Async XLA Ops:
  5.2 7.0 %collective-permute-start.1 = (bf16[1,16,3072]{2,1,0:T(8,128)(2,1)S(1)}, bf16[1,16,3072]{2,1,0:T(8,128)(2,1)S(1)}, u32[]{:S(2)}, u32[]{:S(2)}) collective-permute-start(bf16[1,16,3072]{2,1,0:T(8,128)(2,1)S(1)} %maximum_bitcast_fusion), channel_id=1, source_target_pairs={{0,12},{2,14},{4,8},{6,10},{8,4},{10,6},{12,0},{14,2},{16,28},{18,... | collective-permute-start | bytes 294920 | tf_op jit(solution)/shard_map/ppermute | solution.py:670
  11.1 5.4 collective-permute-start.2
  18.3 5.0 collective-permute-start.4
  25.2 7.3 %collective-permute-start.10 = (bf16[2,48,1024]{2,1,0:T(8,128)(2,1)S(1)}, bf16[2,48,1024]{2,1,0:T(8,128)(2,1)S(1)}, u32[]{:S(2)}, u32[]{:S(2)}) collective-permute-start(bf16[2,48,1024]{2,1,0:T(8,128)(2,1)S(1)} %pad_maximum_fusion.25), channel_id=1, source_target_pairs={{0,4},{2,6},{4,0},{6,2},{8,12},{10,14},{12,8},{14,10},{16,20},{18,... | collective-permute-start | bytes 589832 | tf_op jit(solution)/shard_map/ppermute | solution.py:670
  25.3 7.2 %collective-permute-start.9 = (bf16[2,48,1152]{2,1,0:T(8,128)(2,1)S(1)}, bf16[2,48,1152]{2,1,0:T(8,128)(2,1)S(1)}, u32[]{:S(2)}, u32[]{:S(2)}) collective-permute-start(bf16[2,48,1152]{2,1,0:T(8,128)(2,1)S(1)} %pad_maximum_fusion.22), channel_id=1, source_target_pairs={{0,64},{2,66},{4,68},{6,70},{8,72},{10,74},{12,76},{14,78},{16,80}... | collective-permute-start | bytes 663560 | tf_op jit(solution)/shard_map/ppermute | solution.py:670
  25.4 7.2 %collective-permute-start.8 = (bf16[2,48,1152]{2,1,0:T(8,128)(2,1)S(1)}, bf16[2,48,1152]{2,1,0:T(8,128)(2,1)S(1)}, u32[]{:S(2)}, u32[]{:S(2)}) collective-permute-start(bf16[2,48,1152]{2,1,0:T(8,128)(2,1)S(1)} %pad_maximum_fusion.21), channel_id=1, source_target_pairs={{0,48},{2,50},{4,52},{6,54},{8,56},{10,58},{12,60},{14,62},{16,32}... | collective-permute-start | bytes 663560 | tf_op jit(solution)/shard_map/ppermute | solution.py:670
  26.4 6.0 %collective-permute-start.6 = (bf16[2,16,3072]{2,1,0:T(8,128)(2,1)S(1)}, bf16[2,16,3072]{2,1,0:T(8,128)(2,1)S(1)}, u32[]{:S(2)}, u32[]{:S(2)}) collective-permute-start(bf16[2,16,3072]{2,1,0:T(8,128)(2,1)S(1)} %pad_maximum_fusion.23), channel_id=1, source_target_pairs={{0,12},{2,14},{4,8},{6,10},{8,4},{10,6},{12,0},{14,2},{16,28},{18,... | collective-permute-start | bytes 589832 | tf_op jit(solution)/shard_map/ppermute | solution.py:670
  32.6 8.3 %collective-permute-start.12 = (bf16[4,16,3072]{2,1,0:T(8,128)(2,1)S(1)}, bf16[4,16,3072]{2,1,0:T(8,128)(2,1)S(1)}, u32[]{:S(2)}, u32[]{:S(2)}) collective-permute-start(bf16[4,16,3072]{2,1,0:T(8,128)(2,1)S(1)} %pad_maximum_fusion.17), channel_id=1, source_target_pairs={{0,48},{2,50},{4,52},{6,54},{8,56},{10,58},{12,60},{14,62},{16,32}... | collective-permute-start | bytes 1179656 | tf_op jit(solution)/shard_map/ppermute | solution.py:670
  34.4 6.9 %collective-permute-start.11 = (bf16[4,16,3072]{2,1,0:T(8,128)(2,1)S(1)}, bf16[4,16,3072]{2,1,0:T(8,128)(2,1)S(1)}, u32[]{:S(2)}, u32[]{:S(2)}) collective-permute-start(bf16[4,16,3072]{2,1,0:T(8,128)(2,1)S(1)} %pad_maximum_fusion.16), channel_id=1, source_target_pairs={{0,16},{2,18},{4,20},{6,22},{8,24},{10,26},{12,28},{14,30},{16,0},... | collective-permute-start | bytes 1179656 | tf_op jit(solution)/shard_map/ppermute | solution.py:670
  34.4 8.1 %collective-permute-start.15 = (bf16[4,48,1024]{2,1,0:T(8,128)(2,1)S(1)}, bf16[4,48,1024]{2,1,0:T(8,128)(2,1)S(1)}, u32[]{:S(2)}, u32[]{:S(2)}) collective-permute-start(bf16[4,48,1024]{2,1,0:T(8,128)(2,1)S(1)} %pad_maximum_fusion.18), channel_id=1, source_target_pairs={{0,12},{2,14},{4,8},{6,10},{8,4},{10,6},{12,0},{14,2},{16,28},{18,... | collective-permute-start | bytes 1179656 | tf_op jit(solution)/shard_map/ppermute | solution.py:670
  35.1 7.6 %collective-permute-start.14 = (bf16[4,48,1152]{2,1,0:T(8,128)(2,1)S(1)}, bf16[4,48,1152]{2,1,0:T(8,128)(2,1)S(1)}, u32[]{:S(2)}, u32[]{:S(2)}) collective-permute-start(bf16[4,48,1152]{2,1,0:T(8,128)(2,1)S(1)} %pad_maximum_fusion.14), channel_id=1, source_target_pairs={{0,4},{2,6},{4,0},{6,2},{8,12},{10,14},{12,8},{14,10},{16,20},{18,... | collective-permute-start | bytes 1327112 | tf_op jit(solution)/shard_map/ppermute | solution.py:670
  35.1 7.7 %collective-permute-start.13 = (bf16[4,48,1152]{2,1,0:T(8,128)(2,1)S(1)}, bf16[4,48,1152]{2,1,0:T(8,128)(2,1)S(1)}, u32[]{:S(2)}, u32[]{:S(2)}) collective-permute-start(bf16[4,48,1152]{2,1,0:T(8,128)(2,1)S(1)} %pad_maximum_fusion.13), channel_id=1, source_target_pairs={{0,64},{2,66},{4,68},{6,70},{8,72},{10,74},{12,76},{14,78},{16,80}... | collective-permute-start | bytes 1327112 | tf_op jit(solution)/shard_map/ppermute | solution.py:670
  42.9 15.7 %collective-permute-start.17 = (bf16[8,16,3072]{2,1,0:T(8,128)(2,1)S(1)}, bf16[8,16,3072]{2,1,0:T(8,128)(2,1)S(1)}, u32[]{:S(2)}, u32[]{:S(2)}) collective-permute-start(bf16[8,16,3072]{2,1,0:T(8,128)(2,1)S(1)} %pad_maximum_fusion.10), channel_id=1, source_target_pairs={{0,64},{2,66},{4,68},{6,70},{8,72},{10,74},{12,76},{14,78},{16,80}... | collective-permute-start | bytes 2359304 | tf_op jit(solution)/shard_map/ppermute | solution.py:670
  44.3 16.9 %collective-permute-start.20 = (bf16[8,48,1024]{2,1,0:T(8,128)(2,1)S(1)}, bf16[8,48,1024]{2,1,0:T(8,128)(2,1)S(1)}, u32[]{:S(2)}, u32[]{:S(2)}) collective-permute-start(bf16[8,48,1024]{2,1,0:T(8,128)(2,1)S(1)} %pad_maximum_fusion.11), channel_id=1, source_target_pairs={{0,16},{2,18},{4,20},{6,22},{8,24},{10,26},{12,28},{14,30},{16,0},... | collective-permute-start | bytes 2359304 | tf_op jit(solution)/shard_map/ppermute | solution.py:670
  45.7 25.8 %collective-permute-start.16 = (bf16[8,16,3072]{2,1,0:T(8,128)(2,1)S(1)}, bf16[8,16,3072]{2,1,0:T(8,128)(2,1)S(1)}, u32[]{:S(2)}, u32[]{:S(2)}) collective-permute-start(bf16[8,16,3072]{2,1,0:T(8,128)(2,1)S(1)} %pad_maximum_fusion.9), channel_id=1, source_target_pairs={{0,48},{2,50},{4,52},{6,54},{8,56},{10,58},{12,60},{14,62},{16,32}... | collective-permute-start | bytes 2359304 | tf_op jit(solution)/shard_map/ppermute | solution.py:670
  46.5 39.1 %collective-permute-start.21 = (bf16[3,48,1536]{2,1,0:T(8,128)(2,1)S(1)}, bf16[3,48,1536]{2,1,0:T(8,128)(2,1)S(1)}, u32[]{:S(2)}, u32[]{:S(2)}) collective-permute-start(bf16[3,48,1536]{2,1,0:T(8,128)(2,1)S(1)} %get-tuple-element.323), channel_id=1, source_target_pairs={{0,2},{2,4},{4,6},{6,8},{8,10},{10,12},{12,14},{14,16},{16,18},{18... | collective-permute-start | bytes 1327112 | tf_op jit(solution)/shard_map/ppermute | solution.py:801
  57.8 25.0 %collective-permute-start.19 = (bf16[8,48,1152]{2,1,0:T(8,128)(2,1)S(1)}, bf16[8,48,1152]{2,1,0:T(8,128)(2,1)S(1)}, u32[]{:S(2)}, u32[]{:S(2)}) collective-permute-start(bf16[8,48,1152]{2,1,0:T(8,128)(2,1)S(1)} %pad_maximum_fusion.8), channel_id=1, source_target_pairs={{0,12},{2,14},{4,8},{6,10},{8,4},{10,6},{12,0},{14,2},{16,28},{18,... | collective-permute-start | bytes 2654216 | tf_op jit(solution)/shard_map/ppermute | solution.py:670
  58.6 25.6 %collective-permute-start.18 = (bf16[8,48,1152]{2,1,0:T(8,128)(2,1)S(1)}, bf16[8,48,1152]{2,1,0:T(8,128)(2,1)S(1)}, u32[]{:S(2)}, u32[]{:S(2)}) collective-permute-start(bf16[8,48,1152]{2,1,0:T(8,128)(2,1)S(1)} %pad_maximum_fusion.7), channel_id=1, source_target_pairs={{0,4},{2,6},{4,0},{6,2},{8,12},{10,14},{12,8},{14,10},{16,20},{18,... | collective-permute-start | bytes 2654216 | tf_op jit(solution)/shard_map/ppermute | solution.py:670
  61.2 25.2 %collective-permute-start.22 = (bf16[3,48,1536]{2,1,0:T(8,128)(2,1)S(1)}, bf16[3,48,1536]{2,1,0:T(8,128)(2,1)S(1)}, u32[]{:S(2)}, u32[]{:S(2)}) collective-permute-start(bf16[3,48,1536]{2,1,0:T(8,128)(2,1)S(1)} %get-tuple-element.322), channel_id=1, source_target_pairs={{2,0},{4,2},{6,4},{8,6},{10,8},{12,10},{14,12},{16,14},{18,16},{20... | collective-permute-start | bytes 1327112 | tf_op jit(solution)/shard_map/ppermute | solution.py:802
  87.1 41.8 %collective-permute-start.25 = (bf16[16,48,1152]{2,1,0:T(8,128)(2,1)}, bf16[16,48,1152]{2,1,0:T(8,128)(2,1)}, u32[]{:S(2)}, u32[]{:S(2)}) collective-permute-start(bf16[16,48,1152]{2,1,0:T(8,128)(2,1)} %pad_maximum_fusion.refs_0_), channel_id=1, source_target_pairs={{0,12},{2,14},{4,8},{6,10},{8,4},{10,6},{12,0},{14,2},{16,28},{18,... | collective-permute-start | bytes 5308424 | tf_op jit(solution)/shard_map/ppermute | solution.py:670
  87.1 41.8 %collective-permute-start.26 = (bf16[16,48,1152]{2,1,0:T(8,128)(2,1)}, bf16[16,48,1152]{2,1,0:T(8,128)(2,1)}, u32[]{:S(2)}, u32[]{:S(2)}) collective-permute-start(bf16[16,48,1152]{2,1,0:T(8,128)(2,1)} %pad_maximum_fusion.1.refs_2_), channel_id=1, source_target_pairs={{0,16},{2,18},{4,20},{6,22},{8,24},{10,26},{12,28},{14,30},{16,0},... | collective-permute-start | bytes 5308424 | tf_op jit(solution)/shard_map/ppermute | solution.py:670
  88.0 35.0 %collective-permute-start.23 = (bf16[16,16,3072]{2,1,0:T(8,128)(2,1)}, bf16[16,16,3072]{2,1,0:T(8,128)(2,1)}, u32[]{:S(2)}, u32[]{:S(2)}) collective-permute-start(bf16[16,16,3072]{2,1,0:T(8,128)(2,1)} %pad_maximum_fusion.2), channel_id=1, source_target_pairs={{0,64},{2,66},{4,68},{6,70},{8,72},{10,74},{12,76},{14,78},{16,80}... | collective-permute-start | bytes 4718600 | tf_op jit(solution)/shard_map/ppermute | solution.py:670
  89.2 36.4 %collective-permute-start.24 = (bf16[16,16,3072]{2,1,0:T(8,128)(2,1)}, bf16[16,16,3072]{2,1,0:T(8,128)(2,1)}, u32[]{:S(2)}, u32[]{:S(2)}) collective-permute-start(bf16[16,16,3072]{2,1,0:T(8,128)(2,1)} %pad_maximum_fusion.3), channel_id=1, source_target_pairs={{0,4},{2,6},{4,0},{6,2},{8,12},{10,14},{12,8},{14,10},{16,20},{18,... | collective-permute-start | bytes 4718600 | tf_op jit(solution)/shard_map/ppermute | solution.py:670
  91.1 37.8 %collective-permute-start.27 = (bf16[16,48,1024]{2,1,0:T(8,128)(2,1)}, bf16[16,48,1024]{2,1,0:T(8,128)(2,1)}, u32[]{:S(2)}, u32[]{:S(2)}) collective-permute-start(bf16[16,48,1024]{2,1,0:T(8,128)(2,1)} %pad_maximum_fusion.4.refs_4_), channel_id=1, source_target_pairs={{0,48},{2,50},{4,52},{6,54},{8,56},{10,58},{12,60},{14,62},{16,32}... | collective-permute-start | bytes 4718600 | tf_op jit(solution)/shard_map/ppermute | solution.py:670
  130.5 6.1 %collective-permute-start.28 = (bf16[32,16,3072]{2,1,0:T(8,128)(2,1)S(1)}, bf16[32,16,3072]{2,1,0:T(8,128)(2,1)S(1)}, u32[]{:S(2)}, u32[]{:S(2)}) collective-permute-start(bf16[32,16,3072]{2,1,0:T(8,128)(2,1)S(1)} %constant_dynamic-update-slice_fusion.5), channel_id=1, source_target_pairs={{0,2},{2,0},{4,6},{6,4},{8,10},{10,8},{12,14},{14,12},{16,18},{18,... | collective-permute-start | bytes 9437192 | tf_op jit(solution)/shard_map/ppermute | solution.py:670
  137.4 12.5 %collective-permute-start.29 = (bf16[144,1024]{1,0:T(8,128)(2,1)S(1)}, bf16[144,1024]{1,0:T(8,128)(2,1)S(1)}, u32[]{:S(2)}, u32[]{:S(2)}) collective-permute-start(bf16[144,1024]{1,0:T(8,128)(2,1)S(1)} %slice.619), channel_id=1, source_target_pairs={{0,124},{2,126},{4,8},{6,10},{8,4},{10,6},{12,16},{14,18},{16,12},... | collective-permute-start | bytes 884744 | tf_op jit(solution)/shard_map/ppermute | solution.py:834
  141.2 31.7 %collective-permute-start.32 = (bf16[32,16,3072]{2,1,0:T(8,128)(2,1)S(1)}, bf16[32,16,3072]{2,1,0:T(8,128)(2,1)S(1)}, u32[]{:S(2)}, u32[]{:S(2)}) collective-permute-start(bf16[32,16,3072]{2,1,0:T(8,128)(2,1)S(1)} %constant_dynamic-update-slice_fusion.7), channel_id=1, source_target_pairs={{0,2},{2,0},{4,6},{6,4},{8,10},{10,8},{12,14},{14,12},{16,18},{18,... | collective-permute-start | bytes 9437192 | tf_op jit(solution)/shard_map/ppermute | solution.py:670
  159.2 10.4 %collective-permute-start.31 = (bf16[144,1024]{1,0:T(8,128)(2,1)S(1)}, bf16[144,1024]{1,0:T(8,128)(2,1)S(1)}, u32[]{:S(2)}, u32[]{:S(2)}) collective-permute-start(bf16[144,1024]{1,0:T(8,128)(2,1)S(1)} %fusion.50.refs_1_), channel_id=1, source_target_pairs={{0,1},{1,0},{2,3},{3,2},{4,5},{5,4},{6,7},{7,6},{8,9},{9,8},{10,11... | collective-permute-start | bytes 884744 | tf_op jit(solution)/shard_map/ppermute | solution.py:788
  162.7 16.9 %collective-permute-start.35 = (bf16[576,1536]{1,0:T(8,128)(2,1)S(1)}, bf16[576,1536]{1,0:T(8,128)(2,1)S(1)}, u32[]{:S(2)}, u32[]{:S(2)}) collective-permute-start(bf16[576,1536]{1,0:T(8,128)(2,1)S(1)} %shard_map.357.refs_0_), channel_id=1, source_target_pairs={{0,2},{2,0},{4,6},{6,4},{8,10},{10,8},{12,14},{14,12},{16,18},{18,... | collective-permute-start | bytes 5308424 | tf_op jit(solution)/shard_map/ppermute | solution.py:670
  163.4 27.0 %collective-permute-start.34 = (bf16[1536,256]{1,0:T(8,128)(2,1)S(1)}, bf16[1536,256]{1,0:T(8,128)(2,1)S(1)}, u32[]{:S(2)}, u32[]{:S(2)}) collective-permute-start(bf16[1536,256]{1,0:T(8,128)(2,1)S(1)} %bitcast.150), channel_id=1, source_target_pairs={{0,2},{2,0},{4,6},{6,4},{8,10},{10,8},{12,14},{14,12},{16,18},{18,... | collective-permute-start | bytes 2359304 | tf_op jit(solution)/shard_map/ppermute | solution.py:670
  176.9 13.3 %collective-permute-start.33 = (bf16[144,1024]{1,0:T(8,128)(2,1)S(1)}, bf16[144,1024]{1,0:T(8,128)(2,1)S(1)}, u32[]{:S(2)}, u32[]{:S(2)}) collective-permute-start(bf16[144,1024]{1,0:T(8,128)(2,1)S(1)} %fusion.55.own_ref), channel_id=1, source_target_pairs={{0,1},{1,0},{2,3},{3,2},{4,5},{5,4},{6,7},{7,6},{8,9},{9,8},{10,11... | collective-permute-start | bytes 884744 | tf_op jit(solution)/shard_map/ppermute | solution.py:788
  205.6 13.4 %collective-permute-start.37 = (bf16[6,24,1536]{2,1,0:T(8,128)(2,1)S(1)}, bf16[6,24,1536]{2,1,0:T(8,128)(2,1)S(1)}, u32[]{:S(2)}, u32[]{:S(2)}) collective-permute-start(bf16[6,24,1536]{2,1,0:T(8,128)(2,1)S(1)} %bitcast.147), channel_id=1, source_target_pairs={{0,1},{1,0},{2,3},{3,2},{4,5},{5,4},{6,7},{7,6},{8,9},{9,8},{10,11... | collective-permute-start | bytes 1327112 | tf_op jit(solution)/shard_map/ppermute | solution.py:788
  225.3 42.7 %collective-permute-start.41 = (bf16[12,48,1536]{2,1,0:T(8,128)(2,1)}, bf16[12,48,1536]{2,1,0:T(8,128)(2,1)}, u32[]{:S(2)}, u32[]{:S(2)}) collective-permute-start(bf16[12,48,1536]{2,1,0:T(8,128)(2,1)} %bitcast.30.own_ref), channel_id=1, source_target_pairs={{0,1},{1,0},{2,3},{3,2},{4,5},{5,4},{6,7},{7,6},{8,9},{9,8},{10,11... | collective-permute-start | bytes 5308424 | tf_op jit(solution)/shard_map/ppermute | solution.py:788
  241.0 32.5 %collective-permute-start.39 = (bf16[1,24,1024]{2,1,0:T(8,128)(2,1)}, bf16[1,24,1024]{2,1,0:T(8,128)(2,1)}, u32[]{:S(2)}, u32[]{:S(2)}) collective-permute-start(bf16[1,24,1024]{2,1,0:T(8,128)(2,1)} %get-tuple-element.352), channel_id=1, source_target_pairs={{0,2},{2,4},{4,6},{6,8},{8,10},{10,12},{12,14},{14,16},{16,18},{18... | collective-permute-start | bytes 147464 | tf_op jit(solution)/shard_map/ppermute | solution.py:801
  241.0 32.5 %collective-permute-start.40 = (bf16[1,24,1024]{2,1,0:T(8,128)(2,1)}, bf16[1,24,1024]{2,1,0:T(8,128)(2,1)}, u32[]{:S(2)}, u32[]{:S(2)}) collective-permute-start(bf16[1,24,1024]{2,1,0:T(8,128)(2,1)} %get-tuple-element.351), channel_id=1, source_target_pairs={{2,0},{4,2},{6,4},{8,6},{10,8},{12,10},{14,12},{16,14},{18,16},{20... | collective-permute-start | bytes 147464 | tf_op jit(solution)/shard_map/ppermute | solution.py:802
  277.8 28.6 %collective-permute-start.45 = (bf16[576,1536]{1,0:T(8,128)(2,1)}, bf16[576,1536]{1,0:T(8,128)(2,1)}, u32[]{:S(2)}, u32[]{:S(2)}) collective-permute-start(bf16[576,1536]{1,0:T(8,128)(2,1)} %copy-done.88), channel_id=1, source_target_pairs={{0,2},{2,0},{4,6},{6,4},{8,10},{10,8},{12,14},{14,12},{16,18},{18,... | collective-permute-start | bytes 5308424 | tf_op jit(solution)/shard_map/ppermute | solution.py:670
  278.9 7.3 %collective-permute-start.42 = (bf16[6,24,512]{2,1,0:T(8,128)(2,1)}, bf16[6,24,512]{2,1,0:T(8,128)(2,1)}, u32[]{:S(2)}, u32[]{:S(2)}) collective-permute-start(bf16[6,24,512]{2,1,0:T(8,128)(2,1)} %get-tuple-element.359), channel_id=1, source_target_pairs={{0,1},{1,0},{2,3},{3,2},{4,5},{5,4},{6,7},{7,6},{8,9},{9,8},{10,11... | collective-permute-start | bytes 442376 | tf_op jit(solution)/shard_map/ppermute | solution.py:788
  303.4 9.3 %collective-permute-start.44 = (bf16[144,1024]{1,0:T(8,128)(2,1)S(1)}, bf16[144,1024]{1,0:T(8,128)(2,1)S(1)}, u32[]{:S(2)}, u32[]{:S(2)}) collective-permute-start(bf16[144,1024]{1,0:T(8,128)(2,1)S(1)} %fusion.57.own_ref), channel_id=1, source_target_pairs={{0,1},{1,0},{2,3},{3,2},{4,5},{5,4},{6,7},{7,6},{8,9},{9,8},{10,11... | collective-permute-start | bytes 884744 | tf_op jit(solution)/shard_map/ppermute | solution.py:788
  312.7 50.2 %collective-permute-start.49 = (bf16[32,16,3072]{2,1,0:T(8,128)(2,1)}, bf16[32,16,3072]{2,1,0:T(8,128)(2,1)}, u32[]{:S(2)}, u32[]{:S(2)}) collective-permute-start(bf16[32,16,3072]{2,1,0:T(8,128)(2,1)} %bitcast.42), channel_id=1, source_target_pairs={{0,2},{2,0},{4,6},{6,4},{8,10},{10,8},{12,14},{14,12},{16,18},{18,... | collective-permute-start | bytes 9437192 | tf_op jit(solution)/shard_map/ppermute | solution.py:670
  315.2 14.1 %collective-permute-start.50 = (bf16[1536,256]{1,0:T(8,128)(2,1)S(1)}, bf16[1536,256]{1,0:T(8,128)(2,1)S(1)}, u32[]{:S(2)}, u32[]{:S(2)}) collective-permute-start(bf16[1536,256]{1,0:T(8,128)(2,1)S(1)} %select_convert_fusion), channel_id=1, source_target_pairs={{0,2},{2,0},{4,6},{6,4},{8,10},{10,8},{12,14},{14,12},{16,18},{18,... | collective-permute-start | bytes 2359304 | tf_op jit(solution)/shard_map/ppermute | solution.py:670
  325.2 48.2 %collective-permute-start.48 = (bf16[576,1536]{1,0:T(8,128)(2,1)S(1)}, bf16[576,1536]{1,0:T(8,128)(2,1)S(1)}, u32[]{:S(2)}, u32[]{:S(2)}) collective-permute-start(bf16[576,1536]{1,0:T(8,128)(2,1)S(1)} %add_convert_fusion.own_ref), channel_id=1, source_target_pairs={{0,1},{1,0},{2,3},{3,2},{4,5},{5,4},{6,7},{7,6},{8,9},{9,8},{10,11... | collective-permute-start | bytes 5308424 | tf_op jit(solution)/shard_map/ppermute | solution.py:788
  331.2 36.4 %collective-permute-start.47 = (bf16[144,1024]{1,0:T(8,128)(2,1)S(1)}, bf16[144,1024]{1,0:T(8,128)(2,1)S(1)}, u32[]{:S(2)}, u32[]{:S(2)}) collective-permute-start(bf16[144,1024]{1,0:T(8,128)(2,1)S(1)} %slice.899), channel_id=1, source_target_pairs={{0,124},{2,126},{4,8},{6,10},{8,4},{10,6},{12,16},{14,18},{16,12},... | collective-permute-start | bytes 884744 | tf_op jit(solution)/shard_map/ppermute | solution.py:834
  378.0 14.3 %collective-permute-start.52 = (bf16[32,16,3072]{2,1,0:T(8,128)(2,1)S(1)}, bf16[32,16,3072]{2,1,0:T(8,128)(2,1)S(1)}, u32[]{:S(2)}, u32[]{:S(2)}) collective-permute-start(bf16[32,16,3072]{2,1,0:T(8,128)(2,1)S(1)} %bitcast.149), channel_id=1, source_target_pairs={{0,2},{2,0},{4,6},{6,4},{8,10},{10,8},{12,14},{14,12},{16,18},{18,... | collective-permute-start | bytes 9437192 | tf_op jit(solution)/shard_map/ppermute | solution.py:670
  382.9 5.3 collective-permute-start.55
  382.9 8.0 %collective-permute-start.56 = (bf16[3,48,1536]{2,1,0:T(8,128)(2,1)S(1)}, bf16[3,48,1536]{2,1,0:T(8,128)(2,1)S(1)}, u32[]{:S(2)}, u32[]{:S(2)}) collective-permute-start(bf16[3,48,1536]{2,1,0:T(8,128)(2,1)S(1)} %bitcast.176), channel_id=1, source_target_pairs={{2,0},{4,2},{6,4},{8,6},{10,8},{12,10},{14,12},{16,14},{18,16},{20... | collective-permute-start | bytes 1327112 | tf_op jit(solution)/shard_map/ppermute | solution.py:802
  391.7 57.8 %collective-permute-start.57 = (bf16[16,48,1792]{2,1,0:T(8,128)(2,1)}, bf16[16,48,1792]{2,1,0:T(8,128)(2,1)}, u32[]{:S(2)}, u32[]{:S(2)}) collective-permute-start(bf16[16,48,1792]{2,1,0:T(8,128)(2,1)} %get-tuple-element.225), channel_id=1, source_target_pairs={{0,12},{2,14},{4,8},{6,10},{8,4},{10,6},{12,0},{14,2},{16,28},{18,... | collective-permute-start | bytes 8257544 | tf_op jit(solution)/shard_map/ppermute | solution.py:670
  391.9 55.9 %collective-permute-start.54 = (bf16[16,16,3072]{2,1,0:T(8,128)(2,1)}, bf16[16,16,3072]{2,1,0:T(8,128)(2,1)}, u32[]{:S(2)}, u32[]{:S(2)}) collective-permute-start(bf16[16,16,3072]{2,1,0:T(8,128)(2,1)} %get-tuple-element.218), channel_id=1, source_target_pairs={{0,4},{2,6},{4,0},{6,2},{8,12},{10,14},{12,8},{14,10},{16,20},{18,... | collective-permute-start | bytes 4718600 | tf_op jit(solution)/shard_map/ppermute | solution.py:670
  392.0 55.8 %collective-permute-start.58 = (bf16[16,48,1536]{2,1,0:T(8,128)(2,1)}, bf16[16,48,1536]{2,1,0:T(8,128)(2,1)}, u32[]{:S(2)}, u32[]{:S(2)}) collective-permute-start(bf16[16,48,1536]{2,1,0:T(8,128)(2,1)} %get-tuple-element.226), channel_id=1, source_target_pairs={{0,16},{2,18},{4,20},{6,22},{8,24},{10,26},{12,28},{14,30},{16,0},... | collective-permute-start | bytes 7077896 | tf_op jit(solution)/shard_map/ppermute | solution.py:670
  394.4 55.1 %collective-permute-start.53 = (bf16[16,16,3072]{2,1,0:T(8,128)(2,1)}, bf16[16,16,3072]{2,1,0:T(8,128)(2,1)}, u32[]{:S(2)}, u32[]{:S(2)}) collective-permute-start(bf16[16,16,3072]{2,1,0:T(8,128)(2,1)} %get-tuple-element.313), channel_id=1, source_target_pairs={{0,64},{2,66},{4,68},{6,70},{8,72},{10,74},{12,76},{14,78},{16,80}... | collective-permute-start | bytes 4718600 | tf_op jit(solution)/shard_map/ppermute | solution.py:670
  402.5 70.2 %collective-permute-start.51 = (bf16[144,1024]{1,0:T(8,128)(2,1)}, bf16[144,1024]{1,0:T(8,128)(2,1)}, u32[]{:S(2)}, u32[]{:S(2)}) collective-permute-start(bf16[144,1024]{1,0:T(8,128)(2,1)} %fusion.53.own_ref), channel_id=1, source_target_pairs={{0,1},{1,0},{2,3},{3,2},{4,5},{5,4},{6,7},{7,6},{8,9},{9,8},{10,11... | collective-permute-start | bytes 884744 | tf_op jit(solution)/shard_map/ppermute | solution.py:788
  452.6 45.9 %collective-permute-start.62 = (bf16[8,48,1536]{2,1,0:T(8,128)(2,1)}, bf16[8,48,1536]{2,1,0:T(8,128)(2,1)}, u32[]{:S(2)}, u32[]{:S(2)}) collective-permute-start(bf16[8,48,1536]{2,1,0:T(8,128)(2,1)} %get-tuple-element.307), channel_id=1, source_target_pairs={{0,12},{2,14},{4,8},{6,10},{8,4},{10,6},{12,0},{14,2},{16,28},{18,... | collective-permute-start | bytes 3538952 | tf_op jit(solution)/shard_map/ppermute | solution.py:670
  459.2 39.2 %collective-permute-start.61 = (bf16[8,48,1792]{2,1,0:T(8,128)(2,1)}, bf16[8,48,1792]{2,1,0:T(8,128)(2,1)}, u32[]{:S(2)}, u32[]{:S(2)}) collective-permute-start(bf16[8,48,1792]{2,1,0:T(8,128)(2,1)} %get-tuple-element.305), channel_id=1, source_target_pairs={{0,4},{2,6},{4,0},{6,2},{8,12},{10,14},{12,8},{14,10},{16,20},{18,... | collective-permute-start | bytes 4128776 | tf_op jit(solution)/shard_map/ppermute | solution.py:670
  461.9 36.5 %collective-permute-start.60 = (bf16[8,16,3072]{2,1,0:T(8,128)(2,1)}, bf16[8,16,3072]{2,1,0:T(8,128)(2,1)}, u32[]{:S(2)}, u32[]{:S(2)}) collective-permute-start(bf16[8,16,3072]{2,1,0:T(8,128)(2,1)} %get-tuple-element.309), channel_id=1, source_target_pairs={{0,64},{2,66},{4,68},{6,70},{8,72},{10,74},{12,76},{14,78},{16,80}... | collective-permute-start | bytes 2359304 | tf_op jit(solution)/shard_map/ppermute | solution.py:670
  465.3 33.1 %collective-permute-start.59 = (bf16[8,16,3072]{2,1,0:T(8,128)(2,1)}, bf16[8,16,3072]{2,1,0:T(8,128)(2,1)}, u32[]{:S(2)}, u32[]{:S(2)}) collective-permute-start(bf16[8,16,3072]{2,1,0:T(8,128)(2,1)} %get-tuple-element.310), channel_id=1, source_target_pairs={{0,48},{2,50},{4,52},{6,54},{8,56},{10,58},{12,60},{14,62},{16,32}... | collective-permute-start | bytes 2359304 | tf_op jit(solution)/shard_map/ppermute | solution.py:670
  499.8 23.7 %collective-permute-start.66 = (bf16[4,48,1536]{2,1,0:T(8,128)(2,1)S(1)}, bf16[4,48,1536]{2,1,0:T(8,128)(2,1)S(1)}, u32[]{:S(2)}, u32[]{:S(2)}) collective-permute-start(bf16[4,48,1536]{2,1,0:T(8,128)(2,1)S(1)} %get-tuple-element.319), channel_id=1, source_target_pairs={{0,4},{2,6},{4,0},{6,2},{8,12},{10,14},{12,8},{14,10},{16,20},{18,... | collective-permute-start | bytes 1769480 | tf_op jit(solution)/shard_map/ppermute | solution.py:670
  501.8 21.7 %collective-permute-start.65 = (bf16[4,48,1792]{2,1,0:T(8,128)(2,1)S(1)}, bf16[4,48,1792]{2,1,0:T(8,128)(2,1)S(1)}, u32[]{:S(2)}, u32[]{:S(2)}) collective-permute-start(bf16[4,48,1792]{2,1,0:T(8,128)(2,1)S(1)} %get-tuple-element.317), channel_id=1, source_target_pairs={{0,64},{2,66},{4,68},{6,70},{8,72},{10,74},{12,76},{14,78},{16,80}... | collective-permute-start | bytes 2064392 | tf_op jit(solution)/shard_map/ppermute | solution.py:670
  503.5 20.0 %collective-permute-start.64 = (bf16[4,16,3072]{2,1,0:T(8,128)(2,1)S(1)}, bf16[4,16,3072]{2,1,0:T(8,128)(2,1)S(1)}, u32[]{:S(2)}, u32[]{:S(2)}) collective-permute-start(bf16[4,16,3072]{2,1,0:T(8,128)(2,1)S(1)} %get-tuple-element.325), channel_id=1, source_target_pairs={{0,48},{2,50},{4,52},{6,54},{8,56},{10,58},{12,60},{14,62},{16,32}... | collective-permute-start | bytes 1179656 | tf_op jit(solution)/shard_map/ppermute | solution.py:670
  504.9 18.6 %collective-permute-start.63 = (bf16[4,16,3072]{2,1,0:T(8,128)(2,1)S(1)}, bf16[4,16,3072]{2,1,0:T(8,128)(2,1)S(1)}, u32[]{:S(2)}, u32[]{:S(2)}) collective-permute-start(bf16[4,16,3072]{2,1,0:T(8,128)(2,1)S(1)} %get-tuple-element.327), channel_id=1, source_target_pairs={{0,16},{2,18},{4,20},{6,22},{8,24},{10,26},{12,28},{14,30},{16,0},... | collective-permute-start | bytes 1179656 | tf_op jit(solution)/shard_map/ppermute | solution.py:670
  523.6 8.3 %collective-permute-start.70 = (bf16[2,48,1536]{2,1,0:T(8,128)(2,1)S(1)}, bf16[2,48,1536]{2,1,0:T(8,128)(2,1)S(1)}, u32[]{:S(2)}, u32[]{:S(2)}) collective-permute-start(bf16[2,48,1536]{2,1,0:T(8,128)(2,1)S(1)} %get-tuple-element.331), channel_id=1, source_target_pairs={{0,64},{2,66},{4,68},{6,70},{8,72},{10,74},{12,76},{14,78},{16,80}... | collective-permute-start | bytes 884744 | tf_op jit(solution)/shard_map/ppermute | solution.py:670
  523.8 9.5 %collective-permute-start.69 = (bf16[2,48,1792]{2,1,0:T(8,128)(2,1)S(1)}, bf16[2,48,1792]{2,1,0:T(8,128)(2,1)S(1)}, u32[]{:S(2)}, u32[]{:S(2)}) collective-permute-start(bf16[2,48,1792]{2,1,0:T(8,128)(2,1)S(1)} %get-tuple-element.329), channel_id=1, source_target_pairs={{0,48},{2,50},{4,52},{6,54},{8,56},{10,58},{12,60},{14,62},{16,32}... | collective-permute-start | bytes 1032200 | tf_op jit(solution)/shard_map/ppermute | solution.py:670
  524.8 5.0 collective-permute-start.68
  524.9 6.2 %collective-permute-start.67 = (bf16[2,16,3072]{2,1,0:T(8,128)(2,1)S(1)}, bf16[2,16,3072]{2,1,0:T(8,128)(2,1)S(1)}, u32[]{:S(2)}, u32[]{:S(2)}) collective-permute-start(bf16[2,16,3072]{2,1,0:T(8,128)(2,1)S(1)} %get-tuple-element.334), channel_id=1, source_target_pairs={{0,12},{2,14},{4,8},{6,10},{8,4},{10,6},{12,0},{14,2},{16,28},{18,... | collective-permute-start | bytes 589832 | tf_op jit(solution)/shard_map/ppermute | solution.py:670
  533.3 6.3 %collective-permute-start.74 = (bf16[1,48,1536]{2,1,0:T(8,128)(2,1)S(1)}, bf16[1,48,1536]{2,1,0:T(8,128)(2,1)S(1)}, u32[]{:S(2)}, u32[]{:S(2)}) collective-permute-start(bf16[1,48,1536]{2,1,0:T(8,128)(2,1)S(1)} %slice_add_fusion.33), channel_id=1, source_target_pairs={{0,48},{2,50},{4,52},{6,54},{8,56},{10,58},{12,60},{14,62},{16,32}... | collective-permute-start | bytes 442376 | tf_op jit(solution)/shard_map/ppermute | solution.py:670
  534.4 5.2 collective-permute-start.73
  (140 other events, 1290.3 us)

commit v4 on v3

--- a/solution.py
+++ b/solution.py
@@ -129,6 +129,10 @@
 SCALARS = pl.BlockSpec(memory_space=pltpu.SMEM)
 
 
+def in_hbm(values):
+    return [pltpu.with_memory_space_constraint(v, pltpu.MemorySpace.HBM) for v in values]
+
+
 def map_conv(place, main, low, high, taps, added=None):
     strip, side, channels = main.shape
     count = taps.shape[0]
@@ -138,6 +142,7 @@
     if added is not None:
         specs.append(block3(strip, side))
         args.append(added)
+        args[1:] = in_hbm(args[1:])
     work = strip * side * channels
     return pl.pallas_call(
         forward_kernel if added is None else backward_kernel,
@@ -171,7 +176,7 @@
         ],
         compiler_params=pltpu.CompilerParams(vmem_limit_bytes=24 * 1024 * 1024),
         cost_estimate=pl.CostEstimate(flops=0, bytes_accessed=work // 8, transcendentals=0),
-    )(place, main, low, high, grad)
+    )(place, *in_hbm([main, low, high, grad]))
 
 
 WIDE = 384
@@ -932,14 +937,13 @@
         first += rows
 
 
-def slope_pack_kernel(order, lefts, place, *refs):
-    left_refs, right_ref = refs[:lefts], refs[lefts]
-    extra_ref = refs[lefts + 1] if len(refs) > lefts + 6 else None
-    near_ref, far_ref, turned, tile, sems = refs[-5:]
-    width = right_ref.shape[1]
+def slope_pack_kernel(orders, spans, place, *refs):
+    first_lefts, second_lefts, (right_a, right_b, extra_ref) = refs[:2], refs[2:4], refs[4:7]
+    outs, (turned, tile, sems) = refs[7:-3], refs[-3:]
+    width = right_a.shape[1]
     step = pl.program_id(0)
-    full = turned.shape[0] // width
-    total = full + (extra_ref is not None)
+    per_side = turned.shape[0] // width
+    total = 2 * per_side + 1
     blocks, rows = tile.shape[1], tile.shape[2]
     group = blocks // 4
     chip = place[0] >> 1
@@ -955,37 +959,48 @@
 
     @pl.when(step == 0)
     def _():
-        turn(left_refs, turned)
-
-    @pl.when(step < full)
+        turn(first_lefts, turned)
+
+    @pl.when(step == per_side)
     def _():
+        turn(second_lefts, turned)
+
+    def fill(right):
         for part in range(4):
             lines = slice(part * group * rows, (part + 1) * group * rows)
-            value = jnp.dot(turned[lines, :], right_ref[...], preferred_element_type=jnp.float32)
+            value = jnp.dot(turned[lines, :], right[...], preferred_element_type=jnp.float32)
             tile[slot, part * group : (part + 1) * group] = value.astype(tile.dtype).reshape(
                 group, rows, width
             )
 
-    last = width
-    if extra_ref is not None:
-        last = extra_ref.shape[2]
-
-        @pl.when(step == full)
-        def _():
-            tile[slot, :, :, 0:last] = extra_ref[...]
+    @pl.when(step < per_side)
+    def _():
+        fill(right_a)
+
+    @pl.when((step >= per_side) & (step < 2 * per_side))
+    def _():
+        fill(right_b)
+
+    last = extra_ref.shape[2]
+
+    @pl.when(step == 2 * per_side)
+    def _():
+        tile[slot, :, :, 0:last] = extra_ref[...]
 
     for index in range(total):
-        wide = width if index < full else last
-        cols = pl.ds(index * width, wide)
+        begin = index * width
+        wide = width if index < 2 * per_side else last
+        goal = [i for i, span in enumerate(spans) if span[0] <= begin < span[1]][0]
+        cols = pl.ds(begin - spans[goal][0], wide)
 
         @pl.when(step == index)
-        def _(cols=cols, wide=wide):
+        def _(goal=goal, cols=cols, wide=wide):
             def send(spot, carry):
-                for side, out in enumerate((near_ref, far_ref)):
-                    owner = chip ^ chip_offset(spot + side * (blocks // 2), order, True)
+                for side in range(2):
+                    owner = chip ^ chip_offset(spot + side * (blocks // 2), orders[goal], True)
                     pltpu.make_async_copy(
                         tile.at[slot, owner, :, pl.ds(0, wide)],
-                        out.at[spot, :, cols],
+                        outs[2 * goal + side].at[spot, :, cols],
                         sems.at[slot],
                     ).start()
                 return carry
@@ -998,40 +1013,41 @@
         sent(slot, last).wait()
 
 
-def packed_slopes(place, order, lefts, right, extra=None):
-    channels = lefts[0].shape[1]
-    depth, hidden = right.shape
+def packed_slopes(place, orders, spans, first_lefts, right_a, second_lefts, right_b, extra):
+    channels = first_lefts[0].shape[1]
+    depth, hidden = right_a.shape
     width = 384
     steps = hidden // width
     rows = channels // CHIPS
-    total, more, specs = hidden, [], []
-    if extra is not None:
-        total += extra.shape[1]
-        more = [extra.reshape(CHIPS, rows, extra.shape[1])]
-        specs = [
-            pl.BlockSpec(more[0].shape, lambda i: (0, 0, 0), pipeline_mode=pl.Buffered(1))
-        ]
-    shape = jax.ShapeDtypeStruct((CHIPS // 2, rows, total), jnp.bfloat16)
+    extra = extra.reshape(CHIPS, rows, extra.shape[1])
+    once = pl.Buffered(1)
     return pl.pallas_call(
-        functools.partial(slope_pack_kernel, order, len(lefts)),
-        grid=(steps + len(more),),
+        functools.partial(slope_pack_kernel, orders, spans),
+        grid=(2 * steps + 1,),
         in_specs=[SCALARS]
         + [
-            pl.BlockSpec(left.shape, lambda i: (0, 0), pipeline_mode=pl.Buffered(1))
-            for left in lefts
+            pl.BlockSpec(left.shape, lambda i: (0, 0), pipeline_mode=once)
+            for left in (*first_lefts, *second_lefts)
         ]
-        + [pl.BlockSpec((depth, width), lambda i: (0, jnp.minimum(i, steps - 1)))]
-        + specs,
-        out_specs=[pl.BlockSpec(memory_space=pl.ANY)] * 2,
-        out_shape=[shape, shape],
+        + [
+            pl.BlockSpec((depth, width), lambda i: (0, jnp.minimum(i, steps - 1))),
+            pl.BlockSpec((depth, width), lambda i: (0, jnp.clip(i - steps, 0, steps - 1))),
+            pl.BlockSpec(extra.shape, lambda i: (0, 0, 0), pipeline_mode=once),
+        ],
+        out_specs=[pl.BlockSpec(memory_space=pl.ANY)] * (2 * len(spans)),
+        out_shape=[
+            jax.ShapeDtypeStruct((CHIPS // 2, rows, high - low), jnp.bfloat16)
+            for low, high in spans
+            for _ in range(2)
+        ],
         scratch_shapes=[
             pltpu.VMEM((channels, depth), jnp.bfloat16),
             pltpu.VMEM((2, CHIPS, rows, width), jnp.bfloat16),
             pltpu.SemaphoreType.DMA((2,)),
         ],
-        compiler_params=pltpu.CompilerParams(vmem_limit_bytes=32 * 1024 * 1024),
-        cost_estimate=pl.CostEstimate(flops=0, bytes_accessed=1 << 20, transcendentals=0),
-    )(place, *lefts, right, *more)
+        compiler_params=pltpu.CompilerParams(vmem_limit_bytes=40 * 1024 * 1024),
+        cost_estimate=CHEAP,
+    )(place, *first_lefts, *second_lefts, right_a, right_b, extra)
 
 
 def unpacked_map_slopes(core, blocks, widths):
@@ -1274,15 +1290,17 @@
     ).astype(jnp.float32)
     pair_given, late_place = together([pair_back[token_count:].astype(jnp.bfloat16), place])
     pair_other = pair_swap(pair_given)
-    shrink_packed = packed_slopes(late_place, rotated(3), narrowed_grad_pair, widened_low)
-    expand_packed = packed_slopes(
+    map_widths = (widened_low.shape[1], widened_low.shape[1], adapter_slope.shape[1])
+    map_slopes_packed = packed_slopes(
         late_place,
-        rotated(2),
+        [rotated(i) for i in range(2, 5)],
+        even_edges(sum(map_widths), 3),
         [normed_map_low, normed_map_given_low],
         widened_grad_low,
+        narrowed_grad_pair,
+        widened_low,
         adapter_slope.astype(jnp.bfloat16),
     )
-    map_slopes_packed = [*expand_packed, *shrink_packed]
     second_near = split_sum(second_slopes[0], second_far)
     pair_other, normed_map_other, *rest = together(
         [pair_other, normed_map_other, *second_near, *map_slopes_packed]
@@ -1292,6 +1310,12 @@
     qkv_grad = jnp.concatenate([query_grad_rows, pair_back.astype(jnp.bfloat16)], axis=1)
     normed_own = restored(outof(qkv_grad, qkv_parts), 0).astype(jnp.bfloat16)
     normed_other = model_swap(normed_own)
+    conv_gain_slope, convolved_grad_low = norm_back(
+        convolved, normed_map_own, normed_map_other, conv_gain, (jnp.bfloat16,)
+    )
+    convolved_grad_low = convolved_grad_low.reshape(map_shape)
+    convolved_grad_low, qkv_grad = together([convolved_grad_low, qkv_grad])
+    grad_low, grad_high = halo_rows(convolved_grad_low, RADIUS)
     first_slopes = split_rows(
         paired_slopes(
             (normed_first, hidden_picked, normed_two_picked[0]),
@@ -1299,11 +1323,6 @@
         )
     )
     first_far = core_swap(first_slopes[1])
-    conv_gain_slope, convolved_grad_low = norm_back(
-        convolved, normed_map_own, normed_map_other, conv_gain, (jnp.bfloat16,)
-    )
-    convolved_grad_low = convolved_grad_low.reshape(map_shape)
-    grad_low, grad_high = halo_rows(convolved_grad_low, RADIUS)
     grad_low, grad_high, *map_slopes_packed = together(
         [grad_low, grad_high, *map_slopes_packed]
     )
@@ -1311,7 +1330,7 @@
     scatter = Scatter(
         [low for low, _ in near] + list(map_slopes_packed[0::2]),
         [high for _, high in near] + list(map_slopes_packed[1::2]),
-        [rotated(i)[::-1] for i in range(4)],
+        [rotated(i)[::-1] for i in range(5)],
     )
 
     depth_kernel_slope = map_slopes(map_place, high_map, map_low, map_high, convolved_grad_low)
@@ -1344,9 +1363,8 @@
         minor_rows.astype(jnp.bfloat16).reshape(minor_rows.shape[0], lines, LANES),
         ((0, 2 * CHIPS - minor_rows.shape[0]), (0, block_rows - lines), (0, 0)),
     )
-    depth_kernel_slope, highres_grad = scatter.advance(depth_kernel_slope, highres_grad)
     minor_own = row_sums(minor).astype(jnp.bfloat16)
-    (minor_own,) = scatter.advance(minor_own)
+    highres_grad, minor_own = scatter.advance(highres_grad, minor_own)
     minor_copies = row_copies(minor_own)
     (minor_copies,) = scatter.advance(minor_copies)
     minor_all = (
@@ -1357,10 +1375,10 @@
     first_own, second_own, *map_blocks = scatter.result()
     up_own = jnp.concatenate([first_own[:, quad:], second_own[:, :hidden_half]], axis=1)
     down_own = second_own[:, hidden_half:]
-    expand_own, adapter_own, shrink_own = unpacked_map_slopes(
+    expand_own, shrink_own, adapter_own = unpacked_map_slopes(
         core,
         map_blocks,
-        (widened_low.shape[1], adapter_slope.shape[1], widened_low.shape[1]),
+        map_widths,
     )
     firsts = [first_own[:, i * local_width : (i + 1) * local_width] for i in range(4)]
     taps = depth_kernel.shape[0]

time: 557 us -> 543 us (0.975)
  starting transfers between devices: 101 us -> 119 us
  blocking collectives: 38.1 us -> 21.7 us
  local copies, waits for them, and re-layouts: 52.2 us -> 40.3 us
  waiting for transfers between devices: 105 us -> 114 us
  other arithmetic: 52.6 us -> 44.2 us
    all_to_all x1 -> x0, blocking collectives: 19.8 us -> none  [row_sums(): pieces = lax.all_to_all(values, 'dp', 0, 0, tiled=True)]
    ppermute x59 -> x64, starting transfers between devices: 58 us -> 70.9 us  [xor_swap(): return lax.ppermute(values, 'dp', [(i, i ^ mask) for i in range(count)])]
    unnamed x270 -> x248, local copies, waits for them, and re-layouts: 34.6 us -> 25.5 us
    add x18 -> x22, other arithmetic: 24.1 us -> 16.9 us  [split_sum(): return (kept[:half] + other[:half], kept[half:] + other[half:])]
    ppermute x59 -> x64, waiting for transfers between devices: 62 us -> 66.2 us  [xor_swap(): return lax.ppermute(values, 'dp', [(i, i ^ mask) for i in range(count)])]
    pallas_call x2 -> x1, Pallas kernels: 28.6 us -> 28.3 us  [packed_slopes(): pl.pallas_call(functools.partial(slope_pack_kernel, orders, spans), grid=...]
  transfers between devices with their start and end apart: 76 -> 82, of which waited for: 34 -> 33; matrix products, arithmetic and copies ran while one was open for 19% -> 17% of each run, Pallas kernels for 25% -> 24%
where the time goes in v4:
time: 543 us; the launch traced here: 534 us
  Pallas kernels  155 us (29%)
  starting transfers between devices  119 us (22%)
  waiting for transfers between devices  114 us (21%)
  other arithmetic  44.2 us (8%)
  local copies, waits for them, and re-layouts  40.3 us (7%)
  matrix products  36.4 us (7%)
  blocking collectives  21.7 us (4%)
    ppermute x64, starting transfers between devices, xor_swap(): return lax.ppermute(values, 'dp', [(i, i ^ mask) for i in range(count)])  70.9 us
    ppermute x64, waiting for transfers between devices, xor_swap(): return lax.ppermute(values, 'dp', [(i, i ^ mask) for i in range(count)])  66.2 us
    ppermute x9, waiting for transfers between devices, model_swap(): return lax.ppermute(values, 'mp', [(0, 1), (1, 0)])  34.8 us
    pallas_call x3, Pallas kernels, dense(): pl.pallas_call(functools.partial(dense_kernel, flipped, scale is not None...  34.2 us
    pallas_call x2, Pallas kernels, map_conv(): pl.pallas_call(forward_kernel if added is None else backward_kernel, grid...  32.2 us
    pallas_call x1, Pallas kernels, packed_slopes(): pl.pallas_call(functools.partial(slope_pack_kernel, orders, spans), grid=...  28.3 us
    unnamed x248, local copies, waits for them, and re-layouts  25.5 us
    dot_general x17, matrix products, matmul(): return jnp.dot(former, latter, preferred_element_type=jnp.float32)  22.6 us
  transfers between devices with their start and end apart: 82, of which 33 were waited for; matrix products, arithmetic and copies ran while one was open for 17% of the time, Pallas kernels for 24%

profile of v4, /device:TPU:1, one launch (start us, length us, event | category | flops | bytes accessed | tf_op | source)
XLA Modules:
  0.0 533.5 jit_solution(6922233044668655660)
XLA Ops:
  5.2 3.3 collective-permute-start.1
  12.2 4.3 collective-permute-done
  18.3 2.8 collective-permute-start.4
  21.2 2.1 collective-permute-done.4
  27.0 2.6 collective-permute-done.7
  29.7 2.7 collective-permute-done.6
  36.5 4.4 collective-permute-done.12
  46.5 11.3 %collective-permute-start.21 = (bf16[3,48,1536]{2,1,0:T(8,128)(2,1)S(1)}, bf16[3,48,1536]{2,1,0:T(8,128)(2,1)S(1)}, u32[]{:S(2)}, u32[]{:S(2)}) collective-permute-start(bf16[3,48,1536]{2,1,0:T(8,128)(2,1)S(1)} %get-tuple-element.351), channel_id=1, source_target_pairs={{0,2},{2,4},{4,6},{6,8},{8,10},{10,12},{12,14},{14,16},{16,18},{18... | collective-permute-start | bytes 1327112 | tf_op jit(solution)/shard_map/ppermute | solution.py:806
  61.2 9.1 %collective-permute-start.22 = (bf16[3,48,1536]{2,1,0:T(8,128)(2,1)S(1)}, bf16[3,48,1536]{2,1,0:T(8,128)(2,1)S(1)}, u32[]{:S(2)}, u32[]{:S(2)}) collective-permute-start(bf16[3,48,1536]{2,1,0:T(8,128)(2,1)S(1)} %get-tuple-element.350), channel_id=1, source_target_pairs={{2,0},{4,2},{6,4},{8,6},{10,8},{12,10},{14,12},{16,14},{18,16},{20... | collective-permute-start | bytes 1327112 | tf_op jit(solution)/shard_map/ppermute | solution.py:807
  73.0 9.8 %collective-permute-done.19 = bf16[8,48,1152]{2,1,0:T(8,128)(2,1)S(1)} collective-permute-done((bf16[8,48,1152]{2,1,0:T(8,128)(2,1)S(1)}, bf16[8,48,1152]{2,1,0:T(8,128)(2,1)S(1)}, u32[]{:S(2)}, u32[]{:S(2)}) %collective-permute-start.19) | collective-permute-done | bytes 884768 | tf_op jit(solution)/shard_map/ppermute | solution.py:675
  97.2 15.6 %shard_map.356 = f32[12,48,1536]{2,1,0:T(8,128)S(1)} custom-call(s32[2]{0:T(128)S(1)} %pad_add_fusion.place, bf16[12,48,1536]{2,1,0:T(8,128)(2,1)S(1)} %bitcast.128, bf16[3,48,1536]{2,1,0:T(8,128)(2,1)S(1)} %copy-done.27, bf16[3,48,1536]{2,1,0:T(8,128)(2,1)S(1)} %copy-done.29, bf16[49,1536]{1,0:T(8,128)(2,1)S(1)} %copy-done.50), custom_call_target="tpu_custom_call" | custom-call | bytes 110592 | tf_op jit(solution)/shard_map/pallas_call | solution.py:147
  114.2 2.2 constant_dynamic-update-slice_fusion.6
  116.4 6.7 %collective-permute-done.23 = bf16[16,16,3072]{2,1,0:T(8,128)(2,1)} collective-permute-done((bf16[16,16,3072]{2,1,0:T(8,128)(2,1)}, bf16[16,16,3072]{2,1,0:T(8,128)(2,1)}, u32[]{:S(2)}, u32[]{:S(2)}) %collective-permute-start.23) | collective-permute-done | bytes 1572896 | tf_op jit(solution)/shard_map/ppermute | solution.py:675
  123.0 2.5 collective-permute-done.24
  125.6 3.4 collective-permute-done.27.refs_5_
  133.2 3.5 collective-permute-done.28
  137.5 2.2 collective-permute-start.29
  142.0 4.6 shard_map.359
  146.6 2.2 copy-done.6
  153.1 4.5 shard_map.360.refs_4_
  159.3 3.4 collective-permute-start.31
  164.1 5.7 %collective-permute-done.31.refs_2_ = bf16[144,1024]{1,0:T(8,128)(2,1)S(1)} collective-permute-done((bf16[144,1024]{1,0:T(8,128)(2,1)S(1)}, bf16[144,1024]{1,0:T(8,128)(2,1)S(1)}, u32[]{:S(2)}, u32[]{:S(2)}) %collective-permute-start.31) | collective-permute-done | bytes 294944 | tf_op jit(solution)/shard_map/ppermute | solution.py:793
  178.0 2.7 collective-permute-start.33
  180.8 10.6 %fusion.4 = (bf16[1152,1536]{1,0:T(8,128)(2,1)}, bf16[1152,1536]{1,0:T(8,128)(2,1)}) fusion(bf16[1536,1536]{1,0:T(8,128)(2,1)S(1)} %bitcast.135, bf16[576,1536]{1,0:T(8,128)(2,1)S(1)} %collective-permute-done.35.refs_1_, bf16[576,1536]{1,0:T(8,128)(2,1)S(1)} %shard_map.357.refs_0_), kind=kOutput, calls=%fused_computation.5 | convolution fusion | flops 5462360064 | bytes 15335424 | tf_op jit(solution)/shard_map/dot_general | solution.py:818
  192.7 12.4 %shard_map.363 = (f32[576,1536]{1,0:T(8,128)S(1)}, bf16[576,1536]{1,0:T(8,128)(2,1)S(1)}) custom-call(bf16[1152,1536]{1,0:T(8,128)(2,1)} %get-tuple-element.191.refs_0_.refs_5_, bf16[1536,1536]{1,0:T(8,128)(2,1)} %bitcast.130), custom_call_target="tpu_custom_call" | custom-call | bytes 1048576 | tf_op jit(solution)/shard_map/pallas_call | solution.py:494
  206.9 3.2 collective-permute-done.36
  211.9 8.2 %collective-permute-done.37.pool_other_ref = bf16[6,24,1536]{2,1,0:T(8,128)(2,1)S(1)} collective-permute-done((bf16[6,24,1536]{2,1,0:T(8,128)(2,1)S(1)}, bf16[6,24,1536]{2,1,0:T(8,128)(2,1)S(1)}, u32[]{:S(2)}, u32[]{:S(2)}) %collective-permute-start.37) | collective-permute-done | bytes 442400 | tf_op jit(solution)/shard_map/ppermute | solution.py:793
  220.1 3.8 shard_map.364
  230.5 9.3 %shard_map.365.refs_0_.refs_4_ = bf16[1152,1536]{1,0:T(8,128)(2,1)S(1)} custom-call(bf16[576,1536]{1,0:T(8,128)(2,1)} %bitcast.32.refs_0_.refs_2_, bf16[576,1536]{1,0:T(8,128)(2,1)} %collective-permute-done.38.refs_1_.refs_3_, bf16[1536,1536]{1,0:T(8,128)(2,1)} %bitcast.131, bf16[1152,1536]{1,0:T(8,128)(2,1)} %get-tuple-element.326.refs_3_), custom_call_target="tpu_custom_call" | custom-call | bytes 1048576 | tf_op jit(solution)/shard_map/pallas_call | solution.py:494
  244.8 12.6 %shard_map.367 = (f32[576,1536]{1,0:T(8,128)S(1)}, bf16[576,1536]{1,0:T(8,128)(2,1)S(1)}) custom-call(bf16[1152,1536]{1,0:T(8,128)(2,1)} %copy-done, bf16[1536,1536]{1,0:T(8,128)(2,1)} %bitcast.136), custom_call_target="tpu_custom_call" | custom-call | bytes 1048576 | tf_op jit(solution)/shard_map/pallas_call | solution.py:494
  260.4 8.9 %collective-permute-done.41.other_ref = bf16[12,48,1536]{2,1,0:T(8,128)(2,1)} collective-permute-done((bf16[12,48,1536]{2,1,0:T(8,128)(2,1)}, bf16[12,48,1536]{2,1,0:T(8,128)(2,1)}, u32[]{:S(2)}, u32[]{:S(2)}) %collective-permute-start.41) | collective-permute-done | bytes 1769504 | tf_op jit(solution)/shard_map/ppermute | solution.py:793
  269.4 5.4 %shard_map.368 = (bf16[12,48,1536]{2,1,0:T(8,128)(2,1)}, bf16[6,24,1536]{2,1,0:T(8,128)(2,1)S(1)}, f32[1,1536]{1,0:T(1,128)S(1)}) custom-call(s32[2]{0:T(128)S(1)} %copy-done.73, bf16[12,48,1536]{2,1,0:T(8,128)(2,1)} %bitcast.30.own_ref, bf16[12,48,1536]{2,1,0:T(8,128)(2,1)} %collective-permute-done.41.other_ref, bf16[12,48,1536]{2,1,0:T(8,128)(2,1)S(1)} %bitcast.129, ...), custom_call_target="tpu_custom_call" | custom-call | bytes 1048576 | tf_op jit(solution)/shard_map/pallas_call | solution.py:255
  280.1 3.0 collective-permute-start.42
  285.1 2.2 collective-permute-done.42
  287.4 2.3 multiply_add_fusion
  291.9 2.5 fusion.20
  295.1 4.8 shard_map.369
  300.4 2.4 convolution_convert_fusion.3
  305.8 3.0 collective-permute-start.44
  308.9 2.1 add_convert_fusion.own_ref
  311.0 4.2 collective-permute-done.44.other_ref
  321.2 7.0 %shard_map.371 = (bf16[144,512]{1,0:T(8,128)(2,1)S(1)}, f32[576,512]{1,0:T(8,128)S(1)}, f32[576,512]{1,0:T(8,128)S(1)}) custom-call(bf16[144,1536]{1,0:T(8,128)(2,1)S(1)} %copy-done.13, bf16[576,1024]{1,0:T(8,128)(2,1)S(1)} %copy-done.2, bf16[576,1024]{1,0:T(8,128)(2,1)S(1)} %copy-done.2, bf16[144,512]{1,0:T(8,128)(2,1)S(1)} %fusion.63.grad_ref), custom_call_target="tpu_custom_call" | custom-call | bytes 1048576 | tf_op jit(solution)/shard_map/pallas_call | solution.py:378
  328.2 3.1 collective-permute-start.48
  336.6 28.3 %shard_map.372 = (bf16[16,48,1152]{2,1,0:T(8,128)(2,1)S(1)}, bf16[16,48,1152]{2,1,0:T(8,128)(2,1)}, bf16[16,48,1152]{2,1,0:T(8,128)(2,1)S(1)}, bf16[16,48,1152]{...) custom-call(s32[1]{0:T(128)} %bitcast.19.place, bf16[576,1536]{1,0:T(8,128)(2,1)S(1)} %copy-done.11, ...), custom_call_target="tpu_custom_call" | custom-call | bytes 1048576 | tf_op jit(solution)/shard_map/pallas_call | solution.py:1024
  365.0 5.8 %slice_add_fusion.2 = (bf16[16,16,3072]{2,1,0:T(8,128)(2,1)}, bf16[16,16,3072]{2,1,0:T(8,128)(2,1)}) fusion(bf16[32,16,3072]{2,1,0:T(8,128)(2,1)} %collective-permute-done.49, bf16[32,16,3072]{2,1,0:T(8,128)(2,1)S(1)} %bitcast.138), kind=kLoop, calls=%fused_computation.54 | loop fusion | flops 1572864 | bytes 9437184 | tf_op jit(solution)/shard_map/add | solution.py:711
  370.8 5.6 %collective-permute-done.48.other_ref = bf16[576,1536]{1,0:T(8,128)(2,1)S(1)} collective-permute-done((bf16[576,1536]{1,0:T(8,128)(2,1)S(1)}, bf16[576,1536]{1,0:T(8,128)(2,1)S(1)}, u32[]{:S(2)}, u32[]{:S(2)}) %collective-permute-start.48) | collective-permute-done | bytes 1769504 | tf_op jit(solution)/shard_map/ppermute | solution.py:793
  377.5 2.9 shard_map.374
  380.5 3.8 shard_map.375
  387.5 3.0 collective-permute-start.51
  391.6 4.5 collective-permute-done.55.low_ref
  396.1 7.2 %collective-permute-done.56.high_ref = bf16[3,48,1536]{2,1,0:T(8,128)(2,1)S(1)} collective-permute-done((bf16[3,48,1536]{2,1,0:T(8,128)(2,1)S(1)}, bf16[3,48,1536]{2,1,0:T(8,128)(2,1)S(1)}, u32[]{:S(2)}, u32[]{:S(2)}) %collective-permute-start.56) | collective-permute-done | bytes 442400 | tf_op jit(solution)/shard_map/ppermute | solution.py:807
  403.3 4.1 collective-permute-start.59
  407.5 2.1 slice_add_fusion
  411.7 17.9 %shard_map.377 = f32[49,1536]{1,0:T(8,128)S(1)} custom-call(s32[2]{0:T(128)S(1)} %copy-done.74, bf16[12,48,1536]{2,1,0:T(8,128)(2,1)} %bitcast.126, bf16[3,48,1536]{2,1,0:T(8,128)(2,1)} %copy-done.26, bf16[3,48,1536]{2,1,0:T(8,128)(2,1)} %copy-done.28, bf16[12,48,1536]{2,1,0:T(8,128)(2,1)} %bitcast.133), custom_call_target="tpu_custom_call" | custom-call | bytes 110592 | tf_op jit(solution)/shard_map/pallas_call | solution.py:167
  432.0 4.2 all-to-all-start
  436.2 16.6 %shard_map.376 = f32[12,48,1536]{2,1,0:T(8,128)} custom-call(s32[2]{0:T(128)S(1)} %copy-done.74, bf16[12,48,1536]{2,1,0:T(8,128)(2,1)} %bitcast.134, bf16[3,48,1536]{2,1,0:T(8,128)(2,1)} %copy-done.99, bf16[3,48,1536]{2,1,0:T(8,128)(2,1)} %copy-done.100, bf16[49,1536]{1,0:T(8,128)(2,1)} %taps_in.3, f32[12,48,1536]{2,1,0:T(8,128)} %copy-done.7), custom_call_target="tpu_custom_call" | custom-call | bytes 110592 | tf_op jit(solution)/shard_map/pallas_call | solution.py:147
  457.7 2.5 collective-permute-start.63
  468.6 21.7 %all_to_all.10 = bf16[64,16,128]{2,1,0:T(8,128)(2,1)S(1)} all-to-all(bf16[64,16,128]{2,1,0:T(8,128)(2,1)S(1)} %broadcast_in_dim.76), channel_id=1, replica_groups=mesh['dp'=64,'mp'=2] {'dp'}, dimensions={0} | all-to-all | bytes 524288 | tf_op jit(solution)/shard_map/all_to_all | solution.py:1075
  493.3 2.0 collective-permute-start.66
  495.7 6.2 %collective-permute-done.69 = bf16[4,48,1024]{2,1,0:T(8,128)(2,1)S(1)} collective-permute-done((bf16[4,48,1024]{2,1,0:T(8,128)(2,1)S(1)}, bf16[4,48,1024]{2,1,0:T(8,128)(2,1)S(1)}, u32[]{:S(2)}, u32[]{:S(2)}) %collective-permute-start.69) | collective-permute-done | bytes 393248 | tf_op jit(solution)/shard_map/ppermute | solution.py:675
  501.9 2.3 collective-permute-done.66
  507.6 2.1 collective-permute-start.70
  510.4 2.0 collective-permute-done.71
  523.3 7.1 %collective-permute-start.80 = (bf16[24,3328]{1,0:T(8,128)(2,1)S(1)}, bf16[24,3328]{1,0:T(8,128)(2,1)S(1)}, u32[]{:S(2)}, u32[]{:S(2)}) collective-permute-start(bf16[24,3328]{1,0:T(8,128)(2,1)S(1)} %select_convert_fusion.1), channel_id=1, source_target_pairs={{0,2},{2,0},{4,6},{6,4},{8,10},{10,8},{12,14},{14,12},{16,18},{18,... | collective-permute-start | bytes 479240 | tf_op jit(solution)/shard_map/ppermute | solution.py:675
  (535 shorter events, 155.9 us)
Async XLA Ops:
  5.2 7.0 %collective-permute-start.1 = (bf16[1,16,3072]{2,1,0:T(8,128)(2,1)S(1)}, bf16[1,16,3072]{2,1,0:T(8,128)(2,1)S(1)}, u32[]{:S(2)}, u32[]{:S(2)}) collective-permute-start(bf16[1,16,3072]{2,1,0:T(8,128)(2,1)S(1)} %maximum_bitcast_fusion), channel_id=1, source_target_pairs={{0,12},{2,14},{4,8},{6,10},{8,4},{10,6},{12,0},{14,2},{16,28},{18,... | collective-permute-start | bytes 294920 | tf_op jit(solution)/shard_map/ppermute | solution.py:675
  25.2 7.3 %collective-permute-start.10 = (bf16[2,48,1024]{2,1,0:T(8,128)(2,1)S(1)}, bf16[2,48,1024]{2,1,0:T(8,128)(2,1)S(1)}, u32[]{:S(2)}, u32[]{:S(2)}) collective-permute-start(bf16[2,48,1024]{2,1,0:T(8,128)(2,1)S(1)} %pad_maximum_fusion.25), channel_id=1, source_target_pairs={{0,4},{2,6},{4,0},{6,2},{8,12},{10,14},{12,8},{14,10},{16,20},{18,... | collective-permute-start | bytes 589832 | tf_op jit(solution)/shard_map/ppermute | solution.py:675
  25.3 7.2 %collective-permute-start.9 = (bf16[2,48,1152]{2,1,0:T(8,128)(2,1)S(1)}, bf16[2,48,1152]{2,1,0:T(8,128)(2,1)S(1)}, u32[]{:S(2)}, u32[]{:S(2)}) collective-permute-start(bf16[2,48,1152]{2,1,0:T(8,128)(2,1)S(1)} %pad_maximum_fusion.22), channel_id=1, source_target_pairs={{0,64},{2,66},{4,68},{6,70},{8,72},{10,74},{12,76},{14,78},{16,80}... | collective-permute-start | bytes 663560 | tf_op jit(solution)/shard_map/ppermute | solution.py:675
  25.4 7.2 %collective-permute-start.8 = (bf16[2,48,1152]{2,1,0:T(8,128)(2,1)S(1)}, bf16[2,48,1152]{2,1,0:T(8,128)(2,1)S(1)}, u32[]{:S(2)}, u32[]{:S(2)}) collective-permute-start(bf16[2,48,1152]{2,1,0:T(8,128)(2,1)S(1)} %pad_maximum_fusion.21), channel_id=1, source_target_pairs={{0,48},{2,50},{4,52},{6,54},{8,56},{10,58},{12,60},{14,62},{16,32}... | collective-permute-start | bytes 663560 | tf_op jit(solution)/shard_map/ppermute | solution.py:675
  32.6 8.3 %collective-permute-start.12 = (bf16[4,16,3072]{2,1,0:T(8,128)(2,1)S(1)}, bf16[4,16,3072]{2,1,0:T(8,128)(2,1)S(1)}, u32[]{:S(2)}, u32[]{:S(2)}) collective-permute-start(bf16[4,16,3072]{2,1,0:T(8,128)(2,1)S(1)} %pad_maximum_fusion.18), channel_id=1, source_target_pairs={{0,48},{2,50},{4,52},{6,54},{8,56},{10,58},{12,60},{14,62},{16,32}... | collective-permute-start | bytes 1179656 | tf_op jit(solution)/shard_map/ppermute | solution.py:675
  34.4 6.9 %collective-permute-start.11 = (bf16[4,16,3072]{2,1,0:T(8,128)(2,1)S(1)}, bf16[4,16,3072]{2,1,0:T(8,128)(2,1)S(1)}, u32[]{:S(2)}, u32[]{:S(2)}) collective-permute-start(bf16[4,16,3072]{2,1,0:T(8,128)(2,1)S(1)} %pad_maximum_fusion.17), channel_id=1, source_target_pairs={{0,16},{2,18},{4,20},{6,22},{8,24},{10,26},{12,28},{14,30},{16,0},... | collective-permute-start | bytes 1179656 | tf_op jit(solution)/shard_map/ppermute | solution.py:675
  34.4 8.1 %collective-permute-start.15 = (bf16[4,48,1024]{2,1,0:T(8,128)(2,1)S(1)}, bf16[4,48,1024]{2,1,0:T(8,128)(2,1)S(1)}, u32[]{:S(2)}, u32[]{:S(2)}) collective-permute-start(bf16[4,48,1024]{2,1,0:T(8,128)(2,1)S(1)} %pad_maximum_fusion.19), channel_id=1, source_target_pairs={{0,12},{2,14},{4,8},{6,10},{8,4},{10,6},{12,0},{14,2},{16,28},{18,... | collective-permute-start | bytes 1179656 | tf_op jit(solution)/shard_map/ppermute | solution.py:675
  35.1 7.6 %collective-permute-start.14 = (bf16[4,48,1152]{2,1,0:T(8,128)(2,1)S(1)}, bf16[4,48,1152]{2,1,0:T(8,128)(2,1)S(1)}, u32[]{:S(2)}, u32[]{:S(2)}) collective-permute-start(bf16[4,48,1152]{2,1,0:T(8,128)(2,1)S(1)} %pad_maximum_fusion.15), channel_id=1, source_target_pairs={{0,4},{2,6},{4,0},{6,2},{8,12},{10,14},{12,8},{14,10},{16,20},{18,... | collective-permute-start | bytes 1327112 | tf_op jit(solution)/shard_map/ppermute | solution.py:675
  35.1 7.7 %collective-permute-start.13 = (bf16[4,48,1152]{2,1,0:T(8,128)(2,1)S(1)}, bf16[4,48,1152]{2,1,0:T(8,128)(2,1)S(1)}, u32[]{:S(2)}, u32[]{:S(2)}) collective-permute-start(bf16[4,48,1152]{2,1,0:T(8,128)(2,1)S(1)} %pad_maximum_fusion.14), channel_id=1, source_target_pairs={{0,64},{2,66},{4,68},{6,70},{8,72},{10,74},{12,76},{14,78},{16,80}... | collective-permute-start | bytes 1327112 | tf_op jit(solution)/shard_map/ppermute | solution.py:675
  42.9 15.7 %collective-permute-start.17 = (bf16[8,16,3072]{2,1,0:T(8,128)(2,1)S(1)}, bf16[8,16,3072]{2,1,0:T(8,128)(2,1)S(1)}, u32[]{:S(2)}, u32[]{:S(2)}) collective-permute-start(bf16[8,16,3072]{2,1,0:T(8,128)(2,1)S(1)} %pad_maximum_fusion.10), channel_id=1, source_target_pairs={{0,64},{2,66},{4,68},{6,70},{8,72},{10,74},{12,76},{14,78},{16,80}... | collective-permute-start | bytes 2359304 | tf_op jit(solution)/shard_map/ppermute | solution.py:675
  44.3 16.9 %collective-permute-start.20 = (bf16[8,48,1024]{2,1,0:T(8,128)(2,1)S(1)}, bf16[8,48,1024]{2,1,0:T(8,128)(2,1)S(1)}, u32[]{:S(2)}, u32[]{:S(2)}) collective-permute-start(bf16[8,48,1024]{2,1,0:T(8,128)(2,1)S(1)} %pad_maximum_fusion.11), channel_id=1, source_target_pairs={{0,16},{2,18},{4,20},{6,22},{8,24},{10,26},{12,28},{14,30},{16,0},... | collective-permute-start | bytes 2359304 | tf_op jit(solution)/shard_map/ppermute | solution.py:675
  45.7 25.9 %collective-permute-start.16 = (bf16[8,16,3072]{2,1,0:T(8,128)(2,1)S(1)}, bf16[8,16,3072]{2,1,0:T(8,128)(2,1)S(1)}, u32[]{:S(2)}, u32[]{:S(2)}) collective-permute-start(bf16[8,16,3072]{2,1,0:T(8,128)(2,1)S(1)} %pad_maximum_fusion.9), channel_id=1, source_target_pairs={{0,48},{2,50},{4,52},{6,54},{8,56},{10,58},{12,60},{14,62},{16,32}... | collective-permute-start | bytes 2359304 | tf_op jit(solution)/shard_map/ppermute | solution.py:675
  46.5 39.1 %collective-permute-start.21 = (bf16[3,48,1536]{2,1,0:T(8,128)(2,1)S(1)}, bf16[3,48,1536]{2,1,0:T(8,128)(2,1)S(1)}, u32[]{:S(2)}, u32[]{:S(2)}) collective-permute-start(bf16[3,48,1536]{2,1,0:T(8,128)(2,1)S(1)} %get-tuple-element.351), channel_id=1, source_target_pairs={{0,2},{2,4},{4,6},{6,8},{8,10},{10,12},{12,14},{14,16},{16,18},{18... | collective-permute-start | bytes 1327112 | tf_op jit(solution)/shard_map/ppermute | solution.py:806
  57.8 25.0 %collective-permute-start.19 = (bf16[8,48,1152]{2,1,0:T(8,128)(2,1)S(1)}, bf16[8,48,1152]{2,1,0:T(8,128)(2,1)S(1)}, u32[]{:S(2)}, u32[]{:S(2)}) collective-permute-start(bf16[8,48,1152]{2,1,0:T(8,128)(2,1)S(1)} %pad_maximum_fusion.8), channel_id=1, source_target_pairs={{0,12},{2,14},{4,8},{6,10},{8,4},{10,6},{12,0},{14,2},{16,28},{18,... | collective-permute-start | bytes 2654216 | tf_op jit(solution)/shard_map/ppermute | solution.py:675
  58.6 25.6 %collective-permute-start.18 = (bf16[8,48,1152]{2,1,0:T(8,128)(2,1)S(1)}, bf16[8,48,1152]{2,1,0:T(8,128)(2,1)S(1)}, u32[]{:S(2)}, u32[]{:S(2)}) collective-permute-start(bf16[8,48,1152]{2,1,0:T(8,128)(2,1)S(1)} %pad_maximum_fusion.7), channel_id=1, source_target_pairs={{0,4},{2,6},{4,0},{6,2},{8,12},{10,14},{12,8},{14,10},{16,20},{18,... | collective-permute-start | bytes 2654216 | tf_op jit(solution)/shard_map/ppermute | solution.py:675
  61.2 25.2 %collective-permute-start.22 = (bf16[3,48,1536]{2,1,0:T(8,128)(2,1)S(1)}, bf16[3,48,1536]{2,1,0:T(8,128)(2,1)S(1)}, u32[]{:S(2)}, u32[]{:S(2)}) collective-permute-start(bf16[3,48,1536]{2,1,0:T(8,128)(2,1)S(1)} %get-tuple-element.350), channel_id=1, source_target_pairs={{2,0},{4,2},{6,4},{8,6},{10,8},{12,10},{14,12},{16,14},{18,16},{20... | collective-permute-start | bytes 1327112 | tf_op jit(solution)/shard_map/ppermute | solution.py:807
  87.1 41.8 %collective-permute-start.25 = (bf16[16,48,1152]{2,1,0:T(8,128)(2,1)}, bf16[16,48,1152]{2,1,0:T(8,128)(2,1)}, u32[]{:S(2)}, u32[]{:S(2)}) collective-permute-start(bf16[16,48,1152]{2,1,0:T(8,128)(2,1)} %pad_maximum_fusion.refs_0_), channel_id=1, source_target_pairs={{0,12},{2,14},{4,8},{6,10},{8,4},{10,6},{12,0},{14,2},{16,28},{18,... | collective-permute-start | bytes 5308424 | tf_op jit(solution)/shard_map/ppermute | solution.py:675
  87.1 41.8 %collective-permute-start.26 = (bf16[16,48,1152]{2,1,0:T(8,128)(2,1)}, bf16[16,48,1152]{2,1,0:T(8,128)(2,1)}, u32[]{:S(2)}, u32[]{:S(2)}) collective-permute-start(bf16[16,48,1152]{2,1,0:T(8,128)(2,1)} %pad_maximum_fusion.1.refs_2_), channel_id=1, source_target_pairs={{0,16},{2,18},{4,20},{6,22},{8,24},{10,26},{12,28},{14,30},{16,0},... | collective-permute-start | bytes 5308424 | tf_op jit(solution)/shard_map/ppermute | solution.py:675
  88.0 35.0 %collective-permute-start.23 = (bf16[16,16,3072]{2,1,0:T(8,128)(2,1)}, bf16[16,16,3072]{2,1,0:T(8,128)(2,1)}, u32[]{:S(2)}, u32[]{:S(2)}) collective-permute-start(bf16[16,16,3072]{2,1,0:T(8,128)(2,1)} %pad_maximum_fusion.2), channel_id=1, source_target_pairs={{0,64},{2,66},{4,68},{6,70},{8,72},{10,74},{12,76},{14,78},{16,80}... | collective-permute-start | bytes 4718600 | tf_op jit(solution)/shard_map/ppermute | solution.py:675
  89.2 36.4 %collective-permute-start.24 = (bf16[16,16,3072]{2,1,0:T(8,128)(2,1)}, bf16[16,16,3072]{2,1,0:T(8,128)(2,1)}, u32[]{:S(2)}, u32[]{:S(2)}) collective-permute-start(bf16[16,16,3072]{2,1,0:T(8,128)(2,1)} %pad_maximum_fusion.3), channel_id=1, source_target_pairs={{0,4},{2,6},{4,0},{6,2},{8,12},{10,14},{12,8},{14,10},{16,20},{18,... | collective-permute-start | bytes 4718600 | tf_op jit(solution)/shard_map/ppermute | solution.py:675
  91.1 37.8 %collective-permute-start.27 = (bf16[16,48,1024]{2,1,0:T(8,128)(2,1)}, bf16[16,48,1024]{2,1,0:T(8,128)(2,1)}, u32[]{:S(2)}, u32[]{:S(2)}) collective-permute-start(bf16[16,48,1024]{2,1,0:T(8,128)(2,1)} %pad_maximum_fusion.4.refs_4_), channel_id=1, source_target_pairs={{0,48},{2,50},{4,52},{6,54},{8,56},{10,58},{12,60},{14,62},{16,32}... | collective-permute-start | bytes 4718600 | tf_op jit(solution)/shard_map/ppermute | solution.py:675
  137.5 12.5 %collective-permute-start.29 = (bf16[144,1024]{1,0:T(8,128)(2,1)S(1)}, bf16[144,1024]{1,0:T(8,128)(2,1)S(1)}, u32[]{:S(2)}, u32[]{:S(2)}) collective-permute-start(bf16[144,1024]{1,0:T(8,128)(2,1)S(1)} %slice.675), channel_id=1, source_target_pairs={{0,124},{2,126},{4,8},{6,10},{8,4},{10,6},{12,16},{14,18},{16,12},... | collective-permute-start | bytes 884744 | tf_op jit(solution)/shard_map/ppermute | solution.py:839
  141.2 31.8 %collective-permute-start.32 = (bf16[32,16,3072]{2,1,0:T(8,128)(2,1)S(1)}, bf16[32,16,3072]{2,1,0:T(8,128)(2,1)S(1)}, u32[]{:S(2)}, u32[]{:S(2)}) collective-permute-start(bf16[32,16,3072]{2,1,0:T(8,128)(2,1)S(1)} %constant_dynamic-update-slice_fusion.7), channel_id=1, source_target_pairs={{0,2},{2,0},{4,6},{6,4},{8,10},{10,8},{12,14},{14,12},{16,18},{18,... | collective-permute-start | bytes 9437192 | tf_op jit(solution)/shard_map/ppermute | solution.py:675
  159.3 10.4 %collective-permute-start.31 = (bf16[144,1024]{1,0:T(8,128)(2,1)S(1)}, bf16[144,1024]{1,0:T(8,128)(2,1)S(1)}, u32[]{:S(2)}, u32[]{:S(2)}) collective-permute-start(bf16[144,1024]{1,0:T(8,128)(2,1)S(1)} %fusion.50.refs_1_), channel_id=1, source_target_pairs={{0,1},{1,0},{2,3},{3,2},{4,5},{5,4},{6,7},{7,6},{8,9},{9,8},{10,11... | collective-permute-start | bytes 884744 | tf_op jit(solution)/shard_map/ppermute | solution.py:793
  162.8 18.0 %collective-permute-start.35 = (bf16[576,1536]{1,0:T(8,128)(2,1)S(1)}, bf16[576,1536]{1,0:T(8,128)(2,1)S(1)}, u32[]{:S(2)}, u32[]{:S(2)}) collective-permute-start(bf16[576,1536]{1,0:T(8,128)(2,1)S(1)} %shard_map.357.refs_0_), channel_id=1, source_target_pairs={{0,2},{2,0},{4,6},{6,4},{8,10},{10,8},{12,14},{14,12},{16,18},{18,... | collective-permute-start | bytes 5308424 | tf_op jit(solution)/shard_map/ppermute | solution.py:675
  163.5 28.1 %collective-permute-start.34 = (bf16[1536,256]{1,0:T(8,128)(2,1)S(1)}, bf16[1536,256]{1,0:T(8,128)(2,1)S(1)}, u32[]{:S(2)}, u32[]{:S(2)}) collective-permute-start(bf16[1536,256]{1,0:T(8,128)(2,1)S(1)} %bitcast.151), channel_id=1, source_target_pairs={{0,2},{2,0},{4,6},{6,4},{8,10},{10,8},{12,14},{14,12},{16,18},{18,... | collective-permute-start | bytes 2359304 | tf_op jit(solution)/shard_map/ppermute | solution.py:675
  178.0 13.3 %collective-permute-start.33 = (bf16[144,1024]{1,0:T(8,128)(2,1)S(1)}, bf16[144,1024]{1,0:T(8,128)(2,1)S(1)}, u32[]{:S(2)}, u32[]{:S(2)}) collective-permute-start(bf16[144,1024]{1,0:T(8,128)(2,1)S(1)} %fusion.55.own_ref), channel_id=1, source_target_pairs={{0,1},{1,0},{2,3},{3,2},{4,5},{5,4},{6,7},{7,6},{8,9},{9,8},{10,11... | collective-permute-start | bytes 884744 | tf_op jit(solution)/shard_map/ppermute | solution.py:793
  206.8 13.4 %collective-permute-start.37 = (bf16[6,24,1536]{2,1,0:T(8,128)(2,1)S(1)}, bf16[6,24,1536]{2,1,0:T(8,128)(2,1)S(1)}, u32[]{:S(2)}, u32[]{:S(2)}) collective-permute-start(bf16[6,24,1536]{2,1,0:T(8,128)(2,1)S(1)} %bitcast.148), channel_id=1, source_target_pairs={{0,1},{1,0},{2,3},{3,2},{4,5},{5,4},{6,7},{7,6},{8,9},{9,8},{10,11... | collective-permute-start | bytes 1327112 | tf_op jit(solution)/shard_map/ppermute | solution.py:793
  226.5 42.7 %collective-permute-start.41 = (bf16[12,48,1536]{2,1,0:T(8,128)(2,1)}, bf16[12,48,1536]{2,1,0:T(8,128)(2,1)}, u32[]{:S(2)}, u32[]{:S(2)}) collective-permute-start(bf16[12,48,1536]{2,1,0:T(8,128)(2,1)} %bitcast.30.own_ref), channel_id=1, source_target_pairs={{0,1},{1,0},{2,3},{3,2},{4,5},{5,4},{6,7},{7,6},{8,9},{9,8},{10,11... | collective-permute-start | bytes 5308424 | tf_op jit(solution)/shard_map/ppermute | solution.py:793
  242.3 32.5 %collective-permute-start.39 = (bf16[1,24,1024]{2,1,0:T(8,128)(2,1)}, bf16[1,24,1024]{2,1,0:T(8,128)(2,1)}, u32[]{:S(2)}, u32[]{:S(2)}) collective-permute-start(bf16[1,24,1024]{2,1,0:T(8,128)(2,1)} %get-tuple-element.384), channel_id=1, source_target_pairs={{0,2},{2,4},{4,6},{6,8},{8,10},{10,12},{12,14},{14,16},{16,18},{18... | collective-permute-start | bytes 147464 | tf_op jit(solution)/shard_map/ppermute | solution.py:806
  242.3 32.5 %collective-permute-start.40 = (bf16[1,24,1024]{2,1,0:T(8,128)(2,1)}, bf16[1,24,1024]{2,1,0:T(8,128)(2,1)}, u32[]{:S(2)}, u32[]{:S(2)}) collective-permute-start(bf16[1,24,1024]{2,1,0:T(8,128)(2,1)} %get-tuple-element.383), channel_id=1, source_target_pairs={{2,0},{4,2},{6,4},{8,6},{10,8},{12,10},{14,12},{16,14},{18,16},{20... | collective-permute-start | bytes 147464 | tf_op jit(solution)/shard_map/ppermute | solution.py:807
  279.1 29.8 %collective-permute-start.45 = (bf16[576,1536]{1,0:T(8,128)(2,1)}, bf16[576,1536]{1,0:T(8,128)(2,1)}, u32[]{:S(2)}, u32[]{:S(2)}) collective-permute-start(bf16[576,1536]{1,0:T(8,128)(2,1)} %copy-done.80), channel_id=1, source_target_pairs={{0,2},{2,0},{4,6},{6,4},{8,10},{10,8},{12,14},{14,12},{16,18},{18,... | collective-permute-start | bytes 5308424 | tf_op jit(solution)/shard_map/ppermute | solution.py:675
  280.1 7.3 %collective-permute-start.42 = (bf16[6,24,512]{2,1,0:T(8,128)(2,1)}, bf16[6,24,512]{2,1,0:T(8,128)(2,1)}, u32[]{:S(2)}, u32[]{:S(2)}) collective-permute-start(bf16[6,24,512]{2,1,0:T(8,128)(2,1)} %get-tuple-element.391), channel_id=1, source_target_pairs={{0,1},{1,0},{2,3},{3,2},{4,5},{5,4},{6,7},{7,6},{8,9},{9,8},{10,11... | collective-permute-start | bytes 442376 | tf_op jit(solution)/shard_map/ppermute | solution.py:793
  305.8 9.3 %collective-permute-start.44 = (bf16[144,1024]{1,0:T(8,128)(2,1)S(1)}, bf16[144,1024]{1,0:T(8,128)(2,1)S(1)}, u32[]{:S(2)}, u32[]{:S(2)}) collective-permute-start(bf16[144,1024]{1,0:T(8,128)(2,1)S(1)} %fusion.57.own_ref), channel_id=1, source_target_pairs={{0,1},{1,0},{2,3},{3,2},{4,5},{5,4},{6,7},{7,6},{8,9},{9,8},{10,11... | collective-permute-start | bytes 884744 | tf_op jit(solution)/shard_map/ppermute | solution.py:793
  315.1 49.8 %collective-permute-start.49 = (bf16[32,16,3072]{2,1,0:T(8,128)(2,1)}, bf16[32,16,3072]{2,1,0:T(8,128)(2,1)}, u32[]{:S(2)}, u32[]{:S(2)}) collective-permute-start(bf16[32,16,3072]{2,1,0:T(8,128)(2,1)} %bitcast.42), channel_id=1, source_target_pairs={{0,2},{2,0},{4,6},{6,4},{8,10},{10,8},{12,14},{14,12},{16,18},{18,... | collective-permute-start | bytes 9437192 | tf_op jit(solution)/shard_map/ppermute | solution.py:675
  317.7 14.7 %collective-permute-start.50 = (bf16[1536,256]{1,0:T(8,128)(2,1)S(1)}, bf16[1536,256]{1,0:T(8,128)(2,1)S(1)}, u32[]{:S(2)}, u32[]{:S(2)}) collective-permute-start(bf16[1536,256]{1,0:T(8,128)(2,1)S(1)} %select_convert_fusion), channel_id=1, source_target_pairs={{0,2},{2,0},{4,6},{6,4},{8,10},{10,8},{12,14},{14,12},{16,18},{18,... | collective-permute-start | bytes 2359304 | tf_op jit(solution)/shard_map/ppermute | solution.py:675
  328.2 48.2 %collective-permute-start.48 = (bf16[576,1536]{1,0:T(8,128)(2,1)S(1)}, bf16[576,1536]{1,0:T(8,128)(2,1)S(1)}, u32[]{:S(2)}, u32[]{:S(2)}) collective-permute-start(bf16[576,1536]{1,0:T(8,128)(2,1)S(1)} %add_convert_fusion.own_ref), channel_id=1, source_target_pairs={{0,1},{1,0},{2,3},{3,2},{4,5},{5,4},{6,7},{7,6},{8,9},{9,8},{10,11... | collective-permute-start | bytes 5308424 | tf_op jit(solution)/shard_map/ppermute | solution.py:793
  335.1 35.7 %collective-permute-start.47 = (bf16[144,1024]{1,0:T(8,128)(2,1)}, bf16[144,1024]{1,0:T(8,128)(2,1)}, u32[]{:S(2)}, u32[]{:S(2)}) collective-permute-start(bf16[144,1024]{1,0:T(8,128)(2,1)} %slice.969), channel_id=1, source_target_pairs={{0,124},{2,126},{4,8},{6,10},{8,4},{10,6},{12,16},{14,18},{16,12},... | collective-permute-start | bytes 884744 | tf_op jit(solution)/shard_map/ppermute | solution.py:839
  384.3 19.1 %collective-permute-start.52 = (bf16[32,16,3072]{2,1,0:T(8,128)(2,1)S(1)}, bf16[32,16,3072]{2,1,0:T(8,128)(2,1)S(1)}, u32[]{:S(2)}, u32[]{:S(2)}) collective-permute-start(bf16[32,16,3072]{2,1,0:T(8,128)(2,1)S(1)} %bitcast.150), channel_id=1, source_target_pairs={{0,2},{2,0},{4,6},{6,4},{8,10},{10,8},{12,14},{14,12},{16,18},{18,... | collective-permute-start | bytes 9437192 | tf_op jit(solution)/shard_map/ppermute | solution.py:675
  387.5 22.1 %collective-permute-start.51 = (bf16[144,1024]{1,0:T(8,128)(2,1)S(1)}, bf16[144,1024]{1,0:T(8,128)(2,1)S(1)}, u32[]{:S(2)}, u32[]{:S(2)}) collective-permute-start(bf16[144,1024]{1,0:T(8,128)(2,1)S(1)} %fusion.53.own_ref), channel_id=1, source_target_pairs={{0,1},{1,0},{2,3},{3,2},{4,5},{5,4},{6,7},{7,6},{8,9},{9,8},{10,11... | collective-permute-start | bytes 884744 | tf_op jit(solution)/shard_map/ppermute | solution.py:793
  390.9 12.5 %collective-permute-start.56 = (bf16[3,48,1536]{2,1,0:T(8,128)(2,1)S(1)}, bf16[3,48,1536]{2,1,0:T(8,128)(2,1)S(1)}, u32[]{:S(2)}, u32[]{:S(2)}) collective-permute-start(bf16[3,48,1536]{2,1,0:T(8,128)(2,1)S(1)} %get-tuple-element.348), channel_id=1, source_target_pairs={{2,0},{4,2},{6,4},{8,6},{10,8},{12,10},{14,12},{16,14},{18,16},{20... | collective-permute-start | bytes 1327112 | tf_op jit(solution)/shard_map/ppermute | solution.py:807
  391.3 61.6 %collective-permute-start.54 = (bf16[16,16,3072]{2,1,0:T(8,128)(2,1)}, bf16[16,16,3072]{2,1,0:T(8,128)(2,1)}, u32[]{:S(2)}, u32[]{:S(2)}) collective-permute-start(bf16[16,16,3072]{2,1,0:T(8,128)(2,1)} %get-tuple-element.236), channel_id=1, source_target_pairs={{0,4},{2,6},{4,0},{6,2},{8,12},{10,14},{12,8},{14,10},{16,20},{18,... | collective-permute-start | bytes 4718600 | tf_op jit(solution)/shard_map/ppermute | solution.py:675
  403.3 49.6 %collective-permute-start.57 = (bf16[16,48,1152]{2,1,0:T(8,128)(2,1)}, bf16[16,48,1152]{2,1,0:T(8,128)(2,1)}, u32[]{:S(2)}, u32[]{:S(2)}) collective-permute-start(bf16[16,48,1152]{2,1,0:T(8,128)(2,1)} %get-tuple-element.244), channel_id=1, source_target_pairs={{0,12},{2,14},{4,8},{6,10},{8,4},{10,6},{12,0},{14,2},{16,28},{18,... | collective-permute-start | bytes 5308424 | tf_op jit(solution)/shard_map/ppermute | solution.py:675
  403.3 49.6 %collective-permute-start.58 = (bf16[16,48,1152]{2,1,0:T(8,128)(2,1)}, bf16[16,48,1152]{2,1,0:T(8,128)(2,1)}, u32[]{:S(2)}, u32[]{:S(2)}) collective-permute-start(bf16[16,48,1152]{2,1,0:T(8,128)(2,1)} %get-tuple-element.245), channel_id=1, source_target_pairs={{0,16},{2,18},{4,20},{6,22},{8,24},{10,26},{12,28},{14,30},{16,0},... | collective-permute-start | bytes 5308424 | tf_op jit(solution)/shard_map/ppermute | solution.py:675
  403.3 49.6 %collective-permute-start.59 = (bf16[16,48,1024]{2,1,0:T(8,128)(2,1)}, bf16[16,48,1024]{2,1,0:T(8,128)(2,1)}, u32[]{:S(2)}, u32[]{:S(2)}) collective-permute-start(bf16[16,48,1024]{2,1,0:T(8,128)(2,1)} %get-tuple-element.246), channel_id=1, source_target_pairs={{0,48},{2,50},{4,52},{6,54},{8,56},{10,58},{12,60},{14,62},{16,32}... | collective-permute-start | bytes 4718600 | tf_op jit(solution)/shard_map/ppermute | solution.py:675
  409.6 43.4 %collective-permute-start.53 = (bf16[16,16,3072]{2,1,0:T(8,128)(2,1)}, bf16[16,16,3072]{2,1,0:T(8,128)(2,1)}, u32[]{:S(2)}, u32[]{:S(2)}) collective-permute-start(bf16[16,16,3072]{2,1,0:T(8,128)(2,1)} %get-tuple-element.341), channel_id=1, source_target_pairs={{0,64},{2,66},{4,68},{6,70},{8,72},{10,74},{12,76},{14,78},{16,80}... | collective-permute-start | bytes 4718600 | tf_op jit(solution)/shard_map/ppermute | solution.py:675
  432.0 20.8 %all-to-all-start = ((bf16[64,16,128]{2,1,0:T(8,128)(2,1)}), bf16[64,16,128]{2,1,0:T(8,128)(2,1)S(1)}, u32[]{:S(2)}, u32[]{:S(2)}) async-start(bf16[64,16,128]{2,1,0:T(8,128)(2,1)} %pad.16), calls=%async_computation | async-start | bytes 524288 | tf_op jit(solution)/shard_map/all_to_all | solution.py:1069
  454.7 35.5 %collective-permute-start.64 = (bf16[8,48,1024]{2,1,0:T(8,128)(2,1)S(1)}, bf16[8,48,1024]{2,1,0:T(8,128)(2,1)S(1)}, u32[]{:S(2)}, u32[]{:S(2)}) collective-permute-start(bf16[8,48,1024]{2,1,0:T(8,128)(2,1)S(1)} %get-tuple-element.335), channel_id=1, source_target_pairs={{0,16},{2,18},{4,20},{6,22},{8,24},{10,26},{12,28},{14,30},{16,0},... | collective-permute-start | bytes 2359304 | tf_op jit(solution)/shard_map/ppermute | solution.py:675
  457.7 32.6 %collective-permute-start.63 = (bf16[8,48,1152]{2,1,0:T(8,128)(2,1)S(1)}, bf16[8,48,1152]{2,1,0:T(8,128)(2,1)S(1)}, u32[]{:S(2)}, u32[]{:S(2)}) collective-permute-start(bf16[8,48,1152]{2,1,0:T(8,128)(2,1)S(1)} %get-tuple-element.331), channel_id=1, source_target_pairs={{0,12},{2,14},{4,8},{6,10},{8,4},{10,6},{12,0},{14,2},{16,28},{18,... | collective-permute-start | bytes 2654216 | tf_op jit(solution)/shard_map/ppermute | solution.py:675
  461.8 28.4 %collective-permute-start.62 = (bf16[8,48,1152]{2,1,0:T(8,128)(2,1)S(1)}, bf16[8,48,1152]{2,1,0:T(8,128)(2,1)S(1)}, u32[]{:S(2)}, u32[]{:S(2)}) collective-permute-start(bf16[8,48,1152]{2,1,0:T(8,128)(2,1)S(1)} %get-tuple-element.333), channel_id=1, source_target_pairs={{0,4},{2,6},{4,0},{6,2},{8,12},{10,14},{12,8},{14,10},{16,20},{18,... | collective-permute-start | bytes 2654216 | tf_op jit(solution)/shard_map/ppermute | solution.py:675
  463.6 26.6 %collective-permute-start.61 = (bf16[8,16,3072]{2,1,0:T(8,128)(2,1)S(1)}, bf16[8,16,3072]{2,1,0:T(8,128)(2,1)S(1)}, u32[]{:S(2)}, u32[]{:S(2)}) collective-permute-start(bf16[8,16,3072]{2,1,0:T(8,128)(2,1)S(1)} %get-tuple-element.337), channel_id=1, source_target_pairs={{0,64},{2,66},{4,68},{6,70},{8,72},{10,74},{12,76},{14,78},{16,80}... | collective-permute-start | bytes 2359304 | tf_op jit(solution)/shard_map/ppermute | solution.py:675
  466.6 23.6 %collective-permute-start.60 = (bf16[8,16,3072]{2,1,0:T(8,128)(2,1)S(1)}, bf16[8,16,3072]{2,1,0:T(8,128)(2,1)S(1)}, u32[]{:S(2)}, u32[]{:S(2)}) collective-permute-start(bf16[8,16,3072]{2,1,0:T(8,128)(2,1)S(1)} %get-tuple-element.339), channel_id=1, source_target_pairs={{0,48},{2,50},{4,52},{6,54},{8,56},{10,58},{12,60},{14,62},{16,32}... | collective-permute-start | bytes 2359304 | tf_op jit(solution)/shard_map/ppermute | solution.py:675
  490.3 11.6 %collective-permute-start.69 = (bf16[4,48,1024]{2,1,0:T(8,128)(2,1)S(1)}, bf16[4,48,1024]{2,1,0:T(8,128)(2,1)S(1)}, u32[]{:S(2)}, u32[]{:S(2)}) collective-permute-start(bf16[4,48,1024]{2,1,0:T(8,128)(2,1)S(1)} %get-tuple-element.353), channel_id=1, source_target_pairs={{0,12},{2,14},{4,8},{6,10},{8,4},{10,6},{12,0},{14,2},{16,28},{18,... | collective-permute-start | bytes 1179656 | tf_op jit(solution)/shard_map/ppermute | solution.py:675
  491.4 13.5 %collective-permute-start.68 = (bf16[4,48,1152]{2,1,0:T(8,128)(2,1)S(1)}, bf16[4,48,1152]{2,1,0:T(8,128)(2,1)S(1)}, u32[]{:S(2)}, u32[]{:S(2)}) collective-permute-start(bf16[4,48,1152]{2,1,0:T(8,128)(2,1)S(1)} %get-tuple-element.345), channel_id=1, source_target_pairs={{0,4},{2,6},{4,0},{6,2},{8,12},{10,14},{12,8},{14,10},{16,20},{18,... | collective-permute-start | bytes 1327112 | tf_op jit(solution)/shard_map/ppermute | solution.py:675
  492.1 12.8 %collective-permute-start.67 = (bf16[4,48,1152]{2,1,0:T(8,128)(2,1)S(1)}, bf16[4,48,1152]{2,1,0:T(8,128)(2,1)S(1)}, u32[]{:S(2)}, u32[]{:S(2)}) collective-permute-start(bf16[4,48,1152]{2,1,0:T(8,128)(2,1)S(1)} %get-tuple-element.347), channel_id=1, source_target_pairs={{0,64},{2,66},{4,68},{6,70},{8,72},{10,74},{12,76},{14,78},{16,80}... | collective-permute-start | bytes 1327112 | tf_op jit(solution)/shard_map/ppermute | solution.py:675
  493.3 10.9 %collective-permute-start.66 = (bf16[4,16,3072]{2,1,0:T(8,128)(2,1)S(1)}, bf16[4,16,3072]{2,1,0:T(8,128)(2,1)S(1)}, u32[]{:S(2)}, u32[]{:S(2)}) collective-permute-start(bf16[4,16,3072]{2,1,0:T(8,128)(2,1)S(1)} %get-tuple-element.355), channel_id=1, source_target_pairs={{0,48},{2,50},{4,52},{6,54},{8,56},{10,58},{12,60},{14,62},{16,32}... | collective-permute-start | bytes 1179656 | tf_op jit(solution)/shard_map/ppermute | solution.py:675
  495.4 9.4 %collective-permute-start.65 = (bf16[4,16,3072]{2,1,0:T(8,128)(2,1)S(1)}, bf16[4,16,3072]{2,1,0:T(8,128)(2,1)S(1)}, u32[]{:S(2)}, u32[]{:S(2)}) collective-permute-start(bf16[4,16,3072]{2,1,0:T(8,128)(2,1)S(1)} %get-tuple-element.356), channel_id=1, source_target_pairs={{0,16},{2,18},{4,20},{6,22},{8,24},{10,26},{12,28},{14,30},{16,0},... | collective-permute-start | bytes 1179656 | tf_op jit(solution)/shard_map/ppermute | solution.py:675
  505.7 8.3 %collective-permute-start.73 = (bf16[2,48,1152]{2,1,0:T(8,128)(2,1)S(1)}, bf16[2,48,1152]{2,1,0:T(8,128)(2,1)S(1)}, u32[]{:S(2)}, u32[]{:S(2)}) collective-permute-start(bf16[2,48,1152]{2,1,0:T(8,128)(2,1)S(1)} %get-tuple-element.359), channel_id=1, source_target_pairs={{0,64},{2,66},{4,68},{6,70},{8,72},{10,74},{12,76},{14,78},{16,80}... | collective-permute-start | bytes 663560 | tf_op jit(solution)/shard_map/ppermute | solution.py:675
  506.0 7.9 %collective-permute-start.72 = (bf16[2,48,1152]{2,1,0:T(8,128)(2,1)S(1)}, bf16[2,48,1152]{2,1,0:T(8,128)(2,1)S(1)}, u32[]{:S(2)}, u32[]{:S(2)}) collective-permute-start(bf16[2,48,1152]{2,1,0:T(8,128)(2,1)S(1)} %get-tuple-element.361), channel_id=1, source_target_pairs={{0,48},{2,50},{4,52},{6,54},{8,56},{10,58},{12,60},{14,62},{16,32}... | collective-permute-start | bytes 663560 | tf_op jit(solution)/shard_map/ppermute | solution.py:675
  507.6 6.3 %collective-permute-start.70 = (bf16[2,16,3072]{2,1,0:T(8,128)(2,1)S(1)}, bf16[2,16,3072]{2,1,0:T(8,128)(2,1)S(1)}, u32[]{:S(2)}, u32[]{:S(2)}) collective-permute-start(bf16[2,16,3072]{2,1,0:T(8,128)(2,1)S(1)} %get-tuple-element.366), channel_id=1, source_target_pairs={{0,12},{2,14},{4,8},{6,10},{8,4},{10,6},{12,0},{14,2},{16,28},{18,... | collective-permute-start | bytes 589832 | tf_op jit(solution)/shard_map/ppermute | solution.py:675
  514.0 7.6 %collective-permute-start.79 = (bf16[1,48,1024]{2,1,0:T(8,128)(2,1)S(1)}, bf16[1,48,1024]{2,1,0:T(8,128)(2,1)S(1)}, u32[]{:S(2)}, u32[]{:S(2)}) collective-permute-start(bf16[1,48,1024]{2,1,0:T(8,128)(2,1)S(1)} %slice_add_fusion.42), channel_id=1, source_target_pairs={{0,64},{2,66},{4,68},{6,70},{8,72},{10,74},{12,76},{14,78},{16,80}... | collective-permute-start | bytes 294920 | tf_op jit(solution)/shard_map/ppermute | solution.py:675
  515.4 7.6 %collective-permute-start.78 = (bf16[1,48,1152]{2,1,0:T(8,128)(2,1)S(1)}, bf16[1,48,1152]{2,1,0:T(8,128)(2,1)S(1)}, u32[]{:S(2)}, u32[]{:S(2)}) collective-permute-start(bf16[1,48,1152]{2,1,0:T(8,128)(2,1)S(1)} %slice_add_fusion.38), channel_id=1, source_target_pairs={{0,48},{2,50},{4,52},{6,54},{8,56},{10,58},{12,60},{14,62},{16,32}... | collective-permute-start | bytes 331784 | tf_op jit(solution)/shard_map/ppermute | solution.py:675
  516.8 6.1 %collective-permute-start.77 = (bf16[1,48,1152]{2,1,0:T(8,128)(2,1)S(1)}, bf16[1,48,1152]{2,1,0:T(8,128)(2,1)S(1)}, u32[]{:S(2)}, u32[]{:S(2)}) collective-permute-start(bf16[1,48,1152]{2,1,0:T(8,128)(2,1)S(1)} %slice_add_fusion.39), channel_id=1, source_target_pairs={{0,16},{2,18},{4,20},{6,22},{8,24},{10,26},{12,28},{14,30},{16,0},... | collective-permute-start | bytes 331784 | tf_op jit(solution)/shard_map/ppermute | solution.py:675
  523.3 8.5 %collective-permute-start.80 = (bf16[24,3328]{1,0:T(8,128)(2,1)S(1)}, bf16[24,3328]{1,0:T(8,128)(2,1)S(1)}, u32[]{:S(2)}, u32[]{:S(2)}) collective-permute-start(bf16[24,3328]{1,0:T(8,128)(2,1)S(1)} %select_convert_fusion.1), channel_id=1, source_target_pairs={{0,2},{2,0},{4,6},{6,4},{8,10},{10,8},{12,14},{14,12},{16,18},{18,... | collective-permute-start | bytes 479240 | tf_op jit(solution)/shard_map/ppermute | solution.py:675
  (135 other events, 1254.2 us)

commit v5 on v4

--- a/solution.py
+++ b/solution.py
@@ -74,7 +74,7 @@
         out_ref[row] = window_sum(wide, taps, shifted, row, side, False)
         return carry
 
-    lax.fori_loop(0, strip, step, 0)
+    lax.fori_loop(0, strip, step, 0, unroll=2)
 
 
 def backward_kernel(place, main_ref, low_ref, high_ref, taps_in, add_ref, out_ref, wide, taps, shifted):
@@ -90,7 +90,7 @@
         out_ref[row] = jnp.where(keep, total, 0.0)
         return carry
 
-    lax.fori_loop(0, strip, step, 0)
+    lax.fori_loop(0, strip, step, 0, unroll=2)
 
 
 def slope_kernel(place, main_ref, low_ref, high_ref, grad_ref, out_ref, wide, padded):
@@ -115,7 +115,7 @@
             return tuple(fresh)
 
         start = tuple(jnp.zeros((8, LANES), jnp.float32) for _ in range(len(group) * WINDOW))
-        sums = lax.fori_loop(0, strip, step, start)
+        sums = lax.fori_loop(0, strip, step, start, unroll=4)
         for i, a in enumerate(group):
             for b in range(WINDOW):
                 tap = a * WINDOW + b
@@ -694,13 +694,16 @@
 def gathered_parts(blocks, orders, early, work):
     held = [block[None] for block in blocks]
     count, last = len(blocks), len(RINGS) - 1
+    tied = early
     for step in range(last):
         other = [xor_swap(part, order[step]) for part, order in zip(held, orders)]
         held = [jnp.concatenate([a, b], axis=0) for a, b in zip(held, other)]
-        done = together(held + (early if step == last - 1 else []))
+        done = together(held + (tied if step == last - 2 else []))
         held = done[:count]
+        if step == last - 2:
+            tied = done[count:]
     other = [xor_swap(part, order[last]) for part, order in zip(held, orders)]
-    done = together(other + work(*done[count:]))
+    done = together(other + work(*tied))
     return held, done[:count], done[count:]
 
 

time: 543 us -> 538 us (level)
  starting transfers between devices: 119 us -> 109 us
  waiting for transfers between devices: 114 us -> 121 us
    ppermute x3, starting transfers between devices: 10.1 us -> 1.01 us  [halo_rows(): high = lax.ppermute(block[:width], 'dp', backward)]
    ppermute x64, waiting for transfers between devices: 66.2 us -> 75.2 us  [xor_swap(): return lax.ppermute(values, 'dp', [(i, i ^ mask) for i in range(count)])]
    ppermute x3, starting transfers between devices: 11.6 us -> 5.08 us  [halo_rows(): low = lax.ppermute(block[block.shape[0] - width:], 'dp', forward)]
  transfers between devices with their start and end apart: 82 -> 82, of which waited for: 33 -> 32; matrix products, arithmetic and copies ran while one was open for 17% -> 17% of each run, Pallas kernels for 24% -> 24%
where the time goes in v5:
time: 538 us; the launch traced here: 528 us
  Pallas kernels  151 us (28%)
  waiting for transfers between devices  121 us (22%)
  starting transfers between devices  109 us (20%)
  other arithmetic  44.2 us (8%)
  local copies, waits for them, and re-layouts  42 us (8%)
  matrix products  36.4 us (7%)
  blocking collectives  21.7 us (4%)
    ppermute x64, waiting for transfers between devices, xor_swap(): return lax.ppermute(values, 'dp', [(i, i ^ mask) for i in range(count)])  75.2 us
    ppermute x64, starting transfers between devices, xor_swap(): return lax.ppermute(values, 'dp', [(i, i ^ mask) for i in range(count)])  73.2 us
    pallas_call x3, Pallas kernels, dense(): pl.pallas_call(functools.partial(dense_kernel, flipped, scale is not None...  34.2 us
    ppermute x9, waiting for transfers between devices, model_swap(): return lax.ppermute(values, 'mp', [(0, 1), (1, 0)])  33.7 us
    pallas_call x2, Pallas kernels, map_conv(): pl.pallas_call(forward_kernel if added is None else backward_kernel, grid...  31.4 us
    pallas_call x1, Pallas kernels, packed_slopes(): pl.pallas_call(functools.partial(slope_pack_kernel, orders, spans), grid=...  28.3 us
    unnamed x248, local copies, waits for them, and re-layouts  27.2 us
    dot_general x17, matrix products, matmul(): return jnp.dot(former, latter, preferred_element_type=jnp.float32)  22.6 us
  transfers between devices with their start and end apart: 82, of which 32 were waited for; matrix products, arithmetic and copies ran while one was open for 17% of the time, Pallas kernels for 24%

profile of v5, /device:TPU:1, one launch (start us, length us, event | category | flops | bytes accessed | tf_op | source)
XLA Modules:
  0.0 528.4 jit_solution(11573355142410856356)
XLA Ops:
  5.2 3.3 collective-permute-start.1
  12.2 4.3 collective-permute-done
  18.3 2.8 collective-permute-start.4
  21.2 2.1 collective-permute-done.4
  27.0 2.6 collective-permute-done.7
  29.7 2.7 collective-permute-done.6
  34.5 4.8 collective-permute-start.16
  39.4 3.2 collective-permute-start.15
  44.4 11.5 %collective-permute-done.15 = bf16[4,48,1024]{2,1,0:T(8,128)(2,1)S(1)} collective-permute-done((bf16[4,48,1024]{2,1,0:T(8,128)(2,1)S(1)}, bf16[4,48,1024]{2,1,0:T(8,128)(2,1)S(1)}, u32[]{:S(2)}, u32[]{:S(2)}) %collective-permute-start.15) | collective-permute-done | bytes 393248 | tf_op jit(solution)/shard_map/ppermute | solution.py:675
  61.6 14.5 %collective-permute-done.19 = bf16[8,16,3072]{2,1,0:T(8,128)(2,1)S(1)} collective-permute-done((bf16[8,16,3072]{2,1,0:T(8,128)(2,1)S(1)}, bf16[8,16,3072]{2,1,0:T(8,128)(2,1)S(1)}, u32[]{:S(2)}, u32[]{:S(2)}) %collective-permute-start.19) | collective-permute-done | bytes 786464 | tf_op jit(solution)/shard_map/ppermute | solution.py:675
  84.5 2.9 collective-permute-start.23
  94.9 15.1 %shard_map.356 = f32[12,48,1536]{2,1,0:T(8,128)S(1)} custom-call(s32[2]{0:T(128)S(1)} %pad_add_fusion.place, bf16[12,48,1536]{2,1,0:T(8,128)(2,1)S(1)} %bitcast.128, bf16[3,48,1536]{2,1,0:T(8,128)(2,1)S(1)} %copy-done.27, bf16[3,48,1536]{2,1,0:T(8,128)(2,1)S(1)} %copy-done.29, bf16[49,1536]{1,0:T(8,128)(2,1)S(1)} %copy-done.50), custom_call_target="tpu_custom_call" | custom-call | bytes 110592 | tf_op jit(solution)/shard_map/pallas_call | solution.py:147
  111.3 2.2 constant_dynamic-update-slice_fusion.6
  113.4 5.6 %collective-permute-done.23 = bf16[16,16,3072]{2,1,0:T(8,128)(2,1)} collective-permute-done((bf16[16,16,3072]{2,1,0:T(8,128)(2,1)}, bf16[16,16,3072]{2,1,0:T(8,128)(2,1)}, u32[]{:S(2)}, u32[]{:S(2)}) %collective-permute-start.23) | collective-permute-done | bytes 1572896 | tf_op jit(solution)/shard_map/ppermute | solution.py:675
  123.7 4.6 collective-permute-start.28
  129.8 3.7 collective-permute-done.28
  134.4 3.8 collective-permute-start.29
  140.6 4.6 shard_map.359
  145.2 2.2 copy-done.6
  150.0 4.5 shard_map.360.refs_4_
  156.2 3.5 collective-permute-start.31
  161.0 5.8 %collective-permute-done.31.refs_2_ = bf16[144,1024]{1,0:T(8,128)(2,1)S(1)} collective-permute-done((bf16[144,1024]{1,0:T(8,128)(2,1)S(1)}, bf16[144,1024]{1,0:T(8,128)(2,1)S(1)}, u32[]{:S(2)}, u32[]{:S(2)}) %collective-permute-start.31) | collective-permute-done | bytes 294944 | tf_op jit(solution)/shard_map/ppermute | solution.py:796
  175.1 2.7 collective-permute-start.33
  177.8 10.6 %fusion.4 = (bf16[1152,1536]{1,0:T(8,128)(2,1)}, bf16[1152,1536]{1,0:T(8,128)(2,1)}) fusion(bf16[1536,1536]{1,0:T(8,128)(2,1)S(1)} %bitcast.135, bf16[576,1536]{1,0:T(8,128)(2,1)S(1)} %collective-permute-done.35.refs_1_, bf16[576,1536]{1,0:T(8,128)(2,1)S(1)} %shard_map.357.refs_0_), kind=kOutput, calls=%fused_computation.5 | convolution fusion | flops 5462360064 | bytes 15335424 | tf_op jit(solution)/shard_map/dot_general | solution.py:821
  189.8 12.4 %shard_map.363 = (f32[576,1536]{1,0:T(8,128)S(1)}, bf16[576,1536]{1,0:T(8,128)(2,1)S(1)}) custom-call(bf16[1152,1536]{1,0:T(8,128)(2,1)} %get-tuple-element.191.refs_0_.refs_5_, bf16[1536,1536]{1,0:T(8,128)(2,1)} %bitcast.130), custom_call_target="tpu_custom_call" | custom-call | bytes 1048576 | tf_op jit(solution)/shard_map/pallas_call | solution.py:494
  203.9 3.2 collective-permute-done.36
  208.9 8.2 %collective-permute-done.37.pool_other_ref = bf16[6,24,1536]{2,1,0:T(8,128)(2,1)S(1)} collective-permute-done((bf16[6,24,1536]{2,1,0:T(8,128)(2,1)S(1)}, bf16[6,24,1536]{2,1,0:T(8,128)(2,1)S(1)}, u32[]{:S(2)}, u32[]{:S(2)}) %collective-permute-start.37) | collective-permute-done | bytes 442400 | tf_op jit(solution)/shard_map/ppermute | solution.py:796
  217.1 3.8 shard_map.364
  227.5 9.3 %shard_map.365.refs_0_.refs_4_ = bf16[1152,1536]{1,0:T(8,128)(2,1)S(1)} custom-call(bf16[576,1536]{1,0:T(8,128)(2,1)} %bitcast.32.refs_0_.refs_2_, bf16[576,1536]{1,0:T(8,128)(2,1)} %collective-permute-done.38.refs_1_.refs_3_, bf16[1536,1536]{1,0:T(8,128)(2,1)} %bitcast.131, bf16[1152,1536]{1,0:T(8,128)(2,1)} %get-tuple-element.326.refs_3_), custom_call_target="tpu_custom_call" | custom-call | bytes 1048576 | tf_op jit(solution)/shard_map/pallas_call | solution.py:494
  241.8 12.6 %shard_map.367 = (f32[576,1536]{1,0:T(8,128)S(1)}, bf16[576,1536]{1,0:T(8,128)(2,1)S(1)}) custom-call(bf16[1152,1536]{1,0:T(8,128)(2,1)} %copy-done, bf16[1536,1536]{1,0:T(8,128)(2,1)} %bitcast.136), custom_call_target="tpu_custom_call" | custom-call | bytes 1048576 | tf_op jit(solution)/shard_map/pallas_call | solution.py:494
  257.4 8.9 %collective-permute-done.41.other_ref = bf16[12,48,1536]{2,1,0:T(8,128)(2,1)} collective-permute-done((bf16[12,48,1536]{2,1,0:T(8,128)(2,1)}, bf16[12,48,1536]{2,1,0:T(8,128)(2,1)}, u32[]{:S(2)}, u32[]{:S(2)}) %collective-permute-start.41) | collective-permute-done | bytes 1769504 | tf_op jit(solution)/shard_map/ppermute | solution.py:796
  266.4 5.4 %shard_map.368 = (bf16[12,48,1536]{2,1,0:T(8,128)(2,1)}, bf16[6,24,1536]{2,1,0:T(8,128)(2,1)S(1)}, f32[1,1536]{1,0:T(1,128)S(1)}) custom-call(s32[2]{0:T(128)S(1)} %copy-done.73, bf16[12,48,1536]{2,1,0:T(8,128)(2,1)} %bitcast.30.own_ref, bf16[12,48,1536]{2,1,0:T(8,128)(2,1)} %collective-permute-done.41.other_ref, bf16[12,48,1536]{2,1,0:T(8,128)(2,1)S(1)} %bitcast.129, ...), custom_call_target="tpu_custom_call" | custom-call | bytes 1048576 | tf_op jit(solution)/shard_map/pallas_call | solution.py:255
  277.1 3.0 collective-permute-start.42
  282.1 2.2 collective-permute-done.42
  284.4 2.3 multiply_add_fusion
  288.9 2.5 fusion.20
  292.1 4.8 shard_map.369
  297.4 2.4 convolution_convert_fusion.3
  302.8 3.0 collective-permute-start.44
  305.9 2.1 add_convert_fusion.own_ref
  308.0 4.2 collective-permute-done.44.other_ref
  318.2 7.0 %shard_map.371 = (bf16[144,512]{1,0:T(8,128)(2,1)S(1)}, f32[576,512]{1,0:T(8,128)S(1)}, f32[576,512]{1,0:T(8,128)S(1)}) custom-call(bf16[144,1536]{1,0:T(8,128)(2,1)S(1)} %copy-done.13, bf16[576,1024]{1,0:T(8,128)(2,1)S(1)} %copy-done.2, bf16[576,1024]{1,0:T(8,128)(2,1)S(1)} %copy-done.2, bf16[144,512]{1,0:T(8,128)(2,1)S(1)} %fusion.63.grad_ref), custom_call_target="tpu_custom_call" | custom-call | bytes 1048576 | tf_op jit(solution)/shard_map/pallas_call | solution.py:378
  325.2 3.1 collective-permute-start.48
  332.1 2.7 collective-permute-start.47
  334.8 28.3 %shard_map.372 = (bf16[16,48,1152]{2,1,0:T(8,128)(2,1)S(1)}, bf16[16,48,1152]{2,1,0:T(8,128)(2,1)}, bf16[16,48,1152]{2,1,0:T(8,128)(2,1)S(1)}, bf16[16,48,1152]{...) custom-call(s32[1]{0:T(128)} %bitcast.19.place, bf16[576,1536]{1,0:T(8,128)(2,1)S(1)} %copy-done.11, ...), custom_call_target="tpu_custom_call" | custom-call | bytes 1048576 | tf_op jit(solution)/shard_map/pallas_call | solution.py:1027
  363.2 5.8 %slice_add_fusion.2 = (bf16[16,16,3072]{2,1,0:T(8,128)(2,1)}, bf16[16,16,3072]{2,1,0:T(8,128)(2,1)}) fusion(bf16[32,16,3072]{2,1,0:T(8,128)(2,1)} %collective-permute-done.49, bf16[32,16,3072]{2,1,0:T(8,128)(2,1)S(1)} %bitcast.138), kind=kLoop, calls=%fused_computation.54 | loop fusion | flops 1572864 | bytes 9437184 | tf_op jit(solution)/shard_map/add | solution.py:714
  369.0 4.4 collective-permute-done.48.other_ref
  374.5 2.9 shard_map.374
  377.5 3.8 shard_map.375
  384.5 3.0 collective-permute-start.51
  388.6 4.5 collective-permute-done.55.low_ref
  393.1 7.2 %collective-permute-done.56.high_ref = bf16[3,48,1536]{2,1,0:T(8,128)(2,1)S(1)} collective-permute-done((bf16[3,48,1536]{2,1,0:T(8,128)(2,1)S(1)}, bf16[3,48,1536]{2,1,0:T(8,128)(2,1)S(1)}, u32[]{:S(2)}, u32[]{:S(2)}) %collective-permute-start.56) | collective-permute-done | bytes 442400 | tf_op jit(solution)/shard_map/ppermute | solution.py:810
  400.3 6.4 %collective-permute-start.59 = (bf16[16,48,1024]{2,1,0:T(8,128)(2,1)}, bf16[16,48,1024]{2,1,0:T(8,128)(2,1)}, u32[]{:S(2)}, u32[]{:S(2)}) collective-permute-start(bf16[16,48,1024]{2,1,0:T(8,128)(2,1)} %get-tuple-element.246), channel_id=1, source_target_pairs={{0,48},{2,50},{4,52},{6,54},{8,56},{10,58},{12,60},{14,62},{16,32}... | collective-permute-start | bytes 4718600 | tf_op jit(solution)/shard_map/ppermute | solution.py:675
  406.7 2.1 slice_add_fusion
  409.2 15.1 %shard_map.377 = f32[49,1536]{1,0:T(8,128)S(1)} custom-call(s32[2]{0:T(128)S(1)} %copy-done.74, bf16[12,48,1536]{2,1,0:T(8,128)(2,1)} %bitcast.126, bf16[3,48,1536]{2,1,0:T(8,128)(2,1)} %copy-done.26, bf16[3,48,1536]{2,1,0:T(8,128)(2,1)} %copy-done.28, bf16[12,48,1536]{2,1,0:T(8,128)(2,1)} %bitcast.133), custom_call_target="tpu_custom_call" | custom-call | bytes 110592 | tf_op jit(solution)/shard_map/pallas_call | solution.py:167
  426.7 4.6 all-to-all-start
  431.3 16.3 %shard_map.376 = f32[12,48,1536]{2,1,0:T(8,128)} custom-call(s32[2]{0:T(128)S(1)} %copy-done.74, bf16[12,48,1536]{2,1,0:T(8,128)(2,1)} %bitcast.134, bf16[3,48,1536]{2,1,0:T(8,128)(2,1)} %copy-done.99, bf16[3,48,1536]{2,1,0:T(8,128)(2,1)} %copy-done.100, bf16[49,1536]{1,0:T(8,128)(2,1)} %taps_in.3, f32[12,48,1536]{2,1,0:T(8,128)} %copy-done.7), custom_call_target="tpu_custom_call" | custom-call | bytes 110592 | tf_op jit(solution)/shard_map/pallas_call | solution.py:147
  452.6 2.5 collective-permute-start.63
  463.5 21.7 %all_to_all.10 = bf16[64,16,128]{2,1,0:T(8,128)(2,1)S(1)} all-to-all(bf16[64,16,128]{2,1,0:T(8,128)(2,1)S(1)} %broadcast_in_dim.76), channel_id=1, replica_groups=mesh['dp'=64,'mp'=2] {'dp'}, dimensions={0} | all-to-all | bytes 524288 | tf_op jit(solution)/shard_map/all_to_all | solution.py:1078
  488.2 2.0 collective-permute-start.66
  490.6 6.2 %collective-permute-done.69 = bf16[4,48,1024]{2,1,0:T(8,128)(2,1)S(1)} collective-permute-done((bf16[4,48,1024]{2,1,0:T(8,128)(2,1)S(1)}, bf16[4,48,1024]{2,1,0:T(8,128)(2,1)S(1)}, u32[]{:S(2)}, u32[]{:S(2)}) %collective-permute-start.69) | collective-permute-done | bytes 393248 | tf_op jit(solution)/shard_map/ppermute | solution.py:675
  496.8 2.3 collective-permute-done.66
  505.3 2.2 collective-permute-done.71
  518.2 7.1 %collective-permute-start.80 = (bf16[24,3328]{1,0:T(8,128)(2,1)S(1)}, bf16[24,3328]{1,0:T(8,128)(2,1)S(1)}, u32[]{:S(2)}, u32[]{:S(2)}) collective-permute-start(bf16[24,3328]{1,0:T(8,128)(2,1)S(1)} %select_convert_fusion.1), channel_id=1, source_target_pairs={{0,2},{2,0},{4,6},{6,4},{8,10},{10,8},{12,14},{14,12},{16,18},{18,... | collective-permute-start | bytes 479240 | tf_op jit(solution)/shard_map/ppermute | solution.py:675
  (535 shorter events, 150.3 us)
Async XLA Ops:
  5.2 7.0 %collective-permute-start.1 = (bf16[1,16,3072]{2,1,0:T(8,128)(2,1)S(1)}, bf16[1,16,3072]{2,1,0:T(8,128)(2,1)S(1)}, u32[]{:S(2)}, u32[]{:S(2)}) collective-permute-start(bf16[1,16,3072]{2,1,0:T(8,128)(2,1)S(1)} %maximum_bitcast_fusion), channel_id=1, source_target_pairs={{0,12},{2,14},{4,8},{6,10},{8,4},{10,6},{12,0},{14,2},{16,28},{18,... | collective-permute-start | bytes 294920 | tf_op jit(solution)/shard_map/ppermute | solution.py:675
  25.2 7.3 %collective-permute-start.10 = (bf16[2,48,1024]{2,1,0:T(8,128)(2,1)S(1)}, bf16[2,48,1024]{2,1,0:T(8,128)(2,1)S(1)}, u32[]{:S(2)}, u32[]{:S(2)}) collective-permute-start(bf16[2,48,1024]{2,1,0:T(8,128)(2,1)S(1)} %pad_maximum_fusion.25), channel_id=1, source_target_pairs={{0,4},{2,6},{4,0},{6,2},{8,12},{10,14},{12,8},{14,10},{16,20},{18,... | collective-permute-start | bytes 589832 | tf_op jit(solution)/shard_map/ppermute | solution.py:675
  25.3 7.2 %collective-permute-start.9 = (bf16[2,48,1152]{2,1,0:T(8,128)(2,1)S(1)}, bf16[2,48,1152]{2,1,0:T(8,128)(2,1)S(1)}, u32[]{:S(2)}, u32[]{:S(2)}) collective-permute-start(bf16[2,48,1152]{2,1,0:T(8,128)(2,1)S(1)} %pad_maximum_fusion.22), channel_id=1, source_target_pairs={{0,64},{2,66},{4,68},{6,70},{8,72},{10,74},{12,76},{14,78},{16,80}... | collective-permute-start | bytes 663560 | tf_op jit(solution)/shard_map/ppermute | solution.py:675
  25.4 7.2 %collective-permute-start.8 = (bf16[2,48,1152]{2,1,0:T(8,128)(2,1)S(1)}, bf16[2,48,1152]{2,1,0:T(8,128)(2,1)S(1)}, u32[]{:S(2)}, u32[]{:S(2)}) collective-permute-start(bf16[2,48,1152]{2,1,0:T(8,128)(2,1)S(1)} %pad_maximum_fusion.21), channel_id=1, source_target_pairs={{0,48},{2,50},{4,52},{6,54},{8,56},{10,58},{12,60},{14,62},{16,32}... | collective-permute-start | bytes 663560 | tf_op jit(solution)/shard_map/ppermute | solution.py:675
  32.6 9.9 %collective-permute-start.12 = (bf16[4,16,3072]{2,1,0:T(8,128)(2,1)S(1)}, bf16[4,16,3072]{2,1,0:T(8,128)(2,1)S(1)}, u32[]{:S(2)}, u32[]{:S(2)}) collective-permute-start(bf16[4,16,3072]{2,1,0:T(8,128)(2,1)S(1)} %pad_maximum_fusion.18), channel_id=1, source_target_pairs={{0,48},{2,50},{4,52},{6,54},{8,56},{10,58},{12,60},{14,62},{16,32}... | collective-permute-start | bytes 1179656 | tf_op jit(solution)/shard_map/ppermute | solution.py:675
  34.4 8.2 %collective-permute-start.11 = (bf16[4,16,3072]{2,1,0:T(8,128)(2,1)S(1)}, bf16[4,16,3072]{2,1,0:T(8,128)(2,1)S(1)}, u32[]{:S(2)}, u32[]{:S(2)}) collective-permute-start(bf16[4,16,3072]{2,1,0:T(8,128)(2,1)S(1)} %pad_maximum_fusion.17), channel_id=1, source_target_pairs={{0,16},{2,18},{4,20},{6,22},{8,24},{10,26},{12,28},{14,30},{16,0},... | collective-permute-start | bytes 1179656 | tf_op jit(solution)/shard_map/ppermute | solution.py:675
  34.5 23.4 %collective-permute-start.16 = (bf16[3,48,1536]{2,1,0:T(8,128)(2,1)S(1)}, bf16[3,48,1536]{2,1,0:T(8,128)(2,1)S(1)}, u32[]{:S(2)}, u32[]{:S(2)}) collective-permute-start(bf16[3,48,1536]{2,1,0:T(8,128)(2,1)S(1)} %get-tuple-element.351), channel_id=1, source_target_pairs={{0,2},{2,4},{4,6},{6,8},{8,10},{10,12},{12,14},{14,16},{16,18},{18... | collective-permute-start | bytes 1327112 | tf_op jit(solution)/shard_map/ppermute | solution.py:809
  39.4 19.3 %collective-permute-start.17 = (bf16[3,48,1536]{2,1,0:T(8,128)(2,1)S(1)}, bf16[3,48,1536]{2,1,0:T(8,128)(2,1)S(1)}, u32[]{:S(2)}, u32[]{:S(2)}) collective-permute-start(bf16[3,48,1536]{2,1,0:T(8,128)(2,1)S(1)} %get-tuple-element.350), channel_id=1, source_target_pairs={{2,0},{4,2},{6,4},{8,6},{10,8},{12,10},{14,12},{16,14},{18,16},{20... | collective-permute-start | bytes 1327112 | tf_op jit(solution)/shard_map/ppermute | solution.py:810
  39.4 16.6 %collective-permute-start.15 = (bf16[4,48,1024]{2,1,0:T(8,128)(2,1)S(1)}, bf16[4,48,1024]{2,1,0:T(8,128)(2,1)S(1)}, u32[]{:S(2)}, u32[]{:S(2)}) collective-permute-start(bf16[4,48,1024]{2,1,0:T(8,128)(2,1)S(1)} %pad_maximum_fusion.19), channel_id=1, source_target_pairs={{0,12},{2,14},{4,8},{6,10},{8,4},{10,6},{12,0},{14,2},{16,28},{18,... | collective-permute-start | bytes 1179656 | tf_op jit(solution)/shard_map/ppermute | solution.py:675
  42.6 13.5 %collective-permute-start.14 = (bf16[4,48,1152]{2,1,0:T(8,128)(2,1)S(1)}, bf16[4,48,1152]{2,1,0:T(8,128)(2,1)S(1)}, u32[]{:S(2)}, u32[]{:S(2)}) collective-permute-start(bf16[4,48,1152]{2,1,0:T(8,128)(2,1)S(1)} %pad_maximum_fusion.15), channel_id=1, source_target_pairs={{0,4},{2,6},{4,0},{6,2},{8,12},{10,14},{12,8},{14,10},{16,20},{18,... | collective-permute-start | bytes 1327112 | tf_op jit(solution)/shard_map/ppermute | solution.py:675
  42.6 15.2 %collective-permute-start.13 = (bf16[4,48,1152]{2,1,0:T(8,128)(2,1)S(1)}, bf16[4,48,1152]{2,1,0:T(8,128)(2,1)S(1)}, u32[]{:S(2)}, u32[]{:S(2)}) collective-permute-start(bf16[4,48,1152]{2,1,0:T(8,128)(2,1)S(1)} %pad_maximum_fusion.14), channel_id=1, source_target_pairs={{0,64},{2,66},{4,68},{6,70},{8,72},{10,74},{12,76},{14,78},{16,80}... | collective-permute-start | bytes 1327112 | tf_op jit(solution)/shard_map/ppermute | solution.py:675
  59.5 16.6 %collective-permute-start.19 = (bf16[8,16,3072]{2,1,0:T(8,128)(2,1)S(1)}, bf16[8,16,3072]{2,1,0:T(8,128)(2,1)S(1)}, u32[]{:S(2)}, u32[]{:S(2)}) collective-permute-start(bf16[8,16,3072]{2,1,0:T(8,128)(2,1)S(1)} %pad_maximum_fusion.10), channel_id=1, source_target_pairs={{0,64},{2,66},{4,68},{6,70},{8,72},{10,74},{12,76},{14,78},{16,80}... | collective-permute-start | bytes 2359304 | tf_op jit(solution)/shard_map/ppermute | solution.py:675
  60.0 17.4 %collective-permute-start.22 = (bf16[8,48,1024]{2,1,0:T(8,128)(2,1)S(1)}, bf16[8,48,1024]{2,1,0:T(8,128)(2,1)S(1)}, u32[]{:S(2)}, u32[]{:S(2)}) collective-permute-start(bf16[8,48,1024]{2,1,0:T(8,128)(2,1)S(1)} %pad_maximum_fusion.11), channel_id=1, source_target_pairs={{0,16},{2,18},{4,20},{6,22},{8,24},{10,26},{12,28},{14,30},{16,0},... | collective-permute-start | bytes 2359304 | tf_op jit(solution)/shard_map/ppermute | solution.py:675
  60.5 18.1 %collective-permute-start.18 = (bf16[8,16,3072]{2,1,0:T(8,128)(2,1)S(1)}, bf16[8,16,3072]{2,1,0:T(8,128)(2,1)S(1)}, u32[]{:S(2)}, u32[]{:S(2)}) collective-permute-start(bf16[8,16,3072]{2,1,0:T(8,128)(2,1)S(1)} %pad_maximum_fusion.9), channel_id=1, source_target_pairs={{0,48},{2,50},{4,52},{6,54},{8,56},{10,58},{12,60},{14,62},{16,32}... | collective-permute-start | bytes 2359304 | tf_op jit(solution)/shard_map/ppermute | solution.py:675
  61.6 19.7 %collective-permute-start.21 = (bf16[8,48,1152]{2,1,0:T(8,128)(2,1)S(1)}, bf16[8,48,1152]{2,1,0:T(8,128)(2,1)S(1)}, u32[]{:S(2)}, u32[]{:S(2)}) collective-permute-start(bf16[8,48,1152]{2,1,0:T(8,128)(2,1)S(1)} %pad_maximum_fusion.8), channel_id=1, source_target_pairs={{0,12},{2,14},{4,8},{6,10},{8,4},{10,6},{12,0},{14,2},{16,28},{18,... | collective-permute-start | bytes 2654216 | tf_op jit(solution)/shard_map/ppermute | solution.py:675
  61.6 21.1 %collective-permute-start.20 = (bf16[8,48,1152]{2,1,0:T(8,128)(2,1)S(1)}, bf16[8,48,1152]{2,1,0:T(8,128)(2,1)S(1)}, u32[]{:S(2)}, u32[]{:S(2)}) collective-permute-start(bf16[8,48,1152]{2,1,0:T(8,128)(2,1)S(1)} %pad_maximum_fusion.7), channel_id=1, source_target_pairs={{0,4},{2,6},{4,0},{6,2},{8,12},{10,14},{12,8},{14,10},{16,20},{18,... | collective-permute-start | bytes 2654216 | tf_op jit(solution)/shard_map/ppermute | solution.py:675
  84.1 38.1 %collective-permute-start.25 = (bf16[16,48,1152]{2,1,0:T(8,128)(2,1)}, bf16[16,48,1152]{2,1,0:T(8,128)(2,1)}, u32[]{:S(2)}, u32[]{:S(2)}) collective-permute-start(bf16[16,48,1152]{2,1,0:T(8,128)(2,1)} %pad_maximum_fusion.refs_0_), channel_id=1, source_target_pairs={{0,12},{2,14},{4,8},{6,10},{8,4},{10,6},{12,0},{14,2},{16,28},{18,... | collective-permute-start | bytes 5308424 | tf_op jit(solution)/shard_map/ppermute | solution.py:675
  84.1 38.1 %collective-permute-start.26 = (bf16[16,48,1152]{2,1,0:T(8,128)(2,1)}, bf16[16,48,1152]{2,1,0:T(8,128)(2,1)}, u32[]{:S(2)}, u32[]{:S(2)}) collective-permute-start(bf16[16,48,1152]{2,1,0:T(8,128)(2,1)} %pad_maximum_fusion.1.refs_2_), channel_id=1, source_target_pairs={{0,16},{2,18},{4,20},{6,22},{8,24},{10,26},{12,28},{14,30},{16,0},... | collective-permute-start | bytes 5308424 | tf_op jit(solution)/shard_map/ppermute | solution.py:675
  84.5 34.6 %collective-permute-start.23 = (bf16[16,16,3072]{2,1,0:T(8,128)(2,1)}, bf16[16,16,3072]{2,1,0:T(8,128)(2,1)}, u32[]{:S(2)}, u32[]{:S(2)}) collective-permute-start(bf16[16,16,3072]{2,1,0:T(8,128)(2,1)} %pad_maximum_fusion.2), channel_id=1, source_target_pairs={{0,64},{2,66},{4,68},{6,70},{8,72},{10,74},{12,76},{14,78},{16,80}... | collective-permute-start | bytes 4718600 | tf_op jit(solution)/shard_map/ppermute | solution.py:675
  87.4 32.8 %collective-permute-start.24 = (bf16[16,16,3072]{2,1,0:T(8,128)(2,1)}, bf16[16,16,3072]{2,1,0:T(8,128)(2,1)}, u32[]{:S(2)}, u32[]{:S(2)}) collective-permute-start(bf16[16,16,3072]{2,1,0:T(8,128)(2,1)} %pad_maximum_fusion.3), channel_id=1, source_target_pairs={{0,4},{2,6},{4,0},{6,2},{8,12},{10,14},{12,8},{14,10},{16,20},{18,... | collective-permute-start | bytes 4718600 | tf_op jit(solution)/shard_map/ppermute | solution.py:675
  87.4 34.2 %collective-permute-start.27 = (bf16[16,48,1024]{2,1,0:T(8,128)(2,1)}, bf16[16,48,1024]{2,1,0:T(8,128)(2,1)}, u32[]{:S(2)}, u32[]{:S(2)}) collective-permute-start(bf16[16,48,1024]{2,1,0:T(8,128)(2,1)} %pad_maximum_fusion.4.refs_4_), channel_id=1, source_target_pairs={{0,48},{2,50},{4,52},{6,54},{8,56},{10,58},{12,60},{14,62},{16,32}... | collective-permute-start | bytes 4718600 | tf_op jit(solution)/shard_map/ppermute | solution.py:675
  123.7 9.9 %collective-permute-start.28 = (bf16[32,16,3072]{2,1,0:T(8,128)(2,1)S(1)}, bf16[32,16,3072]{2,1,0:T(8,128)(2,1)S(1)}, u32[]{:S(2)}, u32[]{:S(2)}) collective-permute-start(bf16[32,16,3072]{2,1,0:T(8,128)(2,1)S(1)} %constant_dynamic-update-slice_fusion.5), channel_id=1, source_target_pairs={{0,2},{2,0},{4,6},{6,4},{8,10},{10,8},{12,14},{14,12},{16,18},{18,... | collective-permute-start | bytes 9437192 | tf_op jit(solution)/shard_map/ppermute | solution.py:675
  134.4 12.9 %collective-permute-start.29 = (bf16[144,1024]{1,0:T(8,128)(2,1)S(1)}, bf16[144,1024]{1,0:T(8,128)(2,1)S(1)}, u32[]{:S(2)}, u32[]{:S(2)}) collective-permute-start(bf16[144,1024]{1,0:T(8,128)(2,1)S(1)} %slice.675), channel_id=1, source_target_pairs={{0,124},{2,126},{4,8},{6,10},{8,4},{10,6},{12,16},{14,18},{16,12},... | collective-permute-start | bytes 884744 | tf_op jit(solution)/shard_map/ppermute | solution.py:842
  139.8 30.3 %collective-permute-start.32 = (bf16[32,16,3072]{2,1,0:T(8,128)(2,1)S(1)}, bf16[32,16,3072]{2,1,0:T(8,128)(2,1)S(1)}, u32[]{:S(2)}, u32[]{:S(2)}) collective-permute-start(bf16[32,16,3072]{2,1,0:T(8,128)(2,1)S(1)} %constant_dynamic-update-slice_fusion.7), channel_id=1, source_target_pairs={{0,2},{2,0},{4,6},{6,4},{8,10},{10,8},{12,14},{14,12},{16,18},{18,... | collective-permute-start | bytes 9437192 | tf_op jit(solution)/shard_map/ppermute | solution.py:675
  156.2 10.6 %collective-permute-start.31 = (bf16[144,1024]{1,0:T(8,128)(2,1)S(1)}, bf16[144,1024]{1,0:T(8,128)(2,1)S(1)}, u32[]{:S(2)}, u32[]{:S(2)}) collective-permute-start(bf16[144,1024]{1,0:T(8,128)(2,1)S(1)} %fusion.50.refs_1_), channel_id=1, source_target_pairs={{0,1},{1,0},{2,3},{3,2},{4,5},{5,4},{6,7},{7,6},{8,9},{9,8},{10,11... | collective-permute-start | bytes 884744 | tf_op jit(solution)/shard_map/ppermute | solution.py:796
  159.8 18.1 %collective-permute-start.35 = (bf16[576,1536]{1,0:T(8,128)(2,1)S(1)}, bf16[576,1536]{1,0:T(8,128)(2,1)S(1)}, u32[]{:S(2)}, u32[]{:S(2)}) collective-permute-start(bf16[576,1536]{1,0:T(8,128)(2,1)S(1)} %shard_map.357.refs_0_), channel_id=1, source_target_pairs={{0,2},{2,0},{4,6},{6,4},{8,10},{10,8},{12,14},{14,12},{16,18},{18,... | collective-permute-start | bytes 5308424 | tf_op jit(solution)/shard_map/ppermute | solution.py:675
  160.5 28.2 %collective-permute-start.34 = (bf16[1536,256]{1,0:T(8,128)(2,1)S(1)}, bf16[1536,256]{1,0:T(8,128)(2,1)S(1)}, u32[]{:S(2)}, u32[]{:S(2)}) collective-permute-start(bf16[1536,256]{1,0:T(8,128)(2,1)S(1)} %bitcast.151), channel_id=1, source_target_pairs={{0,2},{2,0},{4,6},{6,4},{8,10},{10,8},{12,14},{14,12},{16,18},{18,... | collective-permute-start | bytes 2359304 | tf_op jit(solution)/shard_map/ppermute | solution.py:675
  175.1 13.3 %collective-permute-start.33 = (bf16[144,1024]{1,0:T(8,128)(2,1)S(1)}, bf16[144,1024]{1,0:T(8,128)(2,1)S(1)}, u32[]{:S(2)}, u32[]{:S(2)}) collective-permute-start(bf16[144,1024]{1,0:T(8,128)(2,1)S(1)} %fusion.55.own_ref), channel_id=1, source_target_pairs={{0,1},{1,0},{2,3},{3,2},{4,5},{5,4},{6,7},{7,6},{8,9},{9,8},{10,11... | collective-permute-start | bytes 884744 | tf_op jit(solution)/shard_map/ppermute | solution.py:796
  203.8 13.4 %collective-permute-start.37 = (bf16[6,24,1536]{2,1,0:T(8,128)(2,1)S(1)}, bf16[6,24,1536]{2,1,0:T(8,128)(2,1)S(1)}, u32[]{:S(2)}, u32[]{:S(2)}) collective-permute-start(bf16[6,24,1536]{2,1,0:T(8,128)(2,1)S(1)} %bitcast.148), channel_id=1, source_target_pairs={{0,1},{1,0},{2,3},{3,2},{4,5},{5,4},{6,7},{7,6},{8,9},{9,8},{10,11... | collective-permute-start | bytes 1327112 | tf_op jit(solution)/shard_map/ppermute | solution.py:796
  223.5 42.7 %collective-permute-start.41 = (bf16[12,48,1536]{2,1,0:T(8,128)(2,1)}, bf16[12,48,1536]{2,1,0:T(8,128)(2,1)}, u32[]{:S(2)}, u32[]{:S(2)}) collective-permute-start(bf16[12,48,1536]{2,1,0:T(8,128)(2,1)} %bitcast.30.own_ref), channel_id=1, source_target_pairs={{0,1},{1,0},{2,3},{3,2},{4,5},{5,4},{6,7},{7,6},{8,9},{9,8},{10,11... | collective-permute-start | bytes 5308424 | tf_op jit(solution)/shard_map/ppermute | solution.py:796
  239.3 32.5 %collective-permute-start.39 = (bf16[1,24,1024]{2,1,0:T(8,128)(2,1)}, bf16[1,24,1024]{2,1,0:T(8,128)(2,1)}, u32[]{:S(2)}, u32[]{:S(2)}) collective-permute-start(bf16[1,24,1024]{2,1,0:T(8,128)(2,1)} %get-tuple-element.384), channel_id=1, source_target_pairs={{0,2},{2,4},{4,6},{6,8},{8,10},{10,12},{12,14},{14,16},{16,18},{18... | collective-permute-start | bytes 147464 | tf_op jit(solution)/shard_map/ppermute | solution.py:809
  239.3 32.5 %collective-permute-start.40 = (bf16[1,24,1024]{2,1,0:T(8,128)(2,1)}, bf16[1,24,1024]{2,1,0:T(8,128)(2,1)}, u32[]{:S(2)}, u32[]{:S(2)}) collective-permute-start(bf16[1,24,1024]{2,1,0:T(8,128)(2,1)} %get-tuple-element.383), channel_id=1, source_target_pairs={{2,0},{4,2},{6,4},{8,6},{10,8},{12,10},{14,12},{16,14},{18,16},{20... | collective-permute-start | bytes 147464 | tf_op jit(solution)/shard_map/ppermute | solution.py:810
  276.1 29.8 %collective-permute-start.45 = (bf16[576,1536]{1,0:T(8,128)(2,1)}, bf16[576,1536]{1,0:T(8,128)(2,1)}, u32[]{:S(2)}, u32[]{:S(2)}) collective-permute-start(bf16[576,1536]{1,0:T(8,128)(2,1)} %copy-done.80), channel_id=1, source_target_pairs={{0,2},{2,0},{4,6},{6,4},{8,10},{10,8},{12,14},{14,12},{16,18},{18,... | collective-permute-start | bytes 5308424 | tf_op jit(solution)/shard_map/ppermute | solution.py:675
  277.1 7.3 %collective-permute-start.42 = (bf16[6,24,512]{2,1,0:T(8,128)(2,1)}, bf16[6,24,512]{2,1,0:T(8,128)(2,1)}, u32[]{:S(2)}, u32[]{:S(2)}) collective-permute-start(bf16[6,24,512]{2,1,0:T(8,128)(2,1)} %get-tuple-element.391), channel_id=1, source_target_pairs={{0,1},{1,0},{2,3},{3,2},{4,5},{5,4},{6,7},{7,6},{8,9},{9,8},{10,11... | collective-permute-start | bytes 442376 | tf_op jit(solution)/shard_map/ppermute | solution.py:796
  302.8 9.3 %collective-permute-start.44 = (bf16[144,1024]{1,0:T(8,128)(2,1)S(1)}, bf16[144,1024]{1,0:T(8,128)(2,1)S(1)}, u32[]{:S(2)}, u32[]{:S(2)}) collective-permute-start(bf16[144,1024]{1,0:T(8,128)(2,1)S(1)} %fusion.57.own_ref), channel_id=1, source_target_pairs={{0,1},{1,0},{2,3},{3,2},{4,5},{5,4},{6,7},{7,6},{8,9},{9,8},{10,11... | collective-permute-start | bytes 884744 | tf_op jit(solution)/shard_map/ppermute | solution.py:796
  312.1 51.1 %collective-permute-start.49 = (bf16[32,16,3072]{2,1,0:T(8,128)(2,1)}, bf16[32,16,3072]{2,1,0:T(8,128)(2,1)}, u32[]{:S(2)}, u32[]{:S(2)}) collective-permute-start(bf16[32,16,3072]{2,1,0:T(8,128)(2,1)} %bitcast.42), channel_id=1, source_target_pairs={{0,2},{2,0},{4,6},{6,4},{8,10},{10,8},{12,14},{14,12},{16,18},{18,... | collective-permute-start | bytes 9437192 | tf_op jit(solution)/shard_map/ppermute | solution.py:675
  314.7 14.7 %collective-permute-start.50 = (bf16[1536,256]{1,0:T(8,128)(2,1)S(1)}, bf16[1536,256]{1,0:T(8,128)(2,1)S(1)}, u32[]{:S(2)}, u32[]{:S(2)}) collective-permute-start(bf16[1536,256]{1,0:T(8,128)(2,1)S(1)} %select_convert_fusion), channel_id=1, source_target_pairs={{0,2},{2,0},{4,6},{6,4},{8,10},{10,8},{12,14},{14,12},{16,18},{18,... | collective-permute-start | bytes 2359304 | tf_op jit(solution)/shard_map/ppermute | solution.py:675
  325.2 48.2 %collective-permute-start.48 = (bf16[576,1536]{1,0:T(8,128)(2,1)S(1)}, bf16[576,1536]{1,0:T(8,128)(2,1)S(1)}, u32[]{:S(2)}, u32[]{:S(2)}) collective-permute-start(bf16[576,1536]{1,0:T(8,128)(2,1)S(1)} %add_convert_fusion.own_ref), channel_id=1, source_target_pairs={{0,1},{1,0},{2,3},{3,2},{4,5},{5,4},{6,7},{7,6},{8,9},{9,8},{10,11... | collective-permute-start | bytes 5308424 | tf_op jit(solution)/shard_map/ppermute | solution.py:796
  332.1 36.9 %collective-permute-start.47 = (bf16[144,1024]{1,0:T(8,128)(2,1)}, bf16[144,1024]{1,0:T(8,128)(2,1)}, u32[]{:S(2)}, u32[]{:S(2)}) collective-permute-start(bf16[144,1024]{1,0:T(8,128)(2,1)} %slice.969), channel_id=1, source_target_pairs={{0,124},{2,126},{4,8},{6,10},{8,4},{10,6},{12,16},{14,18},{16,12},... | collective-permute-start | bytes 884744 | tf_op jit(solution)/shard_map/ppermute | solution.py:842
  381.3 19.1 %collective-permute-start.52 = (bf16[32,16,3072]{2,1,0:T(8,128)(2,1)S(1)}, bf16[32,16,3072]{2,1,0:T(8,128)(2,1)S(1)}, u32[]{:S(2)}, u32[]{:S(2)}) collective-permute-start(bf16[32,16,3072]{2,1,0:T(8,128)(2,1)S(1)} %bitcast.150), channel_id=1, source_target_pairs={{0,2},{2,0},{4,6},{6,4},{8,10},{10,8},{12,14},{14,12},{16,18},{18,... | collective-permute-start | bytes 9437192 | tf_op jit(solution)/shard_map/ppermute | solution.py:675
  384.5 24.4 %collective-permute-start.51 = (bf16[144,1024]{1,0:T(8,128)(2,1)S(1)}, bf16[144,1024]{1,0:T(8,128)(2,1)S(1)}, u32[]{:S(2)}, u32[]{:S(2)}) collective-permute-start(bf16[144,1024]{1,0:T(8,128)(2,1)S(1)} %fusion.53.own_ref), channel_id=1, source_target_pairs={{0,1},{1,0},{2,3},{3,2},{4,5},{5,4},{6,7},{7,6},{8,9},{9,8},{10,11... | collective-permute-start | bytes 884744 | tf_op jit(solution)/shard_map/ppermute | solution.py:796
  387.9 12.5 %collective-permute-start.56 = (bf16[3,48,1536]{2,1,0:T(8,128)(2,1)S(1)}, bf16[3,48,1536]{2,1,0:T(8,128)(2,1)S(1)}, u32[]{:S(2)}, u32[]{:S(2)}) collective-permute-start(bf16[3,48,1536]{2,1,0:T(8,128)(2,1)S(1)} %get-tuple-element.348), channel_id=1, source_target_pairs={{2,0},{4,2},{6,4},{8,6},{10,8},{12,10},{14,12},{16,14},{18,16},{20... | collective-permute-start | bytes 1327112 | tf_op jit(solution)/shard_map/ppermute | solution.py:810
  388.4 59.3 %collective-permute-start.54 = (bf16[16,16,3072]{2,1,0:T(8,128)(2,1)}, bf16[16,16,3072]{2,1,0:T(8,128)(2,1)}, u32[]{:S(2)}, u32[]{:S(2)}) collective-permute-start(bf16[16,16,3072]{2,1,0:T(8,128)(2,1)} %get-tuple-element.236), channel_id=1, source_target_pairs={{0,4},{2,6},{4,0},{6,2},{8,12},{10,14},{12,8},{14,10},{16,20},{18,... | collective-permute-start | bytes 4718600 | tf_op jit(solution)/shard_map/ppermute | solution.py:675
  400.3 47.4 %collective-permute-start.57 = (bf16[16,48,1152]{2,1,0:T(8,128)(2,1)}, bf16[16,48,1152]{2,1,0:T(8,128)(2,1)}, u32[]{:S(2)}, u32[]{:S(2)}) collective-permute-start(bf16[16,48,1152]{2,1,0:T(8,128)(2,1)} %get-tuple-element.244), channel_id=1, source_target_pairs={{0,12},{2,14},{4,8},{6,10},{8,4},{10,6},{12,0},{14,2},{16,28},{18,... | collective-permute-start | bytes 5308424 | tf_op jit(solution)/shard_map/ppermute | solution.py:675
  400.3 47.4 %collective-permute-start.58 = (bf16[16,48,1152]{2,1,0:T(8,128)(2,1)}, bf16[16,48,1152]{2,1,0:T(8,128)(2,1)}, u32[]{:S(2)}, u32[]{:S(2)}) collective-permute-start(bf16[16,48,1152]{2,1,0:T(8,128)(2,1)} %get-tuple-element.245), channel_id=1, source_target_pairs={{0,16},{2,18},{4,20},{6,22},{8,24},{10,26},{12,28},{14,30},{16,0},... | collective-permute-start | bytes 5308424 | tf_op jit(solution)/shard_map/ppermute | solution.py:675
  400.3 47.3 %collective-permute-start.59 = (bf16[16,48,1024]{2,1,0:T(8,128)(2,1)}, bf16[16,48,1024]{2,1,0:T(8,128)(2,1)}, u32[]{:S(2)}, u32[]{:S(2)}) collective-permute-start(bf16[16,48,1024]{2,1,0:T(8,128)(2,1)} %get-tuple-element.246), channel_id=1, source_target_pairs={{0,48},{2,50},{4,52},{6,54},{8,56},{10,58},{12,60},{14,62},{16,32}... | collective-permute-start | bytes 4718600 | tf_op jit(solution)/shard_map/ppermute | solution.py:675
  408.8 38.9 %collective-permute-start.53 = (bf16[16,16,3072]{2,1,0:T(8,128)(2,1)}, bf16[16,16,3072]{2,1,0:T(8,128)(2,1)}, u32[]{:S(2)}, u32[]{:S(2)}) collective-permute-start(bf16[16,16,3072]{2,1,0:T(8,128)(2,1)} %get-tuple-element.341), channel_id=1, source_target_pairs={{0,64},{2,66},{4,68},{6,70},{8,72},{10,74},{12,76},{14,78},{16,80}... | collective-permute-start | bytes 4718600 | tf_op jit(solution)/shard_map/ppermute | solution.py:675
  426.7 20.9 %all-to-all-start = ((bf16[64,16,128]{2,1,0:T(8,128)(2,1)}), bf16[64,16,128]{2,1,0:T(8,128)(2,1)S(1)}, u32[]{:S(2)}, u32[]{:S(2)}) async-start(bf16[64,16,128]{2,1,0:T(8,128)(2,1)} %pad.16), calls=%async_computation | async-start | bytes 524288 | tf_op jit(solution)/shard_map/all_to_all | solution.py:1072
  449.4 35.7 %collective-permute-start.64 = (bf16[8,48,1024]{2,1,0:T(8,128)(2,1)S(1)}, bf16[8,48,1024]{2,1,0:T(8,128)(2,1)S(1)}, u32[]{:S(2)}, u32[]{:S(2)}) collective-permute-start(bf16[8,48,1024]{2,1,0:T(8,128)(2,1)S(1)} %get-tuple-element.335), channel_id=1, source_target_pairs={{0,16},{2,18},{4,20},{6,22},{8,24},{10,26},{12,28},{14,30},{16,0},... | collective-permute-start | bytes 2359304 | tf_op jit(solution)/shard_map/ppermute | solution.py:675
  452.6 32.6 %collective-permute-start.63 = (bf16[8,48,1152]{2,1,0:T(8,128)(2,1)S(1)}, bf16[8,48,1152]{2,1,0:T(8,128)(2,1)S(1)}, u32[]{:S(2)}, u32[]{:S(2)}) collective-permute-start(bf16[8,48,1152]{2,1,0:T(8,128)(2,1)S(1)} %get-tuple-element.331), channel_id=1, source_target_pairs={{0,12},{2,14},{4,8},{6,10},{8,4},{10,6},{12,0},{14,2},{16,28},{18,... | collective-permute-start | bytes 2654216 | tf_op jit(solution)/shard_map/ppermute | solution.py:675
  456.7 28.4 %collective-permute-start.62 = (bf16[8,48,1152]{2,1,0:T(8,128)(2,1)S(1)}, bf16[8,48,1152]{2,1,0:T(8,128)(2,1)S(1)}, u32[]{:S(2)}, u32[]{:S(2)}) collective-permute-start(bf16[8,48,1152]{2,1,0:T(8,128)(2,1)S(1)} %get-tuple-element.333), channel_id=1, source_target_pairs={{0,4},{2,6},{4,0},{6,2},{8,12},{10,14},{12,8},{14,10},{16,20},{18,... | collective-permute-start | bytes 2654216 | tf_op jit(solution)/shard_map/ppermute | solution.py:675
  458.5 26.6 %collective-permute-start.61 = (bf16[8,16,3072]{2,1,0:T(8,128)(2,1)S(1)}, bf16[8,16,3072]{2,1,0:T(8,128)(2,1)S(1)}, u32[]{:S(2)}, u32[]{:S(2)}) collective-permute-start(bf16[8,16,3072]{2,1,0:T(8,128)(2,1)S(1)} %get-tuple-element.337), channel_id=1, source_target_pairs={{0,64},{2,66},{4,68},{6,70},{8,72},{10,74},{12,76},{14,78},{16,80}... | collective-permute-start | bytes 2359304 | tf_op jit(solution)/shard_map/ppermute | solution.py:675
  461.5 23.6 %collective-permute-start.60 = (bf16[8,16,3072]{2,1,0:T(8,128)(2,1)S(1)}, bf16[8,16,3072]{2,1,0:T(8,128)(2,1)S(1)}, u32[]{:S(2)}, u32[]{:S(2)}) collective-permute-start(bf16[8,16,3072]{2,1,0:T(8,128)(2,1)S(1)} %get-tuple-element.339), channel_id=1, source_target_pairs={{0,48},{2,50},{4,52},{6,54},{8,56},{10,58},{12,60},{14,62},{16,32}... | collective-permute-start | bytes 2359304 | tf_op jit(solution)/shard_map/ppermute | solution.py:675
  485.2 11.6 %collective-permute-start.69 = (bf16[4,48,1024]{2,1,0:T(8,128)(2,1)S(1)}, bf16[4,48,1024]{2,1,0:T(8,128)(2,1)S(1)}, u32[]{:S(2)}, u32[]{:S(2)}) collective-permute-start(bf16[4,48,1024]{2,1,0:T(8,128)(2,1)S(1)} %get-tuple-element.353), channel_id=1, source_target_pairs={{0,12},{2,14},{4,8},{6,10},{8,4},{10,6},{12,0},{14,2},{16,28},{18,... | collective-permute-start | bytes 1179656 | tf_op jit(solution)/shard_map/ppermute | solution.py:675
  486.3 13.5 %collective-permute-start.68 = (bf16[4,48,1152]{2,1,0:T(8,128)(2,1)S(1)}, bf16[4,48,1152]{2,1,0:T(8,128)(2,1)S(1)}, u32[]{:S(2)}, u32[]{:S(2)}) collective-permute-start(bf16[4,48,1152]{2,1,0:T(8,128)(2,1)S(1)} %get-tuple-element.345), channel_id=1, source_target_pairs={{0,4},{2,6},{4,0},{6,2},{8,12},{10,14},{12,8},{14,10},{16,20},{18,... | collective-permute-start | bytes 1327112 | tf_op jit(solution)/shard_map/ppermute | solution.py:675
  487.0 12.8 %collective-permute-start.67 = (bf16[4,48,1152]{2,1,0:T(8,128)(2,1)S(1)}, bf16[4,48,1152]{2,1,0:T(8,128)(2,1)S(1)}, u32[]{:S(2)}, u32[]{:S(2)}) collective-permute-start(bf16[4,48,1152]{2,1,0:T(8,128)(2,1)S(1)} %get-tuple-element.347), channel_id=1, source_target_pairs={{0,64},{2,66},{4,68},{6,70},{8,72},{10,74},{12,76},{14,78},{16,80}... | collective-permute-start | bytes 1327112 | tf_op jit(solution)/shard_map/ppermute | solution.py:675
  488.2 10.9 %collective-permute-start.66 = (bf16[4,16,3072]{2,1,0:T(8,128)(2,1)S(1)}, bf16[4,16,3072]{2,1,0:T(8,128)(2,1)S(1)}, u32[]{:S(2)}, u32[]{:S(2)}) collective-permute-start(bf16[4,16,3072]{2,1,0:T(8,128)(2,1)S(1)} %get-tuple-element.355), channel_id=1, source_target_pairs={{0,48},{2,50},{4,52},{6,54},{8,56},{10,58},{12,60},{14,62},{16,32}... | collective-permute-start | bytes 1179656 | tf_op jit(solution)/shard_map/ppermute | solution.py:675
  490.3 9.4 %collective-permute-start.65 = (bf16[4,16,3072]{2,1,0:T(8,128)(2,1)S(1)}, bf16[4,16,3072]{2,1,0:T(8,128)(2,1)S(1)}, u32[]{:S(2)}, u32[]{:S(2)}) collective-permute-start(bf16[4,16,3072]{2,1,0:T(8,128)(2,1)S(1)} %get-tuple-element.356), channel_id=1, source_target_pairs={{0,16},{2,18},{4,20},{6,22},{8,24},{10,26},{12,28},{14,30},{16,0},... | collective-permute-start | bytes 1179656 | tf_op jit(solution)/shard_map/ppermute | solution.py:675
  500.6 8.3 %collective-permute-start.73 = (bf16[2,48,1152]{2,1,0:T(8,128)(2,1)S(1)}, bf16[2,48,1152]{2,1,0:T(8,128)(2,1)S(1)}, u32[]{:S(2)}, u32[]{:S(2)}) collective-permute-start(bf16[2,48,1152]{2,1,0:T(8,128)(2,1)S(1)} %get-tuple-element.359), channel_id=1, source_target_pairs={{0,64},{2,66},{4,68},{6,70},{8,72},{10,74},{12,76},{14,78},{16,80}... | collective-permute-start | bytes 663560 | tf_op jit(solution)/shard_map/ppermute | solution.py:675
  500.9 7.9 %collective-permute-start.72 = (bf16[2,48,1152]{2,1,0:T(8,128)(2,1)S(1)}, bf16[2,48,1152]{2,1,0:T(8,128)(2,1)S(1)}, u32[]{:S(2)}, u32[]{:S(2)}) collective-permute-start(bf16[2,48,1152]{2,1,0:T(8,128)(2,1)S(1)} %get-tuple-element.361), channel_id=1, source_target_pairs={{0,48},{2,50},{4,52},{6,54},{8,56},{10,58},{12,60},{14,62},{16,32}... | collective-permute-start | bytes 663560 | tf_op jit(solution)/shard_map/ppermute | solution.py:675
  508.9 7.6 %collective-permute-start.79 = (bf16[1,48,1024]{2,1,0:T(8,128)(2,1)S(1)}, bf16[1,48,1024]{2,1,0:T(8,128)(2,1)S(1)}, u32[]{:S(2)}, u32[]{:S(2)}) collective-permute-start(bf16[1,48,1024]{2,1,0:T(8,128)(2,1)S(1)} %slice_add_fusion.42), channel_id=1, source_target_pairs={{0,64},{2,66},{4,68},{6,70},{8,72},{10,74},{12,76},{14,78},{16,80}... | collective-permute-start | bytes 294920 | tf_op jit(solution)/shard_map/ppermute | solution.py:675
  510.3 7.6 %collective-permute-start.78 = (bf16[1,48,1152]{2,1,0:T(8,128)(2,1)S(1)}, bf16[1,48,1152]{2,1,0:T(8,128)(2,1)S(1)}, u32[]{:S(2)}, u32[]{:S(2)}) collective-permute-start(bf16[1,48,1152]{2,1,0:T(8,128)(2,1)S(1)} %slice_add_fusion.38), channel_id=1, source_target_pairs={{0,48},{2,50},{4,52},{6,54},{8,56},{10,58},{12,60},{14,62},{16,32}... | collective-permute-start | bytes 331784 | tf_op jit(solution)/shard_map/ppermute | solution.py:675
  511.7 6.1 %collective-permute-start.77 = (bf16[1,48,1152]{2,1,0:T(8,128)(2,1)S(1)}, bf16[1,48,1152]{2,1,0:T(8,128)(2,1)S(1)}, u32[]{:S(2)}, u32[]{:S(2)}) collective-permute-start(bf16[1,48,1152]{2,1,0:T(8,128)(2,1)S(1)} %slice_add_fusion.39), channel_id=1, source_target_pairs={{0,16},{2,18},{4,20},{6,22},{8,24},{10,26},{12,28},{14,30},{16,0},... | collective-permute-start | bytes 331784 | tf_op jit(solution)/shard_map/ppermute | solution.py:675
  518.2 8.5 %collective-permute-start.80 = (bf16[24,3328]{1,0:T(8,128)(2,1)S(1)}, bf16[24,3328]{1,0:T(8,128)(2,1)S(1)}, u32[]{:S(2)}, u32[]{:S(2)}) collective-permute-start(bf16[24,3328]{1,0:T(8,128)(2,1)S(1)} %select_convert_fusion.1), channel_id=1, source_target_pairs={{0,2},{2,0},{4,6},{6,4},{8,10},{10,8},{12,14},{14,12},{16,18},{18,... | collective-permute-start | bytes 479240 | tf_op jit(solution)/shard_map/ppermute | solution.py:675
  (135 other events, 1233.9 us)
